TPU v7x, 32 devices: a whole 2x2x4 slice. The times are simulated.
32 devices in a mesh: pipe: 2 (over y), dp: 16 (over z, x, core).
Axes of the slice: x: 2, y: 2, z: 4, core: 2. Of those that a mesh axis runs over, the one named last changes fastest.
Arguments:
- hidden_in: bfloat16 [20480, 768], P('dp'), may hold values from -9 to 9
- attend_weight: bfloat16 [2, 768, 2304], P('pipe'), may hold values from -0.21875 to 0.21875
- attend_bias: float32 [2, 1536], P('pipe'), may hold values from -3 to 3
- mixing_weight: bfloat16 [2, 768, 768], P('pipe'), may hold values from -0.875 to 0.875
- mixing_bias: float32 [2, 768], P('pipe'), may hold values from -3 to 3
- norm_gain: float32 [2, 2, 768], P('pipe'), may hold values from 0.1 to 1.9
- norm_shift: float32 [2, 2, 768], P('pipe'), may hold values from -3 to 3
- expand_weight: bfloat16 [2, 768, 3072], P('pipe'), may hold values from -0.21875 to 0.21875
- expand_bias: float32 [2, 3072], P('pipe'), may hold values from -3 to 3
- reduce_weight: bfloat16 [2, 3072, 768], P('pipe'), may hold values from -0.109375 to 0.109375
- reduce_bias: float32 [2, 768], P('pipe'), may hold values from -3 to 3
- colbert_weight: bfloat16 [768, 128], replicated, may hold values from -0.21875 to 0.21875
- pass_lengths: int32 [32, 4], P('dp'), may hold values from 16 to 448, as said below
- positives: int32 [32, 4], P('dp'), may hold values from 0 to 3
Outputs:
- grad_attend_weight: float32 [2, 768, 2304], P('pipe')
- grad_attend_bias: float32 [2, 1536], P('pipe')
- grad_mixing_weight: float32 [2, 768, 768], P('pipe')
- grad_mixing_bias: float32 [2, 768], P('pipe')
- grad_norm_gain: float32 [2, 2, 768], P('pipe')
- grad_norm_shift: float32 [2, 2, 768], P('pipe')
- grad_expand_weight: float32 [2, 768, 3072], P('pipe')
- grad_expand_bias: float32 [2, 3072], P('pipe')
- grad_reduce_weight: float32 [2, 3072, 768], P('pipe')
- grad_reduce_bias: float32 [2, 768], P('pipe')
- grad_colbert_weight: float32 [768, 128], replicated
- loss: float32 [32], P('dp')
- stats: float32 [32, 2, 3], P('dp')
Inputs may be any that keep to these rules, and one draw needn't show every extreme that they name: `pass_lengths`: in each micro-batch the 4 passage lengths sum to at most 512; some micro-batch has a passage of exactly 448 tokens.
All inputs are finite; a program needn't handle non-finite values.
Results may differ from a plain program's by a relative error of at most 0.023.
Values may be sent and summed in bfloat16 or wider, within the bound.
No kernel may reach another device: no remote copies, remote signals or barrier semaphores. Data moves between devices by JAX's collectives and lax.ppermute only.
A program may use at most 320 MiB of HBM per device.

v0:
```python
import jax
import jax.numpy as jnp
from jax import lax
from jax.sharding import PartitionSpec as P

HEAD_DIM = 64
QLEN = 32
NQ = 4
NP = 4
PSLOTS = 512


LAYER_EPSILON = 1e-12
UNIT_EPSILON = 1e-06
SMOOTHING = 0.05
LOGIT_SCALE = 4.0
ROOT_HALF = 0.7071067811865476
NORMAL_PEAK = 0.3989422804014327
PRECISE = lax.Precision.HIGHEST


def passed_along(array, axis, by):
    count = lax.axis_size(axis)
    pairs = [(i, i + by) for i in range(count) if 0 <= i + by < count]
    return lax.ppermute(array, axis, pairs)


def matmul_plain(left, right):
    return jnp.dot(left, right, preferred_element_type=jnp.float32)


def matmul_rows(left, right):
    return lax.dot_general(
        left, right, (((0,), (0,)), ((), ())), preferred_element_type=jnp.float32
    )


def matmul_cols(left, right):
    return lax.dot_general(
        left, right, (((1,), (1,)), ((), ())), preferred_element_type=jnp.float32
    )


def gelu_exact(values):
    return 0.5 * values * (1.0 + lax.erf(values * ROOT_HALF))


def gelu_slope(values):
    return 0.5 * (1.0 + lax.erf(values * ROOT_HALF)) + values * NORMAL_PEAK * jnp.exp(
        -0.5 * values * values
    )


def layout(lengths):
    end_pos = jnp.cumsum(lengths)
    slot_ids = jnp.arange(PSLOTS, dtype=jnp.int32)
    passage_id = jnp.sum((slot_ids[:, None] >= end_pos[None, :]).astype(jnp.int32), axis=1)
    query_ids = jnp.arange(NQ * QLEN, dtype=jnp.int32) // QLEN
    segment = jnp.concatenate([query_ids, NQ + passage_id])
    usable = (segment < NQ + NP).astype(jnp.float32)
    member = (passage_id[None, :] == jnp.arange(NP, dtype=jnp.int32)[:, None]).astype(jnp.float32)
    return (segment, usable, member)


def norm_forward(resid, gain_row, shift_row):
    centre = resid - jnp.mean(resid, axis=1, keepdims=True)
    inv_std = lax.rsqrt(jnp.mean(centre * centre, axis=1, keepdims=True) + LAYER_EPSILON)
    unit_rows = centre * inv_std
    return (unit_rows * gain_row + shift_row, unit_rows, inv_std)


def norm_backward(grad_out, unit_rows, inv_std, gain_row):
    grad_gain = jnp.sum(grad_out * unit_rows, axis=0)
    grad_shift = jnp.sum(grad_out, axis=0)
    grad_unit = grad_out * gain_row
    centred = grad_unit - jnp.mean(grad_unit, axis=1, keepdims=True)
    grad_in = inv_std * (
        centred - unit_rows * jnp.mean(grad_unit * unit_rows, axis=1, keepdims=True)
    )
    return (grad_in, grad_gain, grad_shift)


def split_heads(joined_b):
    row_count = joined_b.shape[0]
    model_width = joined_b.shape[1] // 3
    head_count = model_width // HEAD_DIM
    pieces = [
        joined_b[:, block_index * model_width : (block_index + 1) * model_width].reshape(
            row_count, head_count, HEAD_DIM
        )
        for block_index in range(3)
    ]
    return (pieces[0], pieces[1], pieces[2])


def scores_of(query_rows, key_rows, segment):
    same_seq = segment[:, None] == segment[None, :]
    scores = jnp.einsum(
        "qhd,khd->hqk", query_rows, key_rows, preferred_element_type=jnp.float32
    ) * HEAD_DIM ** (-0.5)
    return jnp.where(same_seq[None], scores, -1e30)


def attend(joined_b, segment):
    query_rows, key_rows, value_rows = split_heads(joined_b)
    scores = scores_of(query_rows, key_rows, segment)
    row_max = jnp.max(scores, axis=2, keepdims=True)
    exp_terms = jnp.exp(scores - row_max)
    totals = jnp.sum(exp_terms, axis=2, keepdims=True)
    softmax_rows = (exp_terms / totals).astype(jnp.bfloat16)
    context = jnp.einsum(
        "hqk,khd->qhd", softmax_rows, value_rows, preferred_element_type=jnp.float32
    )
    return (context.reshape(context.shape[0], -1), row_max + jnp.log(totals))


def attend_back(joined_b, segment, log_total, grad_context_b):
    query_rows, key_rows, value_rows = split_heads(joined_b)
    scores = scores_of(query_rows, key_rows, segment)
    softmax_rows = jnp.exp(scores - log_total)
    grad_heads = grad_context_b.reshape(value_rows.shape)
    grad_probs = jnp.einsum(
        "qhd,khd->hqk", grad_heads, value_rows, preferred_element_type=jnp.float32
    )
    grad_scores = softmax_rows * (
        grad_probs - jnp.sum(softmax_rows * grad_probs, axis=2, keepdims=True)
    )
    grad_scores_b = grad_scores.astype(jnp.bfloat16)
    head_scale = HEAD_DIM ** (-0.5)
    grad_query = (
        jnp.einsum("hqk,khd->qhd", grad_scores_b, key_rows, preferred_element_type=jnp.float32)
        * head_scale
    )
    grad_key = (
        jnp.einsum("hqk,qhd->khd", grad_scores_b, query_rows, preferred_element_type=jnp.float32)
        * head_scale
    )
    grad_value = jnp.einsum(
        "hqk,qhd->khd",
        softmax_rows.astype(jnp.bfloat16),
        grad_heads,
        preferred_element_type=jnp.float32,
    )
    row_count = joined_b.shape[0]
    return jnp.concatenate(
        [
            grad_query.reshape(row_count, -1),
            grad_key.reshape(row_count, -1),
            grad_value.reshape(row_count, -1),
        ],
        axis=1,
    )


def layer_forward(inputs, weights, segment):
    (
        attend_weight,
        attend_bias,
        mixing_weight,
        mixing_bias,
        norm_gain,
        norm_shift,
        expand_weight,
        expand_bias,
        reduce_weight,
        reduce_bias,
    ) = weights
    model_width = inputs.shape[1]
    joined_bias = jnp.concatenate(
        [
            attend_bias[:model_width],
            jnp.zeros((model_width,), jnp.float32),
            attend_bias[model_width:],
        ]
    )
    joined_b = (matmul_plain(inputs, attend_weight) + joined_bias).astype(jnp.bfloat16)
    context, log_total = attend(joined_b, segment)
    context_b = context.astype(jnp.bfloat16)
    branch_one = matmul_plain(context_b, mixing_weight) + mixing_bias
    hidden, unit_one, scale_one = norm_forward(
        inputs.astype(jnp.float32) + branch_one, norm_gain[0], norm_shift[0]
    )
    hidden_b = hidden.astype(jnp.bfloat16)
    inner = matmul_plain(hidden_b, expand_weight) + expand_bias
    active_b = gelu_exact(inner).astype(jnp.bfloat16)
    branch_two = matmul_plain(active_b, reduce_weight) + reduce_bias
    output, unit_two, scale_two = norm_forward(
        hidden_b.astype(jnp.float32) + branch_two, norm_gain[1], norm_shift[1]
    )
    stored = (
        inputs,
        joined_b,
        log_total,
        context_b,
        unit_one,
        scale_one,
        hidden_b,
        inner,
        active_b,
        unit_two,
        scale_two,
    )
    return (output, branch_one, branch_two, stored)


def layer_backward(grad_output, stored, weights, segment):
    (
        attend_weight,
        attend_bias,
        mixing_weight,
        mixing_bias,
        norm_gain,
        norm_shift,
        expand_weight,
        expand_bias,
        reduce_weight,
        reduce_bias,
    ) = weights
    (
        inputs,
        joined_b,
        log_total,
        context_b,
        unit_one,
        scale_one,
        hidden_b,
        inner,
        active_b,
        unit_two,
        scale_two,
    ) = stored
    grad_resid_two, gain_two, shift_two = norm_backward(
        grad_output, unit_two, scale_two, norm_gain[1]
    )
    grad_two_b = grad_resid_two.astype(jnp.bfloat16)
    grad_active = matmul_cols(grad_two_b, reduce_weight)
    grad_inner_b = (grad_active * gelu_slope(inner)).astype(jnp.bfloat16)
    grad_hidden = grad_resid_two + matmul_cols(grad_inner_b, expand_weight)
    grad_resid_one, gain_one, shift_one = norm_backward(
        grad_hidden, unit_one, scale_one, norm_gain[0]
    )
    grad_one_b = grad_resid_one.astype(jnp.bfloat16)
    grad_context_b = matmul_cols(grad_one_b, mixing_weight).astype(jnp.bfloat16)
    grad_joined_b = attend_back(joined_b, segment, log_total, grad_context_b).astype(jnp.bfloat16)
    grad_inputs = grad_resid_one + matmul_cols(grad_joined_b, attend_weight)
    model_width = inputs.shape[1]
    joined_sums = jnp.sum(grad_joined_b, axis=0, dtype=jnp.float32)
    grad_attend_bias = jnp.concatenate([joined_sums[:model_width], joined_sums[2 * model_width :]])
    small_grads = (
        grad_attend_bias,
        jnp.sum(grad_one_b, axis=0, dtype=jnp.float32),
        jnp.stack([gain_one, gain_two]),
        jnp.stack([shift_one, shift_two]),
        jnp.sum(grad_inner_b, axis=0, dtype=jnp.float32),
        jnp.sum(grad_two_b, axis=0, dtype=jnp.float32),
    )
    return (grad_inputs, (grad_joined_b, grad_one_b, grad_inner_b, grad_two_b), small_grads)


def colbert_loss(output_b, colbert_weight, lengths, member, usable, chosen, grad_scale):
    embedded = matmul_plain(output_b, colbert_weight)
    inv_norm = lax.rsqrt(jnp.sum(embedded * embedded, axis=1, keepdims=True) + UNIT_EPSILON)
    unit_vec = embedded * inv_norm
    unit_b = unit_vec.astype(jnp.bfloat16)
    query_count = NQ * QLEN
    similar = matmul_cols(unit_b[:query_count], unit_b[query_count:])
    scaled = similar / SMOOTHING
    passage_ok = usable[query_count:] > 0.5
    row_max = jnp.max(jnp.where(passage_ok[None, :], scaled, -1e30), axis=1, keepdims=True)
    exp_terms = jnp.exp(scaled - row_max)
    totals = jnp.dot(exp_terms, member.T, precision=PRECISE, preferred_element_type=jnp.float32)
    smooth = SMOOTHING * (jnp.log(totals) + row_max - jnp.log(lengths.astype(jnp.float32))[None, :])
    scores = LOGIT_SCALE * jnp.sum(smooth.reshape(NQ, QLEN, NP), axis=1)
    score_max = jnp.max(scores, axis=1, keepdims=True)
    score_exp = jnp.exp(scores - score_max)
    score_total = jnp.sum(score_exp, axis=1, keepdims=True)
    onehot = (chosen[:, None] == jnp.arange(NP, dtype=jnp.int32)[None, :]).astype(jnp.float32)
    pack_loss = jnp.sum(
        jnp.log(score_total[:, 0]) + score_max[:, 0] - jnp.sum(scores * onehot, axis=1)
    )
    grad_scores = (score_exp / score_total - onehot) * grad_scale
    grad_smooth = LOGIT_SCALE * jnp.repeat(grad_scores, QLEN, axis=0)
    grad_totals = grad_smooth * SMOOTHING / totals
    grad_scaled = exp_terms * jnp.dot(
        grad_totals, member, precision=PRECISE, preferred_element_type=jnp.float32
    )
    grad_similar_b = (grad_scaled / SMOOTHING).astype(jnp.bfloat16)
    grad_query = matmul_plain(grad_similar_b, unit_b[query_count:])
    grad_passage = matmul_rows(grad_similar_b, unit_b[:query_count])
    grad_unit = jnp.concatenate([grad_query, grad_passage])
    grad_embed_b = (
        inv_norm * (grad_unit - unit_vec * jnp.sum(grad_unit * unit_vec, axis=1, keepdims=True))
    ).astype(jnp.bfloat16)
    grad_output = matmul_cols(grad_embed_b, colbert_weight)
    return (pack_loss, grad_output, grad_embed_b)


def flatten_rows(leaf):
    return leaf.reshape(-1, leaf.shape[-1])


def shards(
    hidden_in,
    attend_weight,
    attend_bias,
    mixing_weight,
    mixing_bias,
    norm_gain,
    norm_shift,
    expand_weight,
    expand_bias,
    reduce_weight,
    reduce_bias,
    colbert_weight,
    pass_lengths,
    positives,
):
    section_id = lax.axis_index("pipe")
    data_count = lax.axis_size("dp")
    micro_count = pass_lengths.shape[0]
    seq_rows = hidden_in.shape[0] // micro_count
    model_width = hidden_in.shape[1]
    weights = (
        attend_weight[0],
        attend_bias[0],
        mixing_weight[0],
        mixing_bias[0],
        norm_gain[0],
        norm_shift[0],
        expand_weight[0],
        expand_bias[0],
        reduce_weight[0],
        reduce_bias[0],
    )
    layouts = [layout(pass_lengths[micro_index]) for micro_index in range(micro_count)]
    segments = jnp.stack([layout_item[0] for layout_item in layouts])
    usables = jnp.stack([layout_item[1] for layout_item in layouts])
    members = jnp.stack([layout_item[2] for layout_item in layouts])
    grad_scale = 1.0 / (data_count * micro_count * NQ)
    is_first = section_id == 0
    is_last = section_id == 1
    last_weight = is_last.astype(jnp.float32)
    micro_ids = jnp.arange(micro_count, dtype=jnp.int32)
    received = jnp.zeros((seq_rows, model_width), jnp.bfloat16)
    forward_store = []
    squares = jnp.zeros((micro_count, 3), jnp.float32)
    losses = jnp.zeros((micro_count,), jnp.float32)
    for tick_index in range(micro_count + 1):
        offset = tick_index - section_id
        micro_index = jnp.clip(offset, 0, micro_count - 1)
        live_tick = ((offset >= 0) & (offset < micro_count)).astype(jnp.float32)
        slot_weight = (micro_ids == micro_index).astype(jnp.float32) * live_tick
        own_rows = lax.dynamic_slice_in_dim(hidden_in, micro_index * seq_rows, seq_rows, 0)
        inputs = jnp.where(is_first, own_rows, received)
        usable = usables[micro_index]
        output, branch_one, branch_two, stored = layer_forward(
            inputs, weights, segments[micro_index]
        )
        row_mask = usable[:, None]
        inputs_wide = inputs.astype(jnp.float32)
        tick_squares = jnp.stack(
            [
                jnp.sum(row_mask * inputs_wide * inputs_wide),
                jnp.sum(row_mask * branch_one * branch_one),
                jnp.sum(row_mask * branch_two * branch_two),
            ]
        )
        squares = squares + slot_weight[:, None] * tick_squares[None, :]
        output_b = output.astype(jnp.bfloat16)
        pack_loss, grad_output, grad_embed_b = colbert_loss(
            output_b,
            colbert_weight,
            pass_lengths[micro_index],
            members[micro_index],
            usable,
            positives[micro_index],
            grad_scale,
        )
        losses = losses + slot_weight * pack_loss
        forward_store.append((stored, grad_output, output_b, grad_embed_b))
        if tick_index < micro_count:
            received = passed_along(output_b, "pipe", 1)
    forward_stack = jax.tree.map(lambda *leaves: jnp.stack(leaves), *forward_store)
    forward_sel = jax.tree.map(
        lambda leaf: lax.dynamic_slice_in_dim(leaf, section_id, micro_count, 0), forward_stack
    )
    stored_all, loss_grads, outputs_b, grad_embeds_b = forward_sel
    grad_received = jnp.zeros((seq_rows, model_width), jnp.bfloat16)
    backward_store = []
    for tick_index in range(micro_count + 1):
        micro_index = jnp.clip(tick_index - 1 + section_id, 0, micro_count - 1)
        stored = jax.tree.map(lambda leaf: leaf[micro_index], stored_all)
        upstream = jnp.where(is_last, loss_grads[micro_index], grad_received.astype(jnp.float32))
        grad_inputs, big_grads, small_grads = layer_backward(
            upstream, stored, weights, segments[micro_index]
        )
        backward_store.append((big_grads, small_grads))
        if tick_index < micro_count:
            grad_received = passed_along(grad_inputs.astype(jnp.bfloat16), "pipe", -1)
    backward_stack = jax.tree.map(lambda *leaves: jnp.stack(leaves), *backward_store)
    backward_sel = jax.tree.map(
        lambda leaf: lax.dynamic_slice_in_dim(leaf, 1 - section_id, micro_count, 0), backward_stack
    )
    big_sel, small_sel = backward_sel
    grad_joined_all, grad_one_all, grad_inner_all, grad_two_all = big_sel
    small_sums = jax.tree.map(lambda leaf: jnp.sum(leaf, axis=0), small_sel)
    (
        grad_attend_bias,
        grad_mixing_bias,
        grad_gain,
        grad_shift,
        grad_expand_bias,
        grad_reduce_bias,
    ) = small_sums
    inputs_all = stored_all[0]
    context_all = stored_all[3]
    hidden_all = stored_all[6]
    active_all = stored_all[8]
    grad_colbert = matmul_rows(flatten_rows(outputs_b), flatten_rows(grad_embeds_b)) * last_weight
    grad_attend = matmul_rows(flatten_rows(inputs_all), flatten_rows(grad_joined_all))
    grad_mixing = matmul_rows(flatten_rows(context_all), flatten_rows(grad_one_all))
    grad_expand = matmul_rows(flatten_rows(hidden_all), flatten_rows(grad_inner_all))
    grad_reduce = matmul_rows(flatten_rows(active_all), flatten_rows(grad_two_all))
    shares = (
        lax.psum_scatter(grad_attend[None], "dp", scatter_dimension=1, tiled=True),
        lax.psum_scatter(grad_attend_bias[None], "dp", scatter_dimension=1, tiled=True),
        lax.psum_scatter(grad_mixing[None], "dp", scatter_dimension=1, tiled=True),
        lax.psum_scatter(grad_mixing_bias[None], "dp", scatter_dimension=1, tiled=True),
        lax.psum_scatter(grad_gain[None], "dp", scatter_dimension=2, tiled=True),
        lax.psum_scatter(grad_shift[None], "dp", scatter_dimension=2, tiled=True),
        lax.psum_scatter(grad_expand[None], "dp", scatter_dimension=1, tiled=True),
        lax.psum_scatter(grad_expand_bias[None], "dp", scatter_dimension=1, tiled=True),
        lax.psum_scatter(grad_reduce[None], "dp", scatter_dimension=1, tiled=True),
        lax.psum_scatter(grad_reduce_bias[None], "dp", scatter_dimension=1, tiled=True),
        lax.psum_scatter(grad_colbert[None], "dp", scatter_dimension=1, tiled=True),
    )
    summed = (
        lax.all_gather(shares[0].astype(jnp.bfloat16), "dp", axis=1, tiled=True).astype(
            jnp.float32
        ),
        lax.all_gather(shares[1].astype(jnp.bfloat16), "dp", axis=1, tiled=True).astype(
            jnp.float32
        ),
        lax.all_gather(shares[2].astype(jnp.bfloat16), "dp", axis=1, tiled=True).astype(
            jnp.float32
        ),
        lax.all_gather(shares[3].astype(jnp.bfloat16), "dp", axis=1, tiled=True).astype(
            jnp.float32
        ),
        lax.all_gather(shares[4].astype(jnp.bfloat16), "dp", axis=2, tiled=True).astype(
            jnp.float32
        ),
        lax.all_gather(shares[5].astype(jnp.bfloat16), "dp", axis=2, tiled=True).astype(
            jnp.float32
        ),
        lax.all_gather(shares[6].astype(jnp.bfloat16), "dp", axis=1, tiled=True).astype(
            jnp.float32
        ),
        lax.all_gather(shares[7].astype(jnp.bfloat16), "dp", axis=1, tiled=True).astype(
            jnp.float32
        ),
        lax.all_gather(shares[8].astype(jnp.bfloat16), "dp", axis=1, tiled=True).astype(
            jnp.float32
        ),
        lax.all_gather(shares[9].astype(jnp.bfloat16), "dp", axis=1, tiled=True).astype(
            jnp.float32
        ),
        lax.all_gather(shares[10].astype(jnp.bfloat16), "dp", axis=1, tiled=True).astype(
            jnp.float32
        ),
    )
    colbert_data = summed[10][0]
    section_rows = (jnp.arange(2, dtype=jnp.int32) == section_id).astype(jnp.float32)
    square_parts = section_rows[None, :, None] * squares[:, None, :]
    square_sum, loss_sum, colbert_sum = (
        lax.psum(square_parts.astype(jnp.bfloat16), "pipe").astype(jnp.float32),
        lax.psum((losses * last_weight).astype(jnp.bfloat16), "pipe").astype(jnp.float32),
        lax.psum(colbert_data.astype(jnp.bfloat16), "pipe").astype(jnp.float32),
    )
    count_micro = jnp.sum(usables, axis=1)
    stats = jnp.sqrt(square_sum / (count_micro[:, None, None] * model_width))
    loss = loss_sum / NQ
    return (
        summed[0],
        summed[1],
        summed[2],
        summed[3],
        summed[4],
        summed[5],
        summed[6],
        summed[7],
        summed[8],
        summed[9],
        colbert_sum,
        loss,
        stats,
    )


def solution(mesh):
    placed = (
        P("dp", None),
        P("pipe", None, None),
        P("pipe", None),
        P("pipe", None, None),
        P("pipe", None),
        P("pipe", None, None),
        P("pipe", None, None),
        P("pipe", None, None),
        P("pipe", None),
        P("pipe", None, None),
        P("pipe", None),
        P(),
        P("dp", None),
        P("dp", None),
    )
    return jax.shard_map(
        shards,
        mesh=mesh,
        in_specs=placed,
        out_specs=(
            P("pipe", None, None),
            P("pipe", None),
            P("pipe", None, None),
            P("pipe", None),
            P("pipe", None, None),
            P("pipe", None, None),
            P("pipe", None, None),
            P("pipe", None),
            P("pipe", None, None),
            P("pipe", None),
            P(),
            P("dp"),
            P("dp", None, None),
        ),
        check_vma=False,
    )
```

profile of v0, /device:TPU:0, one launch (start us, length us, event | category | flops | bytes accessed | tf_op | source)
XLA Modules:
  0.0 1634.0 jit_solution(17998584361065711991)
XLA Ops:
  29.9 12.0 fusion
  41.9 11.2 fusion.3
  53.1 13.0 fusion.177
  72.9 7.8 add_bitcast_fusion.2
  142.9 12.0 fusion.1
  154.9 11.2 fusion.4
  166.2 13.0 fusion.176
  184.0 7.8 add_bitcast_fusion.1
  237.7 12.0 fusion.2
  249.8 11.2 fusion.5
  262.4 12.8 fusion.175
  280.0 7.8 add_bitcast_fusion
  343.9 9.5 pad_maximum_fusion
  353.4 13.0 convert_reduce_fusion.2
  385.1 11.0 fusion.375
  396.1 12.6 fusion.178
  408.8 13.6 multiply_reduce_fusion.2
  422.3 14.1 multiply_convert_fusion.2
  467.8 11.1 fusion.376
  490.5 8.8 convert_reduce_fusion.1
  510.6 11.9 fusion.181
  522.6 13.9 multiply_reduce_fusion.1
  536.4 14.1 multiply_convert_fusion.1
  571.5 10.9 fusion.377
  596.3 9.9 convert_reduce_fusion
  623.4 20.1 %multiply_reduce_fusion = (f32[12,640]{1,0:T(8,128)S(1)}, f32[12,640,640]{1,2,0:T(8,128)}) fusion(f32[12,640,640]{1,2,0:T(8,128)} %fusion.377, f32[12,640]{1,0:T(8,128)} %get-tuple-element.176, pred[640,640]{0,1:T(8,128)(4,1)} %broadcast_compare_fusion, bf16[640,12,64]{0,2,1:T(8,128)(2,1)} %bitcast.649, bf16[640,12,64]{0,2,1:T(8,128)(2,1)} %bitcast.644), kind=kOutput, calls=%fused_computation.2 | convolution fusion | flops 653713920 | bytes 41758720 | tf_op jit(solution)/shard_map/qhd,khd->hqk/dot_general | solution.py:122
  643.5 18.2 %multiply_convert_fusion = bf16[12,640,640]{1,2,0:T(8,128)(2,1)} fusion(f32[12,640,640]{1,2,0:T(8,128)} %get-tuple-element.241, f32[12,640,640]{1,2,0:T(8,128)} %fusion.377, f32[12,640]{1,0:T(8,128)S(1)} %get-tuple-element.240, f32[12,640]{1,0:T(8,128)S(1)} %copy-done.74, pred[640,640]{0,1:T(8,128)(4,1)S(1)} %copy-done.54), kind=kLoop, calls=%fused_computation.1 | loop fusion | flops 29491200 | bytes 49623040 | tf_op jit(solution)/shard_map/convert_element_type | solution.py:128
  661.7 12.7 fusion.184
  676.7 8.3 multiply_convert_fusion.6
  696.3 17.8 %fusion.71 = f32[1,768,2304]{2,1,0:T(8,128)} fusion(s32[]{:T(128)S(6)} %select_n.195, bf16[1,640,768]{2,1,0:T(8,128)(2,1)} %copy.209, bf16[1,640,768]{2,1,0:T(8,128)(2,1)} %copy.210, bf16[1,640,768]{2,1,0:T(8,128)(2,1)} %copy.211, bf16[1,640,768]{2,1,0:T(8,128)(2,1)} %copy.219, bf16[1,640,768]{2,1,0:T(8,128)(2,1)} %copy.220, ...), kind=kOutput, calls=%fused_computation.121 | convolution fusion | flops 4584898560 | bytes 18874376 | tf_op jit(solution)/shard_map/dot_general | solution.py:33
  714.2 14.7 fusion.68
  728.9 14.4 fusion.65
  751.8 24.8 %all_gather.43 = bf16[1,768,128]{2,1,0:T(8,128)(2,1)} all-gather(bf16[1,48,128]{2,1,0:T(8,128)(2,1)S(1)} %convert_element_type.558), channel_id=1, replica_groups=mesh['pipe'=2,'dp'=16] {'dp'}, dimensions={1}, use_global_device_ids=true | all-gather | bytes 208896 | tf_op jit(solution)/shard_map/all_gather | solution.py:468
  815.5 109.4 %reduce-scatter.30.cloned.1.call-done = f32[1,192,768]{2,1,0:T(8,128)} async-done(((f32[1,3072,768]{2,1,0:T(8,128)}), f32[1,192,768]{2,1,0:T(8,128)}) %reduce-scatter.30.cloned.1.call-update) | async-done | bytes 589840 | tf_op jit(solution)/shard_map/reduce_scatter | solution.py:433
  926.8 113.8 %reduce-scatter.28.cloned.1.call-done = f32[1,48,3072]{2,1,0:T(8,128)} async-done(((f32[1,768,3072]{2,1,0:T(8,128)}), f32[1,48,3072]{2,1,0:T(8,128)}) %reduce-scatter.28.cloned.1.call-update) | async-done | bytes 589840 | tf_op jit(solution)/shard_map/reduce_scatter | solution.py:431
  1067.0 57.4 %reduce-scatter.36.cloned.1.call-done = f32[48,1]{1,0:T(8,128)} async-done(((f32[768,1]{1,0:T(8,128)}), f32[48,1]{1,0:T(8,128)}) %reduce-scatter.36.cloned.1.call-update) | async-done | bytes 208
  1125.2 57.4 %reduce-scatter.44.cloned.1.call-done = f32[48,1]{1,0:T(8,128)} async-done(((f32[768,1]{1,0:T(8,128)}), f32[48,1]{1,0:T(8,128)}) %reduce-scatter.44.cloned.1.call-update) | async-done | bytes 208
  1185.0 56.2 %reduce-scatter.40.cloned.1.call-done = f32[48,2]{1,0:T(8,128)} async-done(((f32[768,2]{1,0:T(8,128)}), f32[48,2]{1,0:T(8,128)}) %reduce-scatter.40.cloned.1.call-update) | async-done | bytes 400
  1242.7 22.1 %all_gather.38 = bf16[1,2,768]{1,0,2:T(2,128)(2,1)} all-gather(bf16[1,2,48]{1,0,2:T(2,128)(2,1)} %copy.234), channel_id=1, replica_groups=mesh['pipe'=2,'dp'=16] {'dp'}, dimensions={2}, use_global_device_ids=true | all-gather | bytes 3264 | tf_op jit(solution)/shard_map/all_gather | solution.py:453
  1266.6 32.6 %reduce-scatter.38.cloned.1.call-done = f32[48,2]{1,0:T(8,128)} async-done(((f32[768,2]{1,0:T(8,128)}), f32[48,2]{1,0:T(8,128)}) %reduce-scatter.38.cloned.1.call-update) | async-done | bytes 400
  1300.7 22.1 %all_gather.37 = bf16[1,2,768]{1,0,2:T(2,128)(2,1)} all-gather(bf16[1,2,48]{1,0,2:T(2,128)(2,1)} %copy.233), channel_id=1, replica_groups=mesh['pipe'=2,'dp'=16] {'dp'}, dimensions={2}, use_global_device_ids=true | all-gather | bytes 3264 | tf_op jit(solution)/shard_map/all_gather | solution.py:450
  1324.6 34.2 %reduce-scatter.34.cloned.1.call-done = f32[96,1]{1,0:T(8,128)} async-done(((f32[1536,1]{1,0:T(8,128)}), f32[96,1]{1,0:T(8,128)}) %reduce-scatter.34.cloned.1.call-update) | async-done | bytes 400
  1361.2 59.5 %reduce-scatter.42.cloned.1.call-done = f32[192,1]{1,0:T(8,128)} async-done(((f32[3072,1]{1,0:T(8,128)}), f32[192,1]{1,0:T(8,128)}) %reduce-scatter.42.cloned.1.call-update) | async-done | bytes 784
  1423.1 58.2 %all-reduce.4 = (bf16[1536]{0:T(1024)(128)(2,1)}, bf16[768]{0:T(1024)(128)(2,1)}, bf16[768]{0:T(1024)(128)(2,1)}, bf16[3072]{0:T(1024)(128)(2,1)}) all-reduce(bf16[1536]{0:T(1024)(128)(2,1)S(1)} %dynamic-update-slice, bf16[768]{0:T(1024)(128)(2,1)} %copy-done.119, ...), channel_id=1, replica_groups=mesh['pipe'=2,'dp'=16] {'dp'}, use_global_device_ids=true, to_apply=%add | all-reduce | flops 6144 | bytes 24576
  1489.2 21.3 %all-gather.5.cloned.1.call-done = bf16[1,768,2304]{2,1,0:T(8,128)(2,1)} async-done(((bf16[1,48,2304]{2,1,0:T(8,128)(2,1)}), bf16[1,768,2304]{2,1,0:T(8,128)(2,1)}) %all-gather.5.cloned.1.call-update) | async-done | bytes 3538960 | tf_op jit(solution)/shard_map/all_gather | solution.py:438
  1515.9 49.2 %all-gather.11.cloned.1.call-done = bf16[1,3072,768]{2,1,0:T(8,128)(2,1)} async-done(((bf16[1,192,768]{2,1,0:T(8,128)(2,1)}), bf16[1,3072,768]{2,1,0:T(8,128)(2,1)}) %all-gather.11.cloned.1.call-update) | async-done | bytes 4718608 | tf_op jit(solution)/shard_map/all_gather | solution.py:462
  1571.9 48.0 %all-gather.9.cloned.1.call-done = bf16[1,768,3072]{2,1,0:T(8,128)(2,1)} async-done(((bf16[1,48,3072]{2,1,0:T(8,128)(2,1)}), bf16[1,768,3072]{2,1,0:T(8,128)(2,1)}) %all-gather.9.cloned.1.call-update) | async-done | bytes 4718608 | tf_op jit(solution)/shard_map/all_gather | solution.py:456
  1619.9 7.4 convert_element_type.543
  (714 shorter events, 449.9 us)
Async XLA Ops:
  7.2 743.9 %reduce-scatter.32.cloned.1.call-start = ((), (), s32[]{:S(2)}) async-start(), calls=%async_computation.19 | async-start | bytes 417792 | tf_op jit(solution)/shard_map/reduce_scatter | solution.py:435
  53.1 13.1 copy-start.5
  53.1 13.1 copy-start.139
  71.0 14.6 copy-start.84
  72.9 12.8 copy-start.21
  87.8 40.9 %collective-permute-start = (bf16[640,768]{1,0:T(8,128)(2,1)}, bf16[640,768]{1,0:T(8,128)(2,1)}, u32[]{:S(2)}, u32[]{:S(2)}) collective-permute-start(bf16[640,768]{1,0:T(8,128)(2,1)} %get-tuple-element.153), channel_id=1, source_target_pairs={{0,16},{1,17},{2,18},{3,19},{4,20},{5,21},{6,22},{7,23},{8,24},{9,... | collective-permute-start | bytes 2949128 | tf_op jit(solution)/shard_map/ppermute | solution.py:25
  166.2 13.1 copy-start.25
  166.2 13.1 copy-start.140
  184.0 12.7 copy-start.19
  200.5 23.0 %collective-permute-start.1 = (bf16[640,768]{1,0:T(8,128)(2,1)}, bf16[640,768]{1,0:T(8,128)(2,1)}, u32[]{:S(2)}, u32[]{:S(2)}) collective-permute-start(bf16[640,768]{1,0:T(8,128)(2,1)} %get-tuple-element.155), channel_id=1, source_target_pairs={{0,16},{1,17},{2,18},{3,19},{4,20},{5,21},{6,22},{7,23},{8,24},{9,... | collective-permute-start | bytes 2949128 | tf_op jit(solution)/shard_map/ppermute | solution.py:25
  262.4 12.9 copy-start.23
  262.4 12.9 copy-start.141
  280.0 12.9 copy-start.20
  353.4 13.0 copy-start.3
  353.4 13.0 copy-start.32
  396.1 12.6 copy-start.49
  422.3 14.1 copy-start.28
  457.7 25.7 %collective-permute-start.2 = (bf16[640,768]{1,0:T(8,128)(2,1)}, bf16[640,768]{1,0:T(8,128)(2,1)}, u32[]{:S(2)}, u32[]{:S(2)}) collective-permute-start(bf16[640,768]{1,0:T(8,128)(2,1)} %add_convert_fusion.4), channel_id=1, source_target_pairs={{16,0},{17,1},{18,2},{19,3},{20,4},{21,5},{22,6},{23,7},{24,8},{25... | collective-permute-start | bytes 2949128 | tf_op jit(solution)/shard_map/ppermute | solution.py:25
  467.8 22.6 %slice-start.10 = ((s8[4718592]{0:T(1024)(128)(4,1)}), s8[4194304]{0:T(1024)(128)(4,1)S(1)}, s32[]{:S(2)}) async-start(s8[4718592]{0:T(1024)(128)(4,1)} %bitcast.694), calls=%async_computation.37 | async-start | bytes 8388608
  467.8 22.6 %slice-start.11 = ((s8[4718592]{0:T(1024)(128)(4,1)}), s8[524288]{0:T(1024)(128)(4,1)S(1)}, s32[]{:S(2)}) async-start(s8[4718592]{0:T(1024)(128)(4,1)} %bitcast.694), calls=%async_computation.38 | async-start | bytes 1048576
  487.3 12.0 slice-start
  487.3 12.0 slice-start.12
  510.6 12.0 copy-start.50
  522.5 33.0 %copy-start.48 = (bf16[12,64,640]{2,1,0:T(8,128)(2,1)}, bf16[12,64,640]{2,1,0:T(8,128)(2,1)S(1)}, u32[]{:S(2)}) copy-start(bf16[12,64,640]{2,1,0:T(8,128)(2,1)S(1)} %fusion.181) | copy-start | bytes 2949124
  536.4 14.1 copy-start.29
  559.2 30.1 %collective-permute-start.3 = (bf16[640,768]{1,0:T(8,128)(2,1)}, bf16[640,768]{1,0:T(8,128)(2,1)}, u32[]{:S(2)}, u32[]{:S(2)}) collective-permute-start(bf16[640,768]{1,0:T(8,128)(2,1)} %add_convert_fusion.3), channel_id=1, source_target_pairs={{16,0},{17,1},{18,2},{19,3},{20,4},{21,5},{22,6},{23,7},{24,8},{25... | collective-permute-start | bytes 2949128 | tf_op jit(solution)/shard_map/ppermute | solution.py:25
  564.3 247.7 %reduce-scatter.26.cloned.1.call-start = ((), (), s32[]{:S(2)}) async-start(), calls=%async_computation.13 | async-start | bytes 2506752 | tf_op jit(solution)/shard_map/reduce_scatter | solution.py:427
  593.1 13.1 slice-start.2
  593.1 13.1 slice-start.14
  623.3 190.4 %reduce-scatter.24.cloned.1.call-start = ((), (), s32[]{:S(2)}) async-start(), calls=%async_computation.11 | async-start | bytes 7520256 | tf_op jit(solution)/shard_map/reduce_scatter | solution.py:425
  623.4 20.1 %copy-start.54 = (pred[640,640]{0,1:T(8,128)(4,1)S(1)}, pred[640,640]{0,1:T(8,128)(4,1)}, u32[]{:S(2)}) copy-start(pred[640,640]{0,1:T(8,128)(4,1)} %broadcast_compare_fusion) | copy-start | bytes 1228804
  623.4 20.1 %copy-start.74 = (f32[12,640]{1,0:T(8,128)S(1)}, f32[12,640]{1,0:T(8,128)}, u32[]{:S(2)}) copy-start(f32[12,640]{1,0:T(8,128)} %get-tuple-element.176) | copy-start | bytes 92164
  643.5 18.2 %copy-start.51 = (bf16[640,768]{0,1:T(8,128)(2,1)S(1)}, bf16[640,768]{0,1:T(8,128)(2,1)}, u32[]{:S(2)}) copy-start(bf16[640,768]{0,1:T(8,128)(2,1)} %copy.224) | copy-start | bytes 2949124
  714.2 210.7 %reduce-scatter.30.cloned.1.call-start = ((), (), s32[]{:S(2)}) async-start(), calls=%async_computation.17 | async-start | bytes 10027008 | tf_op jit(solution)/shard_map/reduce_scatter | solution.py:433
  728.9 311.6 %reduce-scatter.28.cloned.1.call-start = ((), (), s32[]{:S(2)}) async-start(), calls=%async_computation.15 | async-start | bytes 10027008 | tf_op jit(solution)/shard_map/reduce_scatter | solution.py:431
  743.4 321.9 %all-reduce.8.cloned.1.call-start = ((), (), s32[]{:S(2)}) async-start(), calls=%async_computation.20 | async-start | bytes 393216 | tf_op jit(solution)/shard_map/psum | solution.py:478
  776.6 347.8 %reduce-scatter.36.cloned.1.call-start = ((), (), s32[]{:S(2)}) async-start(), calls=%async_computation.22 | async-start | bytes 417792
  791.8 390.8 %reduce-scatter.44.cloned.1.call-start = ((), (), s32[]{:S(2)}) async-start(), calls=%async_computation.26 | async-start | bytes 417792
  796.0 445.1 %reduce-scatter.40.cloned.1.call-start = ((), (), s32[]{:S(2)}) async-start(), calls=%async_computation.24 | async-start | bytes 417792
  802.3 496.9 %reduce-scatter.38.cloned.1.call-start = ((), (), s32[]{:S(2)}) async-start(), calls=%async_computation.23 | async-start | bytes 417792
  807.3 551.4 %reduce-scatter.34.cloned.1.call-start = ((), (), s32[]{:S(2)}) async-start(), calls=%async_computation.21 | async-start | bytes 835584
  809.3 238.2 %copy-start.121 = (f32[4]{0:T(128)S(1)}, f32[4]{0:T(128)}, u32[]{:S(2)}) copy-start(f32[4]{0:T(128)} %copy-done.120) | copy-start | bytes 52
  809.4 611.4 %reduce-scatter.42.cloned.1.call-start = ((), (), s32[]{:S(2)}) async-start(), calls=%async_computation.25 | async-start | bytes 1671168
  812.0 674.4 %all-gather.7.cloned.1.call-start = ((), (), s32[]{:S(2)}) async-start(), calls=%async_computation.14 | async-start | bytes 1253376 | tf_op jit(solution)/shard_map/all_gather | solution.py:444
  813.6 696.8 %all-gather.5.cloned.1.call-start = ((), (), s32[]{:S(2)}) async-start(), calls=%async_computation.12 | async-start | bytes 3760128 | tf_op jit(solution)/shard_map/all_gather | solution.py:438
  815.5 749.7 %all-gather.11.cloned.1.call-start = ((), (), s32[]{:S(2)}) async-start(), calls=%async_computation.18 | async-start | bytes 5013504 | tf_op jit(solution)/shard_map/all_gather | solution.py:462
  926.7 693.2 %all-gather.9.cloned.1.call-start = ((), (), s32[]{:S(2)}) async-start(), calls=%async_computation.16 | async-start | bytes 5013504 | tf_op jit(solution)/shard_map/all_gather | solution.py:456
  1184.1 238.1 %copy-start.119 = (bf16[768]{0:T(1024)(128)(2,1)}, bf16[768]{0:T(1024)(128)(2,1)S(1)}, u32[]{:S(2)}) copy-start(bf16[768]{0:T(1024)(128)(2,1)S(1)} %dynamic-update-slice.1) | copy-start | bytes 4612
  (145 other events, 679.0 us)
Sparse Core Ops, SparseCore 0:
  564.4 58.6 reduce-scatter.31
  627.9 61.9 reduce-scatter.25
  714.3 94.5 reduce-scatter.23
  814.0 110.8 reduce-scatter.29
  929.4 111.0 reduce-scatter.27
  1042.8 22.1 all-reduce.7
  1068.8 55.5 reduce-scatter.35
  1127.9 54.6 reduce-scatter.43
  1186.5 54.6 reduce-scatter.39
  1244.5 54.6 reduce-scatter.37
  1303.2 55.5 reduce-scatter.33
  1362.3 58.3 reduce-scatter.41
  1423.8 37.5 all-gather.6
  1464.4 46.0 all-gather.4
  1512.8 52.2 all-gather.10
  1568.1 51.7 all-gather.8
where the time goes:
time: 1640 us; the launch traced here: 1630 us
  waiting for transfers between devices  644 us (39%)
  matrix products  410 us (25%)
  other arithmetic  255 us (16%)
  local copies, waits for them, and re-layouts  164 us (10%)
  blocking collectives  133 us (8%)
  between operations  18.2 us (1%)
    unnamed x22, waiting for transfers between devices  298 us
    reduce_scatter x1, waiting for transfers between devices, shards(): lax.psum_scatter(grad_expand[None], 'dp', scatter_dimension=1, tiled=True)  114 us
    reduce_scatter x1, waiting for transfers between devices, shards(): lax.psum_scatter(grad_reduce[None], 'dp', scatter_dimension=1, tiled=True)  109 us
    dot_general x17, matrix products, matmul_cols(): lax.dot_general(left, right, (((1,), (1,)), ((), ())), preferred_element_...  70.2 us
    dot_general x6, matrix products, scores_of(): jnp.einsum('qhd,khd->hqk', query_rows, key_rows, preferred_element_type=j...  69.1 us
    dot_general x8, matrix products, matmul_rows(): lax.dot_general(left, right, (((0,), (0,)), ((), ())), preferred_element_...  59.9 us
    unnamed x1, blocking collectives  58.2 us
    slice x24, local copies, waits for them, and re-layouts, split_heads(): joined_b[:, block_index * model_width:(block_index + 1) * model_width]  53.1 us
  transfers between devices with their start and end apart: 20, of which 12 were waited for; matrix products, arithmetic and copies ran while one was open for 22% of the time, Pallas kernels for 0%

commit v1 on v0

--- a/solution.py
+++ b/solution.py
@@ -52,7 +52,8 @@
 
 
 def layout(lengths):
-    end_pos = jnp.cumsum(lengths)
+    places = jnp.arange(NP, dtype=jnp.int32)
+    end_pos = jnp.sum(jnp.where(places[None, :] <= places[:, None], lengths[None, :], 0), axis=1)
     slot_ids = jnp.arange(PSLOTS, dtype=jnp.int32)
     passage_id = jnp.sum((slot_ids[:, None] >= end_pos[None, :]).astype(jnp.int32), axis=1)
     query_ids = jnp.arange(NQ * QLEN, dtype=jnp.int32) // QLEN
@@ -293,6 +294,53 @@
     ).astype(jnp.bfloat16)
     grad_output = matmul_cols(grad_embed_b, colbert_weight)
     return (pack_loss, grad_output, grad_embed_b)
+
+
+def swapped(array, bit):
+    count = lax.axis_size("dp")
+    return lax.ppermute(array, "dp", [(i, i ^ bit) for i in range(count)])
+
+
+def piece(array, index):
+    return lax.dynamic_index_in_dim(array, index, 0, keepdims=False)
+
+
+def placed_at(array, update, index):
+    return lax.dynamic_update_index_in_dim(array, update, index, 0)
+
+
+def sum_low(*arrays):
+    total = arrays[0].astype(jnp.float32)
+    for array in arrays[1:]:
+        total = total + array.astype(jnp.float32)
+    return total.astype(jnp.bfloat16)
+
+
+def summed_over_data(partial):
+    count = lax.axis_size("dp")
+    rows, columns = partial.shape
+    if count != 16:
+        share = lax.psum_scatter(partial, "dp", scatter_dimension=0, tiled=True)
+        return lax.all_gather(share, "dp", axis=0, tiled=True).astype(jnp.float32)
+    place = lax.axis_index("dp")
+    core, along_x, along_z = place & 1, (place >> 1) & 1, place >> 2
+    halves = partial.reshape(2, rows // 2, columns)
+    half = sum_low(piece(halves, core), swapped(piece(halves, 1 - core), 1))
+    quarters = half.reshape(2, rows // 4, columns)
+    quarter = sum_low(piece(quarters, along_x), swapped(piece(quarters, 1 - along_x), 2))
+    parts = quarter.reshape(4, rows // 16, columns)
+    arrived = [swapped(piece(parts, along_z ^ step), 4 * step) for step in (1, 2, 3)]
+    share = sum_low(piece(parts, along_z), *arrived)
+    parts = placed_at(jnp.zeros_like(parts), share, along_z)
+    for step in (1, 2, 3):
+        parts = placed_at(parts, swapped(share, 4 * step), along_z ^ step)
+    quarter = parts.reshape(rows // 4, columns)
+    quarters = placed_at(jnp.zeros_like(quarters), quarter, along_x)
+    quarters = placed_at(quarters, swapped(quarter, 2), 1 - along_x)
+    half = quarters.reshape(rows // 2, columns)
+    other = swapped(half, 1)
+    whole = jnp.stack([jnp.where(core == 0, half, other), jnp.where(core == 0, other, half)])
+    return whole.reshape(rows, columns).astype(jnp.float32)
 
 
 def flatten_rows(leaf):
@@ -421,76 +469,42 @@
     grad_mixing = matmul_rows(flatten_rows(context_all), flatten_rows(grad_one_all))
     grad_expand = matmul_rows(flatten_rows(hidden_all), flatten_rows(grad_inner_all))
     grad_reduce = matmul_rows(flatten_rows(active_all), flatten_rows(grad_two_all))
-    shares = (
-        lax.psum_scatter(grad_attend[None], "dp", scatter_dimension=1, tiled=True),
-        lax.psum_scatter(grad_attend_bias[None], "dp", scatter_dimension=1, tiled=True),
-        lax.psum_scatter(grad_mixing[None], "dp", scatter_dimension=1, tiled=True),
-        lax.psum_scatter(grad_mixing_bias[None], "dp", scatter_dimension=1, tiled=True),
-        lax.psum_scatter(grad_gain[None], "dp", scatter_dimension=2, tiled=True),
-        lax.psum_scatter(grad_shift[None], "dp", scatter_dimension=2, tiled=True),
-        lax.psum_scatter(grad_expand[None], "dp", scatter_dimension=1, tiled=True),
-        lax.psum_scatter(grad_expand_bias[None], "dp", scatter_dimension=1, tiled=True),
-        lax.psum_scatter(grad_reduce[None], "dp", scatter_dimension=1, tiled=True),
-        lax.psum_scatter(grad_reduce_bias[None], "dp", scatter_dimension=1, tiled=True),
-        lax.psum_scatter(grad_colbert[None], "dp", scatter_dimension=1, tiled=True),
-    )
-    summed = (
-        lax.all_gather(shares[0].astype(jnp.bfloat16), "dp", axis=1, tiled=True).astype(
-            jnp.float32
-        ),
-        lax.all_gather(shares[1].astype(jnp.bfloat16), "dp", axis=1, tiled=True).astype(
-            jnp.float32
-        ),
-        lax.all_gather(shares[2].astype(jnp.bfloat16), "dp", axis=1, tiled=True).astype(
-            jnp.float32
-        ),
-        lax.all_gather(shares[3].astype(jnp.bfloat16), "dp", axis=1, tiled=True).astype(
-            jnp.float32
-        ),
-        lax.all_gather(shares[4].astype(jnp.bfloat16), "dp", axis=2, tiled=True).astype(
-            jnp.float32
-        ),
-        lax.all_gather(shares[5].astype(jnp.bfloat16), "dp", axis=2, tiled=True).astype(
-            jnp.float32
-        ),
-        lax.all_gather(shares[6].astype(jnp.bfloat16), "dp", axis=1, tiled=True).astype(
-            jnp.float32
-        ),
-        lax.all_gather(shares[7].astype(jnp.bfloat16), "dp", axis=1, tiled=True).astype(
-            jnp.float32
-        ),
-        lax.all_gather(shares[8].astype(jnp.bfloat16), "dp", axis=1, tiled=True).astype(
-            jnp.float32
-        ),
-        lax.all_gather(shares[9].astype(jnp.bfloat16), "dp", axis=1, tiled=True).astype(
-            jnp.float32
-        ),
-        lax.all_gather(shares[10].astype(jnp.bfloat16), "dp", axis=1, tiled=True).astype(
-            jnp.float32
-        ),
-    )
-    colbert_data = summed[10][0]
+    small_parts = [
+        grad_attend_bias,
+        grad_mixing_bias,
+        grad_gain.reshape(-1),
+        grad_shift.reshape(-1),
+        grad_expand_bias,
+        grad_reduce_bias,
+    ]
+    small_sum = lax.psum(jnp.concatenate(small_parts), "dp")
+    cuts = [0]
+    for part in small_parts:
+        cuts.append(cuts[-1] + part.shape[0])
+    smalls = [small_sum[cuts[i] : cuts[i + 1]] for i in range(len(small_parts))]
+    colbert_sum = lax.psum(grad_colbert.astype(jnp.bfloat16), ("pipe", "dp")).astype(jnp.float32)
+    big_sums = [
+        summed_over_data(part.astype(jnp.bfloat16))
+        for part in (grad_reduce, grad_expand, grad_mixing, grad_attend)
+    ]
     section_rows = (jnp.arange(2, dtype=jnp.int32) == section_id).astype(jnp.float32)
     square_parts = section_rows[None, :, None] * squares[:, None, :]
-    square_sum, loss_sum, colbert_sum = (
-        lax.psum(square_parts.astype(jnp.bfloat16), "pipe").astype(jnp.float32),
-        lax.psum((losses * last_weight).astype(jnp.bfloat16), "pipe").astype(jnp.float32),
-        lax.psum(colbert_data.astype(jnp.bfloat16), "pipe").astype(jnp.float32),
-    )
+    square_sum = lax.psum(square_parts, "pipe")
+    loss_sum = lax.psum(losses * last_weight, "pipe")
     count_micro = jnp.sum(usables, axis=1)
     stats = jnp.sqrt(square_sum / (count_micro[:, None, None] * model_width))
     loss = loss_sum / NQ
     return (
-        summed[0],
-        summed[1],
-        summed[2],
-        summed[3],
-        summed[4],
-        summed[5],
-        summed[6],
-        summed[7],
-        summed[8],
-        summed[9],
+        big_sums[3][None],
+        smalls[0][None],
+        big_sums[2][None],
+        smalls[1][None],
+        smalls[2].reshape(1, 2, model_width),
+        smalls[3].reshape(1, 2, model_width),
+        big_sums[1][None],
+        smalls[4][None],
+        big_sums[0][None],
+        smalls[5][None],
         colbert_sum,
         loss,
         stats,

time: 1640 us -> 1190 us (0.73)
  waiting for transfers between devices: 644 us -> 198 us
  starting transfers between devices: 11.3 us -> 91.4 us
  blocking collectives: 133 us -> 67.4 us
  matrix products: 410 us -> 380 us
    unnamed x22 -> x1, waiting for transfers between devices: 298 us -> 0.02 us
    reduce_scatter x5 -> x0, waiting for transfers between devices: 223 us -> none  [the longest x1 114 us: shards(): lax.psum_scatter(grad_expand[None], 'dp', scatter_dimension=1, tiled=True)]
    ppermute x0 -> x40, waiting for transfers between devices: none -> 123 us  [swapped(): return lax.ppermute(array, 'dp', [(i, i ^ bit) for i in range(count)])]
    all_gather x4 -> x0, waiting for transfers between devices: 118 us -> none  [the longest x1 49.2 us: shards(): lax.all_gather(shares[8].astype(jnp.bfloat16), 'dp', axis=1, tiled=True)]
    ppermute x0 -> x40, starting transfers between devices: none -> 80.6 us  [swapped(): return lax.ppermute(array, 'dp', [(i, i ^ bit) for i in range(count)])]
    all_gather x3 -> x0, blocking collectives: 69 us -> none  [the longest x1 24.8 us: shards(): lax.all_gather(shares[10].astype(jnp.bfloat16), 'dp', axis=1, tiled=True)]
    psum x1, waiting for transfers between devices: 0.01 us -> 65.9 us  [shards(): lax.psum(grad_colbert.astype(jnp.bfloat16), ('pipe', 'dp'))]
    psum x1 -> x2, blocking collectives: 5.43 us -> 67.4 us  [the longest x1 61.8 us: shards(): small_sum = lax.psum(jnp.concatenate(small_parts), 'dp')]
  transfers between devices with their start and end apart: 20 -> 45, of which waited for: 12 -> 18; matrix products, arithmetic and copies ran while one was open for 22% -> 20% of each run, Pallas kernels for 0% -> 0%
where the time goes in v1:
time: 1190 us; the launch traced here: 1170 us
  matrix products  380 us (32%)
  other arithmetic  240 us (20%)
  waiting for transfers between devices  198 us (17%)
  local copies, waits for them, and re-layouts  178 us (15%)
  starting transfers between devices  91.4 us (8%)
  blocking collectives  67.4 us (6%)
  between operations  16.8 us (1%)
    ppermute x40, waiting for transfers between devices, swapped(): return lax.ppermute(array, 'dp', [(i, i ^ bit) for i in range(count)])  123 us
    ppermute x40, starting transfers between devices, swapped(): return lax.ppermute(array, 'dp', [(i, i ^ bit) for i in range(count)])  80.6 us
    dot_general x6, matrix products, scores_of(): jnp.einsum('qhd,khd->hqk', query_rows, key_rows, preferred_element_type=j...  66.2 us
    psum x1, waiting for transfers between devices, shards(): lax.psum(grad_colbert.astype(jnp.bfloat16), ('pipe', 'dp'))  65.9 us
    dot_general x17, matrix products, matmul_cols(): lax.dot_general(left, right, (((1,), (1,)), ((), ())), preferred_element_...  65.6 us
    psum x1, blocking collectives, shards(): small_sum = lax.psum(jnp.concatenate(small_parts), 'dp')  61.8 us
    slice x24, local copies, waits for them, and re-layouts, split_heads(): joined_b[:, block_index * model_width:(block_index + 1) * model_width]  57 us
    dot_general x18, matrix products, matmul_plain(): return jnp.dot(left, right, preferred_element_type=jnp.float32)  56.1 us
  transfers between devices with their start and end apart: 45, of which 18 were waited for; matrix products, arithmetic and copies ran while one was open for 20% of the time, Pallas kernels for 0%

profile of v1, /device:TPU:0, one launch (start us, length us, event | category | flops | bytes accessed | tf_op | source)
XLA Modules:
  0.0 1172.9 jit_solution(6548663969843069051)
XLA Ops:
  25.7 12.0 %fusion = (f32[12,640]{1,0:T(8,128)}, f32[12,640,640]{1,2,0:T(8,128)}) fusion(pred[640,640]{0,1:T(8,128)(4,1)} %broadcast_compare_fusion.5, bf16[640,12,64]{0,2,1:T(8,128)(2,1)} %bitcast.821, bf16[640,12,64]{0,2,1:T(8,128)(2,1)} %bitcast.822), kind=kOutput, calls=%fused_computation.19 | convolution fusion | flops 643883520 | bytes 22067200 | tf_op jit(solution)/shard_map/qhd,khd->hqk/dot_general | solution.py:99
  37.7 11.2 fusion.3
  48.9 13.9 %fusion.179 = bf16[12,64,640]{2,1,0:T(8,128)(2,1)} fusion(bf16[640,12,64]{0,2,1:T(8,128)(2,1)} %bitcast.850, f32[12,640,640]{1,2,0:T(8,128)} %get-tuple-element.201, f32[12,640]{1,0:T(8,128)} %fusion.3, f32[12,640]{1,0:T(8,128)} %get-tuple-element.200, pred[640,640]{0,1:T(8,128)(4,1)} %broadcast_compare_fusion.5), kind=kOutput, calls=%fused_computation.333 | convolution fusion | flops 654213120 | bytes 22097920 | tf_op jit(solution)/shard_map/hqk,khd->qhd/dot_general | solution.py:112
  79.1 7.7 add_bitcast_fusion.2
  94.0 5.9 collective-permute-start
  156.8 12.0 %fusion.1 = (f32[12,640]{1,0:T(8,128)}, f32[12,640,640]{1,2,0:T(8,128)}) fusion(pred[640,640]{0,1:T(8,128)(4,1)} %broadcast_compare_fusion.4, bf16[640,12,64]{0,2,1:T(8,128)(2,1)} %bitcast.825, bf16[640,12,64]{0,2,1:T(8,128)(2,1)} %bitcast.827), kind=kOutput, calls=%fused_computation.20 | convolution fusion | flops 643883520 | bytes 22067200 | tf_op jit(solution)/shard_map/qhd,khd->hqk/dot_general | solution.py:99
  168.8 11.2 fusion.4
  180.0 13.0 %fusion.178 = bf16[12,64,640]{2,1,0:T(8,128)(2,1)S(1)} fusion(bf16[640,12,64]{0,2,1:T(8,128)(2,1)} %bitcast.851, f32[12,640,640]{1,2,0:T(8,128)} %get-tuple-element.207, f32[12,640]{1,0:T(8,128)} %fusion.4, f32[12,640]{1,0:T(8,128)} %get-tuple-element.206, pred[640,640]{0,1:T(8,128)(4,1)} %broadcast_compare_fusion.4), kind=kOutput, calls=%fused_computation.332 | convolution fusion | flops 654213120 | bytes 22097920 | tf_op jit(solution)/shard_map/hqk,khd->qhd/dot_general | solution.py:112
  197.8 7.8 add_bitcast_fusion.1
  254.9 12.0 %fusion.2 = (f32[12,640]{1,0:T(8,128)}, f32[12,640,640]{1,2,0:T(8,128)}) fusion(pred[640,640]{0,1:T(8,128)(4,1)} %broadcast_compare_fusion.2, bf16[640,12,64]{0,2,1:T(8,128)(2,1)} %bitcast.826, bf16[640,12,64]{0,2,1:T(8,128)(2,1)} %bitcast.828), kind=kOutput, calls=%fused_computation.21 | convolution fusion | flops 643883520 | bytes 22067200 | tf_op jit(solution)/shard_map/qhd,khd->hqk/dot_general | solution.py:99
  266.9 11.2 fusion.5
  278.2 13.0 %fusion.177 = bf16[12,64,640]{2,1,0:T(8,128)(2,1)S(1)} fusion(bf16[640,12,64]{0,2,1:T(8,128)(2,1)} %bitcast.852, f32[12,640,640]{1,2,0:T(8,128)} %get-tuple-element.213, f32[12,640]{1,0:T(8,128)} %fusion.5, f32[12,640]{1,0:T(8,128)} %get-tuple-element.212, pred[640,640]{0,1:T(8,128)(4,1)} %broadcast_compare_fusion.2), kind=kOutput, calls=%fused_computation.331 | convolution fusion | flops 654213120 | bytes 22097920 | tf_op jit(solution)/shard_map/hqk,khd->qhd/dot_general | solution.py:112
  295.9 7.8 add_bitcast_fusion
  341.7 7.8 pad_maximum_fusion
  349.6 11.4 convert_reduce_fusion.2
  365.5 7.1 fusion.151
  399.4 11.0 fusion.400
  410.5 11.6 fusion.180
  422.1 13.9 %multiply_reduce_fusion.2 = (f32[12,640]{1,0:T(8,128)S(1)}, f32[12,640,640]{1,2,0:T(8,128)}) fusion(f32[12,640,640]{1,2,0:T(8,128)} %fusion.400, f32[12,640]{1,0:T(8,128)S(1)} %copy-done.87, pred[640,640]{0,1:T(8,128)(4,1)S(1)} %copy-done.59, bf16[640,12,64]{0,2,1:T(8,128)(2,1)S(1)} %bitcast.824, bf16[640,12,64]{0,2,1:T(8,128)(2,1)S(1)} %bitcast.829), kind=kOutput, calls=%fused_computation.8 | convolution fusion | flops 653713920 | bytes 41758720 | tf_op jit(solution)/shard_map/qhd,khd->hqk/dot_general | solution.py:123
  436.0 14.1 %multiply_convert_fusion.2 = bf16[12,640,640]{1,2,0:T(8,128)(2,1)S(1)} fusion(f32[12,640,640]{1,2,0:T(8,128)} %get-tuple-element.238, f32[12,640,640]{1,2,0:T(8,128)} %fusion.400, f32[12,640]{1,0:T(8,128)S(1)} %get-tuple-element.237, f32[12,640]{1,0:T(8,128)S(1)} %copy-done.87, pred[640,640]{0,1:T(8,128)(4,1)S(1)} %copy-done.59), kind=kLoop, calls=%fused_computation.7 | loop fusion | flops 29491200 | bytes 49623040 | tf_op jit(solution)/shard_map/convert_element_type | solution.py:129
  465.2 5.6 all-reduce
  513.5 11.0 fusion.401
  525.1 8.2 fusion.402
  533.9 65.9 %all-reduce.3.cloned.1.call-done = bf16[768,128]{1,0:T(8,128)(2,1)} async-done(((bf16[768,128]{1,0:T(8,128)(2,1)}), bf16[768,128]{1,0:T(8,128)(2,1)}) %all-reduce.3.cloned.1.call-update) | async-done | bytes 196624 | tf_op jit(solution)/shard_map/psum | solution.py:485
  607.8 10.0 convert_reduce_fusion.1
  629.1 11.9 %fusion.183 = bf16[12,64,640]{2,1,0:T(8,128)(2,1)S(1)} fusion(bf16[640,12,64]{0,2,1:T(8,128)(2,1)} %bitcast.832, f32[12,640,640]{1,2,0:T(8,128)} %fusion.401, f32[12,640]{1,0:T(8,128)} %get-tuple-element.175, pred[640,640]{0,1:T(8,128)(4,1)} %broadcast_compare_fusion.1), kind=kOutput, calls=%fused_computation.335 | convolution fusion | flops 649297920 | bytes 22067200 | tf_op jit(solution)/shard_map/hqk,qhd->khd/dot_general | solution.py:139
  641.0 14.1 %multiply_reduce_fusion.1 = (f32[12,640]{1,0:T(8,128)S(1)}, f32[12,640,640]{1,2,0:T(8,128)}) fusion(f32[12,640,640]{1,2,0:T(8,128)} %fusion.401, f32[12,640]{1,0:T(8,128)S(1)} %copy-done.86, pred[640,640]{0,1:T(8,128)(4,1)S(1)} %copy-done.58, bf16[640,12,64]{0,2,1:T(8,128)(2,1)S(1)} %bitcast.833, bf16[640,12,64]{0,2,1:T(8,128)(2,1)S(1)} %bitcast.815), kind=kOutput, calls=%fused_computation.5 | convolution fusion | flops 653713920 | bytes 41758720 | tf_op jit(solution)/shard_map/qhd,khd->hqk/dot_general | solution.py:123
  655.1 14.1 %multiply_convert_fusion.1 = bf16[12,640,640]{1,2,0:T(8,128)(2,1)S(1)} fusion(f32[12,640,640]{1,2,0:T(8,128)} %get-tuple-element.241, f32[12,640,640]{1,2,0:T(8,128)} %fusion.401, f32[12,640]{1,0:T(8,128)S(1)} %get-tuple-element.240, f32[12,640]{1,0:T(8,128)S(1)} %copy-done.86, pred[640,640]{0,1:T(8,128)(4,1)S(1)} %copy-done.58), kind=kLoop, calls=%fused_computation.4 | loop fusion | flops 29491200 | bytes 49623040 | tf_op jit(solution)/shard_map/convert_element_type | solution.py:129
  693.2 9.8 collective-permute-done.3
  709.9 9.1 convert_reduce_fusion
  729.9 12.9 %fusion.186 = bf16[12,64,640]{2,1,0:T(8,128)(2,1)} fusion(bf16[640,12,64]{0,2,1:T(8,128)(2,1)} %bitcast.830, f32[12,640,640]{1,2,0:T(8,128)} %fusion.402, f32[12,640]{1,0:T(8,128)} %get-tuple-element.174, pred[640,640]{0,1:T(8,128)(4,1)} %broadcast_compare_fusion), kind=kOutput, calls=%fused_computation.336 | convolution fusion | flops 649297920 | bytes 22067200 | tf_op jit(solution)/shard_map/hqk,qhd->khd/dot_general | solution.py:139
  742.8 13.7 %multiply_reduce_fusion = (f32[12,640]{1,0:T(8,128)S(1)}, f32[12,640,640]{1,2,0:T(8,128)}) fusion(f32[12,640,640]{1,2,0:T(8,128)} %fusion.402, f32[12,640]{1,0:T(8,128)S(1)} %copy-done.85, pred[640,640]{0,1:T(8,128)(4,1)S(1)} %copy-done.57, bf16[640,12,64]{0,2,1:T(8,128)(2,1)S(1)} %bitcast.831, bf16[640,12,64]{0,2,1:T(8,128)(2,1)S(1)} %bitcast.811), kind=kOutput, calls=%fused_computation.2 | convolution fusion | flops 653713920 | bytes 41758720 | tf_op jit(solution)/shard_map/qhd,khd->hqk/dot_general | solution.py:123
  756.5 13.9 %multiply_convert_fusion = bf16[12,640,640]{1,2,0:T(8,128)(2,1)S(1)} fusion(f32[12,640,640]{1,2,0:T(8,128)} %get-tuple-element.244, f32[12,640,640]{1,2,0:T(8,128)} %fusion.402, f32[12,640]{1,0:T(8,128)S(1)} %get-tuple-element.243, f32[12,640]{1,0:T(8,128)S(1)} %copy-done.85, pred[640,640]{0,1:T(8,128)(4,1)S(1)} %copy-done.57), kind=kLoop, calls=%fused_computation.1 | loop fusion | flops 29491200 | bytes 49623040 | tf_op jit(solution)/shard_map/convert_element_type | solution.py:129
  778.0 12.2 %bitcast_convert_fusion = bf16[3072,768]{1,0:T(8,128)(2,1)S(1)} fusion(s32[]{:T(128)S(6)} %select_n.330, bf16[1,640,3072]{2,1,0:T(8,128)(2,1)S(1)} %bitcast.875, bf16[1,640,3072]{2,1,0:T(8,128)(2,1)} %bitcast.876, bf16[1,640,3072]{2,1,0:T(8,128)(2,1)} %bitcast.878, s32[]{:T(128)S(6)} %select_n.345, bf16[1,640,768]{2,1,0:T(8,128)(2,1)S(1)} %copy-done.73, ...), kind=kOutput, calls=%fused_computation.46 | convolution fusion | flops 6051987456 | bytes 19464200 | tf_op jit(solution)/shard_map/dot_general | solution.py:33
  821.6 16.1 %bitcast_convert_fusion.2 = bf16[768,2304]{1,0:T(8,128)(2,1)S(1)} fusion(s32[]{:T(128)S(6)} %select_n.345, bf16[1,640,768]{2,1,0:T(8,128)(2,1)} %copy.152, bf16[1,640,768]{2,1,0:T(8,128)(2,1)} %copy.153, bf16[1,640,768]{2,1,0:T(8,128)(2,1)} %copy.154, bf16[1,640,768]{2,1,0:T(8,128)(2,1)} %copy.162, bf16[1,640,768]{2,1,0:T(8,128)(2,1)} %copy.163, ...), kind=kOutput, calls=%fused_computation.103 | convolution fusion | flops 4586668032 | bytes 15335432 | tf_op jit(solution)/shard_map/dot_general | solution.py:33
  846.6 61.8 %psum.28 = f32[9216]{0:T(1024)} all-reduce(f32[9216]{0:T(1024)} %constant_dynamic-update-slice_fusion.7), channel_id=1, replica_groups=mesh['pipe'=2,'dp'=16] {'dp'}, use_global_device_ids=true, to_apply=%region_85.86 | all-reduce | flops 9216 | bytes 73728 | tf_op jit(solution)/shard_map/psum | solution.py:480
  916.1 11.9 %bitcast_convert_fusion.1 = bf16[768,3072]{1,0:T(8,128)(2,1)S(1)} fusion(s32[]{:T(128)S(6)} %select_n.345, bf16[1,640,3072]{2,1,0:T(8,128)(2,1)} %bitcast.877, bf16[1,640,3072]{2,1,0:T(8,128)(2,1)} %bitcast.879, bf16[1,640,3072]{2,1,0:T(8,128)(2,1)} %bitcast.880, s32[]{:T(128)S(6)} %select_n.330, bf16[1,640,768]{2,1,0:T(8,128)(2,1)} %bitcast.773, ...), kind=kOutput, calls=%fused_computation.47 | convolution fusion | flops 6051987456 | bytes 19464200 | tf_op jit(solution)/shard_map/dot_general | solution.py:33
  960.1 16.9 %collective-permute-done.5 = bf16[192,2304]{1,0:T(8,128)(2,1)S(1)} collective-permute-done((bf16[192,2304]{1,0:T(8,128)(2,1)S(1)}, bf16[192,2304]{1,0:T(8,128)(2,1)S(1)}, u32[]{:S(2)}, u32[]{:S(2)}) %collective-permute-start.5) | collective-permute-done | bytes 884768 | tf_op jit(solution)/shard_map/ppermute | solution.py:301
  987.9 10.5 collective-permute-done.7
  1008.7 11.1 collective-permute-done.10
  1030.7 7.6 collective-permute-done.36
  1039.3 7.8 collective-permute-done.37
  1048.9 20.7 %collective-permute-start.39 = (bf16[192,768]{1,0:T(8,128)(2,1)S(1)}, bf16[192,768]{1,0:T(8,128)(2,1)S(1)}, u32[]{:S(2)}, u32[]{:S(2)}) collective-permute-start(bf16[192,768]{1,0:T(8,128)(2,1)S(1)} %get-tuple-element.90), channel_id=1, source_target_pairs={{0,4},{1,5},{2,6},{3,7},{4,0},{5,1},{6,2},{7,3},{8,12},{9,13},{10,... | collective-permute-start | bytes 884744 | tf_op jit(solution)/shard_map/ppermute | solution.py:301
  1070.3 5.5 collective-permute-done.27
  1079.6 15.3 %collective-permute-start.29 = (bf16[48,3072]{1,0:T(8,128)(2,1)S(1)}, bf16[48,3072]{1,0:T(8,128)(2,1)S(1)}, u32[]{:S(2)}, u32[]{:S(2)}) collective-permute-start(bf16[48,3072]{1,0:T(8,128)(2,1)S(1)} %get-tuple-element.96), channel_id=1, source_target_pairs={{0,4},{1,5},{2,6},{3,7},{4,0},{5,1},{6,2},{7,3},{8,12},{9,13},{10,... | collective-permute-start | bytes 884744 | tf_op jit(solution)/shard_map/ppermute | solution.py:301
  1095.6 5.4 collective-permute-done.40
  1105.4 17.0 %collective-permute-done.30 = bf16[48,3072]{1,0:T(8,128)(2,1)S(1)} collective-permute-done((bf16[48,3072]{1,0:T(8,128)(2,1)S(1)}, bf16[48,3072]{1,0:T(8,128)(2,1)S(1)}, u32[]{:S(2)}, u32[]{:S(2)}) %collective-permute-start.30) | collective-permute-done | bytes 294944 | tf_op jit(solution)/shard_map/ppermute | solution.py:301
  1129.6 20.4 %collective-permute-done.32 = bf16[192,3072]{1,0:T(8,128)(2,1)S(1)} collective-permute-done((bf16[192,3072]{1,0:T(8,128)(2,1)S(1)}, bf16[192,3072]{1,0:T(8,128)(2,1)S(1)}, u32[]{:S(2)}, u32[]{:S(2)}) %collective-permute-start.32) | collective-permute-done | bytes 1179680 | tf_op jit(solution)/shard_map/ppermute | solution.py:301
  (840 shorter events, 499.9 us)
Async XLA Ops:
  7.2 592.5 %all-reduce.3.cloned.1.call-start = ((), (), s32[]{:S(2)}) async-start(), calls=%async_computation | async-start | bytes 393216 | tf_op jit(solution)/shard_map/psum | solution.py:485
  94.0 48.6 %collective-permute-start = (bf16[640,768]{1,0:T(8,128)(2,1)}, bf16[640,768]{1,0:T(8,128)(2,1)}, u32[]{:S(2)}, u32[]{:S(2)}) collective-permute-start(bf16[640,768]{1,0:T(8,128)(2,1)} %get-tuple-element.137), channel_id=1, source_target_pairs={{0,16},{1,17},{2,18},{3,19},{4,20},{5,21},{6,22},{7,23},{8,24},{9,... | collective-permute-start | bytes 2949128 | tf_op jit(solution)/shard_map/ppermute | solution.py:25
  214.4 26.3 %collective-permute-start.1 = (bf16[640,768]{1,0:T(8,128)(2,1)}, bf16[640,768]{1,0:T(8,128)(2,1)}, u32[]{:S(2)}, u32[]{:S(2)}) collective-permute-start(bf16[640,768]{1,0:T(8,128)(2,1)} %get-tuple-element.139), channel_id=1, source_target_pairs={{0,16},{1,17},{2,18},{3,19},{4,20},{5,21},{6,22},{7,23},{8,24},{9,... | collective-permute-start | bytes 2949128 | tf_op jit(solution)/shard_map/ppermute | solution.py:25
  422.1 36.9 %copy-start.50 = (bf16[12,64,640]{2,1,0:T(8,128)(2,1)}, bf16[12,64,640]{2,1,0:T(8,128)(2,1)S(1)}, u32[]{:S(2)}) copy-start(bf16[12,64,640]{2,1,0:T(8,128)(2,1)S(1)} %fusion.180) | copy-start | bytes 2949124
  476.1 125.3 %collective-permute-start.2 = (bf16[640,768]{1,0:T(8,128)(2,1)}, bf16[640,768]{1,0:T(8,128)(2,1)}, u32[]{:S(2)}, u32[]{:S(2)}) collective-permute-start(bf16[640,768]{1,0:T(8,128)(2,1)} %add_convert_fusion.4), channel_id=1, source_target_pairs={{16,0},{17,1},{18,2},{19,3},{20,4},{21,5},{22,6},{23,7},{24,8},{25... | collective-permute-start | bytes 2949128 | tf_op jit(solution)/shard_map/ppermute | solution.py:25
  641.0 42.0 %copy-start.52 = (bf16[12,64,640]{2,1,0:T(8,128)(2,1)}, bf16[12,64,640]{2,1,0:T(8,128)(2,1)S(1)}, u32[]{:S(2)}) copy-start(bf16[12,64,640]{2,1,0:T(8,128)(2,1)S(1)} %fusion.183) | copy-start | bytes 2949124
  677.9 25.1 %collective-permute-start.3 = (bf16[640,768]{1,0:T(8,128)(2,1)}, bf16[640,768]{1,0:T(8,128)(2,1)}, u32[]{:S(2)}, u32[]{:S(2)}) collective-permute-start(bf16[640,768]{1,0:T(8,128)(2,1)} %add_convert_fusion.3), channel_id=1, source_target_pairs={{16,0},{17,1},{18,2},{19,3},{20,4},{21,5},{22,6},{23,7},{24,8},{25... | collective-permute-start | bytes 2949128 | tf_op jit(solution)/shard_map/ppermute | solution.py:25
  791.9 163.2 %collective-permute-start.34 = (bf16[1536,768]{1,0:T(8,128)(2,1)}, bf16[1536,768]{1,0:T(8,128)(2,1)}, u32[]{:S(2)}, u32[]{:S(2)}) collective-permute-start(bf16[1536,768]{1,0:T(8,128)(2,1)} %dynamic-slice_bitcast_fusion.3), channel_id=1, source_target_pairs={{0,1},{1,0},{2,3},{3,2},{4,5},{5,4},{6,7},{7,6},{8,9},{9,8},{10,11... | collective-permute-start | bytes 7077896 | tf_op jit(solution)/shard_map/ppermute | solution.py:301
  799.5 42.3 %collective-permute-start.14 = (bf16[384,768]{1,0:T(8,128)(2,1)}, bf16[384,768]{1,0:T(8,128)(2,1)}, u32[]{:S(2)}, u32[]{:S(2)}) collective-permute-start(bf16[384,768]{1,0:T(8,128)(2,1)} %dynamic-slice_bitcast_fusion.9), channel_id=1, source_target_pairs={{0,1},{1,0},{2,3},{3,2},{4,5},{5,4},{6,7},{7,6},{8,9},{9,8},{10,11... | collective-permute-start | bytes 1769480 | tf_op jit(solution)/shard_map/ppermute | solution.py:301
  843.8 66.6 %collective-permute-start.15 = (bf16[192,768]{1,0:T(8,128)(2,1)}, bf16[192,768]{1,0:T(8,128)(2,1)}, u32[]{:S(2)}, u32[]{:S(2)}) collective-permute-start(bf16[192,768]{1,0:T(8,128)(2,1)} %dynamic-slice_bitcast_fusion.16), channel_id=1, source_target_pairs={{0,2},{1,3},{2,0},{3,1},{4,6},{5,7},{6,4},{7,5},{8,10},{9,11},{10,... | collective-permute-start | bytes 884744 | tf_op jit(solution)/shard_map/ppermute | solution.py:301
  909.7 42.3 %collective-permute-start.4 = (bf16[384,2304]{1,0:T(8,128)(2,1)}, bf16[384,2304]{1,0:T(8,128)(2,1)}, u32[]{:S(2)}, u32[]{:S(2)}) collective-permute-start(bf16[384,2304]{1,0:T(8,128)(2,1)} %dynamic-slice_bitcast_fusion.5), channel_id=1, source_target_pairs={{0,1},{1,0},{2,3},{3,2},{4,5},{5,4},{6,7},{7,6},{8,9},{9,8},{10,11... | collective-permute-start | bytes 5308424 | tf_op jit(solution)/shard_map/ppermute | solution.py:301
  911.6 16.3 %collective-permute-start.16 = (bf16[48,768]{1,0:T(8,128)(2,1)S(1)}, bf16[48,768]{1,0:T(8,128)(2,1)S(1)}, u32[]{:S(2)}, u32[]{:S(2)}) collective-permute-start(bf16[48,768]{1,0:T(8,128)(2,1)S(1)} %get-tuple-element.171), channel_id=1, source_target_pairs={{0,4},{1,5},{2,6},{3,7},{4,0},{5,1},{6,2},{7,3},{8,12},{9,13},{10,... | collective-permute-start | bytes 221192 | tf_op jit(solution)/shard_map/ppermute | solution.py:301
  911.7 16.3 %collective-permute-start.17 = (bf16[48,768]{1,0:T(8,128)(2,1)S(1)}, bf16[48,768]{1,0:T(8,128)(2,1)S(1)}, u32[]{:S(2)}, u32[]{:S(2)}) collective-permute-start(bf16[48,768]{1,0:T(8,128)(2,1)S(1)} %get-tuple-element.173), channel_id=1, source_target_pairs={{0,8},{1,9},{2,10},{3,11},{4,12},{5,13},{6,14},{7,15},{8,0},{9,1},... | collective-permute-start | bytes 221192 | tf_op jit(solution)/shard_map/ppermute | solution.py:301
  911.8 16.2 %collective-permute-start.18 = (bf16[48,768]{1,0:T(8,128)(2,1)S(1)}, bf16[48,768]{1,0:T(8,128)(2,1)S(1)}, u32[]{:S(2)}, u32[]{:S(2)}) collective-permute-start(bf16[48,768]{1,0:T(8,128)(2,1)S(1)} %get-tuple-element.172), channel_id=1, source_target_pairs={{0,12},{1,13},{2,14},{3,15},{4,8},{5,9},{6,10},{7,11},{8,4},{9,5},... | collective-permute-start | bytes 221192 | tf_op jit(solution)/shard_map/ppermute | solution.py:301
  930.1 4.7 collective-permute-start.19
  931.8 50.3 %collective-permute-start.24 = (bf16[384,3072]{1,0:T(8,128)(2,1)}, bf16[384,3072]{1,0:T(8,128)(2,1)}, u32[]{:S(2)}, u32[]{:S(2)}) collective-permute-start(bf16[384,3072]{1,0:T(8,128)(2,1)} %dynamic-slice_bitcast_fusion.4), channel_id=1, source_target_pairs={{0,1},{1,0},{2,3},{3,2},{4,5},{5,4},{6,7},{7,6},{8,9},{9,8},{10,11... | collective-permute-start | bytes 7077896 | tf_op jit(solution)/shard_map/ppermute | solution.py:301
  933.6 9.3 collective-permute-start.20
  934.8 8.8 collective-permute-start.21
  944.2 7.6 collective-permute-start.22
  951.9 2.9 collective-permute-start.23
  954.5 22.5 %collective-permute-start.5 = (bf16[192,2304]{1,0:T(8,128)(2,1)S(1)}, bf16[192,2304]{1,0:T(8,128)(2,1)S(1)}, u32[]{:S(2)}, u32[]{:S(2)}) collective-permute-start(bf16[192,2304]{1,0:T(8,128)(2,1)S(1)} %dynamic-slice_bitcast_fusion.8), channel_id=1, source_target_pairs={{0,2},{1,3},{2,0},{3,1},{4,6},{5,7},{6,4},{7,5},{8,10},{9,11},{10,... | collective-permute-start | bytes 2654216 | tf_op jit(solution)/shard_map/ppermute | solution.py:301
  954.9 27.2 %slice-start.6 = ((s8[4718592]{0:T(1024)(128)(4,1)}), s8[4194304]{0:T(1024)(128)(4,1)S(1)}, s32[]{:S(2)}) async-start(s8[4718592]{0:T(1024)(128)(4,1)} %bitcast.798), calls=%async_computation.7 | async-start | bytes 8388608
  958.3 61.6 %collective-permute-start.35 = (bf16[768,768]{1,0:T(8,128)(2,1)S(1)}, bf16[768,768]{1,0:T(8,128)(2,1)S(1)}, u32[]{:S(2)}, u32[]{:S(2)}) collective-permute-start(bf16[768,768]{1,0:T(8,128)(2,1)S(1)} %dynamic-slice_bitcast_fusion.6), channel_id=1, source_target_pairs={{0,2},{1,3},{2,0},{3,1},{4,6},{5,7},{6,4},{7,5},{8,10},{9,11},{10,... | collective-permute-start | bytes 3538952 | tf_op jit(solution)/shard_map/ppermute | solution.py:301
  977.3 10.6 collective-permute-start.6
  979.7 18.7 %collective-permute-start.7 = (bf16[48,2304]{1,0:T(8,128)(2,1)S(1)}, bf16[48,2304]{1,0:T(8,128)(2,1)S(1)}, u32[]{:S(2)}, u32[]{:S(2)}) collective-permute-start(bf16[48,2304]{1,0:T(8,128)(2,1)S(1)} %get-tuple-element.170), channel_id=1, source_target_pairs={{0,8},{1,9},{2,10},{3,11},{4,12},{5,13},{6,14},{7,15},{8,0},{9,1},... | collective-permute-start | bytes 663560 | tf_op jit(solution)/shard_map/ppermute | solution.py:301
  980.0 18.4 %collective-permute-start.8 = (bf16[48,2304]{1,0:T(8,128)(2,1)S(1)}, bf16[48,2304]{1,0:T(8,128)(2,1)S(1)}, u32[]{:S(2)}, u32[]{:S(2)}) collective-permute-start(bf16[48,2304]{1,0:T(8,128)(2,1)S(1)} %get-tuple-element.169), channel_id=1, source_target_pairs={{0,12},{1,13},{2,14},{3,15},{4,8},{5,9},{6,10},{7,11},{8,4},{9,5},... | collective-permute-start | bytes 663560 | tf_op jit(solution)/shard_map/ppermute | solution.py:301
  998.6 10.1 collective-permute-start.9
  1002.1 25.8 %collective-permute-start.25 = (bf16[192,3072]{1,0:T(8,128)(2,1)S(1)}, bf16[192,3072]{1,0:T(8,128)(2,1)S(1)}, u32[]{:S(2)}, u32[]{:S(2)}) collective-permute-start(bf16[192,3072]{1,0:T(8,128)(2,1)S(1)} %dynamic-slice_bitcast_fusion.7), channel_id=1, source_target_pairs={{0,2},{1,3},{2,0},{3,1},{4,6},{5,7},{6,4},{7,5},{8,10},{9,11},{10,... | collective-permute-start | bytes 3538952 | tf_op jit(solution)/shard_map/ppermute | solution.py:301
  1002.4 17.4 %collective-permute-start.10 = (bf16[48,2304]{1,0:T(8,128)(2,1)S(1)}, bf16[48,2304]{1,0:T(8,128)(2,1)S(1)}, u32[]{:S(2)}, u32[]{:S(2)}) collective-permute-start(bf16[48,2304]{1,0:T(8,128)(2,1)S(1)} %get-tuple-element.108), channel_id=1, source_target_pairs={{0,8},{1,9},{2,10},{3,11},{4,12},{5,13},{6,14},{7,15},{8,0},{9,1},... | collective-permute-start | bytes 663560 | tf_op jit(solution)/shard_map/ppermute | solution.py:301
  1002.7 17.2 %collective-permute-start.11 = (bf16[48,2304]{1,0:T(8,128)(2,1)S(1)}, bf16[48,2304]{1,0:T(8,128)(2,1)S(1)}, u32[]{:S(2)}, u32[]{:S(2)}) collective-permute-start(bf16[48,2304]{1,0:T(8,128)(2,1)S(1)} %get-tuple-element.108), channel_id=1, source_target_pairs={{0,12},{1,13},{2,14},{3,15},{4,8},{5,9},{6,10},{7,11},{8,4},{9,5},... | collective-permute-start | bytes 663560 | tf_op jit(solution)/shard_map/ppermute | solution.py:301
  1020.3 18.0 %collective-permute-start.36 = (bf16[192,768]{1,0:T(8,128)(2,1)S(1)}, bf16[192,768]{1,0:T(8,128)(2,1)S(1)}, u32[]{:S(2)}, u32[]{:S(2)}) collective-permute-start(bf16[192,768]{1,0:T(8,128)(2,1)S(1)} %get-tuple-element.160), channel_id=1, source_target_pairs={{0,4},{1,5},{2,6},{3,7},{4,0},{5,1},{6,2},{7,3},{8,12},{9,13},{10,... | collective-permute-start | bytes 884744 | tf_op jit(solution)/shard_map/ppermute | solution.py:301
  1023.6 23.5 %collective-permute-start.37 = (bf16[192,768]{1,0:T(8,128)(2,1)S(1)}, bf16[192,768]{1,0:T(8,128)(2,1)S(1)}, u32[]{:S(2)}, u32[]{:S(2)}) collective-permute-start(bf16[192,768]{1,0:T(8,128)(2,1)S(1)} %get-tuple-element.162), channel_id=1, source_target_pairs={{0,8},{1,9},{2,10},{3,11},{4,12},{5,13},{6,14},{7,15},{8,0},{9,1},... | collective-permute-start | bytes 884744 | tf_op jit(solution)/shard_map/ppermute | solution.py:301
  1024.0 24.7 %collective-permute-start.38 = (bf16[192,768]{1,0:T(8,128)(2,1)S(1)}, bf16[192,768]{1,0:T(8,128)(2,1)S(1)}, u32[]{:S(2)}, u32[]{:S(2)}) collective-permute-start(bf16[192,768]{1,0:T(8,128)(2,1)S(1)} %get-tuple-element.161), channel_id=1, source_target_pairs={{0,12},{1,13},{2,14},{3,15},{4,8},{5,9},{6,10},{7,11},{8,4},{9,5},... | collective-permute-start | bytes 884744 | tf_op jit(solution)/shard_map/ppermute | solution.py:301
  1028.4 41.2 %collective-permute-start.26 = (bf16[48,3072]{1,0:T(8,128)(2,1)S(1)}, bf16[48,3072]{1,0:T(8,128)(2,1)S(1)}, u32[]{:S(2)}, u32[]{:S(2)}) collective-permute-start(bf16[48,3072]{1,0:T(8,128)(2,1)S(1)} %get-tuple-element.163), channel_id=1, source_target_pairs={{0,4},{1,5},{2,6},{3,7},{4,0},{5,1},{6,2},{7,3},{8,12},{9,13},{10,... | collective-permute-start | bytes 884744 | tf_op jit(solution)/shard_map/ppermute | solution.py:301
  1030.0 45.7 %collective-permute-start.27 = (bf16[48,3072]{1,0:T(8,128)(2,1)S(1)}, bf16[48,3072]{1,0:T(8,128)(2,1)S(1)}, u32[]{:S(2)}, u32[]{:S(2)}) collective-permute-start(bf16[48,3072]{1,0:T(8,128)(2,1)S(1)} %get-tuple-element.165), channel_id=1, source_target_pairs={{0,8},{1,9},{2,10},{3,11},{4,12},{5,13},{6,14},{7,15},{8,0},{9,1},... | collective-permute-start | bytes 884744 | tf_op jit(solution)/shard_map/ppermute | solution.py:301
  1038.3 41.0 %collective-permute-start.28 = (bf16[48,3072]{1,0:T(8,128)(2,1)S(1)}, bf16[48,3072]{1,0:T(8,128)(2,1)S(1)}, u32[]{:S(2)}, u32[]{:S(2)}) collective-permute-start(bf16[48,3072]{1,0:T(8,128)(2,1)S(1)} %get-tuple-element.164), channel_id=1, source_target_pairs={{0,12},{1,13},{2,14},{3,15},{4,8},{5,9},{6,10},{7,11},{8,4},{9,5},... | collective-permute-start | bytes 884744 | tf_op jit(solution)/shard_map/ppermute | solution.py:301
  1047.1 77.5 %collective-permute-start.12 = (bf16[192,2304]{1,0:T(8,128)(2,1)S(1)}, bf16[192,2304]{1,0:T(8,128)(2,1)S(1)}, u32[]{:S(2)}, u32[]{:S(2)}) collective-permute-start(bf16[192,2304]{1,0:T(8,128)(2,1)S(1)} %bitcast.839), channel_id=1, source_target_pairs={{0,2},{1,3},{2,0},{3,1},{4,6},{5,7},{6,4},{7,5},{8,10},{9,11},{10,... | collective-permute-start | bytes 2654216 | tf_op jit(solution)/shard_map/ppermute | solution.py:301
  1048.9 46.0 %collective-permute-start.39 = (bf16[192,768]{1,0:T(8,128)(2,1)S(1)}, bf16[192,768]{1,0:T(8,128)(2,1)S(1)}, u32[]{:S(2)}, u32[]{:S(2)}) collective-permute-start(bf16[192,768]{1,0:T(8,128)(2,1)S(1)} %get-tuple-element.90), channel_id=1, source_target_pairs={{0,4},{1,5},{2,6},{3,7},{4,0},{5,1},{6,2},{7,3},{8,12},{9,13},{10,... | collective-permute-start | bytes 884744 | tf_op jit(solution)/shard_map/ppermute | solution.py:301
  1069.6 31.5 %collective-permute-start.40 = (bf16[192,768]{1,0:T(8,128)(2,1)S(1)}, bf16[192,768]{1,0:T(8,128)(2,1)S(1)}, u32[]{:S(2)}, u32[]{:S(2)}) collective-permute-start(bf16[192,768]{1,0:T(8,128)(2,1)S(1)} %get-tuple-element.90), channel_id=1, source_target_pairs={{0,8},{1,9},{2,10},{3,11},{4,12},{5,13},{6,14},{7,15},{8,0},{9,1},... | collective-permute-start | bytes 884744 | tf_op jit(solution)/shard_map/ppermute | solution.py:301
  1075.8 28.9 %collective-permute-start.41 = (bf16[192,768]{1,0:T(8,128)(2,1)S(1)}, bf16[192,768]{1,0:T(8,128)(2,1)S(1)}, u32[]{:S(2)}, u32[]{:S(2)}) collective-permute-start(bf16[192,768]{1,0:T(8,128)(2,1)S(1)} %get-tuple-element.90), channel_id=1, source_target_pairs={{0,12},{1,13},{2,14},{3,15},{4,8},{5,9},{6,10},{7,11},{8,4},{9,5},... | collective-permute-start | bytes 884744 | tf_op jit(solution)/shard_map/ppermute | solution.py:301
  1079.6 25.8 %collective-permute-start.29 = (bf16[48,3072]{1,0:T(8,128)(2,1)S(1)}, bf16[48,3072]{1,0:T(8,128)(2,1)S(1)}, u32[]{:S(2)}, u32[]{:S(2)}) collective-permute-start(bf16[48,3072]{1,0:T(8,128)(2,1)S(1)} %get-tuple-element.96), channel_id=1, source_target_pairs={{0,4},{1,5},{2,6},{3,7},{4,0},{5,1},{6,2},{7,3},{8,12},{9,13},{10,... | collective-permute-start | bytes 884744 | tf_op jit(solution)/shard_map/ppermute | solution.py:301
  1094.9 27.5 %collective-permute-start.30 = (bf16[48,3072]{1,0:T(8,128)(2,1)S(1)}, bf16[48,3072]{1,0:T(8,128)(2,1)S(1)}, u32[]{:S(2)}, u32[]{:S(2)}) collective-permute-start(bf16[48,3072]{1,0:T(8,128)(2,1)S(1)} %get-tuple-element.96), channel_id=1, source_target_pairs={{0,8},{1,9},{2,10},{3,11},{4,12},{5,13},{6,14},{7,15},{8,0},{9,1},... | collective-permute-start | bytes 884744 | tf_op jit(solution)/shard_map/ppermute | solution.py:301
  1101.1 21.4 %collective-permute-start.31 = (bf16[48,3072]{1,0:T(8,128)(2,1)S(1)}, bf16[48,3072]{1,0:T(8,128)(2,1)S(1)}, u32[]{:S(2)}, u32[]{:S(2)}) collective-permute-start(bf16[48,3072]{1,0:T(8,128)(2,1)S(1)} %get-tuple-element.96), channel_id=1, source_target_pairs={{0,12},{1,13},{2,14},{3,15},{4,8},{5,9},{6,10},{7,11},{8,4},{9,5},... | collective-permute-start | bytes 884744 | tf_op jit(solution)/shard_map/ppermute | solution.py:301
  1104.7 24.7 %collective-permute-start.42 = (bf16[768,768]{1,0:T(8,128)(2,1)S(1)}, bf16[768,768]{1,0:T(8,128)(2,1)S(1)}, u32[]{:S(2)}, u32[]{:S(2)}) collective-permute-start(bf16[768,768]{1,0:T(8,128)(2,1)S(1)} %bitcast.804), channel_id=1, source_target_pairs={{0,2},{1,3},{2,0},{3,1},{4,6},{5,7},{6,4},{7,5},{8,10},{9,11},{10,... | collective-permute-start | bytes 3538952 | tf_op jit(solution)/shard_map/ppermute | solution.py:301
  1122.5 27.6 %collective-permute-start.32 = (bf16[192,3072]{1,0:T(8,128)(2,1)S(1)}, bf16[192,3072]{1,0:T(8,128)(2,1)S(1)}, u32[]{:S(2)}, u32[]{:S(2)}) collective-permute-start(bf16[192,3072]{1,0:T(8,128)(2,1)S(1)} %bitcast.802), channel_id=1, source_target_pairs={{0,2},{1,3},{2,0},{3,1},{4,6},{5,7},{6,4},{7,5},{8,10},{9,11},{10,... | collective-permute-start | bytes 3538952 | tf_op jit(solution)/shard_map/ppermute | solution.py:301
  1124.7 25.6 %collective-permute-start.13 = (bf16[384,2304]{1,0:T(8,128)(2,1)S(1)}, bf16[384,2304]{1,0:T(8,128)(2,1)S(1)}, u32[]{:S(2)}, u32[]{:S(2)}) collective-permute-start(bf16[384,2304]{1,0:T(8,128)(2,1)S(1)} %bitcast.792), channel_id=1, source_target_pairs={{0,1},{1,0},{2,3},{3,2},{4,5},{5,4},{6,7},{7,6},{8,9},{9,8},{10,11... | collective-permute-start | bytes 5308424 | tf_op jit(solution)/shard_map/ppermute | solution.py:301
  1129.6 24.9 %collective-permute-start.43 = (bf16[1536,768]{1,0:T(8,128)(2,1)S(1)}, bf16[1536,768]{1,0:T(8,128)(2,1)S(1)}, u32[]{:S(2)}, u32[]{:S(2)}) collective-permute-start(bf16[1536,768]{1,0:T(8,128)(2,1)S(1)} %bitcast.770), channel_id=1, source_target_pairs={{0,1},{1,0},{2,3},{3,2},{4,5},{5,4},{6,7},{7,6},{8,9},{9,8},{10,11... | collective-permute-start | bytes 7077896 | tf_op jit(solution)/shard_map/ppermute | solution.py:301
  1150.2 9.6 collective-permute-start.33
  (197 other events, 1199.6 us)
Sparse Core Ops, SparseCore 0:
  476.3 123.4 all-reduce.2

commit v2 on v1

v2 whole, which is shorter than its diff:
```python
import functools
import jax
import jax.numpy as jnp
from jax import lax
from jax.experimental import pallas as pl
from jax.experimental.pallas import tpu as pltpu
from jax.sharding import PartitionSpec as P

HEAD_DIM = 64
QLEN = 32
NQ = 4
NP = 4
PSLOTS = 512
LAYER_EPSILON = 1e-12
UNIT_EPSILON = 1e-06
SMOOTHING = 0.05
LOGIT_SCALE = 4.0
ROOT_HALF = 0.7071067811865476
NORMAL_PEAK = 0.3989422804014327
BF = jnp.bfloat16
F32 = jnp.float32
QROWS = NQ * QLEN
SLAB = 256
FFBLOCK = 768
VMEM_LIMIT = 56 * 1024 * 1024
NEG = -1e30


def dot_nn(a, b):
    return jnp.dot(a, b, preferred_element_type=F32)


def dot_nt(a, b):
    return lax.dot_general(a, b, (((1,), (1,)), ((), ())), preferred_element_type=F32)


def dot_tn(a, b):
    return lax.dot_general(a, b, (((0,), (0,)), ((), ())), preferred_element_type=F32)


def gelu_pair(u):
    z = jnp.abs(u) * ROOT_HALF
    t = 1.0 / (1.0 + 0.3275911 * z)
    e = jnp.exp(-0.5 * u * u)
    poly = ((((1.061405429 * t - 1.453152027) * t) + 1.421413741) * t - 0.284496736) * t + 0.254829592
    tail = 0.5 * poly * t * e
    phi = jnp.where(u >= 0, 1.0 - tail, tail)
    return u * phi, phi + NORMAL_PEAK * u * e


def norm_rows(resid):
    centre = resid - jnp.mean(resid, axis=1, keepdims=True)
    inv = lax.rsqrt(jnp.mean(centre * centre, axis=1, keepdims=True) + LAYER_EPSILON)
    return centre * inv, inv


def ends_of(info, micro):
    base = 1 + micro * NP
    ends = []
    total = jnp.int32(0)
    for j in range(NP):
        total = total + info[base + j]
        ends.append(total)
    return ends


def passage_of(place, ends):
    out = jnp.zeros(place.shape, jnp.int32)
    for end in ends:
        out = out + jnp.where(place >= end, 1, 0)
    return out


def fwd_micro(info, tick, micros):
    return jnp.minimum(jnp.maximum(tick - info[0], 0), micros - 1)


def bwd_micro(info, tick, micros):
    return jnp.minimum(jnp.maximum(tick - 1 + info[0], 0), micros - 1)


def fill_masks(info, micro, bias_ref):
    ends = ends_of(info, micro)
    down = passage_of(lax.broadcasted_iota(jnp.int32, (PSLOTS, 1), 0), ends)
    across = passage_of(lax.broadcasted_iota(jnp.int32, (1, PSLOTS), 1), ends)
    bias_ref[...] = jnp.where(down == across, 0.0, NEG).astype(F32)


def query_bias():
    down = lax.broadcasted_iota(jnp.int32, (QROWS, QROWS), 0) // QLEN
    across = lax.broadcasted_iota(jnp.int32, (QROWS, QROWS), 1) // QLEN
    return jnp.where(down == across, 0.0, NEG).astype(F32)


def usable_rows(info, micro, rows):
    ends = ends_of(info, micro)
    place = lax.broadcasted_iota(jnp.int32, (rows, 1), 0)
    return (place < QROWS + ends[-1]).astype(F32)


def half_lanes(value, h):
    lane = lax.broadcasted_iota(jnp.int32, (1, 128), 1) // HEAD_DIM
    return jnp.where(lane == h, value, jnp.zeros_like(value))


def attn_fwd_body(tick, micros, first_tick, info, hid, rec, wq, wk, wv, bq, bv, wm, bm, gain, shift, *rest):
    rest = rest[8:] if not first_tick else rest
    x_out, joined_out, lse_out, ctx_out, hid_out, n_out, inv_out, sq_out, acc, bias, xs, otr, vtr = rest
    g = pl.program_id(0)
    micro = fwd_micro(info, tick, micros)
    rows = hid.shape[0]

    @pl.when(g == 0)
    def _():
        if first_tick:
            xs[...] = hid[...]
        else:
            xs[...] = jnp.where(info[0] == 0, hid[...], rec[...])
        x_out[...] = xs[...]
        fill_masks(info, micro, bias)

    x = xs[...]
    q = (dot_nn(x, wq[...]) + bq[...]).astype(BF)
    joined_out[:, 0:SLAB] = q
    k = dot_nn(x, wk[...]).astype(BF)
    joined_out[:, SLAB : 2 * SLAB] = k
    v32 = dot_nn(x, wv[...]) + bv[...]
    v = v32.astype(BF)
    joined_out[:, 2 * SLAB : 3 * SLAB] = v
    vtr[...] = jnp.transpose(v)
    qbias = query_bias()
    for pair in range(SLAB // 128):
        cols = slice(pair * 128, pair * 128 + 128)
        qs = joined_out[:, cols] * BF(HEAD_DIM**-0.5)
        ks = joined_out[:, SLAB + pair * 128 : SLAB + pair * 128 + 128]
        for h in range(2):
            head = pair * 2 + h
            qm = half_lanes(qs, h)
            vh = slice(head * HEAD_DIM, head * HEAD_DIM + HEAD_DIM)
            st = dot_nt(ks[:QROWS], qm[:QROWS]) + qbias
            top = jnp.max(st, axis=0, keepdims=True)
            p = jnp.exp(st - top)
            total = jnp.sum(p, axis=0, keepdims=True)
            lse_out[head : head + 1, 0:QROWS] = top + jnp.log(total)
            otr[vh, 0:QROWS] = dot_nn(vtr[vh, 0:QROWS], p.astype(BF)) * (1.0 / total)
            for c in range(PSLOTS // 256):
                at = slice(QROWS + c * 256, QROWS + c * 256 + 256)
                st = dot_nt(ks[QROWS:], qm[at]) + bias[:, c * 256 : c * 256 + 256]
                top = jnp.max(st, axis=0, keepdims=True)
                p = jnp.exp(st - top)
                total = jnp.sum(p, axis=0, keepdims=True)
                lse_out[head : head + 1, at] = top + jnp.log(total)
                otr[vh, at] = dot_nn(vtr[vh, QROWS:], p.astype(BF)) * (1.0 / total)
    ctx = jnp.transpose(otr[...]).astype(BF)
    ctx_out[...] = ctx
    part = dot_nn(ctx, wm[...])

    @pl.when(g == 0)
    def _():
        acc[...] = part

    @pl.when(g > 0)
    def _():
        acc[...] += part

    @pl.when(g == pl.num_programs(0) - 1)
    def _():
        b1 = acc[...] + bm[...]
        x32 = xs[...].astype(F32)
        n, inv = norm_rows(x32 + b1)
        hid_out[...] = (n * gain[...] + shift[...]).astype(BF)
        n_out[...] = n.astype(BF)
        inv_out[...] = inv
        mask = usable_rows(info, micro, rows)
        sq_out[0:1, :] = jnp.sum(mask * x32 * x32, axis=0, keepdims=True)
        sq_out[1:2, :] = jnp.sum(mask * b1 * b1, axis=0, keepdims=True)


def attn_forward(tick, micros, info, hidden_in, received, weights, old):
    (wa, ba, wm, bm, gains, shifts) = weights
    rows = hidden_in.shape[0] // micros
    width = hidden_in.shape[1]
    steps = width // SLAB
    first = old is None
    slot = lambda info: fwd_micro(info, tick, micros)
    one = lambda *shape: pl.BlockSpec(shape, lambda g, info: (0,) * len(shape))
    in_specs = [
        pl.BlockSpec((rows, width), lambda g, info: (slot(info), 0)),
        one(rows, width),
        pl.BlockSpec((width, SLAB), lambda g, info: (0, g)),
        pl.BlockSpec((width, SLAB), lambda g, info: (0, steps + g)),
        pl.BlockSpec((width, SLAB), lambda g, info: (0, 2 * steps + g)),
        pl.BlockSpec((1, SLAB), lambda g, info: (0, g)),
        pl.BlockSpec((1, SLAB), lambda g, info: (0, steps + g)),
        pl.BlockSpec((SLAB, width), lambda g, info: (g, 0)),
        one(1, width),
        one(1, width),
        one(1, width),
    ]
    args = [hidden_in, received, wa, wa, wa, ba, ba, wm, bm, gains[0:1], shifts[0:1]]
    shapes = [
        ((micros, rows, width), BF, (None, rows, width), lambda g, i: (slot(i), 0, 0)),
        ((micros, steps, rows, 3 * SLAB), BF, (None, None, rows, 3 * SLAB), lambda g, i: (slot(i), g, 0, 0)),
        ((micros, steps, 8, rows), F32, (None, None, 8, rows), lambda g, i: (slot(i), g, 0, 0)),
        ((micros, rows, width), BF, (None, rows, SLAB), lambda g, i: (slot(i), 0, g)),
        ((micros, rows, width), BF, (None, rows, width), lambda g, i: (slot(i), 0, 0)),
        ((micros, rows, width), BF, (None, rows, width), lambda g, i: (slot(i), 0, 0)),
        ((micros, rows, 1), F32, (None, rows, 1), lambda g, i: (slot(i), 0, 0)),
        ((micros, 8, width), F32, (None, 8, width), lambda g, i: (slot(i), 0, 0)),
    ]
    return call(
        functools.partial(attn_fwd_body, tick, micros, first),
        steps, info, args, in_specs, shapes, old,
        [
            pltpu.VMEM((rows, width), F32),
            pltpu.VMEM((PSLOTS, PSLOTS), F32),
            pltpu.VMEM((rows, width), BF),
            pltpu.VMEM((SLAB, rows), F32),
            pltpu.VMEM((SLAB, rows), BF),
        ],
        flops=2 * rows * width * width * 4 + 4 * 12 * 64 * rows * rows,
    )


def call(body, steps, info, args, in_specs, shapes, old, scratch, flops):
    aliases = {}
    if old is not None:
        in_specs = in_specs + [pl.BlockSpec(memory_space=pl.ANY)] * len(old)
        aliases = {1 + len(args) + i: i for i in range(len(old))}
        args = args + list(old)
    return pl.pallas_call(
        body,
        out_shape=[jax.ShapeDtypeStruct(s[0], s[1]) for s in shapes],
        grid_spec=pltpu.PrefetchScalarGridSpec(
            num_scalar_prefetch=1,
            grid=(steps,),
            in_specs=in_specs,
            out_specs=[pl.BlockSpec(s[2], s[3]) for s in shapes],
            scratch_shapes=scratch,
        ),
        input_output_aliases=aliases,
        compiler_params=pltpu.CompilerParams(
            dimension_semantics=("arbitrary",), vmem_limit_bytes=VMEM_LIMIT
        ),
        cost_estimate=pl.CostEstimate(flops=flops, bytes_accessed=20_000_000, transcendentals=0),
    )(info, *args)


def ffn_fwd_body(tick, micros, first_tick, info, hid, we, be, wr, br, gain, shift, *rest):
    rest = rest[6:] if not first_tick else rest
    act_out, slope_out, out_all, n_out, inv_out, sq_out, send_out, acc = rest
    j = pl.program_id(0)
    micro = fwd_micro(info, tick, micros)
    rows = hid.shape[0]
    step = 128
    for r in range(rows // step):
        at = slice(r * step, r * step + step)
        inner = dot_nn(hid[at], we[...]) + be[...]
        active, slope = gelu_pair(inner)
        active = active.astype(BF)
        act_out[at] = active
        slope_out[at] = slope.astype(BF)
        part = dot_nn(active, wr[...])

        @pl.when(j == 0)
        def _():
            acc[at] = part

        @pl.when(j > 0)
        def _():
            acc[at] += part

    @pl.when(j == pl.num_programs(0) - 1)
    def _():
        b2 = acc[...] + br[...]
        n, inv = norm_rows(hid[...].astype(F32) + b2)
        out = (n * gain[...] + shift[...]).astype(BF)
        out_all[...] = out
        send_out[...] = out
        n_out[...] = n.astype(BF)
        inv_out[...] = inv
        mask = usable_rows(info, micro, rows)
        sq_out[0:1, :] = jnp.sum(mask * b2 * b2, axis=0, keepdims=True)


def ffn_forward(tick, micros, info, hidden, weights, old):
    (we, be, wr, br, gains, shifts) = weights
    _, rows, width = hidden.shape
    ff = we.shape[1]
    steps = ff // FFBLOCK
    first = old is None
    slot = lambda info: fwd_micro(info, tick, micros)
    one = lambda *shape: pl.BlockSpec(shape, lambda g, info: (0,) * len(shape))
    in_specs = [
        pl.BlockSpec((None, rows, width), lambda g, i: (slot(i), 0, 0)),
        pl.BlockSpec((width, FFBLOCK), lambda g, i: (0, g)),
        pl.BlockSpec((1, FFBLOCK), lambda g, i: (0, g)),
        pl.BlockSpec((FFBLOCK, width), lambda g, i: (g, 0)),
        one(1, width),
        one(1, width),
        one(1, width),
    ]
    args = [hidden, we, be, wr, br, gains[1:2], shifts[1:2]]
    shapes = [
        ((micros, rows, ff), BF, (None, rows, FFBLOCK), lambda g, i: (slot(i), 0, g)),
        ((micros, rows, ff), BF, (None, rows, FFBLOCK), lambda g, i: (slot(i), 0, g)),
        ((micros, rows, width), BF, (None, rows, width), lambda g, i: (slot(i), 0, 0)),
        ((micros, rows, width), BF, (None, rows, width), lambda g, i: (slot(i), 0, 0)),
        ((micros, rows, 1), F32, (None, rows, 1), lambda g, i: (slot(i), 0, 0)),
        ((micros, 8, width), F32, (None, 8, width), lambda g, i: (slot(i), 0, 0)),
        ((rows, width), BF, (rows, width), lambda g, i: (0, 0)),
    ]
    return call(
        functools.partial(ffn_fwd_body, tick, micros, first),
        steps, info, args, in_specs, shapes, old,
        [pltpu.VMEM((rows, width), F32)],
        flops=4 * rows * width * ff,
    )


def column_sum(value):
    return jnp.sum(value, axis=0, keepdims=True)


def norm_rows_back(grad_out, n, inv, gain):
    grad_unit = grad_out * gain
    mean_grad = jnp.mean(grad_unit, axis=1, keepdims=True)
    mean_along = jnp.mean(grad_unit * n, axis=1, keepdims=True)
    return inv * (grad_unit - mean_grad - n * mean_along)


def loss_parts(info, micro, micros, grad_scale, out_b, wc):
    ends = ends_of(info, micro)
    embedded = dot_nn(out_b, wc)
    inv_norm = lax.rsqrt(jnp.sum(embedded * embedded, axis=1, keepdims=True) + UNIT_EPSILON)
    unit = embedded * inv_norm
    unit_b = unit.astype(BF)
    queries, passages = unit_b[:QROWS], unit_b[QROWS:]
    scaled = dot_nt(queries, passages) / SMOOTHING
    owner = passage_of(lax.broadcasted_iota(jnp.int32, (1, PSLOTS), 1), ends)
    top = jnp.max(jnp.where(owner < NP, scaled, NEG), axis=1, keepdims=True)
    terms = jnp.exp(scaled - top)
    lane = lax.broadcasted_iota(jnp.int32, (1, 128), 1)
    totals = jnp.ones((QROWS, 128), F32)
    lengths = jnp.ones((1, 128), F32)
    for j in range(NP):
        total = jnp.sum(jnp.where(owner == j, terms, 0.0), axis=1, keepdims=True)
        totals = jnp.where(lane == j, total, totals)
        lengths = jnp.where(lane == j, info[1 + micro * NP + j].astype(F32), lengths)
    smooth = SMOOTHING * (jnp.log(totals) + top - jnp.log(lengths))
    grouped = jnp.sum(smooth.reshape(NQ, QLEN, 128), axis=1, keepdims=True)
    scores = LOGIT_SCALE * grouped
    scores = jnp.where(lane[None] < NP, scores, NEG)
    score_max = jnp.max(scores, axis=2, keepdims=True)
    score_exp = jnp.exp(scores - score_max)
    score_total = jnp.sum(score_exp, axis=2, keepdims=True)
    query = lax.broadcasted_iota(jnp.int32, (NQ, 1, 128), 0)
    chosen = jnp.zeros((NQ, 1, 128), jnp.int32)
    for i in range(NQ):
        chosen = jnp.where(query == i, info[1 + micros * NP + micro * NQ + i], chosen)
    onehot = (chosen == lane[None]).astype(F32)
    own_score = jnp.sum(jnp.where(chosen == lane[None], scores, 0.0), axis=2, keepdims=True)
    losses = jnp.log(score_total) + score_max - own_score
    loss = jnp.sum(losses, axis=0)
    grad_scores = (score_exp / score_total - onehot) * grad_scale
    grad_smooth = jnp.broadcast_to(LOGIT_SCALE * grad_scores, (NQ, QLEN, 128)).reshape(QROWS, 128)
    share = grad_smooth / totals
    weight = jnp.zeros((QROWS, PSLOTS), F32)
    for j in range(NP):
        weight = jnp.where(owner == j, share[:, j : j + 1], weight)
    grad_similar = jnp.where(owner < NP, terms * weight, 0.0).astype(BF)
    grad_unit = jnp.concatenate([dot_nn(grad_similar, passages), dot_tn(grad_similar, queries)])
    grad_embed = inv_norm * (grad_unit - unit * jnp.sum(grad_unit * unit, axis=1, keepdims=True))
    return loss, grad_embed.astype(BF)


def ffn_bwd_body(tick, micros, grad_scale, first_tick, info, out_all, wc, rec, n2, inv2, gain2, slope, wr, we, n1, inv1, gain1, *rest):
    rest = rest[6:] if not first_tick else rest
    two_out, inner_out, one_out, emb_out, small_out, ff_out, resid_out, acc, resid, grad = rest
    j = pl.program_id(0)
    micro = bwd_micro(info, tick, micros)

    @pl.when(j == 0)
    def _():
        small_out[...] = jnp.zeros(small_out.shape, F32)

        @pl.when(info[0] == 1)
        def _():
            loss, grad_embed = loss_parts(info, micro, micros, grad_scale, out_all[...], wc[...])
            emb_out[...] = grad_embed
            grad[...] = dot_nt(grad_embed, wc[...])
            small_out[6:7, 0:128] = jnp.broadcast_to(loss, (1, 128))

        @pl.when(info[0] == 0)
        def _():
            emb_out[...] = jnp.zeros(emb_out.shape, BF)
            grad[...] = rec[...].astype(F32)

        upstream = grad[...]
        n = n2[...].astype(F32)
        small_out[0:1, :] = column_sum(upstream * n)
        small_out[1:2, :] = column_sum(upstream)
        d_two = norm_rows_back(upstream, n, inv2[...], gain2[...])
        resid[...] = d_two
        d_two_b = d_two.astype(BF)
        two_out[...] = d_two_b
        small_out[2:3, :] = column_sum(d_two_b.astype(F32))

    rows = two_out.shape[0]
    step = 128
    total = jnp.zeros((1, FFBLOCK), F32)
    for r in range(rows // step):
        at = slice(r * step, r * step + step)
        d_act = dot_nt(two_out[at], wr[...])
        d_inner = (d_act * slope[at].astype(F32)).astype(BF)
        inner_out[at] = d_inner
        total = total + column_sum(d_inner.astype(F32))
        part = dot_nt(d_inner, we[...])

        @pl.when(j == 0)
        def _():
            acc[at] = part

        @pl.when(j > 0)
        def _():
            acc[at] += part
    ff_out[0:1, :] = total

    @pl.when(j == pl.num_programs(0) - 1)
    def _():
        upstream = resid[...] + acc[...]
        n = n1[...].astype(F32)
        small_out[3:4, :] = column_sum(upstream * n)
        small_out[4:5, :] = column_sum(upstream)
        d_one = norm_rows_back(upstream, n, inv1[...], gain1[...])
        resid_out[...] = d_one
        d_one_b = d_one.astype(BF)
        one_out[...] = d_one_b
        small_out[5:6, :] = column_sum(d_one_b.astype(F32))


def ffn_backward(tick, micros, grad_scale, info, received, kept, weights, old):
    (out_all, n2, inv2, slope, n1, inv1) = kept
    (wc, gains, wr, we) = weights
    _, rows, width = out_all.shape
    ff = we.shape[1]
    steps = ff // FFBLOCK
    first = old is None
    slot = lambda info: bwd_micro(info, tick, micros)
    one = lambda *shape: pl.BlockSpec(shape, lambda g, info: (0,) * len(shape))
    at_slot = lambda *shape: pl.BlockSpec((None,) + shape, lambda g, i: (slot(i), 0, 0))
    in_specs = [
        at_slot(rows, width),
        one(*wc.shape),
        one(rows, width),
        at_slot(rows, width),
        at_slot(rows, 1),
        one(1, width),
        pl.BlockSpec((None, rows, FFBLOCK), lambda g, i: (slot(i), 0, g)),
        pl.BlockSpec((FFBLOCK, width), lambda g, i: (g, 0)),
        pl.BlockSpec((width, FFBLOCK), lambda g, i: (0, g)),
        at_slot(rows, width),
        at_slot(rows, 1),
        one(1, width),
    ]
    args = [out_all, wc, received, n2, inv2, gains[1:2], slope, wr, we, n1, inv1, gains[0:1]]
    emb = wc.shape[1]
    shapes = [
        ((micros, rows, width), BF, (None, rows, width), lambda g, i: (slot(i), 0, 0)),
        ((micros, rows, ff), BF, (None, rows, FFBLOCK), lambda g, i: (slot(i), 0, g)),
        ((micros, rows, width), BF, (None, rows, width), lambda g, i: (slot(i), 0, 0)),
        ((micros, rows, emb), BF, (None, rows, emb), lambda g, i: (slot(i), 0, 0)),
        ((micros, 8, width), F32, (None, 8, width), lambda g, i: (slot(i), 0, 0)),
        ((micros, 8, ff), F32, (None, 8, FFBLOCK), lambda g, i: (slot(i), 0, g)),
        ((rows, width), F32, (rows, width), lambda g, i: (0, 0)),
    ]
    return call(
        functools.partial(ffn_bwd_body, tick, micros, grad_scale, first),
        steps, info, args, in_specs, shapes, old,
        [pltpu.VMEM((rows, width), F32), pltpu.VMEM((rows, width), F32), pltpu.VMEM((rows, width), F32)],
        flops=4 * rows * width * ff,
    )


def attn_bwd_body(tick, micros, first_tick, info, resid, one_b, joined, lse, ctx, wm, wq, wk, wv, *rest):
    rest = rest[4:] if not first_tick else rest
    dq_out, dk_out, dv_out, sum_out, send_out, acc, bias, dctx, delta, ktr, dqtr, pbuf, sbuf = rest
    g = pl.program_id(0)
    micro = bwd_micro(info, tick, micros)

    @pl.when(g == 0)
    def _():
        fill_masks(info, micro, bias)

    dctx32 = dot_nt(one_b[...], wm[...])
    dctx[...] = dctx32.astype(BF)
    along = dctx[...].astype(F32) * ctx[...].astype(F32)
    pick = lax.broadcasted_iota(jnp.int32, (8, SLAB), 0) == lax.broadcasted_iota(jnp.int32, (8, SLAB), 1) // HEAD_DIM
    delta[...] = lax.dot_general(
        pick.astype(F32), along, (((1,), (1,)), ((), ())),
        precision=lax.Precision.HIGHEST, preferred_element_type=F32,
    )
    ktr[...] = jnp.transpose(joined[:, SLAB : 2 * SLAB])
    qbias = query_bias()
    for pair in range(SLAB // 128):
        lo = pair * 128
        qs = joined[:, lo : lo + 128] * BF(HEAD_DIM**-0.5)
        ks = joined[:, SLAB + lo : SLAB + lo + 128]
        vs = joined[:, 2 * SLAB + lo : 2 * SLAB + lo + 128]
        do = dctx[:, lo : lo + 128]
        qms = []
        dos = []
        pq = []
        sq = []
        for h in range(2):
            head = pair * 2 + h
            qm = half_lanes(qs, h)
            dm = half_lanes(do, h)
            qms.append(qm)
            dos.append(dm)
            kh = slice(head * HEAD_DIM, head * HEAD_DIM + HEAD_DIM)
            st = dot_nt(ks[:QROWS], qm[:QROWS]) + qbias
            p = jnp.exp(st - lse[head : head + 1, 0:QROWS])
            dp = dot_nt(vs[:QROWS], dm[:QROWS])
            ds = (p * (dp - delta[head : head + 1, 0:QROWS])).astype(BF)
            pq.append(p.astype(BF))
            sq.append(ds)
            dqtr[kh, 0:QROWS] = dot_nn(ktr[kh, 0:QROWS], ds)
            for c in range(PSLOTS // 256):
                at = slice(QROWS + c * 256, QROWS + c * 256 + 256)
                into = slice(h * PSLOTS + c * 256, h * PSLOTS + c * 256 + 256)
                st = dot_nt(ks[QROWS:], qm[at]) + bias[:, c * 256 : c * 256 + 256]
                p = jnp.exp(st - lse[head : head + 1, at])
                dp = dot_nt(vs[QROWS:], dm[at])
                ds = (p * (dp - delta[head : head + 1, at])).astype(BF)
                pbuf[:, into] = p.astype(BF)
                sbuf[:, into] = ds
                dqtr[kh, at] = dot_nn(ktr[kh, QROWS:], ds)
        both_q = jnp.concatenate(qms)
        rows = qs.shape[0]
        q_heads = jnp.concatenate([qms[0][:QROWS], qms[1][:QROWS]])
        d_heads = jnp.concatenate([dos[0][:QROWS], dos[1][:QROWS]])
        dk_out[0:QROWS, lo : lo + 128] = dot_nn(jnp.concatenate(sq, axis=1), q_heads).astype(BF)
        dv_out[0:QROWS, lo : lo + 128] = dot_nn(jnp.concatenate(pq, axis=1), d_heads).astype(BF)
        q_heads = jnp.concatenate([qms[0][QROWS:], qms[1][QROWS:]])
        d_heads = jnp.concatenate([dos[0][QROWS:], dos[1][QROWS:]])
        dk_out[QROWS:rows, lo : lo + 128] = dot_nn(sbuf[...], q_heads).astype(BF)
        dv_out[QROWS:rows, lo : lo + 128] = dot_nn(pbuf[...], d_heads).astype(BF)
    dq = (jnp.transpose(dqtr[...]) * HEAD_DIM**-0.5).astype(BF)
    dq_out[...] = dq
    dk = dk_out[...]
    dv = dv_out[...]
    sum_out[0:1, 0:SLAB] = column_sum(dq.astype(F32))
    sum_out[0:1, SLAB : 2 * SLAB] = column_sum(dv.astype(F32))
    part = dot_nt(dq, wq[...]) + dot_nt(dk, wk[...]) + dot_nt(dv, wv[...])

    @pl.when(g == 0)
    def _():
        acc[...] = part

    @pl.when(g > 0)
    def _():
        acc[...] += part

    @pl.when(g == pl.num_programs(0) - 1)
    def _():
        send_out[...] = (resid[...] + acc[...]).astype(BF)


def attn_backward(tick, micros, info, resid, one_all, kept, weights, old):
    (joined, lse, ctx) = kept
    (wa, wm) = weights
    _, rows, width = one_all.shape
    steps = width // SLAB
    first = old is None
    slot = lambda info: bwd_micro(info, tick, micros)
    one = lambda *shape: pl.BlockSpec(shape, lambda g, info: (0,) * len(shape))
    in_specs = [
        one(rows, width),
        pl.BlockSpec((None, rows, width), lambda g, i: (slot(i), 0, 0)),
        pl.BlockSpec((None, None, rows, 3 * SLAB), lambda g, i: (slot(i), g, 0, 0)),
        pl.BlockSpec((None, None, 8, rows), lambda g, i: (slot(i), g, 0, 0)),
        pl.BlockSpec((None, rows, SLAB), lambda g, i: (slot(i), 0, g)),
        pl.BlockSpec((SLAB, width), lambda g, i: (g, 0)),
        pl.BlockSpec((width, SLAB), lambda g, i: (0, g)),
        pl.BlockSpec((width, SLAB), lambda g, i: (0, steps + g)),
        pl.BlockSpec((width, SLAB), lambda g, i: (0, 2 * steps + g)),
    ]
    args = [resid, one_all, joined, lse, ctx, wm, wa, wa, wa]
    slab = ((micros, rows, width), BF, (None, rows, SLAB), lambda g, i: (slot(i), 0, g))
    shapes = [
        slab,
        slab,
        slab,
        ((micros, steps, 8, 2 * SLAB), F32, (None, None, 8, 2 * SLAB), lambda g, i: (slot(i), g, 0, 0)),
        ((rows, width), BF, (rows, width), lambda g, i: (0, 0)),
    ]
    return call(
        functools.partial(attn_bwd_body, tick, micros, first),
        steps, info, args, in_specs, shapes, old,
        [
            pltpu.VMEM((rows, width), F32),
            pltpu.VMEM((PSLOTS, PSLOTS), F32),
            pltpu.VMEM((rows, SLAB), BF),
            pltpu.VMEM((8, rows), F32),
            pltpu.VMEM((SLAB, rows), BF),
            pltpu.VMEM((SLAB, rows), F32),
            pltpu.VMEM((PSLOTS, 2 * PSLOTS), BF),
            pltpu.VMEM((PSLOTS, 2 * PSLOTS), BF),
        ],
        flops=2 * rows * width * width * 4 + 10 * 12 * 64 * rows * rows,
    )


def passed_along(array, axis, by):
    count = lax.axis_size(axis)
    pairs = [(i, i + by) for i in range(count) if 0 <= i + by < count]
    return lax.ppermute(array, axis, pairs)


def flatten_rows(leaf):
    return leaf.reshape(-1, leaf.shape[-1])


def swapped(array, bit):
    count = lax.axis_size("dp")
    return lax.ppermute(array, "dp", [(i, i ^ bit) for i in range(count)])


def piece(array, index):
    return lax.dynamic_index_in_dim(array, index, 0, keepdims=False)


def placed_at(array, update, index):
    return lax.dynamic_update_index_in_dim(array, update, index, 0)


def sum_low(*arrays):
    total = arrays[0].astype(F32)
    for array in arrays[1:]:
        total = total + array.astype(F32)
    return total.astype(BF)


def summed_over_data(partial):
    count = lax.axis_size("dp")
    rows, columns = partial.shape
    if count != 16:
        share = lax.psum_scatter(partial, "dp", scatter_dimension=0, tiled=True)
        return lax.all_gather(share, "dp", axis=0, tiled=True).astype(F32)
    place = lax.axis_index("dp")
    core, along_x, along_z = place & 1, (place >> 1) & 1, place >> 2
    halves = partial.reshape(2, rows // 2, columns)
    half = sum_low(piece(halves, core), swapped(piece(halves, 1 - core), 1))
    quarters = half.reshape(2, rows // 4, columns)
    quarter = sum_low(piece(quarters, along_x), swapped(piece(quarters, 1 - along_x), 2))
    parts = quarter.reshape(4, rows // 16, columns)
    arrived = [swapped(piece(parts, along_z ^ step), 4 * step) for step in (1, 2, 3)]
    share = sum_low(piece(parts, along_z), *arrived)
    parts = placed_at(jnp.zeros_like(parts), share, along_z)
    for step in (1, 2, 3):
        parts = placed_at(parts, swapped(share, 4 * step), along_z ^ step)
    quarter = parts.reshape(rows // 4, columns)
    quarters = placed_at(jnp.zeros_like(quarters), quarter, along_x)
    quarters = placed_at(quarters, swapped(quarter, 2), 1 - along_x)
    half = quarters.reshape(rows // 2, columns)
    other = swapped(half, 1)
    whole = jnp.stack([jnp.where(core == 0, half, other), jnp.where(core == 0, other, half)])
    return whole.reshape(rows, columns).astype(F32)


def shards(
    hidden_in,
    attend_weight,
    attend_bias,
    mixing_weight,
    mixing_bias,
    norm_gain,
    norm_shift,
    expand_weight,
    expand_bias,
    reduce_weight,
    reduce_bias,
    colbert_weight,
    pass_lengths,
    positives,
):
    section_id = lax.axis_index("pipe")
    data_count = lax.axis_size("dp")
    micros = pass_lengths.shape[0]
    rows = hidden_in.shape[0] // micros
    width = hidden_in.shape[1]
    grad_scale = 1.0 / (data_count * micros * NQ)
    wa, wm, we, wr = attend_weight[0], mixing_weight[0], expand_weight[0], reduce_weight[0]
    gains, shifts = norm_gain[0], norm_shift[0]
    info = jnp.concatenate(
        [section_id.astype(jnp.int32)[None], pass_lengths.reshape(-1), positives.reshape(-1)]
    )
    attn_weights = (wa, attend_bias, wm, mixing_bias, gains, shifts)
    ffn_weights = (we, expand_bias, wr, reduce_bias, gains, shifts)
    received = jnp.zeros((rows, width), BF)
    attn, ffn = None, None
    for tick in range(micros + 1):
        attn = attn_forward(tick, micros, info, hidden_in, received, attn_weights, attn)
        ffn = ffn_forward(tick, micros, info, attn[4], ffn_weights, ffn and ffn[:6])
        if tick < micros:
            received = passed_along(ffn[6], "pipe", 1)
    inputs, joined, lse, context, hidden, unit_one, inv_one, squares_one = attn
    active, slope, outputs, unit_two, inv_two, squares_two, _ = ffn
    received = jnp.zeros((rows, width), BF)
    ffn_back, attn_back = None, None
    for tick in range(micros + 1):
        ffn_back = ffn_backward(
            tick, micros, grad_scale, info, received,
            (outputs, unit_two, inv_two, slope, unit_one, inv_one),
            (colbert_weight, gains, wr, we), ffn_back and ffn_back[:6],
        )
        attn_back = attn_backward(
            tick, micros, info, ffn_back[6], ffn_back[2], (joined, lse, context), (wa, wm),
            attn_back and attn_back[:4],
        )
        if tick < micros:
            received = passed_along(attn_back[4], "pipe", -1)
    d_two, d_inner, d_one, d_embed, small, small_ff, _ = ffn_back
    d_query, d_key, d_value, joined_sums, _ = attn_back

    def weight_grad(left, right):
        return dot_tn(flatten_rows(left), flatten_rows(right)).astype(BF)

    big_reduce = summed_over_data(weight_grad(active, d_two))
    big_expand = summed_over_data(weight_grad(hidden, d_inner))
    big_rest = summed_over_data(
        jnp.concatenate(
            [weight_grad(inputs, d) for d in (d_query, d_key, d_value)] + [weight_grad(context, d_one)],
            axis=1,
        )
    )
    colbert_sum = lax.psum(weight_grad(outputs, d_embed), ("pipe", "dp")).astype(F32)
    small_sum = jnp.sum(small, axis=0)
    joined_sum = jnp.sum(joined_sums[:, :, 0], axis=0)
    attend_sum = jnp.concatenate(
        [joined_sum[:, :SLAB].reshape(-1), joined_sum[:, SLAB:].reshape(-1)]
    )
    vector = jnp.concatenate(
        [small_sum[:6].reshape(-1), attend_sum, jnp.sum(small_ff[:, 0], axis=0)]
    )
    vector = lax.psum(vector, "dp")
    line = vector[: 8 * width].reshape(8, width)
    squares = jnp.stack(
        [
            jnp.sum(squares_one[:, 0], axis=1),
            jnp.sum(squares_one[:, 1], axis=1),
            jnp.sum(squares_two[:, 0], axis=1),
        ],
        axis=1,
    )
    section_rows = (jnp.arange(2, dtype=jnp.int32) == section_id).astype(F32)
    square_sum = lax.psum(section_rows[None, :, None] * squares[:, None, :], "pipe")
    loss_sum = lax.psum(jnp.where(section_id == 1, small[:, 6, 0], 0.0), "pipe")
    counted = (QROWS + jnp.sum(pass_lengths, axis=1)).astype(F32)
    stats = jnp.sqrt(square_sum / (counted[:, None, None] * width))
    return (
        big_rest[None, :, : 3 * width],
        line[6:8].reshape(1, -1),
        big_rest[None, :, 3 * width :],
        line[5][None],
        jnp.stack([line[3], line[0]])[None],
        jnp.stack([line[4], line[1]])[None],
        big_expand[None],
        vector[8 * width :][None],
        big_reduce[None],
        line[2][None],
        colbert_sum,
        loss_sum / NQ,
        stats,
    )


def solution(mesh):
    placed = (
        P("dp", None),
        P("pipe", None, None),
        P("pipe", None),
        P("pipe", None, None),
        P("pipe", None),
        P("pipe", None, None),
        P("pipe", None, None),
        P("pipe", None, None),
        P("pipe", None),
        P("pipe", None, None),
        P("pipe", None),
        P(),
        P("dp", None),
        P("dp", None),
    )
    return jax.shard_map(
        shards,
        mesh=mesh,
        in_specs=placed,
        out_specs=(
            P("pipe", None, None),
            P("pipe", None),
            P("pipe", None, None),
            P("pipe", None),
            P("pipe", None, None),
            P("pipe", None, None),
            P("pipe", None, None),
            P("pipe", None),
            P("pipe", None, None),
            P("pipe", None),
            P(),
            P("dp"),
            P("dp", None, None),
        ),
        check_vma=False,
    )
```

time: 1190 us -> 966 us (0.81)
  matrix products: 380 us -> 28 us
  Pallas kernels: 0 us -> 305 us
  waiting for transfers between devices: 198 us -> 398 us
  other arithmetic: 240 us -> 41.7 us
  local copies, waits for them, and re-layouts: 178 us -> 43.3 us
  starting transfers between devices: 91.4 us -> 52.7 us
    dot_general x70 -> x7, matrix products: 380 us -> 28 us  [dot_tn(): lax.dot_general(a, b, (((0,), (0,)), ((), ())), preferred_element_type=F32)]
    pallas_call x0 -> x12, Pallas kernels: none -> 305 us  [call(): pl.pallas_call(body, out_shape=[jax.ShapeDtypeStruct(s[0], s[1]) for s in...]
    reduce_sum x44 -> x6, other arithmetic: 80.5 us -> 3.89 us  [the longest x1 0.98 us: shards(): jnp.sum(squares_one[:, 0], axis=1)]
    ppermute x4, waiting for transfers between devices: 9.8 us -> 84.5 us  [passed_along(): return lax.ppermute(array, axis, pairs)]
    ppermute x40 -> x30, waiting for transfers between devices: 123 us -> 193 us  [swapped(): return lax.ppermute(array, 'dp', [(i, i ^ bit) for i in range(count)])]
    slice x32 -> x11, local copies, waits for them, and re-layouts: 62 us -> 5.14 us  [the longest x1 1.38 us: ffn_forward(): args = [hidden, we, be, wr, br, gains[1:2], shifts[1:2]]]
    psum x1, waiting for transfers between devices: 65.9 us -> 120 us  [shards(): lax.psum(weight_grad(outputs, d_embed), ('pipe', 'dp')).astype(F32)]
    convert_element_type x24 -> x11, other arithmetic: 76.3 us -> 22.3 us  [the longest x3 11.1 us: summed_over_data(): return whole.reshape(rows, columns).astype(F32)]
  transfers between devices with their start and end apart: 45 -> 35, of which waited for: 18 -> 13; matrix products, arithmetic and copies ran while one was open for 20% -> 9% of each run, Pallas kernels for 0% -> 3%
where the time goes in v2:
time: 966 us; the launch traced here: 951 us
  waiting for transfers between devices  398 us (41%)
  Pallas kernels  305 us (32%)
  blocking collectives  66.6 us (7%)
  starting transfers between devices  52.7 us (5%)
  local copies, waits for them, and re-layouts  43.3 us (4%)
  other arithmetic  41.7 us (4%)
  matrix products  28 us (3%)
  between operations  15.1 us (2%)
    pallas_call x12, Pallas kernels, call(): pl.pallas_call(body, out_shape=[jax.ShapeDtypeStruct(s[0], s[1]) for s in...  305 us
    ppermute x30, waiting for transfers between devices, swapped(): return lax.ppermute(array, 'dp', [(i, i ^ bit) for i in range(count)])  193 us
    psum x1, waiting for transfers between devices, shards(): lax.psum(weight_grad(outputs, d_embed), ('pipe', 'dp')).astype(F32)  120 us
    ppermute x4, waiting for transfers between devices, passed_along(): return lax.ppermute(array, axis, pairs)  84.5 us
    psum x1, blocking collectives, shards(): vector = lax.psum(vector, 'dp')  61.1 us
    ppermute x30, starting transfers between devices, swapped(): return lax.ppermute(array, 'dp', [(i, i ^ bit) for i in range(count)])  40.2 us
    dot_general x7, matrix products, dot_tn(): lax.dot_general(a, b, (((0,), (0,)), ((), ())), preferred_element_type=F32)  28 us
  transfers between devices with their start and end apart: 35, of which 13 were waited for; matrix products, arithmetic and copies ran while one was open for 9% of the time, Pallas kernels for 3%

profile of v2, /device:TPU:0, one launch (start us, length us, event | category | flops | bytes accessed | tf_op | source)
XLA Modules:
  0.0 950.8 jit_solution(17051163634290640511)
XLA Ops:
  11.7 22.3 %shard_map.237 = (bf16[2,640,768]{2,1,0:T(8,128)(2,1)}, bf16[2,3,640,768]{3,2,1,0:T(8,128)(2,1)}, f32[2,3,8,640]{3,2,1,0:T(8,128)}, bf16[2,640,768]{2,1,0:T(8,12...) custom-call(s32[17]{0:T(128)} %pad_add_fusion.info, ...), custom_call_target="tpu_custom_call" | custom-call | flops 4278190080 | bytes 20000000 | tf_op jit(solution)/shard_map/pallas_call | solution.py:231
  34.0 24.1 %shard_map.238 = (bf16[2,640,3072]{2,1,0:T(8,128)(2,1)}, bf16[2,640,3072]{2,1,0:T(8,128)(2,1)}, bf16[2,640,768]{2,1,0:T(8,128)(2,1)}, bf16[2,640,768]{2,1,0:T(8,...) custom-call(s32[17]{0:T(128)} %pad_add_fusion.info, ...), custom_call_target="tpu_custom_call" | custom-call | flops 6039797760 | bytes 20000000 | tf_op jit(solution)/shard_map/pallas_call | solution.py:231
  58.2 5.1 collective-permute-start
  63.3 21.0 %collective-permute-done.rec = bf16[640,768]{1,0:T(8,128)(2,1)S(1)} collective-permute-done((bf16[640,768]{1,0:T(8,128)(2,1)}, bf16[640,768]{1,0:T(8,128)(2,1)S(1)}, u32[]{:S(2)}, u32[]{:S(2)}) %collective-permute-start) | collective-permute-done | bytes 983072 | tf_op jit(solution)/shard_map/ppermute | solution.py:618
  85.3 22.3 %shard_map.239 = (bf16[2,640,768]{2,1,0:T(8,128)(2,1)}, bf16[2,3,640,768]{3,2,1,0:T(8,128)(2,1)}, f32[2,3,8,640]{3,2,1,0:T(8,128)}, bf16[2,640,768]{2,1,0:T(8,12...) custom-call(s32[17]{0:T(128)} %pad_add_fusion.info, ...), custom_call_target="tpu_custom_call", output_to_operand_aliasing={{0}: (12, {}), {1}: (13, {}), {2}: (14, {}), {3}: (15, {}),... | custom-call | flops 4278190080 | bytes 20000000 | tf_op jit(solution)/shard_map/pallas_call | solution.py:231
  107.6 24.1 %shard_map.240 = (bf16[2,640,3072]{2,1,0:T(8,128)(2,1)}, bf16[2,640,3072]{2,1,0:T(8,128)(2,1)}, bf16[2,640,768]{2,1,0:T(8,128)(2,1)}, bf16[2,640,768]{2,1,0:T(8,...) custom-call(s32[17]{0:T(128)} %pad_add_fusion.info, ...), custom_call_target="tpu_custom_call", output_to_operand_aliasing={{0}: (8, {}), {1}: (9, {}), {2}: (10, {}), {3}: (11, {}), {... | custom-call | flops 6039797760 | bytes 20000000 | tf_op jit(solution)/shard_map/pallas_call | solution.py:231
  131.8 4.7 collective-permute-start.1
  136.5 20.0 %collective-permute-done.1.rec = bf16[640,768]{1,0:T(8,128)(2,1)S(1)} collective-permute-done((bf16[640,768]{1,0:T(8,128)(2,1)}, bf16[640,768]{1,0:T(8,128)(2,1)S(1)}, u32[]{:S(2)}, u32[]{:S(2)}) %collective-permute-start.1) | collective-permute-done | bytes 983072 | tf_op jit(solution)/shard_map/ppermute | solution.py:618
  157.5 22.3 %shard_map.241 = (bf16[2,640,768]{2,1,0:T(8,128)(2,1)}, bf16[2,3,640,768]{3,2,1,0:T(8,128)(2,1)}, f32[2,3,8,640]{3,2,1,0:T(8,128)}, bf16[2,640,768]{2,1,0:T(8,12...) custom-call(s32[17]{0:T(128)} %pad_add_fusion.info, ...), custom_call_target="tpu_custom_call", output_to_operand_aliasing={{0}: (12, {}), {1}: (13, {}), {2}: (14, {}), {3}: (15, {}),... | custom-call | flops 4278190080 | bytes 20000000 | tf_op jit(solution)/shard_map/pallas_call | solution.py:231
  179.8 24.1 %shard_map.242 = (bf16[2,640,3072]{2,1,0:T(8,128)(2,1)}, bf16[2,640,3072]{2,1,0:T(8,128)(2,1)}, bf16[2,640,768]{2,1,0:T(8,128)(2,1)}, bf16[2,640,768]{2,1,0:T(8,...) custom-call(s32[17]{0:T(128)} %pad_add_fusion.info, ...), custom_call_target="tpu_custom_call", output_to_operand_aliasing={{0}: (8, {}), {1}: (9, {}), {2}: (10, {}), {3}: (11, {}), {... | custom-call | flops 6039797760 | bytes 20000000 | tf_op jit(solution)/shard_map/pallas_call | solution.py:231
  203.9 29.5 %shard_map.243 = (bf16[2,640,768]{2,1,0:T(8,128)(2,1)}, bf16[2,640,3072]{2,1,0:T(8,128)(2,1)}, bf16[2,640,768]{2,1,0:T(8,128)(2,1)}, bf16[2,640,128]{2,1,0:T(8,1...) custom-call(s32[17]{0:T(128)} %pad_add_fusion.info, ...), custom_call_target="tpu_custom_call" | custom-call | flops 6039797760 | bytes 20000000 | tf_op jit(solution)/shard_map/pallas_call | solution.py:231
  233.4 25.8 %shard_map.244 = (bf16[2,640,768]{2,1,0:T(8,128)(2,1)}, bf16[2,640,768]{2,1,0:T(8,128)(2,1)}, bf16[2,640,768]{2,1,0:T(8,128)(2,1)}, f32[2,3,8,512]{3,2,1,0:T(8,128)}, bf16[640,768]{1,0:T(8,128)(2,1)}) custom-call(s32[17]{0:T(128)} %pad_add_fusion.info, f32[640,768]{1,0:T(8,128)} %get-tuple-element.130.resid, ...), custom_call_target="tpu_custom_call" | custom-call | flops 6165626880 | bytes 20000000 | tf_op jit(solution)/shard_map/pallas_call | solution.py:231
  260.5 24.4 %collective-permute-done.2.rec = bf16[640,768]{1,0:T(8,128)(2,1)S(1)} collective-permute-done((bf16[640,768]{1,0:T(8,128)(2,1)}, bf16[640,768]{1,0:T(8,128)(2,1)S(1)}, u32[]{:S(2)}, u32[]{:S(2)}) %collective-permute-start.2) | collective-permute-done | bytes 983072 | tf_op jit(solution)/shard_map/ppermute | solution.py:618
  285.9 29.6 %shard_map.245 = (bf16[2,640,768]{2,1,0:T(8,128)(2,1)}, bf16[2,640,3072]{2,1,0:T(8,128)(2,1)}, bf16[2,640,768]{2,1,0:T(8,128)(2,1)}, bf16[2,640,128]{2,1,0:T(8,1...) custom-call(s32[17]{0:T(128)} %pad_add_fusion.info, ...), custom_call_target="tpu_custom_call", output_to_operand_aliasing={{0}: (13, {}), {1}: (14, {}), {2}: (15, {}), {3}: (16, {}),... | custom-call | flops 6039797760 | bytes 20000000 | tf_op jit(solution)/shard_map/pallas_call | solution.py:231
  315.5 26.1 %shard_map.246 = (bf16[2,640,768]{2,1,0:T(8,128)(2,1)}, bf16[2,640,768]{2,1,0:T(8,128)(2,1)}, bf16[2,640,768]{2,1,0:T(8,128)(2,1)}, f32[2,3,8,512]{3,2,1,0:T(8,128)}, bf16[640,768]{1,0:T(8,128)(2,1)}) custom-call(s32[17]{0:T(128)} %pad_add_fusion.info, ...), custom_call_target="tpu_custom_call", output_to_operand_aliasing={{0}: (10, {}), {1}: (11, {}), {2}: (12, {}), {3}: (13, {})} | custom-call | flops 6165626880 | bytes 20000000 | tf_op jit(solution)/shard_map/pallas_call | solution.py:231
  345.7 19.1 %collective-permute-done.3.rec = bf16[640,768]{1,0:T(8,128)(2,1)S(1)} collective-permute-done((bf16[640,768]{1,0:T(8,128)(2,1)}, bf16[640,768]{1,0:T(8,128)(2,1)S(1)}, u32[]{:S(2)}, u32[]{:S(2)}) %collective-permute-start.3) | collective-permute-done | bytes 983072 | tf_op jit(solution)/shard_map/ppermute | solution.py:618
  365.7 29.5 %shard_map.247 = (bf16[2,640,768]{2,1,0:T(8,128)(2,1)}, bf16[2,640,3072]{2,1,0:T(8,128)(2,1)}, bf16[2,640,768]{2,1,0:T(8,128)(2,1)}, bf16[2,640,128]{2,1,0:T(8,1...) custom-call(s32[17]{0:T(128)} %pad_add_fusion.info, ...), custom_call_target="tpu_custom_call", output_to_operand_aliasing={{0}: (13, {}), {1}: (14, {}), {2}: (15, {}), {3}: (16, {}),... | custom-call | flops 6039797760 | bytes 20000000 | tf_op jit(solution)/shard_map/pallas_call | solution.py:231
  395.2 9.5 bitcast_convert_fusion
  407.8 8.4 bitcast_convert_fusion.1
  417.9 25.5 %shard_map.248 = (bf16[2,640,768]{2,1,0:T(8,128)(2,1)}, bf16[2,640,768]{2,1,0:T(8,128)(2,1)}, bf16[2,640,768]{2,1,0:T(8,128)(2,1)}, f32[2,3,8,512]{3,2,1,0:T(8,128)}, bf16[640,768]{1,0:T(8,128)(2,1)}) custom-call(s32[17]{0:T(128)} %pad_add_fusion.info, ...), custom_call_target="tpu_custom_call", output_to_operand_aliasing={{0}: (10, {}), {1}: (11, {}), {2}: (12, {}), {3}: (13, {})} | custom-call | flops 6165626880 | bytes 20000000 | tf_op jit(solution)/shard_map/pallas_call | solution.py:231
  443.5 3.4 bitcast_convert_fusion.8
  450.5 2.4 pad_maximum_fusion
  453.0 6.6 copy.104
  459.6 3.2 dynamic-slice_bitcast_fusion.2
  463.3 3.4 dynamic-slice_bitcast_fusion.1
  466.8 5.5 all-reduce
  474.3 61.1 %psum.28 = f32[9216]{0:T(1024)S(1)} all-reduce(f32[9216]{0:T(1024)S(1)} %pad_maximum_fusion.4), channel_id=1, replica_groups=mesh['pipe'=2,'dp'=16] {'dp'}, use_global_device_ids=true, to_apply=%region_3.4 | all-reduce | flops 9216 | bytes 73728 | tf_op jit(solution)/shard_map/psum | solution.py:747
  538.0 3.1 fusion
  541.6 2.8 fusion.2
  546.0 2.6 fusion.1
  549.3 20.9 %collective-permute-done.25 = bf16[768,768]{1,0:T(8,128)(2,1)S(1)} collective-permute-done((bf16[768,768]{1,0:T(8,128)(2,1)S(1)}, bf16[768,768]{1,0:T(8,128)(2,1)S(1)}, u32[]{:S(2)}, u32[]{:S(2)}) %collective-permute-start.25) | collective-permute-done | bytes 1179680 | tf_op jit(solution)/shard_map/ppermute | solution.py:627
  570.7 4.3 collective-permute-start.28
  575.0 20.5 %collective-permute-done.5 = bf16[192,3072]{1,0:T(8,128)(2,1)S(1)} collective-permute-done((bf16[192,3072]{1,0:T(8,128)(2,1)S(1)}, bf16[192,3072]{1,0:T(8,128)(2,1)S(1)}, u32[]{:S(2)}, u32[]{:S(2)}) %collective-permute-start.5) | collective-permute-done | bytes 1179680 | tf_op jit(solution)/shard_map/ppermute | solution.py:627
  596.0 19.2 %collective-permute-done.15 = bf16[192,3072]{1,0:T(8,128)(2,1)S(1)} collective-permute-done((bf16[192,3072]{1,0:T(8,128)(2,1)S(1)}, bf16[192,3072]{1,0:T(8,128)(2,1)S(1)}, u32[]{:S(2)}, u32[]{:S(2)}) %collective-permute-start.15) | collective-permute-done | bytes 1179680 | tf_op jit(solution)/shard_map/ppermute | solution.py:627
  615.8 3.5 collective-permute-start.16
  623.7 22.9 %collective-permute-done.7 = bf16[48,3072]{1,0:T(8,128)(2,1)S(1)} collective-permute-done((bf16[48,3072]{1,0:T(8,128)(2,1)S(1)}, bf16[48,3072]{1,0:T(8,128)(2,1)S(1)}, u32[]{:S(2)}, u32[]{:S(2)}) %collective-permute-start.7) | collective-permute-done | bytes 294944 | tf_op jit(solution)/shard_map/ppermute | solution.py:627
  646.6 6.7 collective-permute-start.30
  653.6 3.4 collective-permute-start.31
  657.1 15.7 %collective-permute-done.17 = bf16[48,3072]{1,0:T(8,128)(2,1)S(1)} collective-permute-done((bf16[48,3072]{1,0:T(8,128)(2,1)S(1)}, bf16[48,3072]{1,0:T(8,128)(2,1)S(1)}, u32[]{:S(2)}, u32[]{:S(2)}) %collective-permute-start.17) | collective-permute-done | bytes 294944 | tf_op jit(solution)/shard_map/ppermute | solution.py:627
  673.0 6.9 collective-permute-start.19
  680.0 7.1 collective-permute-done.9
  691.6 2.9 collective-permute-start.11
  695.2 39.9 %collective-permute-done.10 = bf16[48,3072]{1,0:T(8,128)(2,1)S(1)} collective-permute-done((bf16[48,3072]{1,0:T(8,128)(2,1)S(1)}, bf16[48,3072]{1,0:T(8,128)(2,1)S(1)}, u32[]{:S(2)}, u32[]{:S(2)}) %collective-permute-start.10) | collective-permute-done | bytes 294944 | tf_op jit(solution)/shard_map/ppermute | solution.py:627
  738.2 46.9 %collective-permute-done.12 = bf16[192,3072]{1,0:T(8,128)(2,1)S(1)} collective-permute-done((bf16[192,3072]{1,0:T(8,128)(2,1)S(1)}, bf16[192,3072]{1,0:T(8,128)(2,1)S(1)}, u32[]{:S(2)}, u32[]{:S(2)}) %collective-permute-start.12) | collective-permute-done | bytes 1179680 | tf_op jit(solution)/shard_map/ppermute | solution.py:627
  792.5 120.3 %all-reduce.3.cloned.1.call-done = bf16[768,128]{1,0:T(8,128)(2,1)} async-done(((bf16[768,128]{1,0:T(8,128)(2,1)}), bf16[768,128]{1,0:T(8,128)(2,1)}) %all-reduce.3.cloned.1.call-update) | async-done | bytes 196624 | tf_op jit(solution)/shard_map/psum | solution.py:738
  928.2 4.5 bitcast_convert_fusion.2
  932.7 3.5 slice_bitcast_fusion
  938.6 5.0 bitcast_convert_fusion.3
  (179 shorter events, 69.8 us)
Async XLA Ops:
  7.2 905.7 %all-reduce.3.cloned.1.call-start = ((), (), s32[]{:S(2)}) async-start(), calls=%async_computation | async-start | bytes 393216 | tf_op jit(solution)/shard_map/psum | solution.py:738
  58.2 26.2 %collective-permute-start = (bf16[640,768]{1,0:T(8,128)(2,1)}, bf16[640,768]{1,0:T(8,128)(2,1)S(1)}, u32[]{:S(2)}, u32[]{:S(2)}) collective-permute-start(bf16[640,768]{1,0:T(8,128)(2,1)} %get-tuple-element.93), channel_id=1, source_target_pairs={{0,16},{1,17},{2,18},{3,19},{4,20},{5,21},{6,22},{7,23},{8,24},{9,... | collective-permute-start | bytes 2949128 | tf_op jit(solution)/shard_map/ppermute | solution.py:618
  131.8 24.7 %collective-permute-start.1 = (bf16[640,768]{1,0:T(8,128)(2,1)}, bf16[640,768]{1,0:T(8,128)(2,1)S(1)}, u32[]{:S(2)}, u32[]{:S(2)}) collective-permute-start(bf16[640,768]{1,0:T(8,128)(2,1)} %get-tuple-element.108), channel_id=1, source_target_pairs={{0,16},{1,17},{2,18},{3,19},{4,20},{5,21},{6,22},{7,23},{8,24},{9,... | collective-permute-start | bytes 2949128 | tf_op jit(solution)/shard_map/ppermute | solution.py:618
  259.2 25.7 %collective-permute-start.2 = (bf16[640,768]{1,0:T(8,128)(2,1)}, bf16[640,768]{1,0:T(8,128)(2,1)S(1)}, u32[]{:S(2)}, u32[]{:S(2)}) collective-permute-start(bf16[640,768]{1,0:T(8,128)(2,1)} %get-tuple-element.135), channel_id=1, source_target_pairs={{16,0},{17,1},{18,2},{19,3},{20,4},{21,5},{22,6},{23,7},{24,8},{25... | collective-permute-start | bytes 2949128 | tf_op jit(solution)/shard_map/ppermute | solution.py:618
  315.5 27.4 %copy-start.17 = (s32[2,4]{1,0:T(2,128)S(1)}, s32[2,4]{1,0:T(2,128)}, u32[]{:S(2)}) copy-start(s32[2,4]{1,0:T(2,128)} %param.26) | copy-start | bytes 100
  341.6 23.2 %collective-permute-start.3 = (bf16[640,768]{1,0:T(8,128)(2,1)}, bf16[640,768]{1,0:T(8,128)(2,1)S(1)}, u32[]{:S(2)}, u32[]{:S(2)}) collective-permute-start(bf16[640,768]{1,0:T(8,128)(2,1)} %get-tuple-element.147), channel_id=1, source_target_pairs={{16,0},{17,1},{18,2},{19,3},{20,4},{21,5},{22,6},{23,7},{24,8},{25... | collective-permute-start | bytes 2949128 | tf_op jit(solution)/shard_map/ppermute | solution.py:618
  395.2 12.5 %copy-start.3 = (bf16[2,640,3072]{2,1,0:T(8,128)(2,1)S(1)}, bf16[2,640,3072]{2,1,0:T(8,128)(2,1)}, u32[]{:S(2)}) copy-start(bf16[2,640,3072]{2,1,0:T(8,128)(2,1)} %get-tuple-element.165) | copy-start | bytes 23592964
  407.7 130.2 %collective-permute-start.24 = (bf16[1536,768]{1,0:T(8,128)(2,1)}, bf16[1536,768]{1,0:T(8,128)(2,1)}, u32[]{:S(2)}, u32[]{:S(2)}) collective-permute-start(bf16[1536,768]{1,0:T(8,128)(2,1)} %dynamic-slice_bitcast_fusion), channel_id=1, source_target_pairs={{0,1},{1,0},{2,3},{3,2},{4,5},{5,4},{6,7},{7,6},{8,9},{9,8},{10,11... | collective-permute-start | bytes 7077896 | tf_op jit(solution)/shard_map/ppermute | solution.py:627
  407.7 8.4 copy-start
  407.7 8.4 copy-start.1
  417.9 25.6 %copy-start.7 = (bf16[2,640,768]{2,1,0:T(8,128)(2,1)S(1)}, bf16[2,640,768]{2,1,0:T(8,128)(2,1)}, u32[]{:S(2)}) copy-start(bf16[2,640,768]{2,1,0:T(8,128)(2,1)} %get-tuple-element.116) | copy-start | bytes 5898244
  443.5 3.4 copy-start.5
  462.8 78.5 %collective-permute-start.4 = (bf16[384,3072]{1,0:T(8,128)(2,1)}, bf16[384,3072]{1,0:T(8,128)(2,1)}, u32[]{:S(2)}, u32[]{:S(2)}) collective-permute-start(bf16[384,3072]{1,0:T(8,128)(2,1)} %dynamic-slice_bitcast_fusion.2), channel_id=1, source_target_pairs={{0,1},{1,0},{2,3},{3,2},{4,5},{5,4},{6,7},{7,6},{8,9},{9,8},{10,11... | collective-permute-start | bytes 7077896 | tf_op jit(solution)/shard_map/ppermute | solution.py:627
  463.3 73.2 %copy-start.2 = (bf16[2,640,768]{2,1,0:T(8,128)(2,1)S(1)}, bf16[2,640,768]{2,1,0:T(8,128)(2,1)}, u32[]{:S(2)}) copy-start(bf16[2,640,768]{2,1,0:T(8,128)(2,1)} %get-tuple-element.124.out_all) | copy-start | bytes 5898244
  463.3 73.2 %copy-start.9 = (bf16[2,640,128]{2,1,0:T(8,128)(2,1)S(1)}, bf16[2,640,128]{2,1,0:T(8,128)(2,1)}, u32[]{:S(2)}) copy-start(bf16[2,640,128]{2,1,0:T(8,128)(2,1)} %get-tuple-element.168) | copy-start | bytes 983044
  466.8 79.3 %collective-permute-start.14 = (bf16[384,3072]{1,0:T(8,128)(2,1)}, bf16[384,3072]{1,0:T(8,128)(2,1)}, u32[]{:S(2)}, u32[]{:S(2)}) collective-permute-start(bf16[384,3072]{1,0:T(8,128)(2,1)} %dynamic-slice_bitcast_fusion.1), channel_id=1, source_target_pairs={{0,1},{1,0},{2,3},{3,2},{4,5},{5,4},{6,7},{7,6},{8,9},{9,8},{10,11... | collective-permute-start | bytes 7077896 | tf_op jit(solution)/shard_map/ppermute | solution.py:627
  536.5 4.7 slice-start
  538.0 3.6 slice-start.1
  541.1 5.0 slice-start.2
  541.2 4.9 slice-start.3
  541.2 29.0 %collective-permute-start.25 = (bf16[768,768]{1,0:T(8,128)(2,1)S(1)}, bf16[768,768]{1,0:T(8,128)(2,1)S(1)}, u32[]{:S(2)}, u32[]{:S(2)}) collective-permute-start(bf16[768,768]{1,0:T(8,128)(2,1)S(1)} %dynamic-slice_bitcast_fusion.3), channel_id=1, source_target_pairs={{0,2},{1,3},{2,0},{3,1},{4,6},{5,7},{6,4},{7,5},{8,10},{9,11},{10,... | collective-permute-start | bytes 3538952 | tf_op jit(solution)/shard_map/ppermute | solution.py:627
  544.4 51.0 %collective-permute-start.5 = (bf16[192,3072]{1,0:T(8,128)(2,1)S(1)}, bf16[192,3072]{1,0:T(8,128)(2,1)S(1)}, u32[]{:S(2)}, u32[]{:S(2)}) collective-permute-start(bf16[192,3072]{1,0:T(8,128)(2,1)S(1)} %dynamic-slice_bitcast_fusion.5), channel_id=1, source_target_pairs={{0,2},{1,3},{2,0},{3,1},{4,6},{5,7},{6,4},{7,5},{8,10},{9,11},{10,... | collective-permute-start | bytes 3538952 | tf_op jit(solution)/shard_map/ppermute | solution.py:627
  548.7 66.5 %collective-permute-start.15 = (bf16[192,3072]{1,0:T(8,128)(2,1)S(1)}, bf16[192,3072]{1,0:T(8,128)(2,1)S(1)}, u32[]{:S(2)}, u32[]{:S(2)}) collective-permute-start(bf16[192,3072]{1,0:T(8,128)(2,1)S(1)} %dynamic-slice_bitcast_fusion.4), channel_id=1, source_target_pairs={{0,2},{1,3},{2,0},{3,1},{4,6},{5,7},{6,4},{7,5},{8,10},{9,11},{10,... | collective-permute-start | bytes 3538952 | tf_op jit(solution)/shard_map/ppermute | solution.py:627
  570.5 45.0 %collective-permute-start.26 = (bf16[192,768]{1,0:T(8,128)(2,1)S(1)}, bf16[192,768]{1,0:T(8,128)(2,1)S(1)}, u32[]{:S(2)}, u32[]{:S(2)}) collective-permute-start(bf16[192,768]{1,0:T(8,128)(2,1)S(1)} %get-tuple-element.187), channel_id=1, source_target_pairs={{0,4},{1,5},{2,6},{3,7},{4,0},{5,1},{6,2},{7,3},{8,12},{9,13},{10,... | collective-permute-start | bytes 884744 | tf_op jit(solution)/shard_map/ppermute | solution.py:627
  570.6 45.1 %collective-permute-start.27 = (bf16[192,768]{1,0:T(8,128)(2,1)S(1)}, bf16[192,768]{1,0:T(8,128)(2,1)S(1)}, u32[]{:S(2)}, u32[]{:S(2)}) collective-permute-start(bf16[192,768]{1,0:T(8,128)(2,1)S(1)} %get-tuple-element.189), channel_id=1, source_target_pairs={{0,8},{1,9},{2,10},{3,11},{4,12},{5,13},{6,14},{7,15},{8,0},{9,1},... | collective-permute-start | bytes 884744 | tf_op jit(solution)/shard_map/ppermute | solution.py:627
  570.7 48.6 %collective-permute-start.28 = (bf16[192,768]{1,0:T(8,128)(2,1)S(1)}, bf16[192,768]{1,0:T(8,128)(2,1)S(1)}, u32[]{:S(2)}, u32[]{:S(2)}) collective-permute-start(bf16[192,768]{1,0:T(8,128)(2,1)S(1)} %get-tuple-element.188), channel_id=1, source_target_pairs={{0,12},{1,13},{2,14},{3,15},{4,8},{5,9},{6,10},{7,11},{8,4},{9,5},... | collective-permute-start | bytes 884744 | tf_op jit(solution)/shard_map/ppermute | solution.py:627
  595.9 26.2 %collective-permute-start.6 = (bf16[48,3072]{1,0:T(8,128)(2,1)S(1)}, bf16[48,3072]{1,0:T(8,128)(2,1)S(1)}, u32[]{:S(2)}, u32[]{:S(2)}) collective-permute-start(bf16[48,3072]{1,0:T(8,128)(2,1)S(1)} %get-tuple-element.193), channel_id=1, source_target_pairs={{0,4},{1,5},{2,6},{3,7},{4,0},{5,1},{6,2},{7,3},{8,12},{9,13},{10,... | collective-permute-start | bytes 884744 | tf_op jit(solution)/shard_map/ppermute | solution.py:627
  615.2 31.4 %collective-permute-start.7 = (bf16[48,3072]{1,0:T(8,128)(2,1)S(1)}, bf16[48,3072]{1,0:T(8,128)(2,1)S(1)}, u32[]{:S(2)}, u32[]{:S(2)}) collective-permute-start(bf16[48,3072]{1,0:T(8,128)(2,1)S(1)} %get-tuple-element.195), channel_id=1, source_target_pairs={{0,8},{1,9},{2,10},{3,11},{4,12},{5,13},{6,14},{7,15},{8,0},{9,1},... | collective-permute-start | bytes 884744 | tf_op jit(solution)/shard_map/ppermute | solution.py:627
  615.6 31.0 %collective-permute-start.8 = (bf16[48,3072]{1,0:T(8,128)(2,1)S(1)}, bf16[48,3072]{1,0:T(8,128)(2,1)S(1)}, u32[]{:S(2)}, u32[]{:S(2)}) collective-permute-start(bf16[48,3072]{1,0:T(8,128)(2,1)S(1)} %get-tuple-element.194), channel_id=1, source_target_pairs={{0,12},{1,13},{2,14},{3,15},{4,8},{5,9},{6,10},{7,11},{8,4},{9,5},... | collective-permute-start | bytes 884744 | tf_op jit(solution)/shard_map/ppermute | solution.py:627
  615.8 37.8 %collective-permute-start.16 = (bf16[48,3072]{1,0:T(8,128)(2,1)S(1)}, bf16[48,3072]{1,0:T(8,128)(2,1)S(1)}, u32[]{:S(2)}, u32[]{:S(2)}) collective-permute-start(bf16[48,3072]{1,0:T(8,128)(2,1)S(1)} %get-tuple-element.190), channel_id=1, source_target_pairs={{0,4},{1,5},{2,6},{3,7},{4,0},{5,1},{6,2},{7,3},{8,12},{9,13},{10,... | collective-permute-start | bytes 884744 | tf_op jit(solution)/shard_map/ppermute | solution.py:627
  619.3 53.4 %collective-permute-start.17 = (bf16[48,3072]{1,0:T(8,128)(2,1)S(1)}, bf16[48,3072]{1,0:T(8,128)(2,1)S(1)}, u32[]{:S(2)}, u32[]{:S(2)}) collective-permute-start(bf16[48,3072]{1,0:T(8,128)(2,1)S(1)} %get-tuple-element.192), channel_id=1, source_target_pairs={{0,8},{1,9},{2,10},{3,11},{4,12},{5,13},{6,14},{7,15},{8,0},{9,1},... | collective-permute-start | bytes 884744 | tf_op jit(solution)/shard_map/ppermute | solution.py:627
  622.2 50.6 %collective-permute-start.18 = (bf16[48,3072]{1,0:T(8,128)(2,1)S(1)}, bf16[48,3072]{1,0:T(8,128)(2,1)S(1)}, u32[]{:S(2)}, u32[]{:S(2)}) collective-permute-start(bf16[48,3072]{1,0:T(8,128)(2,1)S(1)} %get-tuple-element.191), channel_id=1, source_target_pairs={{0,12},{1,13},{2,14},{3,15},{4,8},{5,9},{6,10},{7,11},{8,4},{9,5},... | collective-permute-start | bytes 884744 | tf_op jit(solution)/shard_map/ppermute | solution.py:627
  646.6 40.5 %collective-permute-start.29 = (bf16[192,768]{1,0:T(8,128)(2,1)S(1)}, bf16[192,768]{1,0:T(8,128)(2,1)S(1)}, u32[]{:S(2)}, u32[]{:S(2)}) collective-permute-start(bf16[192,768]{1,0:T(8,128)(2,1)S(1)} %get-tuple-element.176), channel_id=1, source_target_pairs={{0,4},{1,5},{2,6},{3,7},{4,0},{5,1},{6,2},{7,3},{8,12},{9,13},{10,... | collective-permute-start | bytes 884744 | tf_op jit(solution)/shard_map/ppermute | solution.py:627
  646.6 43.2 %collective-permute-start.30 = (bf16[192,768]{1,0:T(8,128)(2,1)S(1)}, bf16[192,768]{1,0:T(8,128)(2,1)S(1)}, u32[]{:S(2)}, u32[]{:S(2)}) collective-permute-start(bf16[192,768]{1,0:T(8,128)(2,1)S(1)} %get-tuple-element.176), channel_id=1, source_target_pairs={{0,8},{1,9},{2,10},{3,11},{4,12},{5,13},{6,14},{7,15},{8,0},{9,1},... | collective-permute-start | bytes 884744 | tf_op jit(solution)/shard_map/ppermute | solution.py:627
  653.6 38.0 %collective-permute-start.31 = (bf16[192,768]{1,0:T(8,128)(2,1)S(1)}, bf16[192,768]{1,0:T(8,128)(2,1)S(1)}, u32[]{:S(2)}, u32[]{:S(2)}) collective-permute-start(bf16[192,768]{1,0:T(8,128)(2,1)S(1)} %get-tuple-element.176), channel_id=1, source_target_pairs={{0,12},{1,13},{2,14},{3,15},{4,8},{5,9},{6,10},{7,11},{8,4},{9,5},... | collective-permute-start | bytes 884744 | tf_op jit(solution)/shard_map/ppermute | solution.py:627
  672.7 14.3 %collective-permute-start.9 = (bf16[48,3072]{1,0:T(8,128)(2,1)S(1)}, bf16[48,3072]{1,0:T(8,128)(2,1)S(1)}, u32[]{:S(2)}, u32[]{:S(2)}) collective-permute-start(bf16[48,3072]{1,0:T(8,128)(2,1)S(1)} %get-tuple-element.180), channel_id=1, source_target_pairs={{0,4},{1,5},{2,6},{3,7},{4,0},{5,1},{6,2},{7,3},{8,12},{9,13},{10,... | collective-permute-start | bytes 884744 | tf_op jit(solution)/shard_map/ppermute | solution.py:627
  673.0 64.6 %collective-permute-start.19 = (bf16[48,3072]{1,0:T(8,128)(2,1)S(1)}, bf16[48,3072]{1,0:T(8,128)(2,1)S(1)}, u32[]{:S(2)}, u32[]{:S(2)}) collective-permute-start(bf16[48,3072]{1,0:T(8,128)(2,1)S(1)} %get-tuple-element.178), channel_id=1, source_target_pairs={{0,4},{1,5},{2,6},{3,7},{4,0},{5,1},{6,2},{7,3},{8,12},{9,13},{10,... | collective-permute-start | bytes 884744 | tf_op jit(solution)/shard_map/ppermute | solution.py:627
  687.1 51.0 %collective-permute-start.20 = (bf16[48,3072]{1,0:T(8,128)(2,1)S(1)}, bf16[48,3072]{1,0:T(8,128)(2,1)S(1)}, u32[]{:S(2)}, u32[]{:S(2)}) collective-permute-start(bf16[48,3072]{1,0:T(8,128)(2,1)S(1)} %get-tuple-element.178), channel_id=1, source_target_pairs={{0,8},{1,9},{2,10},{3,11},{4,12},{5,13},{6,14},{7,15},{8,0},{9,1},... | collective-permute-start | bytes 884744 | tf_op jit(solution)/shard_map/ppermute | solution.py:627
  687.1 98.2 %collective-permute-start.21 = (bf16[48,3072]{1,0:T(8,128)(2,1)S(1)}, bf16[48,3072]{1,0:T(8,128)(2,1)S(1)}, u32[]{:S(2)}, u32[]{:S(2)}) collective-permute-start(bf16[48,3072]{1,0:T(8,128)(2,1)S(1)} %get-tuple-element.178), channel_id=1, source_target_pairs={{0,12},{1,13},{2,14},{3,15},{4,8},{5,9},{6,10},{7,11},{8,4},{9,5},... | collective-permute-start | bytes 884744 | tf_op jit(solution)/shard_map/ppermute | solution.py:627
  689.8 45.3 %collective-permute-start.10 = (bf16[48,3072]{1,0:T(8,128)(2,1)S(1)}, bf16[48,3072]{1,0:T(8,128)(2,1)S(1)}, u32[]{:S(2)}, u32[]{:S(2)}) collective-permute-start(bf16[48,3072]{1,0:T(8,128)(2,1)S(1)} %get-tuple-element.180), channel_id=1, source_target_pairs={{0,8},{1,9},{2,10},{3,11},{4,12},{5,13},{6,14},{7,15},{8,0},{9,1},... | collective-permute-start | bytes 884744 | tf_op jit(solution)/shard_map/ppermute | solution.py:627
  691.6 45.9 %collective-permute-start.11 = (bf16[48,3072]{1,0:T(8,128)(2,1)S(1)}, bf16[48,3072]{1,0:T(8,128)(2,1)S(1)}, u32[]{:S(2)}, u32[]{:S(2)}) collective-permute-start(bf16[48,3072]{1,0:T(8,128)(2,1)S(1)} %get-tuple-element.180), channel_id=1, source_target_pairs={{0,12},{1,13},{2,14},{3,15},{4,8},{5,9},{6,10},{7,11},{8,4},{9,5},... | collective-permute-start | bytes 884744 | tf_op jit(solution)/shard_map/ppermute | solution.py:627
  735.1 181.4 %collective-permute-start.32 = (bf16[768,768]{1,0:T(8,128)(2,1)}, bf16[768,768]{1,0:T(8,128)(2,1)}, u32[]{:S(2)}, u32[]{:S(2)}) collective-permute-start(bf16[768,768]{1,0:T(8,128)(2,1)} %bitcast.80), channel_id=1, source_target_pairs={{0,2},{1,3},{2,0},{3,1},{4,6},{5,7},{6,4},{7,5},{8,10},{9,11},{10,... | collective-permute-start | bytes 3538952 | tf_op jit(solution)/shard_map/ppermute | solution.py:627
  737.6 47.5 %collective-permute-start.12 = (bf16[192,3072]{1,0:T(8,128)(2,1)S(1)}, bf16[192,3072]{1,0:T(8,128)(2,1)S(1)}, u32[]{:S(2)}, u32[]{:S(2)}) collective-permute-start(bf16[192,3072]{1,0:T(8,128)(2,1)S(1)} %bitcast.258), channel_id=1, source_target_pairs={{0,2},{1,3},{2,0},{3,1},{4,6},{5,7},{6,4},{7,5},{8,10},{9,11},{10,... | collective-permute-start | bytes 3538952 | tf_op jit(solution)/shard_map/ppermute | solution.py:627
  738.1 48.7 %copy-start.16 = (f32[9216]{0:T(1024)S(1)}, f32[9216]{0:T(1024)}, u32[]{:S(2)}) copy-start(f32[9216]{0:T(1024)} %copy-done.15) | copy-start | bytes 110596
  785.2 134.7 %collective-permute-start.13 = (bf16[384,3072]{1,0:T(8,128)(2,1)S(1)}, bf16[384,3072]{1,0:T(8,128)(2,1)}, u32[]{:S(2)}, u32[]{:S(2)}) collective-permute-start(bf16[384,3072]{1,0:T(8,128)(2,1)S(1)} %bitcast.248), channel_id=1, source_target_pairs={{0,1},{1,0},{2,3},{3,2},{4,5},{5,4},{6,7},{7,6},{8,9},{9,8},{10,11... | collective-permute-start | bytes 7077896 | tf_op jit(solution)/shard_map/ppermute | solution.py:627
  785.4 132.6 %collective-permute-start.22 = (bf16[192,3072]{1,0:T(8,128)(2,1)S(1)}, bf16[192,3072]{1,0:T(8,128)(2,1)}, u32[]{:S(2)}, u32[]{:S(2)}) collective-permute-start(bf16[192,3072]{1,0:T(8,128)(2,1)S(1)} %bitcast.256), channel_id=1, source_target_pairs={{0,2},{1,3},{2,0},{3,1},{4,6},{5,7},{6,4},{7,5},{8,10},{9,11},{10,... | collective-permute-start | bytes 3538952 | tf_op jit(solution)/shard_map/ppermute | solution.py:627
  917.9 6.1 collective-permute-start.33
  919.4 16.8 %collective-permute-start.23 = (bf16[384,3072]{1,0:T(8,128)(2,1)S(1)}, bf16[384,3072]{1,0:T(8,128)(2,1)}, u32[]{:S(2)}, u32[]{:S(2)}) collective-permute-start(bf16[384,3072]{1,0:T(8,128)(2,1)S(1)} %bitcast.247), channel_id=1, source_target_pairs={{0,1},{1,0},{2,3},{3,2},{4,5},{5,4},{6,7},{7,6},{8,9},{9,8},{10,11... | collective-permute-start | bytes 7077896 | tf_op jit(solution)/shard_map/ppermute | solution.py:627
  (9 other events, 16.2 us)
Sparse Core Ops, SparseCore 0:
  787.5 125.2 all-reduce.2

commit v3 on v2

--- a/solution.py
+++ b/solution.py
@@ -612,6 +612,165 @@
     )
 
 
+def mesh_bits():
+    place = lax.axis_index("dp")
+    bits = []
+    bit = 1
+    while bit < lax.axis_size("dp"):
+        bits.append((bit, (place // bit) % 2))
+        bit *= 2
+    return bits
+
+
+def grad_rows_body(info, left, right, first_out, second_out):
+    step = pl.program_id(0)
+    value = dot_nn(jnp.transpose(left[...]), right[...]).astype(BF)
+
+    @pl.when(step < 2)
+    def _():
+        first_out[...] = value
+
+    @pl.when(step >= 2)
+    def _():
+        second_out[...] = value
+
+
+def grad_rows(half, left, right):
+    tall, wide = left.shape[1], right.shape[1]
+    block = tall // 8
+    out = jax.ShapeDtypeStruct((tall // 4, wide), BF)
+    return pl.pallas_call(
+        grad_rows_body,
+        out_shape=[out, out],
+        grid_spec=pltpu.PrefetchScalarGridSpec(
+            num_scalar_prefetch=1,
+            grid=(4,),
+            in_specs=[
+                pl.BlockSpec((left.shape[0], block), lambda s, h: (0, h[0] * 4 + s)),
+                pl.BlockSpec(right.shape, lambda s, h: (0, 0)),
+            ],
+            out_specs=[
+                pl.BlockSpec((block, wide), lambda s, h: (jnp.minimum(s, 1), 0)),
+                pl.BlockSpec((block, wide), lambda s, h: (jnp.maximum(s - 2, 0), 0)),
+            ],
+        ),
+        compiler_params=pltpu.CompilerParams(vmem_limit_bytes=VMEM_LIMIT),
+        cost_estimate=pl.CostEstimate(flops=left.shape[0] * tall * wide, bytes_accessed=8_000_000, transcendentals=0),
+    )(half, left, right)
+
+
+def grad_columns_body(info, left, right, first_out, second_out, turned):
+    step = pl.program_id(0)
+
+    @pl.when(step == 0)
+    def _():
+        turned[...] = jnp.transpose(left[...])
+
+    value = dot_nn(turned[...], right[...]).astype(BF)
+
+    @pl.when(step < 2)
+    def _():
+        first_out[...] = value
+
+    @pl.when(step >= 2)
+    def _():
+        second_out[...] = value
+
+
+def grad_columns(half, left, right):
+    tall, wide = left.shape[1], right.shape[1]
+    block = wide // 4
+    out = jax.ShapeDtypeStruct((tall // 2, wide // 2), BF)
+    return pl.pallas_call(
+        grad_columns_body,
+        out_shape=[out, out],
+        grid_spec=pltpu.PrefetchScalarGridSpec(
+            num_scalar_prefetch=1,
+            grid=(4,),
+            in_specs=[
+                pl.BlockSpec((left.shape[0], tall // 2), lambda s, h: (0, h[0])),
+                pl.BlockSpec((right.shape[0], block), lambda s, h: (0, s)),
+            ],
+            out_specs=[
+                pl.BlockSpec((tall // 2, block), lambda s, h: (0, jnp.minimum(s, 1))),
+                pl.BlockSpec((tall // 2, block), lambda s, h: (0, jnp.maximum(s - 2, 0))),
+            ],
+            scratch_shapes=[pltpu.VMEM((tall // 2, left.shape[0]), BF)],
+        ),
+        compiler_params=pltpu.CompilerParams(vmem_limit_bytes=VMEM_LIMIT),
+        cost_estimate=pl.CostEstimate(flops=left.shape[0] * tall * wide, bytes_accessed=8_000_000, transcendentals=0),
+    )(half, left, right)
+
+
+def grad_rest_body(info, inputs, context, d_query, d_key, d_value, d_one, first_out, second_out):
+    width = d_one.shape[1]
+    turned = jnp.transpose(inputs[...])
+    first_out[:, :width] = dot_nn(turned, d_query[...]).astype(BF)
+    first_out[:, width:] = dot_nn(turned, d_key[...]).astype(BF)
+    second_out[:, :width] = dot_nn(turned, d_value[...]).astype(BF)
+    second_out[:, width:] = dot_nn(jnp.transpose(context[...]), d_one[...]).astype(BF)
+
+
+def grad_rest(half, inputs, context, d_query, d_key, d_value, d_one):
+    width = inputs.shape[1]
+    out = jax.ShapeDtypeStruct((width // 2, 2 * width), BF)
+    side = pl.BlockSpec((inputs.shape[0], width // 2), lambda s, h: (0, h[0]))
+    full = pl.BlockSpec(d_one.shape, lambda s, h: (0, 0))
+    whole = pl.BlockSpec((width // 2, 2 * width), lambda s, h: (0, 0))
+    return pl.pallas_call(
+        grad_rest_body,
+        out_shape=[out, out],
+        grid_spec=pltpu.PrefetchScalarGridSpec(
+            num_scalar_prefetch=1,
+            grid=(1,),
+            in_specs=[side, side, full, full, full, full],
+            out_specs=[whole, whole],
+        ),
+        compiler_params=pltpu.CompilerParams(vmem_limit_bytes=VMEM_LIMIT),
+        cost_estimate=pl.CostEstimate(flops=inputs.shape[0] * 4 * width * width, bytes_accessed=12_000_000, transcendentals=0),
+    )(half, inputs, context, d_query, d_key, d_value, d_one)
+
+
+def widen_body(info, own_a, own_b, other_a, other_b, *outs):
+    step = pl.program_id(0)
+    for s, (a, b) in enumerate(((own_a, own_b), (other_a, other_b))):
+
+        @pl.when(step == s)
+        def _(a=a, b=b):
+            parts = (a[...].astype(F32), b[...].astype(F32))
+            if len(outs) == 2:
+                third = outs[1].shape[1]
+                outs[0][:, : 2 * third] = parts[0]
+                outs[0][:, 2 * third :] = parts[1][:, :third]
+                outs[1][...] = parts[1][:, third:]
+            elif outs[0].shape[1] == parts[0].shape[1]:
+                outs[0][: parts[0].shape[0]] = parts[0]
+                outs[0][parts[0].shape[0] :] = parts[1]
+            else:
+                outs[0][:, : parts[0].shape[1]] = parts[0]
+                outs[0][:, parts[0].shape[1] :] = parts[1]
+
+
+def widened(core, own, other, out_shapes):
+    small = own[0].shape
+    piece_spec = pl.BlockSpec(small, lambda s, h: (0, 0))
+    return pl.pallas_call(
+        widen_body,
+        out_shape=[jax.ShapeDtypeStruct(shape, F32) for shape in out_shapes],
+        grid_spec=pltpu.PrefetchScalarGridSpec(
+            num_scalar_prefetch=1,
+            grid=(2,),
+            in_specs=[piece_spec] * 4,
+            out_specs=[
+                pl.BlockSpec((shape[0] // 2, shape[1]), lambda s, h: (jnp.where(s == 0, h[0], 1 - h[0]), 0))
+                for shape in out_shapes
+            ],
+        ),
+        compiler_params=pltpu.CompilerParams(vmem_limit_bytes=VMEM_LIMIT),
+        cost_estimate=pl.CostEstimate(flops=0, bytes_accessed=14_000_000, transcendentals=0),
+    )(core, *own, *other)
+
+
 def passed_along(array, axis, by):
     count = lax.axis_size(axis)
     pairs = [(i, i + by) for i in range(count) if 0 <= i + by < count]
@@ -622,51 +781,52 @@
     return leaf.reshape(-1, leaf.shape[-1])
 
 
-def swapped(array, bit):
-    count = lax.axis_size("dp")
-    return lax.ppermute(array, "dp", [(i, i ^ bit) for i in range(count)])
+def swapped(array, bit, axis="dp"):
+    count = lax.axis_size(axis)
+    return lax.ppermute(array, axis, [(i, i ^ bit) for i in range(count)])
 
 
 def piece(array, index):
     return lax.dynamic_index_in_dim(array, index, 0, keepdims=False)
 
 
-def placed_at(array, update, index):
-    return lax.dynamic_update_index_in_dim(array, update, index, 0)
-
-
-def sum_low(*arrays):
-    total = arrays[0].astype(F32)
-    for array in arrays[1:]:
-        total = total + array.astype(F32)
-    return total.astype(BF)
-
-
-def summed_over_data(partial):
-    count = lax.axis_size("dp")
-    rows, columns = partial.shape
-    if count != 16:
-        share = lax.psum_scatter(partial, "dp", scatter_dimension=0, tiled=True)
-        return lax.all_gather(share, "dp", axis=0, tiled=True).astype(F32)
-    place = lax.axis_index("dp")
-    core, along_x, along_z = place & 1, (place >> 1) & 1, place >> 2
-    halves = partial.reshape(2, rows // 2, columns)
-    half = sum_low(piece(halves, core), swapped(piece(halves, 1 - core), 1))
-    quarters = half.reshape(2, rows // 4, columns)
-    quarter = sum_low(piece(quarters, along_x), swapped(piece(quarters, 1 - along_x), 2))
-    parts = quarter.reshape(4, rows // 16, columns)
-    arrived = [swapped(piece(parts, along_z ^ step), 4 * step) for step in (1, 2, 3)]
-    share = sum_low(piece(parts, along_z), *arrived)
-    parts = placed_at(jnp.zeros_like(parts), share, along_z)
-    for step in (1, 2, 3):
-        parts = placed_at(parts, swapped(share, 4 * step), along_z ^ step)
-    quarter = parts.reshape(rows // 4, columns)
-    quarters = placed_at(jnp.zeros_like(quarters), quarter, along_x)
-    quarters = placed_at(quarters, swapped(quarter, 2), 1 - along_x)
-    half = quarters.reshape(rows // 2, columns)
-    other = swapped(half, 1)
-    whole = jnp.stack([jnp.where(core == 0, half, other), jnp.where(core == 0, other, half)])
-    return whole.reshape(rows, columns).astype(F32)
+def sum_low(kept, got):
+    return (kept.astype(F32) + got.astype(F32)).astype(BF)
+
+
+def halved(array, bit):
+    step, mine = bit
+    halves = array.reshape(2, array.shape[0] // 2, array.shape[1])
+    got = swapped(piece(halves, 1 - mine), step)
+    return sum_low(piece(halves, mine), got)
+
+
+def doubled(array, bit):
+    step, mine = bit
+    got = swapped(array, step)
+    both = jnp.zeros((2,) + array.shape, array.dtype)
+    both = lax.dynamic_update_index_in_dim(both, array, mine, 0)
+    both = lax.dynamic_update_index_in_dim(both, got, 1 - mine, 0)
+    return flatten_rows(both)
+
+
+def summed_halves(sent, kept, bits, orders):
+    own, other = [], []
+    for send, keep, order in zip(sent, kept, orders):
+        total = sum_low(keep, swapped(send, 1))
+        for place in order:
+            total = halved(total, bits[place])
+        for place in reversed(order):
+            total = doubled(total, bits[place])
+        own.append(total)
+        other.append(swapped(total, 1))
+    return own, other
+
+
+def all_summed(array, bits):
+    for step, _ in bits:
+        array = (array.astype(F32) + swapped(array, step).astype(F32)).astype(array.dtype)
+    return array
 
 
 def shards(
@@ -696,6 +856,11 @@
     info = jnp.concatenate(
         [section_id.astype(jnp.int32)[None], pass_lengths.reshape(-1), positives.reshape(-1)]
     )
+    bits = mesh_bits()
+    core = bits[0][1].astype(jnp.int32)[None]
+    along_x_first = list(range(1, len(bits)))
+    along_z_first = [2, 1] + list(range(3, len(bits)))
+    orders = (along_x_first, along_z_first)
     attn_weights = (wa, attend_bias, wm, mixing_bias, gains, shifts)
     ffn_weights = (we, expand_bias, wr, reduce_bias, gains, shifts)
     received = jnp.zeros((rows, width), BF)
@@ -707,6 +872,14 @@
             received = passed_along(ffn[6], "pipe", 1)
     inputs, joined, lse, context, hidden, unit_one, inv_one, squares_one = attn
     active, slope, outputs, unit_two, inv_two, squares_two, _ = ffn
+    squares = jnp.stack(
+        [
+            jnp.sum(squares_one[:, 0], axis=1),
+            jnp.sum(squares_one[:, 1], axis=1),
+            jnp.sum(squares_two[:, 0], axis=1),
+        ],
+        axis=1,
+    )
     received = jnp.zeros((rows, width), BF)
     ffn_back, attn_back = None, None
     for tick in range(micros + 1):
@@ -715,63 +888,61 @@
             (outputs, unit_two, inv_two, slope, unit_one, inv_one),
             (colbert_weight, gains, wr, we), ffn_back and ffn_back[:6],
         )
+        if tick == micros - 1:
+            colbert = dot_tn(flatten_rows(outputs), flatten_rows(ffn_back[3])).astype(BF)
+            colbert = jnp.where(section_id == 1, colbert, swapped(colbert, 1, "pipe"))
+            colbert_sum = all_summed(colbert, bits).astype(F32)
+            facts = jnp.concatenate([squares, ffn_back[4][:, 6, 0:1]], axis=1)
+            theirs = swapped(facts, 1, "pipe")
+            first = jnp.where(section_id == 0, facts, theirs)
+            second = jnp.where(section_id == 0, theirs, facts)
+        if tick == micros:
+            d_two, d_inner = flatten_rows(ffn_back[0]), flatten_rows(ffn_back[1])
+            left = flatten_rows(active)
+            sent_reduce, kept_reduce = (grad_rows(half, left, d_two) for half in (1 - core, core))
+            left = flatten_rows(hidden)
+            sent_expand, kept_expand = (grad_columns(half, left, d_inner) for half in (1 - core, core))
         attn_back = attn_backward(
             tick, micros, info, ffn_back[6], ffn_back[2], (joined, lse, context), (wa, wm),
             attn_back and attn_back[:4],
         )
         if tick < micros:
             received = passed_along(attn_back[4], "pipe", -1)
-    d_two, d_inner, d_one, d_embed, small, small_ff, _ = ffn_back
+    small, small_ff = ffn_back[4], ffn_back[5]
     d_query, d_key, d_value, joined_sums, _ = attn_back
-
-    def weight_grad(left, right):
-        return dot_tn(flatten_rows(left), flatten_rows(right)).astype(BF)
-
-    big_reduce = summed_over_data(weight_grad(active, d_two))
-    big_expand = summed_over_data(weight_grad(hidden, d_inner))
-    big_rest = summed_over_data(
-        jnp.concatenate(
-            [weight_grad(inputs, d) for d in (d_query, d_key, d_value)] + [weight_grad(context, d_one)],
-            axis=1,
-        )
-    )
-    colbert_sum = lax.psum(weight_grad(outputs, d_embed), ("pipe", "dp")).astype(F32)
+    sides = [flatten_rows(a) for a in (inputs, context, d_query, d_key, d_value, ffn_back[2])]
+    sent_rest, kept_rest = (grad_rest(half, *sides) for half in (1 - core, core))
     small_sum = jnp.sum(small, axis=0)
     joined_sum = jnp.sum(joined_sums[:, :, 0], axis=0)
     attend_sum = jnp.concatenate(
         [joined_sum[:, :SLAB].reshape(-1), joined_sum[:, SLAB:].reshape(-1)]
     )
     vector = jnp.concatenate(
-        [small_sum[:6].reshape(-1), attend_sum, jnp.sum(small_ff[:, 0], axis=0)]
-    )
-    vector = lax.psum(vector, "dp")
-    line = vector[: 8 * width].reshape(8, width)
-    squares = jnp.stack(
-        [
-            jnp.sum(squares_one[:, 0], axis=1),
-            jnp.sum(squares_one[:, 1], axis=1),
-            jnp.sum(squares_two[:, 0], axis=1),
-        ],
-        axis=1,
-    )
-    section_rows = (jnp.arange(2, dtype=jnp.int32) == section_id).astype(F32)
-    square_sum = lax.psum(section_rows[None, :, None] * squares[:, None, :], "pipe")
-    loss_sum = lax.psum(jnp.where(section_id == 1, small[:, 6, 0], 0.0), "pipe")
+        [small_sum[:6], attend_sum.reshape(2, width), jnp.sum(small_ff[:, 0], axis=0).reshape(-1, width)]
+    )
+    vector = all_summed(vector, bits)
+    halves = summed_halves(sent_reduce, kept_reduce, bits, orders)
+    [big_reduce] = widened(core, *halves, [wr.shape])
+    halves = summed_halves(sent_expand, kept_expand, bits, orders)
+    [big_expand] = widened(core, *halves, [we.shape])
+    halves = summed_halves(sent_rest, kept_rest, bits, orders)
+    big_attend, big_mixing = widened(core, *halves, [wa.shape, wm.shape])
     counted = (QROWS + jnp.sum(pass_lengths, axis=1)).astype(F32)
-    stats = jnp.sqrt(square_sum / (counted[:, None, None] * width))
+    stats = jnp.stack([first[:, :3], second[:, :3]], axis=1)
+    stats = jnp.sqrt(stats / (counted[:, None, None] * width))
     return (
-        big_rest[None, :, : 3 * width],
-        line[6:8].reshape(1, -1),
-        big_rest[None, :, 3 * width :],
-        line[5][None],
-        jnp.stack([line[3], line[0]])[None],
-        jnp.stack([line[4], line[1]])[None],
+        big_attend[None],
+        vector[6:8].reshape(1, -1),
+        big_mixing[None],
+        vector[5][None],
+        jnp.stack([vector[3], vector[0]])[None],
+        jnp.stack([vector[4], vector[1]])[None],
         big_expand[None],
-        vector[8 * width :][None],
+        vector[8:].reshape(1, -1),
         big_reduce[None],
-        line[2][None],
+        vector[2][None],
         colbert_sum,
-        loss_sum / NQ,
+        second[:, 3] / NQ,
         stats,
     )
 

time: 966 us -> 748 us (0.77)
  waiting for transfers between devices: 398 us -> 273 us
  Pallas kernels: 305 us -> 372 us
  blocking collectives: 66.6 us -> 0 us
  other arithmetic: 41.7 us -> 10.8 us
  matrix products: 28 us -> 1.71 us
  local copies, waits for them, and re-layouts: 43.3 us -> 19.5 us
  between operations: 15.1 us -> 2.41 us
    psum x1 -> x0, waiting for transfers between devices: 120 us -> none  [shards(): lax.psum(weight_grad(outputs, d_embed), ('pipe', 'dp')).astype(F32)]
    psum x2 -> x0, blocking collectives: 66.6 us -> none  [the longest x1 61.1 us: shards(): vector = lax.psum(vector, 'dp')]
    pallas_call x0 -> x9, Pallas kernels: none -> 66.5 us  [the longest x3 19.1 us: widened(): pl.pallas_call(widen_body, out_shape=[jax.ShapeDtypeStruct(shape, F32) fo...]
    dot_general x7 -> x1, matrix products: 28 us -> 1.71 us  [dot_tn(): lax.dot_general(a, b, (((0,), (0,)), ((), ())), preferred_element_type=F32)]
    convert_element_type x11 -> x22, other arithmetic: 22.3 us -> 4.14 us  [the longest x18 3.19 us: sum_low(): return (kept.astype(F32) + got.astype(F32)).astype(BF)]
    ppermute x4, waiting for transfers between devices: 84.5 us -> 71.5 us  [passed_along(): return lax.ppermute(array, axis, pairs)]
    ppermute x30 -> x58, waiting for transfers between devices: 193 us -> 202 us  [swapped(): return lax.ppermute(array, axis, [(i, i ^ bit) for i in range(count)])]
    ppermute x30 -> x58, starting transfers between devices: 40.2 us -> 47.1 us  [swapped(): return lax.ppermute(array, axis, [(i, i ^ bit) for i in range(count)])]
  transfers between devices with their start and end apart: 35 -> 62, of which waited for: 13 -> 29; matrix products, arithmetic and copies ran while one was open for 9% -> 2% of each run, Pallas kernels for 3% -> 19%
where the time goes in v3:
time: 748 us; the launch traced here: 740 us
  Pallas kernels  372 us (50%)
  waiting for transfers between devices  273 us (36%)
  starting transfers between devices  59.6 us (8%)
  local copies, waits for them, and re-layouts  19.5 us (3%)
  other arithmetic  10.8 us (1%)
    pallas_call x12, Pallas kernels, call(): pl.pallas_call(body, out_shape=[jax.ShapeDtypeStruct(s[0], s[1]) for s in...  306 us
    ppermute x58, waiting for transfers between devices, swapped(): return lax.ppermute(array, axis, [(i, i ^ bit) for i in range(count)])  202 us
    ppermute x4, waiting for transfers between devices, passed_along(): return lax.ppermute(array, axis, pairs)  71.5 us
    ppermute x58, starting transfers between devices, swapped(): return lax.ppermute(array, axis, [(i, i ^ bit) for i in range(count)])  47.1 us
    pallas_call x3, Pallas kernels, widened(): pl.pallas_call(widen_body, out_shape=[jax.ShapeDtypeStruct(shape, F32) fo...  19.1 us
    pallas_call x2, Pallas kernels, grad_rest(): pl.pallas_call(grad_rest_body, out_shape=[out, out], grid_spec=pltpu.Pref...  16.3 us
    pallas_call x2, Pallas kernels, grad_columns(): pl.pallas_call(grad_columns_body, out_shape=[out, out], grid_spec=pltpu.P...  16.2 us
  transfers between devices with their start and end apart: 62, of which 29 were waited for; matrix products, arithmetic and copies ran while one was open for 2% of the time, Pallas kernels for 19%

profile of v3, /device:TPU:0, one launch (start us, length us, event | category | flops | bytes accessed | tf_op | source)
XLA Modules:
  0.0 739.5 jit_solution(627153359077609738)
XLA Ops:
  5.1 22.3 %shard_map.237 = (bf16[2,640,768]{2,1,0:T(8,128)(2,1)}, bf16[2,3,640,768]{3,2,1,0:T(8,128)(2,1)}, f32[2,3,8,640]{3,2,1,0:T(8,128)}, bf16[2,640,768]{2,1,0:T(8,12...) custom-call(s32[17]{0:T(128)} %pad_add_fusion.info, ...), custom_call_target="tpu_custom_call" | custom-call | flops 4278190080 | bytes 20000000 | tf_op jit(solution)/shard_map/pallas_call | solution.py:231
  27.4 24.1 %shard_map.238 = (bf16[2,640,3072]{2,1,0:T(8,128)(2,1)}, bf16[2,640,3072]{2,1,0:T(8,128)(2,1)}, bf16[2,640,768]{2,1,0:T(8,128)(2,1)}, bf16[2,640,768]{2,1,0:T(8,...) custom-call(s32[17]{0:T(128)} %pad_add_fusion.info, ...), custom_call_target="tpu_custom_call" | custom-call | flops 6039797760 | bytes 20000000 | tf_op jit(solution)/shard_map/pallas_call | solution.py:231
  51.6 5.1 collective-permute-start
  56.7 21.0 %collective-permute-done.rec = bf16[640,768]{1,0:T(8,128)(2,1)S(1)} collective-permute-done((bf16[640,768]{1,0:T(8,128)(2,1)}, bf16[640,768]{1,0:T(8,128)(2,1)S(1)}, u32[]{:S(2)}, u32[]{:S(2)}) %collective-permute-start) | collective-permute-done | bytes 983072 | tf_op jit(solution)/shard_map/ppermute | solution.py:777
  78.7 22.3 %shard_map.239 = (bf16[2,640,768]{2,1,0:T(8,128)(2,1)}, bf16[2,3,640,768]{3,2,1,0:T(8,128)(2,1)}, f32[2,3,8,640]{3,2,1,0:T(8,128)}, bf16[2,640,768]{2,1,0:T(8,12...) custom-call(s32[17]{0:T(128)} %pad_add_fusion.info, ...), custom_call_target="tpu_custom_call", output_to_operand_aliasing={{0}: (12, {}), {1}: (13, {}), {2}: (14, {}), {3}: (15, {}),... | custom-call | flops 4278190080 | bytes 20000000 | tf_op jit(solution)/shard_map/pallas_call | solution.py:231
  101.0 24.1 %shard_map.240 = (bf16[2,640,3072]{2,1,0:T(8,128)(2,1)}, bf16[2,640,3072]{2,1,0:T(8,128)(2,1)}, bf16[2,640,768]{2,1,0:T(8,128)(2,1)}, bf16[2,640,768]{2,1,0:T(8,...) custom-call(s32[17]{0:T(128)} %pad_add_fusion.info, ...), custom_call_target="tpu_custom_call", output_to_operand_aliasing={{0}: (8, {}), {1}: (9, {}), {2}: (10, {}), {3}: (11, {}), {... | custom-call | flops 6039797760 | bytes 20000000 | tf_op jit(solution)/shard_map/pallas_call | solution.py:231
  125.1 4.8 collective-permute-start.1
  129.9 20.0 %collective-permute-done.1.rec = bf16[640,768]{1,0:T(8,128)(2,1)S(1)} collective-permute-done((bf16[640,768]{1,0:T(8,128)(2,1)}, bf16[640,768]{1,0:T(8,128)(2,1)S(1)}, u32[]{:S(2)}, u32[]{:S(2)}) %collective-permute-start.1) | collective-permute-done | bytes 983072 | tf_op jit(solution)/shard_map/ppermute | solution.py:777
  150.8 22.3 %shard_map.241 = (bf16[2,640,768]{2,1,0:T(8,128)(2,1)}, bf16[2,3,640,768]{3,2,1,0:T(8,128)(2,1)}, f32[2,3,8,640]{3,2,1,0:T(8,128)}, bf16[2,640,768]{2,1,0:T(8,12...) custom-call(s32[17]{0:T(128)} %pad_add_fusion.info, ...), custom_call_target="tpu_custom_call", output_to_operand_aliasing={{0}: (12, {}), {1}: (13, {}), {2}: (14, {}), {3}: (15, {}),... | custom-call | flops 4278190080 | bytes 20000000 | tf_op jit(solution)/shard_map/pallas_call | solution.py:231
  173.1 24.1 %shard_map.242 = (bf16[2,640,3072]{2,1,0:T(8,128)(2,1)}, bf16[2,640,3072]{2,1,0:T(8,128)(2,1)}, bf16[2,640,768]{2,1,0:T(8,128)(2,1)}, bf16[2,640,768]{2,1,0:T(8,...) custom-call(s32[17]{0:T(128)} %pad_add_fusion.info, ...), custom_call_target="tpu_custom_call", output_to_operand_aliasing={{0}: (8, {}), {1}: (9, {}), {2}: (10, {}), {3}: (11, {}), {... | custom-call | flops 6039797760 | bytes 20000000 | tf_op jit(solution)/shard_map/pallas_call | solution.py:231
  197.2 29.5 %shard_map.243 = (bf16[2,640,768]{2,1,0:T(8,128)(2,1)}, bf16[2,640,3072]{2,1,0:T(8,128)(2,1)}, bf16[2,640,768]{2,1,0:T(8,128)(2,1)}, bf16[2,640,128]{2,1,0:T(8,1...) custom-call(s32[17]{0:T(128)} %pad_add_fusion.info, ...), custom_call_target="tpu_custom_call" | custom-call | flops 6039797760 | bytes 20000000 | tf_op jit(solution)/shard_map/pallas_call | solution.py:231
  226.7 25.7 %shard_map.244 = (bf16[2,640,768]{2,1,0:T(8,128)(2,1)}, bf16[2,640,768]{2,1,0:T(8,128)(2,1)}, bf16[2,640,768]{2,1,0:T(8,128)(2,1)}, f32[2,3,8,512]{3,2,1,0:T(8,128)}, bf16[640,768]{1,0:T(8,128)(2,1)}) custom-call(s32[17]{0:T(128)} %pad_add_fusion.info, f32[640,768]{1,0:T(8,128)} %get-tuple-element.144.resid, ...), custom_call_target="tpu_custom_call" | custom-call | flops 6165626880 | bytes 20000000 | tf_op jit(solution)/shard_map/pallas_call | solution.py:231
  255.8 22.3 %collective-permute-done.2.rec = bf16[640,768]{1,0:T(8,128)(2,1)S(1)} collective-permute-done((bf16[640,768]{1,0:T(8,128)(2,1)}, bf16[640,768]{1,0:T(8,128)(2,1)S(1)}, u32[]{:S(2)}, u32[]{:S(2)}) %collective-permute-start.2) | collective-permute-done | bytes 983072 | tf_op jit(solution)/shard_map/ppermute | solution.py:777
  279.0 30.1 %shard_map.245 = (bf16[2,640,768]{2,1,0:T(8,128)(2,1)}, bf16[2,640,3072]{2,1,0:T(8,128)(2,1)}, bf16[2,640,768]{2,1,0:T(8,128)(2,1)}, bf16[2,640,128]{2,1,0:T(8,1...) custom-call(s32[17]{0:T(128)} %pad_add_fusion.info, ...), custom_call_target="tpu_custom_call", output_to_operand_aliasing={{0}: (13, {}), {1}: (14, {}), {2}: (15, {}), {3}: (16, {}),... | custom-call | flops 6039797760 | bytes 20000000 | tf_op jit(solution)/shard_map/pallas_call | solution.py:231
  316.8 25.9 %shard_map.246 = (bf16[2,640,768]{2,1,0:T(8,128)(2,1)}, bf16[2,640,768]{2,1,0:T(8,128)(2,1)}, bf16[2,640,768]{2,1,0:T(8,128)(2,1)}, f32[2,3,8,512]{3,2,1,0:T(8,128)}, bf16[640,768]{1,0:T(8,128)(2,1)}) custom-call(s32[17]{0:T(128)} %pad_add_fusion.info, ...), custom_call_target="tpu_custom_call", output_to_operand_aliasing={{0}: (10, {}), {1}: (11, {}), {2}: (12, {}), {3}: (13, {})} | custom-call | flops 6165626880 | bytes 20000000 | tf_op jit(solution)/shard_map/pallas_call | solution.py:231
  345.8 5.6 collective-permute-done.58
  353.6 4.4 collective-permute-done.59
  360.8 8.2 %collective-permute-done.3.rec = bf16[640,768]{1,0:T(8,128)(2,1)S(1)} collective-permute-done((bf16[640,768]{1,0:T(8,128)(2,1)}, bf16[640,768]{1,0:T(8,128)(2,1)S(1)}, u32[]{:S(2)}, u32[]{:S(2)}) %collective-permute-start.3) | collective-permute-done | bytes 983072 | tf_op jit(solution)/shard_map/ppermute | solution.py:777
  369.9 29.5 %shard_map.247 = (bf16[2,640,768]{2,1,0:T(8,128)(2,1)}, bf16[2,640,3072]{2,1,0:T(8,128)(2,1)}, bf16[2,640,768]{2,1,0:T(8,128)(2,1)}, bf16[2,640,128]{2,1,0:T(8,1...) custom-call(s32[17]{0:T(128)} %pad_add_fusion.info, ...), custom_call_target="tpu_custom_call", output_to_operand_aliasing={{0}: (13, {}), {1}: (14, {}), {2}: (15, {}), {3}: (16, {}),... | custom-call | flops 6039797760 | bytes 20000000 | tf_op jit(solution)/shard_map/pallas_call | solution.py:231
  399.4 7.5 %shard_map.255 = (bf16[768,768]{1,0:T(8,128)(2,1)}, bf16[768,768]{1,0:T(8,128)(2,1)}) custom-call(s32[1]{0:T(128)} %bitcast.info, bf16[1280,3072]{1,0:T(8,128)(2,1)} %bitcast.317, bf16[1280,768]{1,0:T(8,128)(2,1)} %bitcast.329), custom_call_target="tpu_custom_call" | custom-call | flops 3019898880 | bytes 8000000 | tf_op jit(solution)/shard_map/pallas_call | solution.py:642
  406.8 7.5 %shard_map.256 = (bf16[768,768]{1,0:T(8,128)(2,1)}, bf16[768,768]{1,0:T(8,128)(2,1)}) custom-call(s32[1]{0:T(128)S(6)} %sub.19.info, bf16[1280,3072]{1,0:T(8,128)(2,1)} %bitcast.318, bf16[1280,768]{1,0:T(8,128)(2,1)} %bitcast.330), custom_call_target="tpu_custom_call" | custom-call | flops 3019898880 | bytes 8000000 | tf_op jit(solution)/shard_map/pallas_call | solution.py:642
  414.3 8.0 %shard_map.253 = (bf16[384,1536]{1,0:T(8,128)(2,1)}, bf16[384,1536]{1,0:T(8,128)(2,1)}) custom-call(s32[1]{0:T(128)S(6)} %sub.19.info, bf16[1280,768]{1,0:T(8,128)(2,1)} %bitcast.319, bf16[1280,3072]{1,0:T(8,128)(2,1)} %bitcast.307), custom_call_target="tpu_custom_call" | custom-call | flops 3019898880 | bytes 8000000 | tf_op jit(solution)/shard_map/pallas_call | solution.py:684
  422.3 25.8 %shard_map.248 = (bf16[2,640,768]{2,1,0:T(8,128)(2,1)}, bf16[2,640,768]{2,1,0:T(8,128)(2,1)}, bf16[2,640,768]{2,1,0:T(8,128)(2,1)}, f32[2,3,8,512]{3,2,1,0:T(8,128)}, bf16[640,768]{1,0:T(8,128)(2,1)}) custom-call(s32[17]{0:T(128)} %pad_add_fusion.info, ...), custom_call_target="tpu_custom_call", output_to_operand_aliasing={{0}: (10, {}), {1}: (11, {}), {2}: (12, {}), {3}: (13, {})} | custom-call | flops 6165626880 | bytes 20000000 | tf_op jit(solution)/shard_map/pallas_call | solution.py:231
  450.7 8.2 %shard_map.252 = (bf16[384,1536]{1,0:T(8,128)(2,1)}, bf16[384,1536]{1,0:T(8,128)(2,1)}) custom-call(s32[1]{0:T(128)} %bitcast.info, bf16[1280,768]{1,0:T(8,128)(2,1)} %bitcast.320, bf16[1280,3072]{1,0:T(8,128)(2,1)} %bitcast.308), custom_call_target="tpu_custom_call" | custom-call | flops 3019898880 | bytes 8000000 | tf_op jit(solution)/shard_map/pallas_call | solution.py:684
  461.1 8.1 %shard_map.249 = (bf16[384,1536]{1,0:T(8,128)(2,1)}, bf16[384,1536]{1,0:T(8,128)(2,1)}) custom-call(s32[1]{0:T(128)} %bitcast.info, bf16[1280,768]{1,0:T(8,128)(2,1)} %bitcast.315, bf16[1280,768]{1,0:T(8,128)(2,1)} %bitcast.305, bf16[1280,768]{1,0:T(8,128)(2,1)} %bitcast.309, bf16[1280,768]{1,0:T(8,128)(2,1)} %bitcast.311, bf16[1280,768]{1,0:T(8,128)(2,1)} %bitcast.313, ...), custom_call_target="tpu_custom_call" | custom-call | flops 3019898880 | bytes 12000000 | tf_op jit(solution)/shard_map/pallas_call | solution.py:720
  470.9 8.1 %shard_map.250 = (bf16[384,1536]{1,0:T(8,128)(2,1)}, bf16[384,1536]{1,0:T(8,128)(2,1)}) custom-call(s32[1]{0:T(128)S(6)} %sub.19.info, bf16[1280,768]{1,0:T(8,128)(2,1)} %bitcast.316, bf16[1280,768]{1,0:T(8,128)(2,1)} %bitcast.306, bf16[1280,768]{1,0:T(8,128)(2,1)} %bitcast.310, bf16[1280,768]{1,0:T(8,128)(2,1)} %bitcast.312, bf16[1280,768]{1,0:T(8,128)(2,1)} %bitcast.314, ...), custom_call_target="tpu_custom_call" | custom-call | flops 3019898880 | bytes 12000000 | tf_op jit(solution)/shard_map/pallas_call | solution.py:720
  489.4 23.2 %collective-permute-done.32 = bf16[192,1536]{1,0:T(8,128)(2,1)S(1)} collective-permute-done((bf16[192,1536]{1,0:T(8,128)(2,1)S(1)}, bf16[192,1536]{1,0:T(8,128)(2,1)S(1)}, u32[]{:S(2)}, u32[]{:S(2)}) %collective-permute-start.32) | collective-permute-done | bytes 589856 | tf_op jit(solution)/shard_map/ppermute | solution.py:786
  516.1 12.7 %collective-permute-done.41 = bf16[384,768]{1,0:T(8,128)(2,1)S(1)} collective-permute-done((bf16[384,768]{1,0:T(8,128)(2,1)S(1)}, bf16[384,768]{1,0:T(8,128)(2,1)S(1)}, u32[]{:S(2)}, u32[]{:S(2)}) %collective-permute-start.41) | collective-permute-done | bytes 589856 | tf_op jit(solution)/shard_map/ppermute | solution.py:786
  530.6 10.8 %collective-permute-done.5 = bf16[192,1536]{1,0:T(8,128)(2,1)S(1)} collective-permute-done((bf16[192,1536]{1,0:T(8,128)(2,1)S(1)}, bf16[192,1536]{1,0:T(8,128)(2,1)S(1)}, u32[]{:S(2)}, u32[]{:S(2)}) %collective-permute-start.5) | collective-permute-done | bytes 589856 | tf_op jit(solution)/shard_map/ppermute | solution.py:786
  542.2 9.9 %collective-permute-done.33 = bf16[96,1536]{1,0:T(8,128)(2,1)S(1)} collective-permute-done((bf16[96,1536]{1,0:T(8,128)(2,1)S(1)}, bf16[96,1536]{1,0:T(8,128)(2,1)S(1)}, u32[]{:S(2)}, u32[]{:S(2)}) %collective-permute-start.33) | collective-permute-done | bytes 294944 | tf_op jit(solution)/shard_map/ppermute | solution.py:786
  555.1 10.1 %collective-permute-done.26 = bf16[96,1536]{1,0:T(8,128)(2,1)S(1)} collective-permute-done((bf16[96,1536]{1,0:T(8,128)(2,1)S(1)}, bf16[96,1536]{1,0:T(8,128)(2,1)S(1)}, u32[]{:S(2)}, u32[]{:S(2)}) %collective-permute-start.26) | collective-permute-done | bytes 294944 | tf_op jit(solution)/shard_map/ppermute | solution.py:786
  570.5 14.1 %collective-permute-done.34 = bf16[48,1536]{1,0:T(8,128)(2,1)S(1)} collective-permute-done((bf16[48,1536]{1,0:T(8,128)(2,1)S(1)}, bf16[48,1536]{1,0:T(8,128)(2,1)S(1)}, u32[]{:S(2)}, u32[]{:S(2)}) %collective-permute-start.34) | collective-permute-done | bytes 147488 | tf_op jit(solution)/shard_map/ppermute | solution.py:786
  584.8 12.2 %collective-permute-done.27 = bf16[48,1536]{1,0:T(8,128)(2,1)S(1)} collective-permute-done((bf16[48,1536]{1,0:T(8,128)(2,1)S(1)}, bf16[48,1536]{1,0:T(8,128)(2,1)S(1)}, u32[]{:S(2)}, u32[]{:S(2)}) %collective-permute-start.27) | collective-permute-done | bytes 147488 | tf_op jit(solution)/shard_map/ppermute | solution.py:786
  597.1 3.0 collective-permute-start.7
  600.3 11.3 %collective-permute-done.14 = bf16[48,1536]{1,0:T(8,128)(2,1)S(1)} collective-permute-done((bf16[48,1536]{1,0:T(8,128)(2,1)S(1)}, bf16[48,1536]{1,0:T(8,128)(2,1)S(1)}, u32[]{:S(2)}, u32[]{:S(2)}) %collective-permute-start.14) | collective-permute-done | bytes 147488 | tf_op jit(solution)/shard_map/ppermute | solution.py:786
  611.7 4.6 collective-permute-done.7
  616.3 9.4 %collective-permute-done.35 = bf16[48,1536]{1,0:T(8,128)(2,1)S(1)} collective-permute-done((bf16[48,1536]{1,0:T(8,128)(2,1)S(1)}, bf16[48,1536]{1,0:T(8,128)(2,1)S(1)}, u32[]{:S(2)}, u32[]{:S(2)}) %collective-permute-start.35) | collective-permute-done | bytes 147488 | tf_op jit(solution)/shard_map/ppermute | solution.py:786
  625.8 10.0 %collective-permute-done.28 = bf16[48,1536]{1,0:T(8,128)(2,1)S(1)} collective-permute-done((bf16[48,1536]{1,0:T(8,128)(2,1)S(1)}, bf16[48,1536]{1,0:T(8,128)(2,1)S(1)}, u32[]{:S(2)}, u32[]{:S(2)}) %collective-permute-start.28) | collective-permute-done | bytes 147488 | tf_op jit(solution)/shard_map/ppermute | solution.py:786
  639.7 4.8 collective-permute-done.15
  646.9 6.0 collective-permute-done.36
  653.8 7.6 %collective-permute-done.29 = bf16[96,1536]{1,0:T(8,128)(2,1)S(1)} collective-permute-done((bf16[96,1536]{1,0:T(8,128)(2,1)S(1)}, bf16[96,1536]{1,0:T(8,128)(2,1)S(1)}, u32[]{:S(2)}, u32[]{:S(2)}) %collective-permute-start.29) | collective-permute-done | bytes 294944 | tf_op jit(solution)/shard_map/ppermute | solution.py:786
  664.3 6.2 collective-permute-done.16
  675.3 19.5 %collective-permute-done.37 = bf16[192,1536]{1,0:T(8,128)(2,1)S(1)} collective-permute-done((bf16[192,1536]{1,0:T(8,128)(2,1)S(1)}, bf16[192,1536]{1,0:T(8,128)(2,1)S(1)}, u32[]{:S(2)}, u32[]{:S(2)}) %collective-permute-start.37) | collective-permute-done | bytes 589856 | tf_op jit(solution)/shard_map/ppermute | solution.py:786
  697.6 7.1 collective-permute-done.46
  706.4 4.7 collective-permute-done.10
  717.8 6.4 shard_map.257
  724.2 6.4 shard_map.254
  732.7 6.3 shard_map.251
  (281 shorter events, 86.3 us)
Async XLA Ops:
  51.6 26.2 %collective-permute-start = (bf16[640,768]{1,0:T(8,128)(2,1)}, bf16[640,768]{1,0:T(8,128)(2,1)S(1)}, u32[]{:S(2)}, u32[]{:S(2)}) collective-permute-start(bf16[640,768]{1,0:T(8,128)(2,1)} %get-tuple-element.106), channel_id=1, source_target_pairs={{0,16},{1,17},{2,18},{3,19},{4,20},{5,21},{6,22},{7,23},{8,24},{9,... | collective-permute-start | bytes 2949128 | tf_op jit(solution)/shard_map/ppermute | solution.py:777
  125.1 24.8 %collective-permute-start.1 = (bf16[640,768]{1,0:T(8,128)(2,1)}, bf16[640,768]{1,0:T(8,128)(2,1)S(1)}, u32[]{:S(2)}, u32[]{:S(2)}) collective-permute-start(bf16[640,768]{1,0:T(8,128)(2,1)} %get-tuple-element.121), channel_id=1, source_target_pairs={{0,16},{1,17},{2,18},{3,19},{4,20},{5,21},{6,22},{7,23},{8,24},{9,... | collective-permute-start | bytes 2949128 | tf_op jit(solution)/shard_map/ppermute | solution.py:777
  252.4 25.7 %collective-permute-start.2 = (bf16[640,768]{1,0:T(8,128)(2,1)}, bf16[640,768]{1,0:T(8,128)(2,1)S(1)}, u32[]{:S(2)}, u32[]{:S(2)}) collective-permute-start(bf16[640,768]{1,0:T(8,128)(2,1)} %get-tuple-element.148), channel_id=1, source_target_pairs={{16,0},{17,1},{18,2},{19,3},{20,4},{21,5},{22,6},{23,7},{24,8},{25... | collective-permute-start | bytes 2949128 | tf_op jit(solution)/shard_map/ppermute | solution.py:777
  312.9 32.7 %collective-permute-start.61 = (f32[2,4]{0,1:T(4,128)S(1)}, f32[2,4]{0,1:T(4,128)S(1)}, u32[]{:S(2)}, u32[]{:S(2)}) collective-permute-start(f32[2,4]{0,1:T(4,128)S(1)} %pad_maximum_fusion.2), channel_id=1, source_target_pairs={{0,16},{16,0},{1,17},{17,1},{2,18},{18,2},{3,19},{19,3},{4,20},{20... | collective-permute-start | bytes 104 | tf_op jit(solution)/shard_map/ppermute | solution.py:786
  316.7 27.3 %collective-permute-start.57 = (bf16[768,128]{1,0:T(8,128)(2,1)S(1)}, bf16[768,128]{1,0:T(8,128)(2,1)S(1)}, u32[]{:S(2)}, u32[]{:S(2)}) collective-permute-start(bf16[768,128]{1,0:T(8,128)(2,1)S(1)} %broadcast_select_fusion), channel_id=1, source_target_pairs={{0,1},{1,0},{2,3},{3,2},{4,5},{5,4},{6,7},{7,6},{8,9},{9,8},{10,11... | collective-permute-start | bytes 589832 | tf_op jit(solution)/shard_map/ppermute | solution.py:786
  342.7 26.2 %collective-permute-start.3 = (bf16[640,768]{1,0:T(8,128)(2,1)}, bf16[640,768]{1,0:T(8,128)(2,1)S(1)}, u32[]{:S(2)}, u32[]{:S(2)}) collective-permute-start(bf16[640,768]{1,0:T(8,128)(2,1)} %get-tuple-element.160), channel_id=1, source_target_pairs={{16,0},{17,1},{18,2},{19,3},{20,4},{21,5},{22,6},{23,7},{24,8},{25... | collective-permute-start | bytes 2949128 | tf_op jit(solution)/shard_map/ppermute | solution.py:777
  358.1 353.0 %collective-permute-start.60 = (bf16[768,128]{1,0:T(8,128)(2,1)S(1)}, bf16[768,128]{1,0:T(8,128)(2,1)S(1)}, u32[]{:S(2)}, u32[]{:S(2)}) collective-permute-start(bf16[768,128]{1,0:T(8,128)(2,1)S(1)} %add_convert_fusion.7), channel_id=1, source_target_pairs={{0,8},{1,9},{2,10},{3,11},{4,12},{5,13},{6,14},{7,15},{8,0},{9,1},... | collective-permute-start | bytes 589832 | tf_op jit(solution)/shard_map/ppermute | solution.py:786
  422.3 56.7 %collective-permute-start.31 = (bf16[384,1536]{1,0:T(8,128)(2,1)}, bf16[384,1536]{1,0:T(8,128)(2,1)S(1)}, u32[]{:S(2)}, u32[]{:S(2)}) collective-permute-start(bf16[384,1536]{1,0:T(8,128)(2,1)} %get-tuple-element.188), channel_id=1, source_target_pairs={{0,1},{1,0},{2,3},{3,2},{4,5},{5,4},{6,7},{7,6},{8,9},{9,8},{10,11... | collective-permute-start | bytes 3538952 | tf_op jit(solution)/shard_map/ppermute | solution.py:786
  458.9 21.0 %collective-permute-start.47 = (bf16[768,768]{1,0:T(8,128)(2,1)}, bf16[768,768]{1,0:T(8,128)(2,1)S(1)}, u32[]{:S(2)}, u32[]{:S(2)}) collective-permute-start(bf16[768,768]{1,0:T(8,128)(2,1)} %get-tuple-element.194), channel_id=1, source_target_pairs={{0,1},{1,0},{2,3},{3,2},{4,5},{5,4},{6,7},{7,6},{8,9},{9,8},{10,11... | collective-permute-start | bytes 3538952 | tf_op jit(solution)/shard_map/ppermute | solution.py:786
  459.0 22.6 %collective-permute-start.24 = (bf16[384,1536]{1,0:T(8,128)(2,1)}, bf16[384,1536]{1,0:T(8,128)(2,1)S(1)}, u32[]{:S(2)}, u32[]{:S(2)}) collective-permute-start(bf16[384,1536]{1,0:T(8,128)(2,1)} %get-tuple-element.186), channel_id=1, source_target_pairs={{0,1},{1,0},{2,3},{3,2},{4,5},{5,4},{6,7},{7,6},{8,9},{9,8},{10,11... | collective-permute-start | bytes 3538952 | tf_op jit(solution)/shard_map/ppermute | solution.py:786
  469.2 9.8 %collective-permute-start.22 = (f32[12,768]{1,0:T(8,128)S(1)}, f32[12,768]{1,0:T(8,128)S(1)}, u32[]{:S(2)}, u32[]{:S(2)}) collective-permute-start(f32[12,768]{1,0:T(8,128)S(1)} %add.238), channel_id=1, source_target_pairs={{0,4},{1,5},{2,6},{3,7},{4,0},{5,1},{6,2},{7,3},{8,12},{9,13},{10,... | collective-permute-start | bytes 110600 | tf_op jit(solution)/shard_map/ppermute | solution.py:786
  481.6 230.1 %collective-permute-start.23 = (f32[12,768]{1,0:T(8,128)S(1)}, f32[12,768]{1,0:T(8,128)S(1)}, u32[]{:S(2)}, u32[]{:S(2)}) collective-permute-start(f32[12,768]{1,0:T(8,128)S(1)} %add.239), channel_id=1, source_target_pairs={{0,8},{1,9},{2,10},{3,11},{4,12},{5,13},{6,14},{7,15},{8,0},{9,1},... | collective-permute-start | bytes 110600 | tf_op jit(solution)/shard_map/ppermute | solution.py:786
  484.7 29.6 %collective-permute-start.48 = (bf16[384,768]{1,0:T(8,128)(2,1)S(1)}, bf16[384,768]{1,0:T(8,128)(2,1)S(1)}, u32[]{:S(2)}, u32[]{:S(2)}) collective-permute-start(bf16[384,768]{1,0:T(8,128)(2,1)S(1)} %dynamic-slice_bitcast_fusion), channel_id=1, source_target_pairs={{0,4},{1,5},{2,6},{3,7},{4,0},{5,1},{6,2},{7,3},{8,12},{9,13},{10,... | collective-permute-start | bytes 1769480 | tf_op jit(solution)/shard_map/ppermute | solution.py:786
  486.3 26.3 %collective-permute-start.32 = (bf16[192,1536]{1,0:T(8,128)(2,1)S(1)}, bf16[192,1536]{1,0:T(8,128)(2,1)S(1)}, u32[]{:S(2)}, u32[]{:S(2)}) collective-permute-start(bf16[192,1536]{1,0:T(8,128)(2,1)S(1)} %dynamic-slice_bitcast_fusion.2), channel_id=1, source_target_pairs={{0,4},{1,5},{2,6},{3,7},{4,0},{5,1},{6,2},{7,3},{8,12},{9,13},{10,... | collective-permute-start | bytes 1769480 | tf_op jit(solution)/shard_map/ppermute | solution.py:786
  487.8 25.5 %collective-permute-start.25 = (bf16[192,1536]{1,0:T(8,128)(2,1)S(1)}, bf16[192,1536]{1,0:T(8,128)(2,1)S(1)}, u32[]{:S(2)}, u32[]{:S(2)}) collective-permute-start(bf16[192,1536]{1,0:T(8,128)(2,1)S(1)} %dynamic-slice_bitcast_fusion.3), channel_id=1, source_target_pairs={{0,2},{1,3},{2,0},{3,1},{4,6},{5,7},{6,4},{7,5},{8,10},{9,11},{10,... | collective-permute-start | bytes 1769480 | tf_op jit(solution)/shard_map/ppermute | solution.py:786
  512.5 16.3 %collective-permute-start.41 = (bf16[384,768]{1,0:T(8,128)(2,1)S(1)}, bf16[384,768]{1,0:T(8,128)(2,1)S(1)}, u32[]{:S(2)}, u32[]{:S(2)}) collective-permute-start(bf16[384,768]{1,0:T(8,128)(2,1)S(1)} %dynamic-slice_bitcast_fusion.1), channel_id=1, source_target_pairs={{0,2},{1,3},{2,0},{3,1},{4,6},{5,7},{6,4},{7,5},{8,10},{9,11},{10,... | collective-permute-start | bytes 1769480 | tf_op jit(solution)/shard_map/ppermute | solution.py:786
  513.3 16.3 %collective-permute-start.12 = (bf16[192,1536]{1,0:T(8,128)(2,1)S(1)}, bf16[192,1536]{1,0:T(8,128)(2,1)S(1)}, u32[]{:S(2)}, u32[]{:S(2)}) collective-permute-start(bf16[192,1536]{1,0:T(8,128)(2,1)S(1)} %dynamic-slice_bitcast_fusion.4), channel_id=1, source_target_pairs={{0,4},{1,5},{2,6},{3,7},{4,0},{5,1},{6,2},{7,3},{8,12},{9,13},{10,... | collective-permute-start | bytes 1769480 | tf_op jit(solution)/shard_map/ppermute | solution.py:786
  514.3 27.1 %collective-permute-start.5 = (bf16[192,1536]{1,0:T(8,128)(2,1)S(1)}, bf16[192,1536]{1,0:T(8,128)(2,1)S(1)}, u32[]{:S(2)}, u32[]{:S(2)}) collective-permute-start(bf16[192,1536]{1,0:T(8,128)(2,1)S(1)} %dynamic-slice_bitcast_fusion.5), channel_id=1, source_target_pairs={{0,2},{1,3},{2,0},{3,1},{4,6},{5,7},{6,4},{7,5},{8,10},{9,11},{10,... | collective-permute-start | bytes 1769480 | tf_op jit(solution)/shard_map/ppermute | solution.py:786
  528.8 24.5 %collective-permute-start.49 = (bf16[192,768]{1,0:T(8,128)(2,1)S(1)}, bf16[192,768]{1,0:T(8,128)(2,1)S(1)}, u32[]{:S(2)}, u32[]{:S(2)}) collective-permute-start(bf16[192,768]{1,0:T(8,128)(2,1)S(1)} %dynamic-slice_bitcast_fusion.6), channel_id=1, source_target_pairs={{0,2},{1,3},{2,0},{3,1},{4,6},{5,7},{6,4},{7,5},{8,10},{9,11},{10,... | collective-permute-start | bytes 884744 | tf_op jit(solution)/shard_map/ppermute | solution.py:786
  529.6 24.5 %collective-permute-start.42 = (bf16[192,768]{1,0:T(8,128)(2,1)S(1)}, bf16[192,768]{1,0:T(8,128)(2,1)S(1)}, u32[]{:S(2)}, u32[]{:S(2)}) collective-permute-start(bf16[192,768]{1,0:T(8,128)(2,1)S(1)} %dynamic-slice_bitcast_fusion.7), channel_id=1, source_target_pairs={{0,4},{1,5},{2,6},{3,7},{4,0},{5,1},{6,2},{7,3},{8,12},{9,13},{10,... | collective-permute-start | bytes 884744 | tf_op jit(solution)/shard_map/ppermute | solution.py:786
  541.4 10.7 %collective-permute-start.33 = (bf16[96,1536]{1,0:T(8,128)(2,1)S(1)}, bf16[96,1536]{1,0:T(8,128)(2,1)S(1)}, u32[]{:S(2)}, u32[]{:S(2)}) collective-permute-start(bf16[96,1536]{1,0:T(8,128)(2,1)S(1)} %dynamic-slice_bitcast_fusion.8), channel_id=1, source_target_pairs={{0,2},{1,3},{2,0},{3,1},{4,6},{5,7},{6,4},{7,5},{8,10},{9,11},{10,... | collective-permute-start | bytes 884744 | tf_op jit(solution)/shard_map/ppermute | solution.py:786
  552.1 13.1 %collective-permute-start.26 = (bf16[96,1536]{1,0:T(8,128)(2,1)S(1)}, bf16[96,1536]{1,0:T(8,128)(2,1)S(1)}, u32[]{:S(2)}, u32[]{:S(2)}) collective-permute-start(bf16[96,1536]{1,0:T(8,128)(2,1)S(1)} %dynamic-slice_bitcast_fusion.9), channel_id=1, source_target_pairs={{0,4},{1,5},{2,6},{3,7},{4,0},{5,1},{6,2},{7,3},{8,12},{9,13},{10,... | collective-permute-start | bytes 884744 | tf_op jit(solution)/shard_map/ppermute | solution.py:786
  553.3 12.5 %collective-permute-start.13 = (bf16[96,1536]{1,0:T(8,128)(2,1)S(1)}, bf16[96,1536]{1,0:T(8,128)(2,1)S(1)}, u32[]{:S(2)}, u32[]{:S(2)}) collective-permute-start(bf16[96,1536]{1,0:T(8,128)(2,1)S(1)} %dynamic-slice_bitcast_fusion.10), channel_id=1, source_target_pairs={{0,2},{1,3},{2,0},{3,1},{4,6},{5,7},{6,4},{7,5},{8,10},{9,11},{10,... | collective-permute-start | bytes 884744 | tf_op jit(solution)/shard_map/ppermute | solution.py:786
  554.0 14.6 %collective-permute-start.6 = (bf16[96,1536]{1,0:T(8,128)(2,1)S(1)}, bf16[96,1536]{1,0:T(8,128)(2,1)S(1)}, u32[]{:S(2)}, u32[]{:S(2)}) collective-permute-start(bf16[96,1536]{1,0:T(8,128)(2,1)S(1)} %dynamic-slice_bitcast_fusion.11), channel_id=1, source_target_pairs={{0,4},{1,5},{2,6},{3,7},{4,0},{5,1},{6,2},{7,3},{8,12},{9,13},{10,... | collective-permute-start | bytes 884744 | tf_op jit(solution)/shard_map/ppermute | solution.py:786
  565.2 31.9 %collective-permute-start.50 = (bf16[96,768]{1,0:T(8,128)(2,1)S(1)}, bf16[96,768]{1,0:T(8,128)(2,1)S(1)}, u32[]{:S(2)}, u32[]{:S(2)}) collective-permute-start(bf16[96,768]{1,0:T(8,128)(2,1)S(1)} %dynamic-slice_bitcast_fusion.12), channel_id=1, source_target_pairs={{0,8},{1,9},{2,10},{3,11},{4,12},{5,13},{6,14},{7,15},{8,0},{9,1},... | collective-permute-start | bytes 442376 | tf_op jit(solution)/shard_map/ppermute | solution.py:786
  565.8 34.4 %collective-permute-start.43 = (bf16[96,768]{1,0:T(8,128)(2,1)S(1)}, bf16[96,768]{1,0:T(8,128)(2,1)S(1)}, u32[]{:S(2)}, u32[]{:S(2)}) collective-permute-start(bf16[96,768]{1,0:T(8,128)(2,1)S(1)} %dynamic-slice_bitcast_fusion.13), channel_id=1, source_target_pairs={{0,8},{1,9},{2,10},{3,11},{4,12},{5,13},{6,14},{7,15},{8,0},{9,1},... | collective-permute-start | bytes 442376 | tf_op jit(solution)/shard_map/ppermute | solution.py:786
  568.7 16.0 %collective-permute-start.34 = (bf16[48,1536]{1,0:T(8,128)(2,1)S(1)}, bf16[48,1536]{1,0:T(8,128)(2,1)S(1)}, u32[]{:S(2)}, u32[]{:S(2)}) collective-permute-start(bf16[48,1536]{1,0:T(8,128)(2,1)S(1)} %dynamic-slice_bitcast_fusion.14), channel_id=1, source_target_pairs={{0,8},{1,9},{2,10},{3,11},{4,12},{5,13},{6,14},{7,15},{8,0},{9,1},... | collective-permute-start | bytes 442376 | tf_op jit(solution)/shard_map/ppermute | solution.py:786
  584.7 12.3 %collective-permute-start.27 = (bf16[48,1536]{1,0:T(8,128)(2,1)S(1)}, bf16[48,1536]{1,0:T(8,128)(2,1)S(1)}, u32[]{:S(2)}, u32[]{:S(2)}) collective-permute-start(bf16[48,1536]{1,0:T(8,128)(2,1)S(1)} %dynamic-slice_bitcast_fusion.15), channel_id=1, source_target_pairs={{0,8},{1,9},{2,10},{3,11},{4,12},{5,13},{6,14},{7,15},{8,0},{9,1},... | collective-permute-start | bytes 442376 | tf_op jit(solution)/shard_map/ppermute | solution.py:786
  597.0 14.6 %collective-permute-start.14 = (bf16[48,1536]{1,0:T(8,128)(2,1)S(1)}, bf16[48,1536]{1,0:T(8,128)(2,1)S(1)}, u32[]{:S(2)}, u32[]{:S(2)}) collective-permute-start(bf16[48,1536]{1,0:T(8,128)(2,1)S(1)} %dynamic-slice_bitcast_fusion.16), channel_id=1, source_target_pairs={{0,8},{1,9},{2,10},{3,11},{4,12},{5,13},{6,14},{7,15},{8,0},{9,1},... | collective-permute-start | bytes 442376 | tf_op jit(solution)/shard_map/ppermute | solution.py:786
  597.1 19.2 %collective-permute-start.7 = (bf16[48,1536]{1,0:T(8,128)(2,1)S(1)}, bf16[48,1536]{1,0:T(8,128)(2,1)S(1)}, u32[]{:S(2)}, u32[]{:S(2)}) collective-permute-start(bf16[48,1536]{1,0:T(8,128)(2,1)S(1)} %dynamic-slice_bitcast_fusion.17), channel_id=1, source_target_pairs={{0,8},{1,9},{2,10},{3,11},{4,12},{5,13},{6,14},{7,15},{8,0},{9,1},... | collective-permute-start | bytes 442376 | tf_op jit(solution)/shard_map/ppermute | solution.py:786
  600.2 35.8 %collective-permute-start.51 = (bf16[96,768]{1,0:T(8,128)(2,1)S(1)}, bf16[96,768]{1,0:T(8,128)(2,1)S(1)}, u32[]{:S(2)}, u32[]{:S(2)}) collective-permute-start(bf16[96,768]{1,0:T(8,128)(2,1)S(1)} %get-tuple-element.226), channel_id=1, source_target_pairs={{0,8},{1,9},{2,10},{3,11},{4,12},{5,13},{6,14},{7,15},{8,0},{9,1},... | collective-permute-start | bytes 442376 | tf_op jit(solution)/shard_map/ppermute | solution.py:786
  611.6 27.4 %collective-permute-start.44 = (bf16[96,768]{1,0:T(8,128)(2,1)S(1)}, bf16[96,768]{1,0:T(8,128)(2,1)S(1)}, u32[]{:S(2)}, u32[]{:S(2)}) collective-permute-start(bf16[96,768]{1,0:T(8,128)(2,1)S(1)} %get-tuple-element.228), channel_id=1, source_target_pairs={{0,8},{1,9},{2,10},{3,11},{4,12},{5,13},{6,14},{7,15},{8,0},{9,1},... | collective-permute-start | bytes 442376 | tf_op jit(solution)/shard_map/ppermute | solution.py:786
  625.7 10.2 %collective-permute-start.28 = (bf16[48,1536]{1,0:T(8,128)(2,1)S(1)}, bf16[48,1536]{1,0:T(8,128)(2,1)S(1)}, u32[]{:S(2)}, u32[]{:S(2)}) collective-permute-start(bf16[48,1536]{1,0:T(8,128)(2,1)S(1)} %get-tuple-element.232), channel_id=1, source_target_pairs={{0,8},{1,9},{2,10},{3,11},{4,12},{5,13},{6,14},{7,15},{8,0},{9,1},... | collective-permute-start | bytes 442376 | tf_op jit(solution)/shard_map/ppermute | solution.py:786
  636.0 10.2 %collective-permute-start.8 = (bf16[48,1536]{1,0:T(8,128)(2,1)S(1)}, bf16[48,1536]{1,0:T(8,128)(2,1)S(1)}, u32[]{:S(2)}, u32[]{:S(2)}) collective-permute-start(bf16[48,1536]{1,0:T(8,128)(2,1)S(1)} %get-tuple-element.236), channel_id=1, source_target_pairs={{0,8},{1,9},{2,10},{3,11},{4,12},{5,13},{6,14},{7,15},{8,0},{9,1},... | collective-permute-start | bytes 442376 | tf_op jit(solution)/shard_map/ppermute | solution.py:786
  639.0 24.4 %collective-permute-start.52 = (bf16[192,768]{1,0:T(8,128)(2,1)S(1)}, bf16[192,768]{1,0:T(8,128)(2,1)S(1)}, u32[]{:S(2)}, u32[]{:S(2)}) collective-permute-start(bf16[192,768]{1,0:T(8,128)(2,1)S(1)} %bitcast.397), channel_id=1, source_target_pairs={{0,2},{1,3},{2,0},{3,1},{4,6},{5,7},{6,4},{7,5},{8,10},{9,11},{10,... | collective-permute-start | bytes 884744 | tf_op jit(solution)/shard_map/ppermute | solution.py:786
  644.5 30.0 %collective-permute-start.45 = (bf16[192,768]{1,0:T(8,128)(2,1)S(1)}, bf16[192,768]{1,0:T(8,128)(2,1)S(1)}, u32[]{:S(2)}, u32[]{:S(2)}) collective-permute-start(bf16[192,768]{1,0:T(8,128)(2,1)S(1)} %bitcast.399), channel_id=1, source_target_pairs={{0,4},{1,5},{2,6},{3,7},{4,0},{5,1},{6,2},{7,3},{8,12},{9,13},{10,... | collective-permute-start | bytes 884744 | tf_op jit(solution)/shard_map/ppermute | solution.py:786
  663.4 10.3 %collective-permute-start.9 = (bf16[96,1536]{1,0:T(8,128)(2,1)S(1)}, bf16[96,1536]{1,0:T(8,128)(2,1)S(1)}, u32[]{:S(2)}, u32[]{:S(2)}) collective-permute-start(bf16[96,1536]{1,0:T(8,128)(2,1)S(1)} %bitcast.392), channel_id=1, source_target_pairs={{0,4},{1,5},{2,6},{3,7},{4,0},{5,1},{6,2},{7,3},{8,12},{9,13},{10,... | collective-permute-start | bytes 884744 | tf_op jit(solution)/shard_map/ppermute | solution.py:786
  670.5 26.3 %collective-permute-start.53 = (bf16[384,768]{1,0:T(8,128)(2,1)S(1)}, bf16[384,768]{1,0:T(8,128)(2,1)S(1)}, u32[]{:S(2)}, u32[]{:S(2)}) collective-permute-start(bf16[384,768]{1,0:T(8,128)(2,1)S(1)} %bitcast.361), channel_id=1, source_target_pairs={{0,4},{1,5},{2,6},{3,7},{4,0},{5,1},{6,2},{7,3},{8,12},{9,13},{10,... | collective-permute-start | bytes 1769480 | tf_op jit(solution)/shard_map/ppermute | solution.py:786
  673.8 21.1 %collective-permute-start.37 = (bf16[192,1536]{1,0:T(8,128)(2,1)S(1)}, bf16[192,1536]{1,0:T(8,128)(2,1)S(1)}, u32[]{:S(2)}, u32[]{:S(2)}) collective-permute-start(bf16[192,1536]{1,0:T(8,128)(2,1)S(1)} %bitcast.356), channel_id=1, source_target_pairs={{0,4},{1,5},{2,6},{3,7},{4,0},{5,1},{6,2},{7,3},{8,12},{9,13},{10,... | collective-permute-start | bytes 1769480 | tf_op jit(solution)/shard_map/ppermute | solution.py:786
  674.6 21.8 %collective-permute-start.30 = (bf16[192,1536]{1,0:T(8,128)(2,1)S(1)}, bf16[192,1536]{1,0:T(8,128)(2,1)S(1)}, u32[]{:S(2)}, u32[]{:S(2)}) collective-permute-start(bf16[192,1536]{1,0:T(8,128)(2,1)S(1)} %bitcast.358), channel_id=1, source_target_pairs={{0,2},{1,3},{2,0},{3,1},{4,6},{5,7},{6,4},{7,5},{8,10},{9,11},{10,... | collective-permute-start | bytes 1769480 | tf_op jit(solution)/shard_map/ppermute | solution.py:786
  694.8 9.9 %collective-permute-start.46 = (bf16[384,768]{1,0:T(8,128)(2,1)S(1)}, bf16[384,768]{1,0:T(8,128)(2,1)S(1)}, u32[]{:S(2)}, u32[]{:S(2)}) collective-permute-start(bf16[384,768]{1,0:T(8,128)(2,1)S(1)} %bitcast.364), channel_id=1, source_target_pairs={{0,2},{1,3},{2,0},{3,1},{4,6},{5,7},{6,4},{7,5},{8,10},{9,11},{10,... | collective-permute-start | bytes 1769480 | tf_op jit(solution)/shard_map/ppermute | solution.py:786
  696.4 9.9 %collective-permute-start.17 = (bf16[192,1536]{1,0:T(8,128)(2,1)S(1)}, bf16[192,1536]{1,0:T(8,128)(2,1)S(1)}, u32[]{:S(2)}, u32[]{:S(2)}) collective-permute-start(bf16[192,1536]{1,0:T(8,128)(2,1)S(1)} %bitcast.360), channel_id=1, source_target_pairs={{0,4},{1,5},{2,6},{3,7},{4,0},{5,1},{6,2},{7,3},{8,12},{9,13},{10,... | collective-permute-start | bytes 1769480 | tf_op jit(solution)/shard_map/ppermute | solution.py:786
  696.8 14.3 %collective-permute-start.10 = (bf16[192,1536]{1,0:T(8,128)(2,1)S(1)}, bf16[192,1536]{1,0:T(8,128)(2,1)S(1)}, u32[]{:S(2)}, u32[]{:S(2)}) collective-permute-start(bf16[192,1536]{1,0:T(8,128)(2,1)S(1)} %bitcast.366), channel_id=1, source_target_pairs={{0,2},{1,3},{2,0},{3,1},{4,6},{5,7},{6,4},{7,5},{8,10},{9,11},{10,... | collective-permute-start | bytes 1769480 | tf_op jit(solution)/shard_map/ppermute | solution.py:786
  706.3 11.5 %collective-permute-start.54 = (bf16[768,768]{1,0:T(8,128)(2,1)S(1)}, bf16[768,768]{1,0:T(8,128)(2,1)}, u32[]{:S(2)}, u32[]{:S(2)}) collective-permute-start(bf16[768,768]{1,0:T(8,128)(2,1)S(1)} %bitcast.347), channel_id=1, source_target_pairs={{0,1},{1,0},{2,3},{3,2},{4,5},{5,4},{6,7},{7,6},{8,9},{9,8},{10,11... | collective-permute-start | bytes 3538952 | tf_op jit(solution)/shard_map/ppermute | solution.py:786
  711.0 13.2 %collective-permute-start.39 = (bf16[384,1536]{1,0:T(8,128)(2,1)S(1)}, bf16[384,1536]{1,0:T(8,128)(2,1)}, u32[]{:S(2)}, u32[]{:S(2)}) collective-permute-start(bf16[384,1536]{1,0:T(8,128)(2,1)S(1)} %bitcast.349), channel_id=1, source_target_pairs={{0,1},{1,0},{2,3},{3,2},{4,5},{5,4},{6,7},{7,6},{8,9},{9,8},{10,11... | collective-permute-start | bytes 3538952 | tf_op jit(solution)/shard_map/ppermute | solution.py:786
  711.1 13.1 %collective-permute-start.38 = (bf16[384,1536]{1,0:T(8,128)(2,1)S(1)}, bf16[384,1536]{1,0:T(8,128)(2,1)}, u32[]{:S(2)}, u32[]{:S(2)}) collective-permute-start(bf16[384,1536]{1,0:T(8,128)(2,1)S(1)} %bitcast.351), channel_id=1, source_target_pairs={{0,1},{1,0},{2,3},{3,2},{4,5},{5,4},{6,7},{7,6},{8,9},{9,8},{10,11... | collective-permute-start | bytes 3538952 | tf_op jit(solution)/shard_map/ppermute | solution.py:786
  711.7 19.0 %collective-permute-start.19 = (bf16[384,1536]{1,0:T(8,128)(2,1)S(1)}, bf16[384,1536]{1,0:T(8,128)(2,1)S(1)}, u32[]{:S(2)}, u32[]{:S(2)}) collective-permute-start(bf16[384,1536]{1,0:T(8,128)(2,1)S(1)} %bitcast.343), channel_id=1, source_target_pairs={{0,1},{1,0},{2,3},{3,2},{4,5},{5,4},{6,7},{7,6},{8,9},{9,8},{10,11... | collective-permute-start | bytes 3538952 | tf_op jit(solution)/shard_map/ppermute | solution.py:786
  712.9 17.8 %collective-permute-start.18 = (bf16[384,1536]{1,0:T(8,128)(2,1)S(1)}, bf16[384,1536]{1,0:T(8,128)(2,1)S(1)}, u32[]{:S(2)}, u32[]{:S(2)}) collective-permute-start(bf16[384,1536]{1,0:T(8,128)(2,1)S(1)} %bitcast.345), channel_id=1, source_target_pairs={{0,1},{1,0},{2,3},{3,2},{4,5},{5,4},{6,7},{7,6},{8,9},{9,8},{10,11... | collective-permute-start | bytes 3538952 | tf_op jit(solution)/shard_map/ppermute | solution.py:786
  (39 other events, 343.8 us)

commit v4 on v3

v4 whole, which is shorter than its diff:
```python
import functools
import jax
import jax.numpy as jnp
from jax import lax
from jax.experimental import pallas as pl
from jax.experimental.pallas import tpu as pltpu
from jax.sharding import PartitionSpec as P

HEAD_DIM = 64
QLEN = 32
NQ = 4
NP = 4
PSLOTS = 512
LAYER_EPSILON = 1e-12
UNIT_EPSILON = 1e-06
SMOOTHING = 0.05
LOGIT_SCALE = 4.0
ROOT_HALF = 0.7071067811865476
NORMAL_PEAK = 0.3989422804014327
BF = jnp.bfloat16
F32 = jnp.float32
QROWS = NQ * QLEN
SLAB = 256
FFBLOCK = 768
VMEM_LIMIT = 56 * 1024 * 1024
NEG = -1e30
FLOPS_FFN = 12_000_000_000
FLOPS_ATTN = 20_000_000_000


def dot_nn(a, b):
    return jnp.dot(a, b, preferred_element_type=F32)


def dot_nt(a, b):
    return lax.dot_general(a, b, (((1,), (1,)), ((), ())), preferred_element_type=F32)


def dot_tn(a, b):
    return lax.dot_general(a, b, (((0,), (0,)), ((), ())), preferred_element_type=F32)


def gelu_pair(u):
    phi = 0.5 + 0.5 * lax.erf(u * ROOT_HALF)
    return u * phi, phi + NORMAL_PEAK * u * jnp.exp(-0.5 * u * u)


def norm_rows(resid):
    centre = resid - jnp.mean(resid, axis=1, keepdims=True)
    inv = lax.rsqrt(jnp.mean(centre * centre, axis=1, keepdims=True) + LAYER_EPSILON)
    return centre * inv, inv


def ends_of(info, micro):
    base = 1 + micro * NP
    ends = []
    total = jnp.int32(0)
    for j in range(NP):
        total = total + info[base + j]
        ends.append(total)
    return ends


def passage_of(place, ends):
    out = jnp.zeros(place.shape, jnp.int32)
    for end in ends:
        out = out + jnp.where(place >= end, 1, 0)
    return out


def when_live(info, section, body):
    pl.when(info[0] == section)(body)


def slot_of(info, section, micro, spare):
    return jnp.where(info[0] == section, micro, spare)


def step_of(info, section, step):
    return jnp.where(info[0] == section, step, 0)


def fill_codes(info, micro, query_code, key_code):
    rows = query_code.shape[0]
    ends = [QROWS + end for end in ends_of(info, micro)]
    place = lax.broadcasted_iota(jnp.int32, (rows, 1), 0)
    segment = jnp.where(place < QROWS, place // QLEN, NQ + passage_of(place, ends))
    lane = lax.broadcasted_iota(jnp.int32, (1, 128), 1) % HEAD_DIM
    query_code[...] = jnp.where(segment == lane, 1.0, 0.0).astype(BF)
    key_code[...] = jnp.where((segment == lane) | (lane > NQ + NP), 0.0, NEG).astype(BF)


def usable_rows(info, micro, rows):
    ends = ends_of(info, micro)
    place = lax.broadcasted_iota(jnp.int32, (rows, 1), 0)
    return (place < QROWS + ends[-1]).astype(F32)


def head_lanes(value, h, others):
    lane = lax.broadcasted_iota(jnp.int32, (1, 128), 1) // HEAD_DIM
    return jnp.where(lane == h, value, others)


def live_only(body, section, micro):
    def kernel(info, *refs):
        when_live(info, section, lambda: body(micro, info, *refs))

    return kernel


def attn_fwd_live(micro, info, hid, wq, wk, wv, bq, bv, wm, bm, gain, shift, *rest):
    x_out, joined_out, lse_out, ctx_out, hid_out, n_out, inv_out, sq_out, acc, qcode, kcode, otr, vtr = rest[-13:]
    g = pl.program_id(0)
    rows = hid.shape[0]

    @pl.when(g == 0)
    def _():
        x_out[...] = hid[...]
        fill_codes(info, micro, qcode, kcode)
        acc[...] = jnp.zeros(acc.shape, F32)

    x = hid[...]
    qkv = dot_nn(x, jnp.concatenate([wq[...], wk[...], wv[...]], axis=1))
    q = (qkv[:, :SLAB] + bq[...]).astype(BF)
    joined_out[:, 0:SLAB] = q
    k = qkv[:, SLAB : 2 * SLAB].astype(BF)
    joined_out[:, SLAB : 2 * SLAB] = k
    v = (qkv[:, 2 * SLAB :] + bv[...]).astype(BF)
    joined_out[:, 2 * SLAB : 3 * SLAB] = v
    vtr[...] = jnp.transpose(v)
    parts = (slice(0, QROWS), slice(QROWS, rows))
    for pair in range(SLAB // 128):
        cols = slice(pair * 128, pair * 128 + 128)
        qs = joined_out[:, cols] * BF(HEAD_DIM**-0.5)
        ks = joined_out[:, SLAB + pair * 128 : SLAB + pair * 128 + 128]
        for h in range(2):
            head = pair * 2 + h
            vh = slice(head * HEAD_DIM, head * HEAD_DIM + HEAD_DIM)
            qh = head_lanes(qs, h, qcode[...])
            kh = head_lanes(ks, h, kcode[...])
            for at in parts:
                st = dot_nt(kh[at], qh[at])
                top = jnp.max(st, axis=0, keepdims=True)
                p = jnp.exp(st - top)
                total = jnp.sum(p, axis=0, keepdims=True)
                lse_out[head : head + 1, at] = top + jnp.log(total)
                otr[vh, at] = dot_nn(vtr[vh, at], p.astype(BF)) * (1.0 / total)
    ctx = jnp.transpose(otr[...]).astype(BF)
    ctx_out[...] = ctx
    acc[...] += dot_nn(ctx, wm[...])

    @pl.when(g == pl.num_programs(0) - 1)
    def _():
        b1 = acc[...] + bm[...]
        x32 = hid[...].astype(F32)
        n, inv = norm_rows(x32 + b1)
        hid_out[...] = (n * gain[...] + shift[...]).astype(BF)
        n_out[...] = n.astype(BF)
        inv_out[...] = inv
        mask = usable_rows(info, micro, rows)
        sq_out[0:1, :] = jnp.sum(mask * x32 * x32, axis=0, keepdims=True)
        sq_out[1:2, :] = jnp.sum(mask * b1 * b1, axis=0, keepdims=True)


def attn_forward(phase, micros, info, source, weights, old):
    (wa, ba, wm, bm, gains, shifts) = weights
    section, micro = phase // micros, phase % micros
    width = source.shape[1]
    rows = source.shape[0] // micros if section == 0 else source.shape[0]
    place = micro if section == 0 else 0
    steps = width // SLAB
    slot = lambda i: slot_of(i, section, micro, micros)
    at = lambda g, i: step_of(i, section, g)
    one = lambda *shape: pl.BlockSpec(shape, lambda g, i: (0,) * len(shape))
    in_specs = [
        pl.BlockSpec((rows, width), lambda g, i: (place, 0)),
        pl.BlockSpec((width, SLAB), lambda g, i: (0, at(g, i))),
        pl.BlockSpec((width, SLAB), lambda g, i: (0, steps + at(g, i))),
        pl.BlockSpec((width, SLAB), lambda g, i: (0, 2 * steps + at(g, i))),
        pl.BlockSpec((1, SLAB), lambda g, i: (0, at(g, i))),
        pl.BlockSpec((1, SLAB), lambda g, i: (0, steps + at(g, i))),
        pl.BlockSpec((SLAB, width), lambda g, i: (at(g, i), 0)),
        one(1, width),
        one(1, width),
        one(1, width),
    ]
    args = [source, wa, wa, wa, ba, ba, wm, bm, gains[0:1], shifts[0:1]]
    slots = micros + 1
    rows_at = lambda shape, kind: ((slots,) + shape, kind, (None,) + shape, lambda g, i: (slot(i), 0, 0))
    shapes = [
        rows_at((rows, width), BF),
        ((slots, steps, rows, 3 * SLAB), BF, (None, None, rows, 3 * SLAB), lambda g, i: (slot(i), at(g, i), 0, 0)),
        ((slots, steps, 8, rows), F32, (None, None, 8, rows), lambda g, i: (slot(i), at(g, i), 0, 0)),
        ((slots, rows, width), BF, (None, rows, SLAB), lambda g, i: (slot(i), 0, at(g, i))),
        rows_at((rows, width), BF),
        rows_at((rows, width), BF),
        rows_at((rows, 1), F32),
        rows_at((8, width), F32),
    ]
    return call(
        live_only(attn_fwd_live, section, micro),
        steps, info, args, in_specs, shapes, old,
        [
            pltpu.VMEM((rows, width), F32),
            pltpu.VMEM((rows, 128), BF),
            pltpu.VMEM((rows, 128), BF),
            pltpu.VMEM((SLAB, rows), F32),
            pltpu.VMEM((SLAB, rows), BF),
        ],
        flops=FLOPS_ATTN,
    )


def call(body, steps, info, args, in_specs, shapes, old, scratch, flops):
    aliases = {}
    if old is not None:
        in_specs = in_specs + [pl.BlockSpec(memory_space=pl.ANY)] * len(old)
        aliases = {1 + len(args) + i: i for i in range(len(old))}
        args = args + list(old)
    return pl.pallas_call(
        body,
        out_shape=[jax.ShapeDtypeStruct(s[0], s[1]) for s in shapes],
        grid_spec=pltpu.PrefetchScalarGridSpec(
            num_scalar_prefetch=1,
            grid=(steps,),
            in_specs=in_specs,
            out_specs=[pl.BlockSpec(s[2], s[3]) for s in shapes],
            scratch_shapes=scratch,
        ),
        input_output_aliases=aliases,
        compiler_params=pltpu.CompilerParams(
            dimension_semantics=("arbitrary",), vmem_limit_bytes=VMEM_LIMIT
        ),
        cost_estimate=pl.CostEstimate(flops=flops, bytes_accessed=20_000_000, transcendentals=0),
    )(info, *args)


def ffn_fwd_live(micro, info, hid, we, be, wr, br, gain, shift, *rest):
    act_out, slope_out, out_all, n_out, inv_out, sq_out, send_out, acc = rest[-8:]
    j = pl.program_id(0)
    rows = hid.shape[0]

    @pl.when(j == 0)
    def _():
        acc[...] = jnp.zeros(acc.shape, F32)

    inner = dot_nn(hid[...], we[...]) + be[...]
    active, slope = gelu_pair(inner)
    active = active.astype(BF)
    act_out[...] = active
    slope_out[...] = slope.astype(BF)
    acc[...] += dot_nn(active, wr[...])

    @pl.when(j == pl.num_programs(0) - 1)
    def _():
        b2 = acc[...] + br[...]
        n, inv = norm_rows(hid[...].astype(F32) + b2)
        out = (n * gain[...] + shift[...]).astype(BF)
        out_all[...] = out
        send_out[...] = out
        n_out[...] = n.astype(BF)
        inv_out[...] = inv
        mask = usable_rows(info, micro, rows)
        sq_out[0:1, :] = jnp.sum(mask * b2 * b2, axis=0, keepdims=True)


def ffn_forward(phase, micros, info, hidden, weights, old):
    (we, be, wr, br, gains, shifts) = weights
    section, micro = phase // micros, phase % micros
    slots, rows, width = hidden.shape
    ff = we.shape[1]
    steps = ff // FFBLOCK
    slot = lambda i: slot_of(i, section, micro, micros)
    at = lambda g, i: step_of(i, section, g)
    one = lambda *shape: pl.BlockSpec(shape, lambda g, i: (0,) * len(shape))
    in_specs = [
        pl.BlockSpec((None, rows, width), lambda g, i: (slot(i), 0, 0)),
        pl.BlockSpec((width, FFBLOCK), lambda g, i: (0, at(g, i))),
        pl.BlockSpec((1, FFBLOCK), lambda g, i: (0, at(g, i))),
        pl.BlockSpec((FFBLOCK, width), lambda g, i: (at(g, i), 0)),
        one(1, width),
        one(1, width),
        one(1, width),
    ]
    args = [hidden, we, be, wr, br, gains[1:2], shifts[1:2]]
    rows_at = lambda shape, kind: ((slots,) + shape, kind, (None,) + shape, lambda g, i: (slot(i), 0, 0))
    wide = ((slots, rows, ff), BF, (None, rows, FFBLOCK), lambda g, i: (slot(i), 0, at(g, i)))
    shapes = [
        wide,
        wide,
        rows_at((rows, width), BF),
        rows_at((rows, width), BF),
        rows_at((rows, 1), F32),
        rows_at((8, width), F32),
        ((rows, width), BF, (rows, width), lambda g, i: (0, 0)),
    ]
    return call(
        live_only(ffn_fwd_live, section, micro),
        steps, info, args, in_specs, shapes, old,
        [pltpu.VMEM((rows, width), F32)],
        flops=FLOPS_FFN,
    )


def column_sum(value):
    return jnp.sum(value, axis=0, keepdims=True)


def norm_rows_back(grad_out, n, inv, gain):
    grad_unit = grad_out * gain
    mean_grad = jnp.mean(grad_unit, axis=1, keepdims=True)
    mean_along = jnp.mean(grad_unit * n, axis=1, keepdims=True)
    return inv * (grad_unit - mean_grad - n * mean_along)


def loss_parts(info, micro, micros, grad_scale, out_b, wc):
    ends = ends_of(info, micro)
    embedded = dot_nn(out_b, wc)
    inv_norm = lax.rsqrt(jnp.sum(embedded * embedded, axis=1, keepdims=True) + UNIT_EPSILON)
    unit = embedded * inv_norm
    unit_b = unit.astype(BF)
    queries, passages = unit_b[:QROWS], unit_b[QROWS:]
    scaled = dot_nt(queries, passages) / SMOOTHING
    owner = passage_of(lax.broadcasted_iota(jnp.int32, (1, PSLOTS), 1), ends)
    top = jnp.max(jnp.where(owner < NP, scaled, NEG), axis=1, keepdims=True)
    terms = jnp.exp(scaled - top)
    lane = lax.broadcasted_iota(jnp.int32, (1, 128), 1)
    totals = jnp.ones((QROWS, 128), F32)
    lengths = jnp.ones((1, 128), F32)
    for j in range(NP):
        total = jnp.sum(jnp.where(owner == j, terms, 0.0), axis=1, keepdims=True)
        totals = jnp.where(lane == j, total, totals)
        lengths = jnp.where(lane == j, info[1 + micro * NP + j].astype(F32), lengths)
    smooth = SMOOTHING * (jnp.log(totals) + top - jnp.log(lengths))
    grouped = jnp.sum(smooth.reshape(NQ, QLEN, 128), axis=1, keepdims=True)
    scores = LOGIT_SCALE * grouped
    scores = jnp.where(lane[None] < NP, scores, NEG)
    score_max = jnp.max(scores, axis=2, keepdims=True)
    score_exp = jnp.exp(scores - score_max)
    score_total = jnp.sum(score_exp, axis=2, keepdims=True)
    query = lax.broadcasted_iota(jnp.int32, (NQ, 1, 128), 0)
    chosen = jnp.zeros((NQ, 1, 128), jnp.int32)
    for i in range(NQ):
        chosen = jnp.where(query == i, info[1 + micros * NP + micro * NQ + i], chosen)
    onehot = (chosen == lane[None]).astype(F32)
    own_score = jnp.sum(jnp.where(chosen == lane[None], scores, 0.0), axis=2, keepdims=True)
    losses = jnp.log(score_total) + score_max - own_score
    loss = jnp.sum(losses, axis=0)
    grad_scores = (score_exp / score_total - onehot) * grad_scale
    grad_smooth = jnp.broadcast_to(LOGIT_SCALE * grad_scores, (NQ, QLEN, 128)).reshape(QROWS, 128)
    share = grad_smooth / totals
    weight = jnp.zeros((QROWS, PSLOTS), F32)
    for j in range(NP):
        weight = jnp.where(owner == j, share[:, j : j + 1], weight)
    grad_similar = jnp.where(owner < NP, terms * weight, 0.0).astype(BF)
    grad_unit = jnp.concatenate([dot_nn(grad_similar, passages), dot_tn(grad_similar, queries)])
    grad_embed = inv_norm * (grad_unit - unit * jnp.sum(grad_unit * unit, axis=1, keepdims=True))
    return loss, grad_embed.astype(BF)


def ffn_bwd_live(with_loss, micros, grad_scale, micro, info, *refs):
    if with_loss:
        out_all, wc = refs[:2]
    else:
        rec = refs[0]
    n2, inv2, gain2, slope, wr, we, n1, inv1, gain1 = refs[2 if with_loss else 1 :][:9]
    two_out, inner_out, one_out, emb_out, small_out, ff_out, resid_out, acc, resid = refs[-9:]
    j = pl.program_id(0)

    @pl.when(j == 0)
    def _():
        small_out[...] = jnp.zeros(small_out.shape, F32)
        if with_loss:
            loss, grad_embed = loss_parts(info, micro, micros, grad_scale, out_all[...], wc[...])
            emb_out[...] = grad_embed
            upstream = dot_nt(grad_embed, wc[...])
            small_out[6:7, 0:128] = jnp.broadcast_to(loss, (1, 128))
        else:
            upstream = rec[...].astype(F32)
        acc[...] = jnp.zeros(acc.shape, F32)
        n = n2[...].astype(F32)
        small_out[0:1, :] = column_sum(upstream * n)
        small_out[1:2, :] = column_sum(upstream)
        d_two = norm_rows_back(upstream, n, inv2[...], gain2[...])
        resid[...] = d_two
        d_two_b = d_two.astype(BF)
        two_out[...] = d_two_b
        small_out[2:3, :] = column_sum(d_two_b.astype(F32))

    d_act = dot_nt(two_out[...], wr[...])
    d_inner = (d_act * slope[...].astype(F32)).astype(BF)
    inner_out[...] = d_inner
    ff_out[0:1, :] = column_sum(d_inner.astype(F32))
    acc[...] += dot_nt(d_inner, we[...])

    @pl.when(j == pl.num_programs(0) - 1)
    def _():
        upstream = resid[...] + acc[...]
        n = n1[...].astype(F32)
        small_out[3:4, :] = column_sum(upstream * n)
        small_out[4:5, :] = column_sum(upstream)
        d_one = norm_rows_back(upstream, n, inv1[...], gain1[...])
        resid_out[...] = d_one
        d_one_b = d_one.astype(BF)
        one_out[...] = d_one_b
        small_out[5:6, :] = column_sum(d_one_b.astype(F32))


def ffn_backward(phase, micros, grad_scale, info, received, kept, weights, old):
    (out_all, n2, inv2, slope, n1, inv1) = kept
    (wc, gains, wr, we) = weights
    section, micro = 1 - phase // micros, phase % micros
    slots, rows, width = out_all.shape
    ff = we.shape[1]
    steps = ff // FFBLOCK
    slot = lambda i: slot_of(i, section, micro, micros)
    at = lambda g, i: step_of(i, section, g)
    one = lambda *shape: pl.BlockSpec(shape, lambda g, i: (0,) * len(shape))
    at_slot = lambda *shape: pl.BlockSpec((None,) + shape, lambda g, i: (slot(i), 0, 0))
    if section == 1:
        in_specs = [at_slot(rows, width), one(*wc.shape)]
        args = [out_all, wc]
    else:
        in_specs = [one(rows, width)]
        args = [received]
    in_specs += [
        at_slot(rows, width),
        at_slot(rows, 1),
        one(1, width),
        pl.BlockSpec((None, rows, FFBLOCK), lambda g, i: (slot(i), 0, at(g, i))),
        pl.BlockSpec((FFBLOCK, width), lambda g, i: (at(g, i), 0)),
        pl.BlockSpec((width, FFBLOCK), lambda g, i: (0, at(g, i))),
        at_slot(rows, width),
        at_slot(rows, 1),
        one(1, width),
    ]
    args += [n2, inv2, gains[1:2], slope, wr, we, n1, inv1, gains[0:1]]
    rows_at = lambda shape, kind: ((slots,) + shape, kind, (None,) + shape, lambda g, i: (slot(i), 0, 0))
    shapes = [
        rows_at((rows, width), BF),
        ((slots, rows, ff), BF, (None, rows, FFBLOCK), lambda g, i: (slot(i), 0, at(g, i))),
        rows_at((rows, width), BF),
        rows_at((rows, wc.shape[1]), BF),
        rows_at((8, width), F32),
        ((slots, 8, ff), F32, (None, 8, FFBLOCK), lambda g, i: (slot(i), 0, at(g, i))),
        ((rows, width), F32, (rows, width), lambda g, i: (0, 0)),
    ]
    return call(
        live_only(functools.partial(ffn_bwd_live, section == 1, micros, grad_scale), section, micro),
        steps, info, args, in_specs, shapes, old,
        [pltpu.VMEM((rows, width), F32), pltpu.VMEM((rows, width), F32)],
        flops=FLOPS_FFN,
    )


def attn_bwd_live(with_send, micro, info, one_b, joined, lse, ctx, wm, *rest):
    qcode, kcode, dctx, delta, ktr, dqtr = rest[-6:]
    if with_send:
        resid, wq, wk, wv = rest[:4]
        dq_out, dk_out, dv_out, sum_out, send_out, acc = rest[-12:-6]
    else:
        dq_out, dk_out, dv_out, sum_out = rest[-10:-6]
    g = pl.program_id(0)

    @pl.when(g == 0)
    def _():
        fill_codes(info, micro, qcode, kcode)
        if with_send:
            acc[...] = jnp.zeros(acc.shape, F32)

    dctx32 = dot_nt(one_b[...], wm[...])
    dctx[...] = dctx32.astype(BF)
    along = dctx[...].astype(F32) * ctx[...].astype(F32)
    pick = lax.broadcasted_iota(jnp.int32, (8, SLAB), 0) == lax.broadcasted_iota(jnp.int32, (8, SLAB), 1) // HEAD_DIM
    delta[...] = lax.dot_general(
        pick.astype(F32), along, (((1,), (1,)), ((), ())),
        precision=lax.Precision.HIGHEST, preferred_element_type=F32,
    )
    ktr[...] = jnp.transpose(joined[:, SLAB : 2 * SLAB])
    rows = one_b.shape[0]
    parts = (slice(0, QROWS), slice(QROWS, rows))
    for pair in range(SLAB // 128):
        lo = pair * 128
        qs = joined[:, lo : lo + 128] * BF(HEAD_DIM**-0.5)
        ks = joined[:, SLAB + lo : SLAB + lo + 128]
        vs = joined[:, 2 * SLAB + lo : 2 * SLAB + lo + 128]
        do = dctx[:, lo : lo + 128]
        qms = [head_lanes(qs, h, jnp.zeros_like(qs)) for h in range(2)]
        dms = [head_lanes(do, h, jnp.zeros_like(do)) for h in range(2)]
        ps, dss = ([], []), ([], [])
        for h in range(2):
            head = pair * 2 + h
            hh = slice(head * HEAD_DIM, head * HEAD_DIM + HEAD_DIM)
            qh = head_lanes(qs, h, qcode[...])
            kh = head_lanes(ks, h, kcode[...])
            for i, at in enumerate(parts):
                p = jnp.exp(dot_nt(kh[at], qh[at]) - lse[head : head + 1, at])
                dp = dot_nt(vs[at], dms[h][at])
                ds = (p * (dp - delta[head : head + 1, at])).astype(BF)
                ps[i].append(p.astype(BF))
                dss[i].append(ds)
                dqtr[hh, at] = dot_nn(ktr[hh, at], ds)
        for i, at in enumerate(parts):
            q_heads = jnp.concatenate([qm[at] for qm in qms])
            d_heads = jnp.concatenate([dm[at] for dm in dms])
            dk_out[at, lo : lo + 128] = dot_nn(jnp.concatenate(dss[i], axis=1), q_heads).astype(BF)
            dv_out[at, lo : lo + 128] = dot_nn(jnp.concatenate(ps[i], axis=1), d_heads).astype(BF)
    dq = (jnp.transpose(dqtr[...]) * HEAD_DIM**-0.5).astype(BF)
    dq_out[...] = dq
    dk = dk_out[...]
    dv = dv_out[...]
    sum_out[0:1, 0:SLAB] = column_sum(dq.astype(F32))
    sum_out[0:1, SLAB : 2 * SLAB] = column_sum(dv.astype(F32))
    if not with_send:
        return
    acc[...] += dot_nt(
        jnp.concatenate([dq, dk, dv], axis=1), jnp.concatenate([wq[...], wk[...], wv[...]], axis=1)
    )

    @pl.when(g == pl.num_programs(0) - 1)
    def _():
        send_out[...] = (resid[...] + acc[...]).astype(BF)


def attn_backward(phase, micros, info, resid, one_all, kept, weights, old, slabs=None):
    (joined, lse, ctx) = kept
    (wa, wm) = weights
    section, micro = 1 - phase // micros, phase % micros
    slots, rows, width = one_all.shape
    count = width // SLAB
    slabs = slabs or range(count)
    with_send = section == 1
    slot = lambda i: slot_of(i, section, micro, micros)
    at = lambda g, i: step_of(i, section, slabs[0] + g)
    in_specs = [
        pl.BlockSpec((None, rows, width), lambda g, i: (slot(i), 0, 0)),
        pl.BlockSpec((None, None, rows, 3 * SLAB), lambda g, i: (slot(i), at(g, i), 0, 0)),
        pl.BlockSpec((None, None, 8, rows), lambda g, i: (slot(i), at(g, i), 0, 0)),
        pl.BlockSpec((None, rows, SLAB), lambda g, i: (slot(i), 0, at(g, i))),
        pl.BlockSpec((SLAB, width), lambda g, i: (at(g, i), 0)),
    ]
    args = [one_all, joined, lse, ctx, wm]
    slab = ((slots, rows, width), BF, (None, rows, SLAB), lambda g, i: (slot(i), 0, at(g, i)))
    shapes = [
        slab,
        slab,
        slab,
        ((slots, count, 8, 2 * SLAB), F32, (None, None, 8, 2 * SLAB), lambda g, i: (slot(i), at(g, i), 0, 0)),
    ]
    scratch = [
        pltpu.VMEM((rows, 128), BF),
        pltpu.VMEM((rows, 128), BF),
        pltpu.VMEM((rows, SLAB), BF),
        pltpu.VMEM((8, rows), F32),
        pltpu.VMEM((SLAB, rows), BF),
        pltpu.VMEM((SLAB, rows), F32),
    ]
    if with_send:
        in_specs += [
            pl.BlockSpec((rows, width), lambda g, i: (0, 0)),
            pl.BlockSpec((width, SLAB), lambda g, i: (0, at(g, i))),
            pl.BlockSpec((width, SLAB), lambda g, i: (0, count + at(g, i))),
            pl.BlockSpec((width, SLAB), lambda g, i: (0, 2 * count + at(g, i))),
        ]
        args += [resid, wa, wa, wa]
        shapes += [((rows, width), BF, (rows, width), lambda g, i: (0, 0))]
        scratch = [pltpu.VMEM((rows, width), F32)] + scratch
    return call(
        live_only(functools.partial(attn_bwd_live, with_send), section, micro),
        len(slabs), info, args, in_specs, shapes, old, scratch,
        flops=FLOPS_ATTN * len(slabs) // count,
    )


def mesh_bits():
    place = lax.axis_index("dp")
    bits = []
    bit = 1
    while bit < lax.axis_size("dp"):
        bits.append((bit, (place // bit) % 2))
        bit *= 2
    return bits


def grad_rows_body(info, left, right, first_out, second_out):
    step = pl.program_id(0)
    value = dot_nn(jnp.transpose(left[...]), right[...]).astype(BF)

    @pl.when(step < 2)
    def _():
        first_out[...] = value

    @pl.when(step >= 2)
    def _():
        second_out[...] = value


def grad_rows(tokens, half, left, right):
    tall, wide = left.shape[1], right.shape[1]
    block = tall // 8
    out = jax.ShapeDtypeStruct((tall // 4, wide), BF)
    return pl.pallas_call(
        grad_rows_body,
        out_shape=[out, out],
        grid_spec=pltpu.PrefetchScalarGridSpec(
            num_scalar_prefetch=1,
            grid=(4,),
            in_specs=[
                pl.BlockSpec((tokens, block), lambda s, h: (0, h[0] * 4 + s)),
                pl.BlockSpec((tokens, wide), lambda s, h: (0, 0)),
            ],
            out_specs=[
                pl.BlockSpec((block, wide), lambda s, h: (jnp.minimum(s, 1), 0)),
                pl.BlockSpec((block, wide), lambda s, h: (jnp.maximum(s - 2, 0), 0)),
            ],
        ),
        compiler_params=pltpu.CompilerParams(vmem_limit_bytes=VMEM_LIMIT),
        cost_estimate=pl.CostEstimate(flops=tokens * tall * wide, bytes_accessed=8_000_000, transcendentals=0),
    )(half, left, right)


def grad_columns_body(info, left, right, first_out, second_out, turned):
    step = pl.program_id(0)

    @pl.when(step == 0)
    def _():
        turned[...] = jnp.transpose(left[...])

    value = dot_nn(turned[...], right[...]).astype(BF)

    @pl.when(step < 2)
    def _():
        first_out[...] = value

    @pl.when(step >= 2)
    def _():
        second_out[...] = value


def grad_columns(tokens, half, left, right):
    tall, wide = left.shape[1], right.shape[1]
    block = wide // 4
    out = jax.ShapeDtypeStruct((tall // 2, wide // 2), BF)
    return pl.pallas_call(
        grad_columns_body,
        out_shape=[out, out],
        grid_spec=pltpu.PrefetchScalarGridSpec(
            num_scalar_prefetch=1,
            grid=(4,),
            in_specs=[
                pl.BlockSpec((tokens, tall // 2), lambda s, h: (0, h[0])),
                pl.BlockSpec((tokens, block), lambda s, h: (0, s)),
            ],
            out_specs=[
                pl.BlockSpec((tall // 2, block), lambda s, h: (0, jnp.minimum(s, 1))),
                pl.BlockSpec((tall // 2, block), lambda s, h: (0, jnp.maximum(s - 2, 0))),
            ],
            scratch_shapes=[pltpu.VMEM((tall // 2, tokens), BF)],
        ),
        compiler_params=pltpu.CompilerParams(vmem_limit_bytes=VMEM_LIMIT),
        cost_estimate=pl.CostEstimate(flops=tokens * tall * wide, bytes_accessed=8_000_000, transcendentals=0),
    )(half, left, right)


def grad_rest_body(with_context, info, inputs, *refs):
    step = pl.program_id(0)
    sent, kept = refs[-2:]
    turned = jnp.transpose(inputs[...])
    parts = []
    if with_context:
        context, d_one = refs[:2]
        parts.append(dot_nn(jnp.transpose(context[...]), d_one[...]).astype(BF))
        refs = refs[2:]
    parts += [dot_nn(turned, right[...]).astype(BF) for right in refs[:-2]]
    for s, out in enumerate((sent, kept)):

        @pl.when(step == s)
        def _(out=out):
            at = 0
            for part in parts:
                out[:, at : at + part.shape[1]] = part
                at += part.shape[1]


def grad_rest(tokens, core, inputs, joined_grads, slabs, context=None, d_one=None):
    width = inputs.shape[1]
    side = pl.BlockSpec((tokens, width // 2), lambda s, h: (0, jnp.where(s == 0, 1 - h[0], h[0])))
    in_specs, args = [side], [inputs]
    columns = 0
    if context is not None:
        in_specs += [side, pl.BlockSpec((tokens, width), lambda s, h: (0, 0))]
        args += [context, d_one]
        columns += width
    for slab in slabs:
        in_specs += [pl.BlockSpec((tokens, SLAB), lambda s, h, slab=slab: (0, slab))] * 3
        args += joined_grads
        columns += 3 * SLAB
    out = jax.ShapeDtypeStruct((width // 2, columns), BF)
    whole = pl.BlockSpec(out.shape, lambda s, h: (0, 0))
    return pl.pallas_call(
        functools.partial(grad_rest_body, context is not None),
        out_shape=[out, out],
        grid_spec=pltpu.PrefetchScalarGridSpec(
            num_scalar_prefetch=1,
            grid=(2,),
            in_specs=in_specs,
            out_specs=[whole, whole],
        ),
        compiler_params=pltpu.CompilerParams(vmem_limit_bytes=VMEM_LIMIT),
        cost_estimate=pl.CostEstimate(flops=2 * tokens * columns * width, bytes_accessed=12_000_000, transcendentals=0),
    )(core, *args)


def widen_body(info, own_a, own_b, other_a, other_b, *outs):
    step = pl.program_id(0)
    for s, (a, b) in enumerate(((own_a, own_b), (other_a, other_b))):

        @pl.when(step == s)
        def _(a=a, b=b):
            parts = (a[...].astype(F32), b[...].astype(F32))
            if len(outs) == 2:
                width = outs[1].shape[1]
                outs[1][...] = parts[0][:, :width]
                slabs = [parts[0][:, width:]] + [
                    parts[1][:, at : at + 3 * SLAB] for at in range(0, parts[1].shape[1], 3 * SLAB)
                ]
                for g, slab in enumerate(slabs):
                    for kind in range(3):
                        at = kind * width + g * SLAB
                        outs[0][:, at : at + SLAB] = slab[:, kind * SLAB : kind * SLAB + SLAB]
            elif outs[0].shape[1] == parts[0].shape[1]:
                outs[0][: parts[0].shape[0]] = parts[0]
                outs[0][parts[0].shape[0] :] = parts[1]
            else:
                outs[0][:, : parts[0].shape[1]] = parts[0]
                outs[0][:, parts[0].shape[1] :] = parts[1]


def widened(core, own, other, out_shapes):
    small = own[0].shape
    piece_spec = pl.BlockSpec(small, lambda s, h: (0, 0))
    return pl.pallas_call(
        widen_body,
        out_shape=[jax.ShapeDtypeStruct(shape, F32) for shape in out_shapes],
        grid_spec=pltpu.PrefetchScalarGridSpec(
            num_scalar_prefetch=1,
            grid=(2,),
            in_specs=[piece_spec] * 4,
            out_specs=[
                pl.BlockSpec((shape[0] // 2, shape[1]), lambda s, h: (jnp.where(s == 0, h[0], 1 - h[0]), 0))
                for shape in out_shapes
            ],
        ),
        compiler_params=pltpu.CompilerParams(vmem_limit_bytes=VMEM_LIMIT),
        cost_estimate=pl.CostEstimate(flops=0, bytes_accessed=14_000_000, transcendentals=0),
    )(core, *own, *other)


def passed_along(array, axis, by):
    count = lax.axis_size(axis)
    pairs = [(i, i + by) for i in range(count) if 0 <= i + by < count]
    return lax.ppermute(array, axis, pairs)


def tied(array, *others):
    return lax.optimization_barrier((array, *others))[0]


def flatten_rows(leaf):
    return leaf.reshape(-1, leaf.shape[-1])


def swapped(array, bit, axis="dp"):
    count = lax.axis_size(axis)
    return lax.ppermute(array, axis, [(i, i ^ bit) for i in range(count)])


def piece(array, index):
    return lax.dynamic_index_in_dim(array, index, 0, keepdims=False)


def sum_low(kept, got):
    return (kept.astype(F32) + got.astype(F32)).astype(BF)


def halved(array, bit):
    step, mine = bit
    halves = array.reshape(2, array.shape[0] // 2, array.shape[1])
    got = swapped(piece(halves, 1 - mine), step)
    return sum_low(piece(halves, mine), got)


def doubled(array, bit):
    step, mine = bit
    got = swapped(array, step)
    both = jnp.zeros((2,) + array.shape, array.dtype)
    both = lax.dynamic_update_index_in_dim(both, array, mine, 0)
    both = lax.dynamic_update_index_in_dim(both, got, 1 - mine, 0)
    return flatten_rows(both)


class Piece:
    def __init__(self, sent, kept, bits, order):
        self.value = sum_low(kept, swapped(sent, 1))
        self.steps = [(halved, bits[place]) for place in order]
        self.steps += [(doubled, bits[place]) for place in reversed(order)]

    def advance(self):
        step, bit = self.steps.pop(0)
        self.value = step(self.value, bit)

    def finish(self):
        while self.steps:
            self.advance()
        return self.value, swapped(self.value, 1)


def advanced(*pieces):
    for one in pieces:
        one.advance()
    return tuple(one.value for one in pieces)


def all_summed(array, bits):
    for step, _ in bits:
        array = (array.astype(F32) + swapped(array, step).astype(F32)).astype(array.dtype)
    return array


def shards(
    hidden_in,
    attend_weight,
    attend_bias,
    mixing_weight,
    mixing_bias,
    norm_gain,
    norm_shift,
    expand_weight,
    expand_bias,
    reduce_weight,
    reduce_bias,
    colbert_weight,
    pass_lengths,
    positives,
):
    section_id = lax.axis_index("pipe")
    data_count = lax.axis_size("dp")
    micros = pass_lengths.shape[0]
    rows = hidden_in.shape[0] // micros
    width = hidden_in.shape[1]
    grad_scale = 1.0 / (data_count * micros * NQ)
    wa, wm, we, wr = attend_weight[0], mixing_weight[0], expand_weight[0], reduce_weight[0]
    gains, shifts = norm_gain[0], norm_shift[0]
    info = jnp.concatenate(
        [section_id.astype(jnp.int32)[None], pass_lengths.reshape(-1), positives.reshape(-1)]
    )
    bits = mesh_bits()
    core = bits[0][1].astype(jnp.int32)[None]
    along_x_first = list(range(1, len(bits)))
    along_z_first = [2, 1] + list(range(3, len(bits)))
    orders = (along_x_first, along_z_first)
    attn_weights = (wa, attend_bias, wm, mixing_bias, gains, shifts)
    ffn_weights = (we, expand_bias, wr, reduce_bias, gains, shifts)
    state = {"attn": None, "ffn": None, "attn_back": None, "ffn_back": None}
    arriving, returning = {}, {}

    def forward(phase, after=()):
        source = hidden_in if phase < micros else arriving[phase - micros]
        source = tied(source, *after)
        attn = attn_forward(phase, micros, info, source, attn_weights, state["attn"])
        old = state["ffn"]
        ffn = ffn_forward(phase, micros, info, attn[4], ffn_weights, old and old[:6])
        state["attn"], state["ffn"] = attn, ffn
        if phase < micros:
            arriving[phase] = passed_along(ffn[6], "pipe", 1)

    def backward_ffn(phase, after=()):
        attn, ffn, old = state["attn"], state["ffn"], state["ffn_back"]
        received = None if phase < micros else tied(returning[phase - micros], *after)
        state["ffn_back"] = ffn_backward(
            phase, micros, grad_scale, info, received,
            (ffn[2], ffn[3], ffn[4], ffn[1], attn[5], attn[6]),
            (colbert_weight, gains, wr, we), old and old[:6],
        )

    def backward_attn(phase, after=(), slabs=None):
        attn, old, ffn_back = state["attn"], state["attn_back"], state["ffn_back"]
        attn_back = attn_backward(
            phase, micros, tied(info, *after), ffn_back[6], ffn_back[2], (attn[1], attn[2], attn[3]), (wa, wm),
            old and old[:4], slabs,
        )
        state["attn_back"] = attn_back
        if phase < micros:
            returning[phase] = passed_along(attn_back[4], "pipe", -1)

    for phase in range(micros):
        forward(phase)
    done = ()
    for phase in range(micros):
        forward(micros + phase, done)
        backward_ffn(phase)
        backward_attn(phase)
        done = (state["attn_back"][3],)
    for phase in range(micros, 2 * micros - 1):
        backward_ffn(phase, done)
        backward_attn(phase)
        done = (state["attn_back"][3],)
    inputs, joined, lse, context, hidden, unit_one, inv_one, squares_one = state["attn"]
    active, slope, outputs, unit_two, inv_two, squares_two, _ = state["ffn"]
    embeds, losses = state["ffn_back"][3], state["ffn_back"][4]
    squares = jnp.stack(
        [
            jnp.sum(squares_one[:micros, 0], axis=1),
            jnp.sum(squares_one[:micros, 1], axis=1),
            jnp.sum(squares_two[:micros, 0], axis=1),
        ],
        axis=1,
    )
    colbert = dot_tn(flatten_rows(outputs[:micros]), flatten_rows(embeds[:micros])).astype(BF)
    facts = jnp.concatenate([squares, losses[:micros, 6, 0:1]], axis=1)
    backward_ffn(2 * micros - 1, done + (colbert, facts))
    colbert = jnp.where(section_id == 1, colbert, swapped(colbert, 1, "pipe"))
    colbert_sum = all_summed(colbert, bits).astype(F32)
    theirs = swapped(facts, 1, "pipe")
    first = jnp.where(section_id == 0, facts, theirs)
    second = jnp.where(section_id == 0, theirs, facts)
    ffn_back = state["ffn_back"]
    tokens = micros * rows
    last = 2 * micros - 1
    d_two, d_inner = flatten_rows(ffn_back[0]), flatten_rows(ffn_back[1])
    left = flatten_rows(active)
    sent, kept = (grad_rows(tokens, half, left, d_two) for half in (1 - core, core))
    pieces = [Piece(s, k, bits, order) for s, k, order in zip(sent, kept, orders)]
    of_reduce = tuple(one.value for one in pieces)
    left = flatten_rows(hidden)
    sent = grad_columns(tokens, 1 - core, left, d_inner)
    kept = grad_columns(tokens, tied(core, *of_reduce), left, d_inner)
    pieces += [Piece(s, k, bits, order) for s, k, order in zip(sent, kept, orders)]
    of_expand = tuple(one.value for one in pieces[2:])
    backward_attn(last, of_expand, (0,))
    x_rows, context_rows, one_rows = (flatten_rows(a) for a in (inputs, context, ffn_back[2]))
    joined_grads = [flatten_rows(a) for a in state["attn_back"][:3]]
    after = advanced(*pieces[:2])
    sent, kept = grad_rest(tokens, tied(core, *after), x_rows, joined_grads, (0,), context_rows, one_rows)
    after = advanced(*pieces[:4])
    backward_attn(last, after + (kept,), tuple(range(1, width // SLAB)))
    pieces += [Piece(sent, kept, bits, orders[0])]
    after = advanced(*pieces[:4])
    joined_grads = [flatten_rows(a) for a in state["attn_back"][:3]]
    sent, kept = grad_rest(tokens, tied(core, *after), x_rows, joined_grads, tuple(range(1, width // SLAB)))
    pieces += [Piece(sent, kept, bits, orders[1])]
    attn_back = state["attn_back"]
    small, small_ff = ffn_back[4], ffn_back[5]
    joined_sums = attn_back[3]
    small_sum = jnp.sum(small[:micros], axis=0)
    joined_sum = jnp.sum(joined_sums[:micros, :, 0], axis=0)
    attend_sum = jnp.concatenate(
        [joined_sum[:, :SLAB].reshape(-1), joined_sum[:, SLAB:].reshape(-1)]
    )
    vector = jnp.concatenate(
        [small_sum[:6], attend_sum.reshape(2, width), jnp.sum(small_ff[:micros, 0], axis=0).reshape(-1, width)]
    )
    vector = all_summed(vector, bits)
    halves = [one.finish() for one in pieces]
    own, other = [h[0] for h in halves], [h[1] for h in halves]
    [big_reduce] = widened(core, own[:2], other[:2], [wr.shape])
    [big_expand] = widened(core, own[2:4], other[2:4], [we.shape])
    big_attend, big_mixing = widened(core, own[4:], other[4:], [wa.shape, wm.shape])
    counted = (QROWS + jnp.sum(pass_lengths, axis=1)).astype(F32)
    stats = jnp.stack([first[:, :3], second[:, :3]], axis=1)
    stats = jnp.sqrt(stats / (counted[:, None, None] * width))
    return (
        big_attend[None],
        vector[6:8].reshape(1, -1),
        big_mixing[None],
        vector[5][None],
        jnp.stack([vector[3], vector[0]])[None],
        jnp.stack([vector[4], vector[1]])[None],
        big_expand[None],
        vector[8:].reshape(1, -1),
        big_reduce[None],
        vector[2][None],
        colbert_sum,
        second[:, 3] / NQ,
        stats,
    )


def solution(mesh):
    placed = (
        P("dp", None),
        P("pipe", None, None),
        P("pipe", None),
        P("pipe", None, None),
        P("pipe", None),
        P("pipe", None, None),
        P("pipe", None, None),
        P("pipe", None, None),
        P("pipe", None),
        P("pipe", None, None),
        P("pipe", None),
        P(),
        P("dp", None),
        P("dp", None),
    )
    return jax.shard_map(
        shards,
        mesh=mesh,
        in_specs=placed,
        out_specs=(
            P("pipe", None, None),
            P("pipe", None),
            P("pipe", None, None),
            P("pipe", None),
            P("pipe", None, None),
            P("pipe", None, None),
            P("pipe", None, None),
            P("pipe", None),
            P("pipe", None, None),
            P("pipe", None),
            P(),
            P("dp"),
            P("dp", None, None),
        ),
        check_vma=False,
    )
```

time: 748 us -> 626 us (0.84)
  Pallas kernels: 372 us -> 255 us
  waiting for transfers between devices: 273 us -> 206 us
  starting transfers between devices: 59.6 us -> 104 us
  other arithmetic: 10.8 us -> 28.6 us
    pallas_call x12 -> x17, Pallas kernels: 306 us -> 190 us  [call(): pl.pallas_call(body, out_shape=[jax.ShapeDtypeStruct(s[0], s[1]) for s in...]
    ppermute x58, starting transfers between devices: 47.1 us -> 97.7 us  [swapped(): return lax.ppermute(array, axis, [(i, i ^ bit) for i in range(count)])]
    ppermute x58, waiting for transfers between devices: 202 us -> 168 us  [swapped(): return lax.ppermute(array, axis, [(i, i ^ bit) for i in range(count)])]
    ppermute x4, waiting for transfers between devices: 71.5 us -> 38.3 us  [passed_along(): return lax.ppermute(array, axis, pairs)]
  transfers between devices with their start and end apart: 62 -> 62, of which waited for: 29 -> 27; matrix products, arithmetic and copies ran while one was open for 2% -> 6% of each run, Pallas kernels for 19% -> 35%
where the time goes in v4:
time: 626 us; the launch traced here: 618 us
  Pallas kernels  255 us (41%)
  waiting for transfers between devices  206 us (33%)
  starting transfers between devices  104 us (17%)
  other arithmetic  28.6 us (5%)
  local copies, waits for them, and re-layouts  20.9 us (3%)
    pallas_call x17, Pallas kernels, call(): pl.pallas_call(body, out_shape=[jax.ShapeDtypeStruct(s[0], s[1]) for s in...  190 us
    ppermute x58, waiting for transfers between devices, swapped(): return lax.ppermute(array, axis, [(i, i ^ bit) for i in range(count)])  168 us
    ppermute x58, starting transfers between devices, swapped(): return lax.ppermute(array, axis, [(i, i ^ bit) for i in range(count)])  97.7 us
    ppermute x4, waiting for transfers between devices, passed_along(): return lax.ppermute(array, axis, pairs)  38.3 us
    pallas_call x3, Pallas kernels, widened(): pl.pallas_call(widen_body, out_shape=[jax.ShapeDtypeStruct(shape, F32) fo...  19.1 us
    pallas_call x2, Pallas kernels, grad_columns(): pl.pallas_call(grad_columns_body, out_shape=[out, out], grid_spec=pltpu.P...  16 us
    pallas_call x2, Pallas kernels, grad_rest(): pl.pallas_call(functools.partial(grad_rest_body, context is not None), ou...  15.5 us
    pallas_call x2, Pallas kernels, grad_rows(): pl.pallas_call(grad_rows_body, out_shape=[out, out], grid_spec=pltpu.Pref...  15 us
  transfers between devices with their start and end apart: 62, of which 27 were waited for; matrix products, arithmetic and copies ran while one was open for 6% of the time, Pallas kernels for 35%

profile of v4, /device:TPU:0, one launch (start us, length us, event | category | flops | bytes accessed | tf_op | source)
XLA Modules:
  0.0 618.2 jit_solution(535766480553466556)
XLA Ops:
  4.1 19.2 %shard_map.237 = (bf16[3,640,768]{2,1,0:T(8,128)(2,1)}, bf16[3,3,640,768]{3,2,1,0:T(8,128)(2,1)}, f32[3,3,8,640]{3,2,1,0:T(8,128)}, bf16[3,640,768]{2,1,0:T(8,12...) custom-call(s32[17]{0:T(128)} %pad_add_fusion.info, ...), custom_call_target="tpu_custom_call" | custom-call | flops 20000000000 | bytes 20000000 | tf_op jit(solution)/shard_map/pallas_call | solution.py:220
  23.3 15.3 %shard_map.239 = (bf16[3,640,3072]{2,1,0:T(8,128)(2,1)}, bf16[3,640,3072]{2,1,0:T(8,128)(2,1)}, bf16[3,640,768]{2,1,0:T(8,128)(2,1)}, bf16[3,640,768]{2,1,0:T(8,...) custom-call(s32[17]{0:T(128)} %pad_add_fusion.info, ...), custom_call_target="tpu_custom_call" | custom-call | flops 12000000000 | bytes 20000000 | tf_op jit(solution)/shard_map/pallas_call | solution.py:220
  40.3 19.2 %shard_map.238 = (bf16[3,640,768]{2,1,0:T(8,128)(2,1)}, bf16[3,3,640,768]{3,2,1,0:T(8,128)(2,1)}, f32[3,3,8,640]{3,2,1,0:T(8,128)}, bf16[3,640,768]{2,1,0:T(8,12...) custom-call(s32[17]{0:T(128)} %pad_add_fusion.info, ...), custom_call_target="tpu_custom_call", output_to_operand_aliasing={{0}: (11, {}), {1}: (12, {}), {2}: (13, {}), {3}: (14, {}),... | custom-call | flops 20000000000 | bytes 20000000 | tf_op jit(solution)/shard_map/pallas_call | solution.py:220
  59.6 15.3 %shard_map.240 = (bf16[3,640,3072]{2,1,0:T(8,128)(2,1)}, bf16[3,640,3072]{2,1,0:T(8,128)(2,1)}, bf16[3,640,768]{2,1,0:T(8,128)(2,1)}, bf16[3,640,768]{2,1,0:T(8,...) custom-call(s32[17]{0:T(128)} %pad_add_fusion.info, ...), custom_call_target="tpu_custom_call", output_to_operand_aliasing={{0}: (8, {}), {1}: (9, {}), {2}: (10, {}), {3}: (11, {}), {... | custom-call | flops 12000000000 | bytes 20000000 | tf_op jit(solution)/shard_map/pallas_call | solution.py:220
  78.5 5.1 shard_map.241
  83.6 5.1 shard_map.242
  88.6 6.6 %shard_map.243 = (bf16[3,640,768]{2,1,0:T(8,128)(2,1)}, bf16[3,640,3072]{2,1,0:T(8,128)(2,1)}, bf16[3,640,768]{2,1,0:T(8,128)(2,1)}, bf16[3,640,128]{2,1,0:T(8,1...) custom-call(s32[17]{0:T(128)} %pad_add_fusion.info, ...), custom_call_target="tpu_custom_call" | custom-call | flops 12000000000 | bytes 20000000 | tf_op jit(solution)/shard_map/pallas_call | solution.py:220
  95.2 4.9 shard_map.244
  101.5 5.3 shard_map.245
  106.8 5.1 shard_map.246
  111.8 6.8 %shard_map.247 = (bf16[3,640,768]{2,1,0:T(8,128)(2,1)}, bf16[3,640,3072]{2,1,0:T(8,128)(2,1)}, bf16[3,640,768]{2,1,0:T(8,128)(2,1)}, bf16[3,640,128]{2,1,0:T(8,1...) custom-call(s32[17]{0:T(128)} %pad_add_fusion.info, ...), custom_call_target="tpu_custom_call", output_to_operand_aliasing={{0}: (12, {}), {1}: (13, {}), {2}: (14, {}), {3}: (15, {}),... | custom-call | flops 12000000000 | bytes 20000000 | tf_op jit(solution)/shard_map/pallas_call | solution.py:220
  118.7 4.9 shard_map.248
  126.8 38.3 %collective-permute-done.3.refs_0_ = bf16[640,768]{1,0:T(8,128)(2,1)S(1)} collective-permute-done((bf16[640,768]{1,0:T(8,128)(2,1)}, bf16[640,768]{1,0:T(8,128)(2,1)S(1)}, u32[]{:S(2)}, u32[]{:S(2)}) %collective-permute-start.3) | collective-permute-done | bytes 983072 | tf_op jit(solution)/shard_map/ppermute | solution.py:762
  166.0 17.4 %shard_map.249 = (bf16[3,640,768]{2,1,0:T(8,128)(2,1)}, bf16[3,640,3072]{2,1,0:T(8,128)(2,1)}, bf16[3,640,768]{2,1,0:T(8,128)(2,1)}, bf16[3,640,128]{2,1,0:T(8,1...) custom-call(s32[17]{0:T(128)} %pad_add_fusion.info, ...), custom_call_target="tpu_custom_call", output_to_operand_aliasing={{0}: (11, {}), {1}: (12, {}), {2}: (13, {}), {3}: (14, {}),... | custom-call | flops 12000000000 | bytes 20000000 | tf_op jit(solution)/shard_map/pallas_call | solution.py:220
  184.9 47.1 %collective-permute-start.61 = (f32[2,4]{0,1:T(4,128)}, f32[2,4]{0,1:T(4,128)S(1)}, u32[]{:S(2)}, u32[]{:S(2)}) collective-permute-start(f32[2,4]{0,1:T(4,128)} %pad_maximum_fusion.2), channel_id=1, source_target_pairs={{0,16},{16,0},{1,17},{17,1},{2,18},{18,2},{3,19},{19,3},{4,20},{20... | collective-permute-start | bytes 104 | tf_op jit(solution)/shard_map/ppermute | solution.py:775
  233.7 19.1 %shard_map.250 = (bf16[3,640,768]{2,1,0:T(8,128)(2,1)}, bf16[3,640,768]{2,1,0:T(8,128)(2,1)}, bf16[3,640,768]{2,1,0:T(8,128)(2,1)}, f32[3,3,8,512]{3,2,1,0:T(8,128)}) custom-call(s32[17]{0:T(128)} %pad_add_fusion.info, ...), custom_call_target="tpu_custom_call", output_to_operand_aliasing={{0}: (6, {}), {1}: (7, {}), {2}: (8, {}), {3}: (9, {})} | custom-call | flops 20000000000 | bytes 20000000 | tf_op jit(solution)/shard_map/pallas_call | solution.py:220
  253.8 17.3 %shard_map.251 = (bf16[3,640,768]{2,1,0:T(8,128)(2,1)}, bf16[3,640,3072]{2,1,0:T(8,128)(2,1)}, bf16[3,640,768]{2,1,0:T(8,128)(2,1)}, bf16[3,640,128]{2,1,0:T(8,1...) custom-call(s32[17]{0:T(128)} %pad_add_fusion.info, ...), custom_call_target="tpu_custom_call", output_to_operand_aliasing={{0}: (11, {}), {1}: (12, {}), {2}: (13, {}), {3}: (14, {}),... | custom-call | flops 12000000000 | bytes 20000000 | tf_op jit(solution)/shard_map/pallas_call | solution.py:220
  271.2 7.5 %shard_map.253 = (bf16[768,768]{1,0:T(8,128)(2,1)}, bf16[768,768]{1,0:T(8,128)(2,1)}) custom-call(s32[1]{0:T(128)S(6)} %sub.19.info, bf16[1920,3072]{1,0:T(8,128)(2,1)} %bitcast.289, bf16[1920,768]{1,0:T(8,128)(2,1)} %bitcast.278), custom_call_target="tpu_custom_call" | custom-call | flops 3019898880 | bytes 8000000 | tf_op jit(solution)/shard_map/pallas_call | solution.py:602
  279.2 8.0 %shard_map.255 = (bf16[384,1536]{1,0:T(8,128)(2,1)}, bf16[384,1536]{1,0:T(8,128)(2,1)}) custom-call(s32[1]{0:T(128)S(6)} %sub.19.info, bf16[1920,768]{1,0:T(8,128)(2,1)} %bitcast.310, bf16[1920,3072]{1,0:T(8,128)(2,1)} %bitcast.275), custom_call_target="tpu_custom_call" | custom-call | flops 3019898880 | bytes 8000000 | tf_op jit(solution)/shard_map/pallas_call | solution.py:644
  287.2 7.5 %shard_map.252 = (bf16[768,768]{1,0:T(8,128)(2,1)}, bf16[768,768]{1,0:T(8,128)(2,1)}) custom-call(s32[1]{0:T(128)} %bitcast.info, bf16[1920,3072]{1,0:T(8,128)(2,1)} %bitcast.290, bf16[1920,768]{1,0:T(8,128)(2,1)} %bitcast.279), custom_call_target="tpu_custom_call" | custom-call | flops 3019898880 | bytes 8000000 | tf_op jit(solution)/shard_map/pallas_call | solution.py:602
  312.9 4.3 collective-permute-done.59
  324.5 8.0 %shard_map.254 = (bf16[384,1536]{1,0:T(8,128)(2,1)}, bf16[384,1536]{1,0:T(8,128)(2,1)}) custom-call(s32[1]{0:T(128)} %bitcast.info, bf16[1920,768]{1,0:T(8,128)(2,1)} %bitcast.311, bf16[1920,3072]{1,0:T(8,128)(2,1)} %bitcast.276), custom_call_target="tpu_custom_call" | custom-call | flops 3019898880 | bytes 8000000 | tf_op jit(solution)/shard_map/pallas_call | solution.py:644
  337.6 9.0 %shard_map.256 = (bf16[3,640,768]{2,1,0:T(8,128)(2,1)}, bf16[3,640,768]{2,1,0:T(8,128)(2,1)}, bf16[3,640,768]{2,1,0:T(8,128)(2,1)}, f32[3,3,8,512]{3,2,1,0:T(8,128)}) custom-call(s32[17]{0:T(128)} %pad_add_fusion.info, bf16[3,640,768]{2,1,0:T(8,128)(2,1)} %get-tuple-element.238.refs_0_, ...), custom_call_target="tpu_custom_call", output_to_operand_aliasing={{0}: (6, {}), {1}: (7, {}), {2}: (8, {}), {3}: (9, {})} | custom-call | flops 6666666496 | bytes 20000000 | tf_op jit(solution)/shard_map/pallas_call | solution.py:220
  358.2 7.8 %shard_map.257 = (bf16[384,1536]{1,0:T(8,128)(2,1)}, bf16[384,1536]{1,0:T(8,128)(2,1)}) custom-call(s32[1]{0:T(128)} %bitcast.info, bf16[1920,768]{1,0:T(8,128)(2,1)} %bitcast.308, bf16[1920,768]{1,0:T(8,128)(2,1)} %bitcast.307, bf16[1920,768]{1,0:T(8,128)(2,1)} %bitcast.277, bf16[1920,768]{1,0:T(8,128)(2,1)} %bitcast.280, bf16[1920,768]{1,0:T(8,128)(2,1)} %bitcast.283, ...), custom_call_target="tpu_custom_call" | custom-call | flops 3019898880 | bytes 12000000 | tf_op jit(solution)/shard_map/pallas_call | solution.py:700
  371.5 13.9 %shard_map.258 = (bf16[3,640,768]{2,1,0:T(8,128)(2,1)}, bf16[3,640,768]{2,1,0:T(8,128)(2,1)}, bf16[3,640,768]{2,1,0:T(8,128)(2,1)}, f32[3,3,8,512]{3,2,1,0:T(8,128)}) custom-call(s32[17]{0:T(128)} %pad_add_fusion.info, bf16[3,640,768]{2,1,0:T(8,128)(2,1)} %get-tuple-element.238.refs_0_, ...), custom_call_target="tpu_custom_call", output_to_operand_aliasing={{0}: (6, {}), {1}: (7, {}), {2}: (8, {}), {3}: (9, {})} | custom-call | flops 13333332992 | bytes 20000000 | tf_op jit(solution)/shard_map/pallas_call | solution.py:220
  387.8 4.0 collective-permute-done.35
  392.9 3.1 collective-permute-done.36
  404.0 4.8 collective-permute-done.18
  408.9 7.8 %collective-permute-done.38 = bf16[48,1536]{1,0:T(8,128)(2,1)S(1)} collective-permute-done((bf16[48,1536]{1,0:T(8,128)(2,1)S(1)}, bf16[48,1536]{1,0:T(8,128)(2,1)S(1)}, u32[]{:S(2)}, u32[]{:S(2)}) %collective-permute-start.38) | collective-permute-done | bytes 147488 | tf_op jit(solution)/shard_map/ppermute | solution.py:775
  416.8 7.7 %shard_map.259 = (bf16[384,1536]{1,0:T(8,128)(2,1)}, bf16[384,1536]{1,0:T(8,128)(2,1)}) custom-call(s32[1]{0:T(128)} %bitcast.info, bf16[1920,768]{1,0:T(8,128)(2,1)} %bitcast.309, bf16[1920,768]{1,0:T(8,128)(2,1)} %bitcast.281, bf16[1920,768]{1,0:T(8,128)(2,1)} %bitcast.284, bf16[1920,768]{1,0:T(8,128)(2,1)} %bitcast.287, bf16[1920,768]{1,0:T(8,128)(2,1)} %bitcast.282, ...), custom_call_target="tpu_custom_call" | custom-call | flops 3019898880 | bytes 12000000 | tf_op jit(solution)/shard_map/pallas_call | solution.py:700
  427.9 9.3 %collective-permute-done.48 = bf16[96,768]{1,0:T(8,128)(2,1)S(1)} collective-permute-done((bf16[96,768]{1,0:T(8,128)(2,1)S(1)}, bf16[96,768]{1,0:T(8,128)(2,1)S(1)}, u32[]{:S(2)}, u32[]{:S(2)}) %collective-permute-start.48) | collective-permute-done | bytes 147488 | tf_op jit(solution)/shard_map/ppermute | solution.py:775
  439.7 4.7 collective-permute-done.52
  447.5 3.6 collective-permute-done.44
  451.5 7.8 %collective-permute-done.40 = bf16[96,1536]{1,0:T(8,128)(2,1)S(1)} collective-permute-done((bf16[96,1536]{1,0:T(8,128)(2,1)S(1)}, bf16[96,1536]{1,0:T(8,128)(2,1)S(1)}, u32[]{:S(2)}, u32[]{:S(2)}) %collective-permute-start.40) | collective-permute-done | bytes 294944 | tf_op jit(solution)/shard_map/ppermute | solution.py:775
  461.9 21.1 %collective-permute-done.45 = bf16[192,1536]{1,0:T(8,128)(2,1)S(1)} collective-permute-done((bf16[192,1536]{1,0:T(8,128)(2,1)S(1)}, bf16[192,1536]{1,0:T(8,128)(2,1)S(1)}, u32[]{:S(2)}, u32[]{:S(2)}) %collective-permute-start.45) | collective-permute-done | bytes 589856 | tf_op jit(solution)/shard_map/ppermute | solution.py:775
  485.3 14.0 %collective-permute-done.41 = bf16[192,1536]{1,0:T(8,128)(2,1)S(1)} collective-permute-done((bf16[192,1536]{1,0:T(8,128)(2,1)S(1)}, bf16[192,1536]{1,0:T(8,128)(2,1)S(1)}, u32[]{:S(2)}, u32[]{:S(2)}) %collective-permute-start.41) | collective-permute-done | bytes 589856 | tf_op jit(solution)/shard_map/ppermute | solution.py:775
  499.7 12.3 %collective-permute-done.11 = bf16[192,1536]{1,0:T(8,128)(2,1)S(1)} collective-permute-done((bf16[192,1536]{1,0:T(8,128)(2,1)S(1)}, bf16[192,1536]{1,0:T(8,128)(2,1)S(1)}, u32[]{:S(2)}, u32[]{:S(2)}) %collective-permute-start.11) | collective-permute-done | bytes 589856 | tf_op jit(solution)/shard_map/ppermute | solution.py:775
  513.6 8.1 %collective-permute-done.12 = bf16[96,1536]{1,0:T(8,128)(2,1)S(1)} collective-permute-done((bf16[96,1536]{1,0:T(8,128)(2,1)S(1)}, bf16[96,1536]{1,0:T(8,128)(2,1)S(1)}, u32[]{:S(2)}, u32[]{:S(2)}) %collective-permute-start.12) | collective-permute-done | bytes 294944 | tf_op jit(solution)/shard_map/ppermute | solution.py:775
  524.1 13.7 %collective-permute-done.13 = bf16[48,1536]{1,0:T(8,128)(2,1)S(1)} collective-permute-done((bf16[48,1536]{1,0:T(8,128)(2,1)S(1)}, bf16[48,1536]{1,0:T(8,128)(2,1)S(1)}, u32[]{:S(2)}, u32[]{:S(2)}) %collective-permute-start.13) | collective-permute-done | bytes 147488 | tf_op jit(solution)/shard_map/ppermute | solution.py:775
  537.9 3.4 collective-permute-start.14
  541.9 5.7 collective-permute-done.14
  550.3 5.3 collective-permute-done.28
  558.6 3.3 collective-permute-done.29
  562.4 13.2 %collective-permute-done.30 = bf16[96,1536]{1,0:T(8,128)(2,1)S(1)} collective-permute-done((bf16[96,1536]{1,0:T(8,128)(2,1)S(1)}, bf16[96,1536]{1,0:T(8,128)(2,1)S(1)}, u32[]{:S(2)}, u32[]{:S(2)}) %collective-permute-start.30) | collective-permute-done | bytes 294944 | tf_op jit(solution)/shard_map/ppermute | solution.py:775
  578.1 10.2 %collective-permute-done.31 = bf16[192,1536]{1,0:T(8,128)(2,1)S(1)} collective-permute-done((bf16[192,1536]{1,0:T(8,128)(2,1)S(1)}, bf16[192,1536]{1,0:T(8,128)(2,1)S(1)}, u32[]{:S(2)}, u32[]{:S(2)}) %collective-permute-start.31) | collective-permute-done | bytes 589856 | tf_op jit(solution)/shard_map/ppermute | solution.py:775
  596.8 6.4 %shard_map.262 = f32[3072,768]{1,0:T(8,128)} custom-call(s32[1]{0:T(128)} %bitcast.info, bf16[768,768]{1,0:T(8,128)(2,1)} %bitcast.333, bf16[768,768]{1,0:T(8,128)(2,1)} %bitcast.331, bf16[768,768]{1,0:T(8,128)(2,1)} %collective-permute-done.54.other_a, bf16[768,768]{1,0:T(8,128)(2,1)} %copy-done.14), custom_call_target="tpu_custom_call" | custom-call | bytes 14000000 | tf_op jit(solution)/shard_map/pallas_call | solution.py:742
  603.2 6.4 %shard_map.261 = f32[768,3072]{1,0:T(8,128)} custom-call(s32[1]{0:T(128)} %bitcast.info, bf16[384,1536]{1,0:T(8,128)(2,1)} %bitcast.337, bf16[384,1536]{1,0:T(8,128)(2,1)} %bitcast.335, bf16[384,1536]{1,0:T(8,128)(2,1)} %collective-permute-done.46.other_a, bf16[384,1536]{1,0:T(8,128)(2,1)} %collective-permute-done.47.other_b), custom_call_target="tpu_custom_call" | custom-call | bytes 14000000 | tf_op jit(solution)/shard_map/pallas_call | solution.py:742
  611.7 6.3 %shard_map.260 = (f32[768,2304]{1,0:T(8,128)}, f32[768,768]{1,0:T(8,128)}) custom-call(s32[1]{0:T(128)} %bitcast.info, bf16[384,1536]{1,0:T(8,128)(2,1)} %bitcast.329, bf16[384,1536]{1,0:T(8,128)(2,1)} %bitcast.327, bf16[384,1536]{1,0:T(8,128)(2,1)} %copy-done.11, bf16[384,1536]{1,0:T(8,128)(2,1)} %copy-done.12), custom_call_target="tpu_custom_call" | custom-call | bytes 14000000 | tf_op jit(solution)/shard_map/pallas_call | solution.py:742
  (297 shorter events, 115.9 us)
Async XLA Ops:
  38.7 38.9 %collective-permute-start.1 = (bf16[640,768]{1,0:T(8,128)(2,1)}, bf16[640,768]{1,0:T(8,128)(2,1)S(1)}, u32[]{:S(2)}, u32[]{:S(2)}) collective-permute-start(bf16[640,768]{1,0:T(8,128)(2,1)} %get-tuple-element.156), channel_id=1, source_target_pairs={{0,16},{1,17},{2,18},{3,19},{4,20},{5,21},{6,22},{7,23},{8,24},{9,... | collective-permute-start | bytes 2949128 | tf_op jit(solution)/shard_map/ppermute | solution.py:762
  74.9 25.3 %collective-permute-start = (bf16[640,768]{1,0:T(8,128)(2,1)}, bf16[640,768]{1,0:T(8,128)(2,1)S(1)}, u32[]{:S(2)}, u32[]{:S(2)}) collective-permute-start(bf16[640,768]{1,0:T(8,128)(2,1)} %get-tuple-element.155), channel_id=1, source_target_pairs={{0,16},{1,17},{2,18},{3,19},{4,20},{5,21},{6,22},{7,23},{8,24},{9,... | collective-permute-start | bytes 2949128 | tf_op jit(solution)/shard_map/ppermute | solution.py:762
  100.2 64.9 %collective-permute-start.3 = (bf16[640,768]{1,0:T(8,128)(2,1)}, bf16[640,768]{1,0:T(8,128)(2,1)S(1)}, u32[]{:S(2)}, u32[]{:S(2)}) collective-permute-start(bf16[640,768]{1,0:T(8,128)(2,1)} %get-tuple-element.210), channel_id=1, source_target_pairs={{16,0},{17,1},{18,2},{19,3},{20,4},{21,5},{22,6},{23,7},{24,8},{25... | collective-permute-start | bytes 2949128 | tf_op jit(solution)/shard_map/ppermute | solution.py:762
  123.6 129.3 %collective-permute-start.2 = (bf16[640,768]{1,0:T(8,128)(2,1)}, bf16[640,768]{1,0:T(8,128)(2,1)S(1)}, u32[]{:S(2)}, u32[]{:S(2)}) collective-permute-start(bf16[640,768]{1,0:T(8,128)(2,1)} %get-tuple-element.209), channel_id=1, source_target_pairs={{16,0},{17,1},{18,2},{19,3},{20,4},{21,5},{22,6},{23,7},{24,8},{25... | collective-permute-start | bytes 2949128 | tf_op jit(solution)/shard_map/ppermute | solution.py:762
  184.9 115.8 %collective-permute-start.61 = (f32[2,4]{0,1:T(4,128)}, f32[2,4]{0,1:T(4,128)S(1)}, u32[]{:S(2)}, u32[]{:S(2)}) collective-permute-start(f32[2,4]{0,1:T(4,128)} %pad_maximum_fusion.2), channel_id=1, source_target_pairs={{0,16},{16,0},{1,17},{17,1},{2,18},{18,2},{3,19},{19,3},{4,20},{20... | collective-permute-start | bytes 104 | tf_op jit(solution)/shard_map/ppermute | solution.py:775
  233.6 61.1 %collective-permute-start.56 = (bf16[768,128]{1,0:T(8,128)(2,1)S(1)}, bf16[768,128]{1,0:T(8,128)(2,1)S(1)}, u32[]{:S(2)}, u32[]{:S(2)}) collective-permute-start(bf16[768,128]{1,0:T(8,128)(2,1)S(1)} %fusion.6), channel_id=1, source_target_pairs={{0,16},{16,0},{1,17},{17,1},{2,18},{18,2},{3,19},{19,3},{4,20},{20... | collective-permute-start | bytes 589832 | tf_op jit(solution)/shard_map/ppermute | solution.py:775
  278.7 41.9 %collective-permute-start.6 = (bf16[768,768]{1,0:T(8,128)(2,1)}, bf16[768,768]{1,0:T(8,128)(2,1)S(1)}, u32[]{:S(2)}, u32[]{:S(2)}) collective-permute-start(bf16[768,768]{1,0:T(8,128)(2,1)} %get-tuple-element.235), channel_id=1, source_target_pairs={{0,1},{1,0},{2,3},{3,2},{4,5},{5,4},{6,7},{7,6},{8,9},{9,8},{10,11... | collective-permute-start | bytes 3538952 | tf_op jit(solution)/shard_map/ppermute | solution.py:775
  278.7 43.9 %collective-permute-start.4 = (bf16[768,768]{1,0:T(8,128)(2,1)}, bf16[768,768]{1,0:T(8,128)(2,1)S(1)}, u32[]{:S(2)}, u32[]{:S(2)}) collective-permute-start(bf16[768,768]{1,0:T(8,128)(2,1)} %get-tuple-element.233), channel_id=1, source_target_pairs={{0,1},{1,0},{2,3},{3,2},{4,5},{5,4},{6,7},{7,6},{8,9},{9,8},{10,11... | collective-permute-start | bytes 3538952 | tf_op jit(solution)/shard_map/ppermute | solution.py:775
  287.2 45.3 %collective-permute-start.9 = (bf16[384,1536]{1,0:T(8,128)(2,1)}, bf16[384,1536]{1,0:T(8,128)(2,1)S(1)}, u32[]{:S(2)}, u32[]{:S(2)}) collective-permute-start(bf16[384,1536]{1,0:T(8,128)(2,1)} %get-tuple-element.244), channel_id=1, source_target_pairs={{0,1},{1,0},{2,3},{3,2},{4,5},{5,4},{6,7},{7,6},{8,9},{9,8},{10,11... | collective-permute-start | bytes 3538952 | tf_op jit(solution)/shard_map/ppermute | solution.py:775
  298.8 36.6 %collective-permute-start.8 = (bf16[384,1536]{1,0:T(8,128)(2,1)}, bf16[384,1536]{1,0:T(8,128)(2,1)}, u32[]{:S(2)}, u32[]{:S(2)}) collective-permute-start(bf16[384,1536]{1,0:T(8,128)(2,1)} %get-tuple-element.242), channel_id=1, source_target_pairs={{0,1},{1,0},{2,3},{3,2},{4,5},{5,4},{6,7},{7,6},{8,9},{9,8},{10,11... | collective-permute-start | bytes 3538952 | tf_op jit(solution)/shard_map/ppermute | solution.py:775
  317.9 270.4 %collective-permute-start.60 = (bf16[768,128]{1,0:T(8,128)(2,1)}, bf16[768,128]{1,0:T(8,128)(2,1)}, u32[]{:S(2)}, u32[]{:S(2)}) collective-permute-start(bf16[768,128]{1,0:T(8,128)(2,1)} %add_convert_fusion.7), channel_id=1, source_target_pairs={{0,8},{1,9},{2,10},{3,11},{4,12},{5,13},{6,14},{7,15},{8,0},{9,1},... | collective-permute-start | bytes 589832 | tf_op jit(solution)/shard_map/ppermute | solution.py:775
  320.9 25.6 %collective-permute-start.7 = (bf16[384,768]{1,0:T(8,128)(2,1)S(1)}, bf16[384,768]{1,0:T(8,128)(2,1)S(1)}, u32[]{:S(2)}, u32[]{:S(2)}) collective-permute-start(bf16[384,768]{1,0:T(8,128)(2,1)S(1)} %dynamic-slice_bitcast_fusion.4), channel_id=1, source_target_pairs={{0,4},{1,5},{2,6},{3,7},{4,0},{5,1},{6,2},{7,3},{8,12},{9,13},{10,... | collective-permute-start | bytes 1769480 | tf_op jit(solution)/shard_map/ppermute | solution.py:775
  322.9 25.4 %collective-permute-start.5 = (bf16[384,768]{1,0:T(8,128)(2,1)S(1)}, bf16[384,768]{1,0:T(8,128)(2,1)}, u32[]{:S(2)}, u32[]{:S(2)}) collective-permute-start(bf16[384,768]{1,0:T(8,128)(2,1)S(1)} %dynamic-slice_bitcast_fusion.5), channel_id=1, source_target_pairs={{0,2},{1,3},{2,0},{3,1},{4,6},{5,7},{6,4},{7,5},{8,10},{9,11},{10,... | collective-permute-start | bytes 1769480 | tf_op jit(solution)/shard_map/ppermute | solution.py:775
  334.2 17.6 %collective-permute-start.23 = (bf16[192,1536]{1,0:T(8,128)(2,1)S(1)}, bf16[192,1536]{1,0:T(8,128)(2,1)}, u32[]{:S(2)}, u32[]{:S(2)}) collective-permute-start(bf16[192,1536]{1,0:T(8,128)(2,1)S(1)} %dynamic-slice_bitcast_fusion.1), channel_id=1, source_target_pairs={{0,4},{1,5},{2,6},{3,7},{4,0},{5,1},{6,2},{7,3},{8,12},{9,13},{10,... | collective-permute-start | bytes 1769480 | tf_op jit(solution)/shard_map/ppermute | solution.py:775
  337.0 18.2 %collective-permute-start.21 = (bf16[192,1536]{1,0:T(8,128)(2,1)S(1)}, bf16[192,1536]{1,0:T(8,128)(2,1)}, u32[]{:S(2)}, u32[]{:S(2)}) collective-permute-start(bf16[192,1536]{1,0:T(8,128)(2,1)S(1)} %dynamic-slice_bitcast_fusion.2), channel_id=1, source_target_pairs={{0,2},{1,3},{2,0},{3,1},{4,6},{5,7},{6,4},{7,5},{8,10},{9,11},{10,... | collective-permute-start | bytes 1769480 | tf_op jit(solution)/shard_map/ppermute | solution.py:775
  346.8 19.2 %collective-permute-start.19 = (bf16[192,768]{1,0:T(8,128)(2,1)S(1)}, bf16[192,768]{1,0:T(8,128)(2,1)}, u32[]{:S(2)}, u32[]{:S(2)}) collective-permute-start(bf16[192,768]{1,0:T(8,128)(2,1)S(1)} %dynamic-slice_bitcast_fusion.9), channel_id=1, source_target_pairs={{0,2},{1,3},{2,0},{3,1},{4,6},{5,7},{6,4},{7,5},{8,10},{9,11},{10,... | collective-permute-start | bytes 884744 | tf_op jit(solution)/shard_map/ppermute | solution.py:775
  349.6 21.5 %collective-permute-start.17 = (bf16[192,768]{1,0:T(8,128)(2,1)S(1)}, bf16[192,768]{1,0:T(8,128)(2,1)S(1)}, u32[]{:S(2)}, u32[]{:S(2)}) collective-permute-start(bf16[192,768]{1,0:T(8,128)(2,1)S(1)} %dynamic-slice_bitcast_fusion.10), channel_id=1, source_target_pairs={{0,4},{1,5},{2,6},{3,7},{4,0},{5,1},{6,2},{7,3},{8,12},{9,13},{10,... | collective-permute-start | bytes 884744 | tf_op jit(solution)/shard_map/ppermute | solution.py:775
  353.0 14.7 %collective-permute-start.24 = (bf16[96,1536]{1,0:T(8,128)(2,1)S(1)}, bf16[96,1536]{1,0:T(8,128)(2,1)S(1)}, u32[]{:S(2)}, u32[]{:S(2)}) collective-permute-start(bf16[96,1536]{1,0:T(8,128)(2,1)S(1)} %dynamic-slice_bitcast_fusion.7), channel_id=1, source_target_pairs={{0,2},{1,3},{2,0},{3,1},{4,6},{5,7},{6,4},{7,5},{8,10},{9,11},{10,... | collective-permute-start | bytes 884744 | tf_op jit(solution)/shard_map/ppermute | solution.py:775
  357.1 29.3 %collective-permute-start.22 = (bf16[96,1536]{1,0:T(8,128)(2,1)}, bf16[96,1536]{1,0:T(8,128)(2,1)S(1)}, u32[]{:S(2)}, u32[]{:S(2)}) collective-permute-start(bf16[96,1536]{1,0:T(8,128)(2,1)} %dynamic-slice_bitcast_fusion.8), channel_id=1, source_target_pairs={{0,4},{1,5},{2,6},{3,7},{4,0},{5,1},{6,2},{7,3},{8,12},{9,13},{10,... | collective-permute-start | bytes 884744 | tf_op jit(solution)/shard_map/ppermute | solution.py:775
  366.0 93.5 %collective-permute-start.10 = (bf16[384,1536]{1,0:T(8,128)(2,1)}, bf16[384,1536]{1,0:T(8,128)(2,1)S(1)}, u32[]{:S(2)}, u32[]{:S(2)}) collective-permute-start(bf16[384,1536]{1,0:T(8,128)(2,1)} %get-tuple-element.253), channel_id=1, source_target_pairs={{0,1},{1,0},{2,3},{3,2},{4,5},{5,4},{6,7},{7,6},{8,9},{9,8},{10,11... | collective-permute-start | bytes 3538952 | tf_op jit(solution)/shard_map/ppermute | solution.py:775
  367.7 32.4 %collective-permute-start.20 = (bf16[96,768]{1,0:T(8,128)(2,1)}, bf16[96,768]{1,0:T(8,128)(2,1)}, u32[]{:S(2)}, u32[]{:S(2)}) collective-permute-start(bf16[96,768]{1,0:T(8,128)(2,1)} %dynamic-slice_bitcast_fusion.15), channel_id=1, source_target_pairs={{0,8},{1,9},{2,10},{3,11},{4,12},{5,13},{6,14},{7,15},{8,0},{9,1},... | collective-permute-start | bytes 442376 | tf_op jit(solution)/shard_map/ppermute | solution.py:775
  371.1 27.9 %collective-permute-start.42 = (bf16[48,1536]{1,0:T(8,128)(2,1)}, bf16[48,1536]{1,0:T(8,128)(2,1)}, u32[]{:S(2)}, u32[]{:S(2)}) collective-permute-start(bf16[48,1536]{1,0:T(8,128)(2,1)} %dynamic-slice_bitcast_fusion.12), channel_id=1, source_target_pairs={{0,8},{1,9},{2,10},{3,11},{4,12},{5,13},{6,14},{7,15},{8,0},{9,1},... | collective-permute-start | bytes 442376 | tf_op jit(solution)/shard_map/ppermute | solution.py:775
  396.0 12.8 %collective-permute-start.18 = (bf16[96,768]{1,0:T(8,128)(2,1)S(1)}, bf16[96,768]{1,0:T(8,128)(2,1)S(1)}, u32[]{:S(2)}, u32[]{:S(2)}) collective-permute-start(bf16[96,768]{1,0:T(8,128)(2,1)S(1)} %dynamic-slice_bitcast_fusion.16), channel_id=1, source_target_pairs={{0,8},{1,9},{2,10},{3,11},{4,12},{5,13},{6,14},{7,15},{8,0},{9,1},... | collective-permute-start | bytes 442376 | tf_op jit(solution)/shard_map/ppermute | solution.py:775
  399.0 17.7 %collective-permute-start.38 = (bf16[48,1536]{1,0:T(8,128)(2,1)S(1)}, bf16[48,1536]{1,0:T(8,128)(2,1)S(1)}, u32[]{:S(2)}, u32[]{:S(2)}) collective-permute-start(bf16[48,1536]{1,0:T(8,128)(2,1)S(1)} %dynamic-slice_bitcast_fusion.13), channel_id=1, source_target_pairs={{0,8},{1,9},{2,10},{3,11},{4,12},{5,13},{6,14},{7,15},{8,0},{9,1},... | collective-permute-start | bytes 442376 | tf_op jit(solution)/shard_map/ppermute | solution.py:775
  400.0 188.9 %collective-permute-start.37 = (f32[12,768]{1,0:T(8,128)S(1)}, f32[12,768]{1,0:T(8,128)}, u32[]{:S(2)}, u32[]{:S(2)}) collective-permute-start(f32[12,768]{1,0:T(8,128)S(1)} %add.253), channel_id=1, source_target_pairs={{0,8},{1,9},{2,10},{3,11},{4,12},{5,13},{6,14},{7,15},{8,0},{9,1},... | collective-permute-start | bytes 110600 | tf_op jit(solution)/shard_map/ppermute | solution.py:775
  408.8 18.8 %collective-permute-start.51 = (bf16[96,768]{1,0:T(8,128)(2,1)S(1)}, bf16[96,768]{1,0:T(8,128)(2,1)S(1)}, u32[]{:S(2)}, u32[]{:S(2)}) collective-permute-start(bf16[96,768]{1,0:T(8,128)(2,1)S(1)} %get-tuple-element.296), channel_id=1, source_target_pairs={{0,8},{1,9},{2,10},{3,11},{4,12},{5,13},{6,14},{7,15},{8,0},{9,1},... | collective-permute-start | bytes 442376 | tf_op jit(solution)/shard_map/ppermute | solution.py:775
  424.8 12.4 %collective-permute-start.48 = (bf16[96,768]{1,0:T(8,128)(2,1)S(1)}, bf16[96,768]{1,0:T(8,128)(2,1)S(1)}, u32[]{:S(2)}, u32[]{:S(2)}) collective-permute-start(bf16[96,768]{1,0:T(8,128)(2,1)S(1)} %get-tuple-element.298), channel_id=1, source_target_pairs={{0,8},{1,9},{2,10},{3,11},{4,12},{5,13},{6,14},{7,15},{8,0},{9,1},... | collective-permute-start | bytes 442376 | tf_op jit(solution)/shard_map/ppermute | solution.py:775
  427.6 11.8 %collective-permute-start.39 = (bf16[48,1536]{1,0:T(8,128)(2,1)S(1)}, bf16[48,1536]{1,0:T(8,128)(2,1)S(1)}, u32[]{:S(2)}, u32[]{:S(2)}) collective-permute-start(bf16[48,1536]{1,0:T(8,128)(2,1)S(1)} %get-tuple-element.302), channel_id=1, source_target_pairs={{0,8},{1,9},{2,10},{3,11},{4,12},{5,13},{6,14},{7,15},{8,0},{9,1},... | collective-permute-start | bytes 442376 | tf_op jit(solution)/shard_map/ppermute | solution.py:775
  447.5 64.8 %collective-permute-start.25 = (bf16[384,1536]{1,0:T(8,128)(2,1)S(1)}, bf16[384,1536]{1,0:T(8,128)(2,1)S(1)}, u32[]{:S(2)}, u32[]{:S(2)}) collective-permute-start(bf16[384,1536]{1,0:T(8,128)(2,1)S(1)} %copy-done.28), channel_id=1, source_target_pairs={{0,1},{1,0},{2,3},{3,2},{4,5},{5,4},{6,7},{7,6},{8,9},{9,8},{10,11... | collective-permute-start | bytes 3538952 | tf_op jit(solution)/shard_map/ppermute | solution.py:775
  459.3 24.1 %collective-permute-start.53 = (bf16[384,768]{1,0:T(8,128)(2,1)S(1)}, bf16[384,768]{1,0:T(8,128)(2,1)S(1)}, u32[]{:S(2)}, u32[]{:S(2)}) collective-permute-start(bf16[384,768]{1,0:T(8,128)(2,1)S(1)} %bitcast.345), channel_id=1, source_target_pairs={{0,4},{1,5},{2,6},{3,7},{4,0},{5,1},{6,2},{7,3},{8,12},{9,13},{10,... | collective-permute-start | bytes 1769480 | tf_op jit(solution)/shard_map/ppermute | solution.py:775
  459.5 23.6 %collective-permute-start.45 = (bf16[192,1536]{1,0:T(8,128)(2,1)S(1)}, bf16[192,1536]{1,0:T(8,128)(2,1)S(1)}, u32[]{:S(2)}, u32[]{:S(2)}) collective-permute-start(bf16[192,1536]{1,0:T(8,128)(2,1)S(1)} %bitcast.341), channel_id=1, source_target_pairs={{0,4},{1,5},{2,6},{3,7},{4,0},{5,1},{6,2},{7,3},{8,12},{9,13},{10,... | collective-permute-start | bytes 1769480 | tf_op jit(solution)/shard_map/ppermute | solution.py:775
  483.1 16.3 %collective-permute-start.41 = (bf16[192,1536]{1,0:T(8,128)(2,1)S(1)}, bf16[192,1536]{1,0:T(8,128)(2,1)S(1)}, u32[]{:S(2)}, u32[]{:S(2)}) collective-permute-start(bf16[192,1536]{1,0:T(8,128)(2,1)S(1)} %bitcast.343), channel_id=1, source_target_pairs={{0,2},{1,3},{2,0},{3,1},{4,6},{5,7},{6,4},{7,5},{8,10},{9,11},{10,... | collective-permute-start | bytes 1769480 | tf_op jit(solution)/shard_map/ppermute | solution.py:775
  483.4 28.6 %collective-permute-start.11 = (bf16[192,1536]{1,0:T(8,128)(2,1)S(1)}, bf16[192,1536]{1,0:T(8,128)(2,1)S(1)}, u32[]{:S(2)}, u32[]{:S(2)}) collective-permute-start(bf16[192,1536]{1,0:T(8,128)(2,1)S(1)} %dynamic-slice_bitcast_fusion.3), channel_id=1, source_target_pairs={{0,2},{1,3},{2,0},{3,1},{4,6},{5,7},{6,4},{7,5},{8,10},{9,11},{10,... | collective-permute-start | bytes 1769480 | tf_op jit(solution)/shard_map/ppermute | solution.py:775
  499.4 22.7 %collective-permute-start.50 = (bf16[384,768]{1,0:T(8,128)(2,1)S(1)}, bf16[384,768]{1,0:T(8,128)(2,1)S(1)}, u32[]{:S(2)}, u32[]{:S(2)}) collective-permute-start(bf16[384,768]{1,0:T(8,128)(2,1)S(1)} %bitcast.347), channel_id=1, source_target_pairs={{0,2},{1,3},{2,0},{3,1},{4,6},{5,7},{6,4},{7,5},{8,10},{9,11},{10,... | collective-permute-start | bytes 1769480 | tf_op jit(solution)/shard_map/ppermute | solution.py:775
  512.0 77.0 %collective-permute-start.55 = (bf16[768,768]{1,0:T(8,128)(2,1)S(1)}, bf16[768,768]{1,0:T(8,128)(2,1)S(1)}, u32[]{:S(2)}, u32[]{:S(2)}) collective-permute-start(bf16[768,768]{1,0:T(8,128)(2,1)S(1)} %bitcast.330), channel_id=1, source_target_pairs={{0,1},{1,0},{2,3},{3,2},{4,5},{5,4},{6,7},{7,6},{8,9},{9,8},{10,11... | collective-permute-start | bytes 3538952 | tf_op jit(solution)/shard_map/ppermute | solution.py:775
  512.2 9.5 %collective-permute-start.12 = (bf16[96,1536]{1,0:T(8,128)(2,1)S(1)}, bf16[96,1536]{1,0:T(8,128)(2,1)S(1)}, u32[]{:S(2)}, u32[]{:S(2)}) collective-permute-start(bf16[96,1536]{1,0:T(8,128)(2,1)S(1)} %dynamic-slice_bitcast_fusion.11), channel_id=1, source_target_pairs={{0,4},{1,5},{2,6},{3,7},{4,0},{5,1},{6,2},{7,3},{8,12},{9,13},{10,... | collective-permute-start | bytes 884744 | tf_op jit(solution)/shard_map/ppermute | solution.py:775
  521.7 19.7 %collective-permute-start.26 = (bf16[192,1536]{1,0:T(8,128)(2,1)S(1)}, bf16[192,1536]{1,0:T(8,128)(2,1)S(1)}, u32[]{:S(2)}, u32[]{:S(2)}) collective-permute-start(bf16[192,1536]{1,0:T(8,128)(2,1)S(1)} %dynamic-slice_bitcast_fusion), channel_id=1, source_target_pairs={{0,4},{1,5},{2,6},{3,7},{4,0},{5,1},{6,2},{7,3},{8,12},{9,13},{10,... | collective-permute-start | bytes 1769480 | tf_op jit(solution)/shard_map/ppermute | solution.py:775
  522.1 15.7 %collective-permute-start.13 = (bf16[48,1536]{1,0:T(8,128)(2,1)S(1)}, bf16[48,1536]{1,0:T(8,128)(2,1)S(1)}, u32[]{:S(2)}, u32[]{:S(2)}) collective-permute-start(bf16[48,1536]{1,0:T(8,128)(2,1)S(1)} %dynamic-slice_bitcast_fusion.17), channel_id=1, source_target_pairs={{0,8},{1,9},{2,10},{3,11},{4,12},{5,13},{6,14},{7,15},{8,0},{9,1},... | collective-permute-start | bytes 442376 | tf_op jit(solution)/shard_map/ppermute | solution.py:775
  537.9 9.7 %collective-permute-start.14 = (bf16[48,1536]{1,0:T(8,128)(2,1)S(1)}, bf16[48,1536]{1,0:T(8,128)(2,1)S(1)}, u32[]{:S(2)}, u32[]{:S(2)}) collective-permute-start(bf16[48,1536]{1,0:T(8,128)(2,1)S(1)} %get-tuple-element.306), channel_id=1, source_target_pairs={{0,8},{1,9},{2,10},{3,11},{4,12},{5,13},{6,14},{7,15},{8,0},{9,1},... | collective-permute-start | bytes 442376 | tf_op jit(solution)/shard_map/ppermute | solution.py:775
  547.6 10.6 %collective-permute-start.15 = (bf16[96,1536]{1,0:T(8,128)(2,1)S(1)}, bf16[96,1536]{1,0:T(8,128)(2,1)S(1)}, u32[]{:S(2)}, u32[]{:S(2)}) collective-permute-start(bf16[96,1536]{1,0:T(8,128)(2,1)S(1)} %bitcast.393), channel_id=1, source_target_pairs={{0,4},{1,5},{2,6},{3,7},{4,0},{5,1},{6,2},{7,3},{8,12},{9,13},{10,... | collective-permute-start | bytes 884744 | tf_op jit(solution)/shard_map/ppermute | solution.py:775
  558.3 19.6 %collective-permute-start.16 = (bf16[192,1536]{1,0:T(8,128)(2,1)S(1)}, bf16[192,1536]{1,0:T(8,128)(2,1)S(1)}, u32[]{:S(2)}, u32[]{:S(2)}) collective-permute-start(bf16[192,1536]{1,0:T(8,128)(2,1)S(1)} %bitcast.348), channel_id=1, source_target_pairs={{0,2},{1,3},{2,0},{3,1},{4,6},{5,7},{6,4},{7,5},{8,10},{9,11},{10,... | collective-permute-start | bytes 1769480 | tf_op jit(solution)/shard_map/ppermute | solution.py:775
  561.9 13.7 %collective-permute-start.30 = (bf16[96,1536]{1,0:T(8,128)(2,1)S(1)}, bf16[96,1536]{1,0:T(8,128)(2,1)S(1)}, u32[]{:S(2)}, u32[]{:S(2)}) collective-permute-start(bf16[96,1536]{1,0:T(8,128)(2,1)S(1)} %bitcast.383), channel_id=1, source_target_pairs={{0,2},{1,3},{2,0},{3,1},{4,6},{5,7},{6,4},{7,5},{8,10},{9,11},{10,... | collective-permute-start | bytes 884744 | tf_op jit(solution)/shard_map/ppermute | solution.py:775
  575.6 12.6 %collective-permute-start.31 = (bf16[192,1536]{1,0:T(8,128)(2,1)S(1)}, bf16[192,1536]{1,0:T(8,128)(2,1)S(1)}, u32[]{:S(2)}, u32[]{:S(2)}) collective-permute-start(bf16[192,1536]{1,0:T(8,128)(2,1)S(1)} %bitcast.338), channel_id=1, source_target_pairs={{0,4},{1,5},{2,6},{3,7},{4,0},{5,1},{6,2},{7,3},{8,12},{9,13},{10,... | collective-permute-start | bytes 1769480 | tf_op jit(solution)/shard_map/ppermute | solution.py:775
  577.9 18.9 %collective-permute-start.54 = (bf16[768,768]{1,0:T(8,128)(2,1)S(1)}, bf16[768,768]{1,0:T(8,128)(2,1)}, u32[]{:S(2)}, u32[]{:S(2)}) collective-permute-start(bf16[768,768]{1,0:T(8,128)(2,1)S(1)} %bitcast.332), channel_id=1, source_target_pairs={{0,1},{1,0},{2,3},{3,2},{4,5},{5,4},{6,7},{7,6},{8,9},{9,8},{10,11... | collective-permute-start | bytes 3538952 | tf_op jit(solution)/shard_map/ppermute | solution.py:775
  588.3 15.0 %collective-permute-start.47 = (bf16[384,1536]{1,0:T(8,128)(2,1)S(1)}, bf16[384,1536]{1,0:T(8,128)(2,1)}, u32[]{:S(2)}, u32[]{:S(2)}) collective-permute-start(bf16[384,1536]{1,0:T(8,128)(2,1)S(1)} %bitcast.334), channel_id=1, source_target_pairs={{0,1},{1,0},{2,3},{3,2},{4,5},{5,4},{6,7},{7,6},{8,9},{9,8},{10,11... | collective-permute-start | bytes 3538952 | tf_op jit(solution)/shard_map/ppermute | solution.py:775
  588.3 14.9 %collective-permute-start.46 = (bf16[384,1536]{1,0:T(8,128)(2,1)S(1)}, bf16[384,1536]{1,0:T(8,128)(2,1)}, u32[]{:S(2)}, u32[]{:S(2)}) collective-permute-start(bf16[384,1536]{1,0:T(8,128)(2,1)S(1)} %bitcast.336), channel_id=1, source_target_pairs={{0,1},{1,0},{2,3},{3,2},{4,5},{5,4},{6,7},{7,6},{8,9},{9,8},{10,11... | collective-permute-start | bytes 3538952 | tf_op jit(solution)/shard_map/ppermute | solution.py:775
  588.9 20.8 %collective-permute-start.32 = (bf16[384,1536]{1,0:T(8,128)(2,1)S(1)}, bf16[384,1536]{1,0:T(8,128)(2,1)S(1)}, u32[]{:S(2)}, u32[]{:S(2)}) collective-permute-start(bf16[384,1536]{1,0:T(8,128)(2,1)S(1)} %bitcast.328), channel_id=1, source_target_pairs={{0,1},{1,0},{2,3},{3,2},{4,5},{5,4},{6,7},{7,6},{8,9},{9,8},{10,11... | collective-permute-start | bytes 3538952 | tf_op jit(solution)/shard_map/ppermute | solution.py:775
  590.1 19.6 %collective-permute-start.33 = (bf16[384,1536]{1,0:T(8,128)(2,1)S(1)}, bf16[384,1536]{1,0:T(8,128)(2,1)S(1)}, u32[]{:S(2)}, u32[]{:S(2)}) collective-permute-start(bf16[384,1536]{1,0:T(8,128)(2,1)S(1)} %bitcast.326), channel_id=1, source_target_pairs={{0,1},{1,0},{2,3},{3,2},{4,5},{5,4},{6,7},{7,6},{8,9},{9,8},{10,11... | collective-permute-start | bytes 3538952 | tf_op jit(solution)/shard_map/ppermute | solution.py:775
  (45 other events, 803.9 us)

commit v5 on v4

--- a/solution.py
+++ b/solution.py
@@ -24,6 +24,8 @@
 FFBLOCK = 768
 VMEM_LIMIT = 56 * 1024 * 1024
 NEG = -1e30
+GRAD_STEPS = 2
+SMALL_VMEM = 26 * 1024 * 1024
 FLOPS_FFN = 12_000_000_000
 FLOPS_ATTN = 20_000_000_000
 
@@ -211,7 +213,7 @@
     )
 
 
-def call(body, steps, info, args, in_specs, shapes, old, scratch, flops):
+def call(body, steps, info, args, in_specs, shapes, old, scratch, flops, limit=VMEM_LIMIT):
     aliases = {}
     if old is not None:
         in_specs = in_specs + [pl.BlockSpec(memory_space=pl.ANY)] * len(old)
@@ -229,9 +231,9 @@
         ),
         input_output_aliases=aliases,
         compiler_params=pltpu.CompilerParams(
-            dimension_semantics=("arbitrary",), vmem_limit_bytes=VMEM_LIMIT
+            dimension_semantics=("arbitrary",), vmem_limit_bytes=limit
         ),
-        cost_estimate=pl.CostEstimate(flops=flops, bytes_accessed=20_000_000, transcendentals=0),
+        cost_estimate=pl.CostEstimate(flops=flops, bytes_accessed=min(20_000_000, flops // 600), transcendentals=0),
     )(info, *args)
 
 
@@ -568,7 +570,8 @@
     return call(
         live_only(functools.partial(attn_bwd_live, with_send), section, micro),
         len(slabs), info, args, in_specs, shapes, old, scratch,
-        flops=FLOPS_ATTN * len(slabs) // count,
+        flops=FLOPS_ATTN * len(slabs) // count // (1 if with_send else 32),
+        limit=VMEM_LIMIT if with_send else SMALL_VMEM,
     )
 
 
@@ -582,133 +585,96 @@
     return bits
 
 
-def grad_rows_body(info, left, right, first_out, second_out):
-    step = pl.program_id(0)
-    value = dot_nn(jnp.transpose(left[...]), right[...]).astype(BF)
-
-    @pl.when(step < 2)
-    def _():
-        first_out[...] = value
-
-    @pl.when(step >= 2)
-    def _():
-        second_out[...] = value
-
-
-def grad_rows(tokens, half, left, right):
-    tall, wide = left.shape[1], right.shape[1]
-    block = tall // 8
-    out = jax.ShapeDtypeStruct((tall // 4, wide), BF)
+def grad_call(body, steps, core, in_specs, args, out_shape, out_specs, flops, limit=SMALL_VMEM):
     return pl.pallas_call(
-        grad_rows_body,
-        out_shape=[out, out],
+        body,
+        out_shape=out_shape,
         grid_spec=pltpu.PrefetchScalarGridSpec(
             num_scalar_prefetch=1,
-            grid=(4,),
-            in_specs=[
-                pl.BlockSpec((tokens, block), lambda s, h: (0, h[0] * 4 + s)),
-                pl.BlockSpec((tokens, wide), lambda s, h: (0, 0)),
-            ],
-            out_specs=[
-                pl.BlockSpec((block, wide), lambda s, h: (jnp.minimum(s, 1), 0)),
-                pl.BlockSpec((block, wide), lambda s, h: (jnp.maximum(s - 2, 0), 0)),
-            ],
+            grid=(steps,),
+            in_specs=in_specs,
+            out_specs=out_specs,
         ),
-        compiler_params=pltpu.CompilerParams(vmem_limit_bytes=VMEM_LIMIT),
-        cost_estimate=pl.CostEstimate(flops=tokens * tall * wide, bytes_accessed=8_000_000, transcendentals=0),
-    )(half, left, right)
-
-
-def grad_columns_body(info, left, right, first_out, second_out, turned):
-    step = pl.program_id(0)
-
-    @pl.when(step == 0)
-    def _():
-        turned[...] = jnp.transpose(left[...])
-
-    value = dot_nn(turned[...], right[...]).astype(BF)
-
-    @pl.when(step < 2)
-    def _():
-        first_out[...] = value
-
-    @pl.when(step >= 2)
-    def _():
-        second_out[...] = value
-
-
-def grad_columns(tokens, half, left, right):
-    tall, wide = left.shape[1], right.shape[1]
-    block = wide // 4
-    out = jax.ShapeDtypeStruct((tall // 2, wide // 2), BF)
-    return pl.pallas_call(
-        grad_columns_body,
-        out_shape=[out, out],
-        grid_spec=pltpu.PrefetchScalarGridSpec(
-            num_scalar_prefetch=1,
-            grid=(4,),
-            in_specs=[
-                pl.BlockSpec((tokens, tall // 2), lambda s, h: (0, h[0])),
-                pl.BlockSpec((tokens, block), lambda s, h: (0, s)),
-            ],
-            out_specs=[
-                pl.BlockSpec((tall // 2, block), lambda s, h: (0, jnp.minimum(s, 1))),
-                pl.BlockSpec((tall // 2, block), lambda s, h: (0, jnp.maximum(s - 2, 0))),
-            ],
-            scratch_shapes=[pltpu.VMEM((tall // 2, tokens), BF)],
-        ),
-        compiler_params=pltpu.CompilerParams(vmem_limit_bytes=VMEM_LIMIT),
-        cost_estimate=pl.CostEstimate(flops=tokens * tall * wide, bytes_accessed=8_000_000, transcendentals=0),
-    )(half, left, right)
+        compiler_params=pltpu.CompilerParams(vmem_limit_bytes=limit),
+        cost_estimate=pl.CostEstimate(flops=flops // 16, bytes_accessed=100_000, transcendentals=0),
+    )(core, *args)
+
+
+def grad_half_body(by_rows, info, left, *refs):
+    rights = refs[: 1 if by_rows else 2]
+    bases, outs = refs[len(rights) : -2], refs[-2:]
+    turned = jnp.transpose(left[...])
+    tall = outs[0].shape[0]
+    for i, out in enumerate(outs):
+        total = dot_nn(turned[i * tall : i * tall + tall], rights[0][...]) if by_rows else dot_nn(turned, rights[i][...])
+        if bases:
+            total = total + bases[i][...].astype(F32)
+        out[...] = total.astype(BF)
+
+
+def grad_half(rows, micro, core, mine, left, right, by_rows, bases):
+    tall, wide = left.shape[1] // 2, right.shape[1]
+    steps = GRAD_STEPS
+    half_of = lambda h: h[0] if mine else 1 - h[0]
+    left_spec = pl.BlockSpec((rows, tall), lambda s, h: (micro, half_of(h)))
+    if by_rows:
+        shape = (tall // 2, wide)
+        rights = [pl.BlockSpec((rows, wide // steps), lambda s, h: (micro, s))]
+    else:
+        shape = (tall, wide // 2)
+        rights = [
+            pl.BlockSpec((rows, wide // 2 // steps), lambda s, h, i=i: (micro, i * steps + s)) for i in range(2)
+        ]
+    spec = pl.BlockSpec((shape[0], shape[1] // steps), lambda s, h: (0, s))
+    args = [left] + [right] * len(rights) + list(bases or ())
+    in_specs = [left_spec] + rights + ([spec, spec] if bases else [])
+    out = jax.ShapeDtypeStruct(shape, BF)
+    return grad_call(
+        functools.partial(grad_half_body, by_rows), steps, core, in_specs, args,
+        [out, out], [spec, spec], 2 * rows * tall * wide, VMEM_LIMIT,
+    )
 
 
 def grad_rest_body(with_context, info, inputs, *refs):
-    step = pl.program_id(0)
-    sent, kept = refs[-2:]
+    out = refs[-1]
     turned = jnp.transpose(inputs[...])
     parts = []
     if with_context:
-        context, d_one = refs[:2]
-        parts.append(dot_nn(jnp.transpose(context[...]), d_one[...]).astype(BF))
+        parts.append(dot_nn(jnp.transpose(refs[0][...]), refs[1][...]))
         refs = refs[2:]
-    parts += [dot_nn(turned, right[...]).astype(BF) for right in refs[:-2]]
-    for s, out in enumerate((sent, kept)):
-
-        @pl.when(step == s)
-        def _(out=out):
-            at = 0
-            for part in parts:
-                out[:, at : at + part.shape[1]] = part
-                at += part.shape[1]
-
-
-def grad_rest(tokens, core, inputs, joined_grads, slabs, context=None, d_one=None):
+    for at in range(0, len(refs) - 3, 3):
+        parts.append(dot_nn(turned, jnp.concatenate([right[...] for right in refs[at : at + 3]], axis=1)))
+    at = 0
+    for part in parts:
+        here = slice(at, at + part.shape[1])
+        total = part if refs[-2] is None else part + refs[-2][:, here].astype(F32)
+        out[:, here] = total.astype(BF)
+        at += part.shape[1]
+
+
+def grad_rest(rows, micro, core, mine, inputs, joined_grads, slabs, context, d_one, base):
     width = inputs.shape[1]
-    side = pl.BlockSpec((tokens, width // 2), lambda s, h: (0, jnp.where(s == 0, 1 - h[0], h[0])))
+    side = pl.BlockSpec((rows, width // 2), lambda s, h: (micro, h[0] if mine else 1 - h[0]))
     in_specs, args = [side], [inputs]
     columns = 0
     if context is not None:
-        in_specs += [side, pl.BlockSpec((tokens, width), lambda s, h: (0, 0))]
+        in_specs += [side, pl.BlockSpec((rows, width), lambda s, h: (micro, 0))]
         args += [context, d_one]
         columns += width
     for slab in slabs:
-        in_specs += [pl.BlockSpec((tokens, SLAB), lambda s, h, slab=slab: (0, slab))] * 3
+        in_specs += [pl.BlockSpec((rows, SLAB), lambda s, h, slab=slab: (micro, slab))] * 3
         args += joined_grads
         columns += 3 * SLAB
     out = jax.ShapeDtypeStruct((width // 2, columns), BF)
     whole = pl.BlockSpec(out.shape, lambda s, h: (0, 0))
-    return pl.pallas_call(
-        functools.partial(grad_rest_body, context is not None),
-        out_shape=[out, out],
-        grid_spec=pltpu.PrefetchScalarGridSpec(
-            num_scalar_prefetch=1,
-            grid=(2,),
-            in_specs=in_specs,
-            out_specs=[whole, whole],
-        ),
-        compiler_params=pltpu.CompilerParams(vmem_limit_bytes=VMEM_LIMIT),
-        cost_estimate=pl.CostEstimate(flops=2 * tokens * columns * width, bytes_accessed=12_000_000, transcendentals=0),
-    )(core, *args)
+    if base is not None:
+        in_specs += [whole]
+        args += [base]
+    body = functools.partial(grad_rest_body, context is not None)
+    return grad_call(
+        body if base is not None else lambda *refs: body(*refs[:-1], None, refs[-1]), 1, core, in_specs, args,
+        out, whole, rows * columns * width,
+    )
 
 
 def widen_body(info, own_a, own_b, other_a, other_b, *outs):
@@ -751,9 +717,20 @@
                 for shape in out_shapes
             ],
         ),
-        compiler_params=pltpu.CompilerParams(vmem_limit_bytes=VMEM_LIMIT),
+        compiler_params=pltpu.CompilerParams(vmem_limit_bytes=SMALL_VMEM),
         cost_estimate=pl.CostEstimate(flops=0, bytes_accessed=14_000_000, transcendentals=0),
     )(core, *own, *other)
+
+
+EXCHANGE = (
+    "SR", "KR", "R0", "SE", "R1", "KE", "E1", "S0", "R0", "E0", "PS", "PK", "R0", "E1", "R1", "P0", "S1",
+    "R1", "E1", "R0", "E0", "S2", "P0", "R1", "QS", "R0", "E1", "QK", "Q0", "E0", "R1", "P0", "R0", "E0",
+    "Q0", "V", "P0", "E0", "R1", "E1", "Q0", "V", "E0", "P0", "Q0", "Q0", "P0", "V", "R0", "E1", "R1", "Q0",
+    "E0", "V", "WR", "E1", "P0", "Q0", "WE", "WP",
+)
+ORDERS = {"R0": 0, "R1": 0, "E0": 0, "E1": 1, "P0": 0, "Q0": 0}
+WIDENED = {"WR": ("R0", "R1"), "WE": ("E0", "E1"), "WP": ("P0", "Q0")}
+KERNELS = ("SR", "KR", "SE", "KE", "S0", "PS", "PK", "S1", "S2", "QS", "QK")
 
 
 def passed_along(array, axis, by):
@@ -783,48 +760,86 @@
     return (kept.astype(F32) + got.astype(F32)).astype(BF)
 
 
-def halved(array, bit):
-    step, mine = bit
+class Sequence:
+    def __init__(self):
+        self.last = ()
+
+    def after(self, array):
+        return tied(array, *self.last)
+
+    def did(self, *arrays):
+        self.last = arrays
+        return arrays
+
+
+class Adder:
+    def __init__(self, sequence, value, bits):
+        self.sequence, self.value = sequence, value
+        self.bits = [step for step, _ in bits]
+        self.got = swapped(value, self.bits[0])
+
+    def take(self):
+        self.bits.pop(0)
+        self.value = sum_low(self.sequence.after(self.value), self.got)
+        self.sequence.did(self.value)
+        if self.bits:
+            self.got = swapped(self.value, self.bits[0])
+
+
+class Piece:
+    def __init__(self, sequence, sent, kept, bits, order):
+        self.sequence = sequence
+        self.value = kept
+        self.steps = [(sum_low, None)]
+        self.steps += [(halved, bits[place]) for place in order]
+        self.steps += [(doubled, bits[place]) for place in reversed(order)]
+        self.got = swapped(sent, 1)
+
+    def send(self):
+        if not self.steps:
+            self.sequence.did(self.value)
+            self.got = swapped(self.value, 1)
+            return
+        step, (bit, mine) = self.steps[0]
+        sent = self.value
+        if step is halved:
+            sent = piece(sent.reshape(2, sent.shape[0] // 2, sent.shape[1]), 1 - mine)
+        self.sequence.did(self.value, sent)
+        self.got = swapped(sent, bit)
+
+    def take(self):
+        step, bit = self.steps.pop(0)
+        value = self.sequence.after(self.value)
+        self.value = step(value, self.got) if bit is None else step(value, self.got, bit[1])
+        self.send()
+
+
+def halved(array, got, mine):
     halves = array.reshape(2, array.shape[0] // 2, array.shape[1])
-    got = swapped(piece(halves, 1 - mine), step)
     return sum_low(piece(halves, mine), got)
 
 
-def doubled(array, bit):
-    step, mine = bit
-    got = swapped(array, step)
+def doubled(array, got, mine):
     both = jnp.zeros((2,) + array.shape, array.dtype)
     both = lax.dynamic_update_index_in_dim(both, array, mine, 0)
     both = lax.dynamic_update_index_in_dim(both, got, 1 - mine, 0)
     return flatten_rows(both)
 
 
-class Piece:
-    def __init__(self, sent, kept, bits, order):
-        self.value = sum_low(kept, swapped(sent, 1))
-        self.steps = [(halved, bits[place]) for place in order]
-        self.steps += [(doubled, bits[place]) for place in reversed(order)]
-
-    def advance(self):
-        step, bit = self.steps.pop(0)
-        self.value = step(self.value, bit)
-
-    def finish(self):
-        while self.steps:
-            self.advance()
-        return self.value, swapped(self.value, 1)
-
-
-def advanced(*pieces):
+def exchange_order(digits):
+    if digits == 4:
+        return EXCHANGE
+    rounds = ("R0", "R1", "E0", "E1", "P0", "Q0") * (2 * digits - 1)
+    return KERNELS + rounds + ("V",) * digits + tuple(WIDENED)
+
+
+def ends_of_pieces(pieces):
+    return [one.value for one in pieces], [one.got for one in pieces]
+
+
+def take(*pieces):
     for one in pieces:
-        one.advance()
-    return tuple(one.value for one in pieces)
-
-
-def all_summed(array, bits):
-    for step, _ in bits:
-        array = (array.astype(F32) + swapped(array, step).astype(F32)).astype(array.dtype)
-    return array
+        one.take()
 
 
 def shards(
@@ -916,56 +931,114 @@
         ],
         axis=1,
     )
-    colbert = dot_tn(flatten_rows(outputs[:micros]), flatten_rows(embeds[:micros])).astype(BF)
-    facts = jnp.concatenate([squares, losses[:micros, 6, 0:1]], axis=1)
-    backward_ffn(2 * micros - 1, done + (colbert, facts))
-    colbert = jnp.where(section_id == 1, colbert, swapped(colbert, 1, "pipe"))
-    colbert_sum = all_summed(colbert, bits).astype(F32)
-    theirs = swapped(facts, 1, "pipe")
-    first = jnp.where(section_id == 0, facts, theirs)
-    second = jnp.where(section_id == 0, theirs, facts)
+    after_back = state["attn_back"][3]
+    colbert = dot_tn(
+        flatten_rows(outputs[:micros]), flatten_rows(tied(embeds, after_back)[:micros])
+    ).astype(BF)
+    facts = tied(jnp.concatenate([squares, losses[:micros, 6, 0:1]], axis=1), after_back)
+    last = 2 * micros - 1
+    slabs = tuple(range(width // SLAB))
+    ffn_back, attn_back = state["ffn_back"], state["attn_back"]
+    lefts = [flatten_rows(a) for a in (active, hidden, inputs, context)]
+
+    bases = {}
+    for micro in range(micros - 1):
+        first_core = tied(core, after_back)
+        d_two, d_inner, d_one = (flatten_rows(ffn_back[i]) for i in range(3))
+        joined_grads = [flatten_rows(a) for a in attn_back[:3]]
+        for mine in (0, 1):
+            old = bases.get(mine, (None,) * 4)
+            bases[mine] = (
+                grad_half(rows, micro, first_core, mine, lefts[0], d_two, True, old[0]),
+                grad_half(rows, micro, first_core, mine, lefts[1], d_inner, False, old[1]),
+                grad_rest(rows, micro, first_core, mine, lefts[2], joined_grads, slabs[:1], lefts[3], d_one, old[2]),
+                grad_rest(rows, micro, first_core, mine, lefts[2], joined_grads, slabs[1:], None, None, old[3]),
+            )
+    backward_ffn(last, (colbert, facts) + tuple(jax.tree.leaves(bases)))
+    bases = bases or {0: (None,) * 4, 1: (None,) * 4}
+    micro = micros - 1
     ffn_back = state["ffn_back"]
-    tokens = micros * rows
-    last = 2 * micros - 1
-    d_two, d_inner = flatten_rows(ffn_back[0]), flatten_rows(ffn_back[1])
-    left = flatten_rows(active)
-    sent, kept = (grad_rows(tokens, half, left, d_two) for half in (1 - core, core))
-    pieces = [Piece(s, k, bits, order) for s, k, order in zip(sent, kept, orders)]
-    of_reduce = tuple(one.value for one in pieces)
-    left = flatten_rows(hidden)
-    sent = grad_columns(tokens, 1 - core, left, d_inner)
-    kept = grad_columns(tokens, tied(core, *of_reduce), left, d_inner)
-    pieces += [Piece(s, k, bits, order) for s, k, order in zip(sent, kept, orders)]
-    of_expand = tuple(one.value for one in pieces[2:])
-    backward_attn(last, of_expand, (0,))
-    x_rows, context_rows, one_rows = (flatten_rows(a) for a in (inputs, context, ffn_back[2]))
-    joined_grads = [flatten_rows(a) for a in state["attn_back"][:3]]
-    after = advanced(*pieces[:2])
-    sent, kept = grad_rest(tokens, tied(core, *after), x_rows, joined_grads, (0,), context_rows, one_rows)
-    after = advanced(*pieces[:4])
-    backward_attn(last, after + (kept,), tuple(range(1, width // SLAB)))
-    pieces += [Piece(sent, kept, bits, orders[0])]
-    after = advanced(*pieces[:4])
-    joined_grads = [flatten_rows(a) for a in state["attn_back"][:3]]
-    sent, kept = grad_rest(tokens, tied(core, *after), x_rows, joined_grads, tuple(range(1, width // SLAB)))
-    pieces += [Piece(sent, kept, bits, orders[1])]
-    attn_back = state["attn_back"]
-    small, small_ff = ffn_back[4], ffn_back[5]
-    joined_sums = attn_back[3]
-    small_sum = jnp.sum(small[:micros], axis=0)
-    joined_sum = jnp.sum(joined_sums[:micros, :, 0], axis=0)
-    attend_sum = jnp.concatenate(
-        [joined_sum[:, :SLAB].reshape(-1), joined_sum[:, SLAB:].reshape(-1)]
-    )
-    vector = jnp.concatenate(
-        [small_sum[:6], attend_sum.reshape(2, width), jnp.sum(small_ff[:micros, 0], axis=0).reshape(-1, width)]
-    )
-    vector = all_summed(vector, bits)
-    halves = [one.finish() for one in pieces]
-    own, other = [h[0] for h in halves], [h[1] for h in halves]
-    [big_reduce] = widened(core, own[:2], other[:2], [wr.shape])
-    [big_expand] = widened(core, own[2:4], other[2:4], [we.shape])
-    big_attend, big_mixing = widened(core, own[4:], other[4:], [wa.shape, wm.shape])
+    d_two, d_inner, d_one = (flatten_rows(ffn_back[i]) for i in range(3))
+    line = Sequence()
+
+    def half_of(mine, left, right, by_rows, which):
+        both = grad_half(rows, micro, line.after(core), mine, left, right, by_rows, bases[mine][which])
+        line.did(*both)
+        return both
+
+    def rest_half(mine, some, which):
+        joined_grads = [flatten_rows(a) for a in state["attn_back"][:3]]
+        extra = (lefts[3], d_one) if which == 2 else (None, None)
+        [one] = line.did(
+            grad_rest(rows, micro, line.after(core), mine, lefts[2], joined_grads, some, *extra, bases[mine][which])
+        )
+        return one
+
+    def slab_back(slab):
+        backward_attn(last, line.last, (slab,))
+        line.did(*state["attn_back"])
+
+    made, pieces, widths = {}, {}, {}
+
+    def run_kernel(name):
+        made[name] = {
+            "SR": lambda: half_of(0, lefts[0], d_two, True, 0),
+            "KR": lambda: half_of(1, lefts[0], d_two, True, 0),
+            "SE": lambda: half_of(0, lefts[1], d_inner, False, 1),
+            "KE": lambda: half_of(1, lefts[1], d_inner, False, 1),
+            "PS": lambda: [rest_half(0, slabs[:1], 2)],
+            "PK": lambda: [rest_half(1, slabs[:1], 2)],
+            "QS": lambda: [rest_half(0, slabs[1:], 3)],
+            "QK": lambda: [rest_half(1, slabs[1:], 3)],
+            "S0": lambda: slab_back(slabs[0]),
+            "S1": lambda: slab_back(slabs[1]),
+            "S2": lambda: [slab_back(slab) for slab in slabs[2:]],
+        }[name]()
+
+    def small_sums():
+        small, small_ff, joined_sums = ffn_back[4], ffn_back[5], state["attn_back"][3]
+        small_sum = jnp.sum(small[:micros], axis=0)
+        joined_sum = jnp.sum(joined_sums[:micros, :, 0], axis=0)
+        attend_sum = jnp.concatenate(
+            [joined_sum[:, :SLAB].reshape(-1), joined_sum[:, SLAB:].reshape(-1)]
+        )
+        of_colbert = tied(colbert, *line.last)
+        of_colbert = jnp.where(section_id == 1, of_colbert, passed_along(of_colbert, "pipe", -1))
+        parts = [
+            small_sum[:6],
+            attend_sum.reshape(2, width),
+            jnp.sum(small_ff[:micros, 0], axis=0).reshape(-1, width),
+            of_colbert.astype(F32).reshape(-1, width),
+        ]
+        return jnp.concatenate(parts).astype(BF)
+
+    senders = {"SR": ("R", "KR", 2), "SE": ("E", "KE", 2), "PS": ("P", "PK", 1), "QS": ("Q", "QK", 1)}
+    for step in exchange_order(len(bits)):
+        if step in pieces:
+            pieces[step].take()
+        elif step[0] == "W":
+            widths[step] = widened(
+                line.after(core), *ends_of_pieces([pieces[one] for one in WIDENED[step]]),
+                {"WR": [wr.shape], "WE": [we.shape], "WP": [wa.shape, wm.shape]}[step],
+            )
+            line.did(*widths[step])
+        else:
+            run_kernel(step)
+            for send, (name, keep, count) in senders.items():
+                if keep == step:
+                    for i, (s, k) in enumerate(zip(made[send], made[keep])):
+                        one = name + str(i)
+                        pieces[one] = Piece(line, s, k, bits, orders[ORDERS[one]])
+            if step == "QK":
+                mine = line.after(facts)
+                made["up"], made["down"] = passed_along(mine, "pipe", 1), passed_along(mine, "pipe", -1)
+                pieces["V"] = Adder(line, small_sums(), bits)
+    first = jnp.where(section_id == 0, facts, made["up"])
+    second = jnp.where(section_id == 0, made["down"], facts)
+    [big_reduce], [big_expand], (big_attend, big_mixing) = (widths[one] for one in ("WR", "WE", "WP"))
+    vector = pieces["V"].value
+    vector = vector.astype(F32)
+    colbert_sum = vector[8 + we.shape[1] // width :].reshape(colbert_weight.shape)
     counted = (QROWS + jnp.sum(pass_lengths, axis=1)).astype(F32)
     stats = jnp.stack([first[:, :3], second[:, :3]], axis=1)
     stats = jnp.sqrt(stats / (counted[:, None, None] * width))
@@ -977,7 +1050,7 @@
         jnp.stack([vector[3], vector[0]])[None],
         jnp.stack([vector[4], vector[1]])[None],
         big_expand[None],
-        vector[8:].reshape(1, -1),
+        vector[8 : 8 + we.shape[1] // width].reshape(1, -1),
         big_reduce[None],
         vector[2][None],
         colbert_sum,

time: 626 us -> 560 us (0.89)
  waiting for transfers between devices: 206 us -> 138 us
  local copies, waits for them, and re-layouts: 20.9 us -> 63.8 us
  starting transfers between devices: 104 us -> 65.3 us
    ppermute x58 -> x52, waiting for transfers between devices: 168 us -> 89.9 us  [swapped(): return lax.ppermute(array, axis, [(i, i ^ bit) for i in range(count)])]
    ppermute x58 -> x52, starting transfers between devices: 97.7 us -> 47.9 us  [swapped(): return lax.ppermute(array, axis, [(i, i ^ bit) for i in range(count)])]
    unnamed x67 -> x137, local copies, waits for them, and re-layouts: 9.56 us -> 40.4 us
    ppermute x4 -> x7, starting transfers between devices: 6.1 us -> 17.4 us  [passed_along(): return lax.ppermute(array, axis, pairs)]
    ppermute x4 -> x7, waiting for transfers between devices: 38.3 us -> 48.5 us  [passed_along(): return lax.ppermute(array, axis, pairs)]
    convert_element_type x18 -> x27, other arithmetic: 9.7 us -> 19.4 us  [sum_low(): return (kept.astype(F32) + got.astype(F32)).astype(BF)]
    pallas_call x17 -> x18, Pallas kernels: 190 us -> 182 us  [call(): pl.pallas_call(body, out_shape=[jax.ShapeDtypeStruct(s[0], s[1]) for s in...]
    pallas_call x6 -> x16, Pallas kernels: 46.6 us -> 53.4 us  [grad_call(): pl.pallas_call(body, out_shape=out_shape, grid_spec=pltpu.PrefetchScalarG...]
  transfers between devices with their start and end apart: 62 -> 59, of which waited for: 27 -> 18; matrix products, arithmetic and copies ran while one was open for 6% -> 10% of each run, Pallas kernels for 35% -> 34%
where the time goes in v5:
time: 560 us; the launch traced here: 551 us
  Pallas kernels  251 us (45%)
  waiting for transfers between devices  138 us (25%)
  starting transfers between devices  65.3 us (12%)
  local copies, waits for them, and re-layouts  63.8 us (11%)
  other arithmetic  28.6 us (5%)
    pallas_call x18, Pallas kernels, call(): pl.pallas_call(body, out_shape=[jax.ShapeDtypeStruct(s[0], s[1]) for s in...  182 us
    ppermute x52, waiting for transfers between devices, swapped(): return lax.ppermute(array, axis, [(i, i ^ bit) for i in range(count)])  89.9 us
    pallas_call x16, Pallas kernels, grad_call(): pl.pallas_call(body, out_shape=out_shape, grid_spec=pltpu.PrefetchScalarG...  53.4 us
    ppermute x7, waiting for transfers between devices, passed_along(): return lax.ppermute(array, axis, pairs)  48.5 us
    ppermute x52, starting transfers between devices, swapped(): return lax.ppermute(array, axis, [(i, i ^ bit) for i in range(count)])  47.9 us
    unnamed x137, local copies, waits for them, and re-layouts  40.4 us
    convert_element_type x27, other arithmetic, sum_low(): return (kept.astype(F32) + got.astype(F32)).astype(BF)  19.4 us
    ppermute x7, starting transfers between devices, passed_along(): return lax.ppermute(array, axis, pairs)  17.4 us
  transfers between devices with their start and end apart: 59, of which 18 were waited for; matrix products, arithmetic and copies ran while one was open for 10% of the time, Pallas kernels for 34%

profile of v5, /device:TPU:0, one launch (start us, length us, event | category | flops | bytes accessed | tf_op | source)
XLA Modules:
  0.0 551.2 jit_solution(16988466227191276665)
XLA Ops:
  4.1 19.2 %shard_map.237 = (bf16[3,640,768]{2,1,0:T(8,128)(2,1)}, bf16[3,3,640,768]{3,2,1,0:T(8,128)(2,1)}, f32[3,3,8,640]{3,2,1,0:T(8,128)}, bf16[3,640,768]{2,1,0:T(8,12...) custom-call(s32[17]{0:T(128)} %pad_add_fusion.info, ...), custom_call_target="tpu_custom_call" | custom-call | flops 20000000000 | bytes 20000000 | tf_op jit(solution)/shard_map/pallas_call | solution.py:222
  23.3 15.3 %shard_map.239 = (bf16[3,640,3072]{2,1,0:T(8,128)(2,1)}, bf16[3,640,3072]{2,1,0:T(8,128)(2,1)}, bf16[3,640,768]{2,1,0:T(8,128)(2,1)}, bf16[3,640,768]{2,1,0:T(8,...) custom-call(s32[17]{0:T(128)} %pad_add_fusion.info, ...), custom_call_target="tpu_custom_call" | custom-call | flops 12000000000 | bytes 20000000 | tf_op jit(solution)/shard_map/pallas_call | solution.py:222
  40.2 19.3 %shard_map.238 = (bf16[3,640,768]{2,1,0:T(8,128)(2,1)}, bf16[3,3,640,768]{3,2,1,0:T(8,128)(2,1)}, f32[3,3,8,640]{3,2,1,0:T(8,128)}, bf16[3,640,768]{2,1,0:T(8,12...) custom-call(s32[17]{0:T(128)} %pad_add_fusion.info, ...), custom_call_target="tpu_custom_call", output_to_operand_aliasing={{0}: (11, {}), {1}: (12, {}), {2}: (13, {}), {3}: (14, {}),... | custom-call | flops 20000000000 | bytes 20000000 | tf_op jit(solution)/shard_map/pallas_call | solution.py:222
  59.5 15.4 %shard_map.240 = (bf16[3,640,3072]{2,1,0:T(8,128)(2,1)}, bf16[3,640,3072]{2,1,0:T(8,128)(2,1)}, bf16[3,640,768]{2,1,0:T(8,128)(2,1)}, bf16[3,640,768]{2,1,0:T(8,...) custom-call(s32[17]{0:T(128)} %pad_add_fusion.info, ...), custom_call_target="tpu_custom_call", output_to_operand_aliasing={{0}: (8, {}), {1}: (9, {}), {2}: (10, {}), {3}: (11, {}), {... | custom-call | flops 12000000000 | bytes 20000000 | tf_op jit(solution)/shard_map/pallas_call | solution.py:222
  77.6 5.0 shard_map.241
  82.7 5.1 shard_map.242
  87.8 6.6 %shard_map.243 = (bf16[3,640,768]{2,1,0:T(8,128)(2,1)}, bf16[3,640,3072]{2,1,0:T(8,128)(2,1)}, bf16[3,640,768]{2,1,0:T(8,128)(2,1)}, bf16[3,640,128]{2,1,0:T(8,1...) custom-call(s32[17]{0:T(128)} %pad_add_fusion.info, ...), custom_call_target="tpu_custom_call" | custom-call | flops 12000000000 | bytes 20000000 | tf_op jit(solution)/shard_map/pallas_call | solution.py:222
  94.3 4.9 shard_map.244
  100.6 5.3 shard_map.245
  105.9 5.1 shard_map.246
  110.9 6.8 %shard_map.247 = (bf16[3,640,768]{2,1,0:T(8,128)(2,1)}, bf16[3,640,3072]{2,1,0:T(8,128)(2,1)}, bf16[3,640,768]{2,1,0:T(8,128)(2,1)}, bf16[3,640,128]{2,1,0:T(8,1...) custom-call(s32[17]{0:T(128)} %pad_add_fusion.info, ...), custom_call_target="tpu_custom_call", output_to_operand_aliasing={{0}: (12, {}), {1}: (13, {}), {2}: (14, {}), {3}: (15, {}),... | custom-call | flops 12000000000 | bytes 20000000 | tf_op jit(solution)/shard_map/pallas_call | solution.py:222
  117.7 4.9 shard_map.248
  125.8 39.3 %collective-permute-done.3.refs_0_ = bf16[640,768]{1,0:T(8,128)(2,1)S(1)} collective-permute-done((bf16[640,768]{1,0:T(8,128)(2,1)}, bf16[640,768]{1,0:T(8,128)(2,1)S(1)}, u32[]{:S(2)}, u32[]{:S(2)}) %collective-permute-start.3) | collective-permute-done | bytes 983072 | tf_op jit(solution)/shard_map/ppermute | solution.py:739
  166.1 17.9 %shard_map.249 = (bf16[3,640,768]{2,1,0:T(8,128)(2,1)}, bf16[3,640,3072]{2,1,0:T(8,128)(2,1)}, bf16[3,640,768]{2,1,0:T(8,128)(2,1)}, bf16[3,640,128]{2,1,0:T(8,1...) custom-call(s32[17]{0:T(128)} %pad_add_fusion.info, ...), custom_call_target="tpu_custom_call", output_to_operand_aliasing={{0}: (11, {}), {1}: (12, {}), {2}: (13, {}), {3}: (14, {}),... | custom-call | flops 12000000000 | bytes 20000000 | tf_op jit(solution)/shard_map/pallas_call | solution.py:222
  189.5 3.5 copy-done.19
  193.0 16.4 %shard_map.250 = (bf16[3,640,768]{2,1,0:T(8,128)(2,1)S(1)}, bf16[3,640,768]{2,1,0:T(8,128)(2,1)S(1)}, bf16[3,640,768]{2,1,0:T(8,128)(2,1)S(1)}, f32[3,3,8,512]{3,2,1,0:T(8,128)S(1)}) custom-call(s32[17]{0:T(128)S(1)} %copy-done.35, bf16[3,640,768]{2,1,0:T(8,128)(2,1)S(1)} %copy-done.11, ...), custom_call_target="tpu_custom_call", output_to_operand_aliasing={{0}: (6, {}), {1}: (7, {}), {2}: (8, {}), {3}: (9, {})} | custom-call | flops 625000000 | bytes 1041666 | tf_op jit(solution)/shard_map/pallas_call | solution.py:222
  217.7 5.2 shard_map.256
  222.9 4.7 shard_map.252
  227.6 5.2 shard_map.255
  232.9 5.4 shard_map.251
  239.6 3.6 collective-permute-done.2.refs_0_
  243.3 17.1 %shard_map.259 = (bf16[3,640,768]{2,1,0:T(8,128)(2,1)}, bf16[3,640,3072]{2,1,0:T(8,128)(2,1)}, bf16[3,640,768]{2,1,0:T(8,128)(2,1)}, bf16[3,640,128]{2,1,0:T(8,1...) custom-call(s32[17]{0:T(128)} %pad_add_fusion.info, ...), custom_call_target="tpu_custom_call", output_to_operand_aliasing={{0}: (11, {}), {1}: (12, {}), {2}: (13, {}), {3}: (14, {}),... | custom-call | flops 12000000000 | bytes 20000000 | tf_op jit(solution)/shard_map/pallas_call | solution.py:222
  260.4 5.8 %shard_map.260 = (bf16[768,768]{1,0:T(8,128)(2,1)}, bf16[768,768]{1,0:T(8,128)(2,1)}) custom-call(s32[1]{0:T(128)} %bitcast.info.refs_0_, bf16[1920,3072]{1,0:T(8,128)(2,1)} %bitcast.363, bf16[1920,768]{1,0:T(8,128)(2,1)} %bitcast.367, bf16[768,768]{1,0:T(8,128)(2,1)} %get-tuple-element.298.refs_1_, bf16[768,768]{1,0:T(8,128)(2,1)} %get-tuple-element.299.refs_2_), custom_call_target="tpu_custom_call" | custom-call | flops 94371840 | bytes 100000 | tf_op jit(solution)/shard_map/pallas_call | solution.py:589
  266.7 5.8 %shard_map.261 = (bf16[768,768]{1,0:T(8,128)(2,1)}, bf16[768,768]{1,0:T(8,128)(2,1)}) custom-call(s32[1]{0:T(128)} %bitcast.info.refs_0_, bf16[1920,3072]{1,0:T(8,128)(2,1)} %bitcast.364, bf16[1920,768]{1,0:T(8,128)(2,1)} %bitcast.368, bf16[768,768]{1,0:T(8,128)(2,1)} %get-tuple-element.307.refs_1_, bf16[768,768]{1,0:T(8,128)(2,1)} %get-tuple-element.308.refs_2_), custom_call_target="tpu_custom_call" | custom-call | flops 94371840 | bytes 100000 | tf_op jit(solution)/shard_map/pallas_call | solution.py:589
  276.3 5.6 %shard_map.262 = (bf16[384,1536]{1,0:T(8,128)(2,1)}, bf16[384,1536]{1,0:T(8,128)(2,1)}) custom-call(s32[1]{0:T(128)} %bitcast.info.refs_0_, bf16[1920,768]{1,0:T(8,128)(2,1)} %bitcast.371, bf16[1920,3072]{1,0:T(8,128)(2,1)} %bitcast.357, bf16[1920,3072]{1,0:T(8,128)(2,1)} %bitcast.358, bf16[384,1536]{1,0:T(8,128)(2,1)} %get-tuple-element.301.refs_2_, ...), custom_call_target="tpu_custom_call" | custom-call | flops 94371840 | bytes 100000 | tf_op jit(solution)/shard_map/pallas_call | solution.py:589
  289.7 5.6 %shard_map.263 = (bf16[384,1536]{1,0:T(8,128)(2,1)}, bf16[384,1536]{1,0:T(8,128)(2,1)}) custom-call(s32[1]{0:T(128)} %bitcast.info.refs_0_, bf16[1920,768]{1,0:T(8,128)(2,1)} %bitcast.372, bf16[1920,3072]{1,0:T(8,128)(2,1)} %bitcast.359, bf16[1920,3072]{1,0:T(8,128)(2,1)} %bitcast.360, bf16[384,1536]{1,0:T(8,128)(2,1)} %get-tuple-element.309.refs_2_, ...), custom_call_target="tpu_custom_call" | custom-call | flops 94371840 | bytes 100000 | tf_op jit(solution)/shard_map/pallas_call | solution.py:589
  302.4 3.5 copy-done.20
  305.9 5.8 %shard_map.264 = (bf16[3,640,768]{2,1,0:T(8,128)(2,1)S(1)}, bf16[3,640,768]{2,1,0:T(8,128)(2,1)S(1)}, bf16[3,640,768]{2,1,0:T(8,128)(2,1)S(1)}, f32[3,3,8,512]{3,2,1,0:T(8,128)S(1)}) custom-call(s32[17]{0:T(128)S(1)} %copy-done.36, bf16[3,640,768]{2,1,0:T(8,128)(2,1)S(1)} %copy-done.12, ...), custom_call_target="tpu_custom_call", output_to_operand_aliasing={{0}: (6, {}), {1}: (7, {}), {2}: (8, {}), {3}: (9, {})} | custom-call | flops 208333328 | bytes 347222 | tf_op jit(solution)/shard_map/pallas_call | solution.py:222
  326.7 12.0 %collective-permute-done.10 = bf16[192,1536]{1,0:T(8,128)(2,1)S(1)} collective-permute-done((bf16[192,1536]{1,0:T(8,128)(2,1)S(1)}, bf16[192,1536]{1,0:T(8,128)(2,1)S(1)}, u32[]{:S(2)}, u32[]{:S(2)}) %collective-permute-start.10) | collective-permute-done | bytes 589856 | tf_op jit(solution)/shard_map/ppermute | solution.py:752
  344.7 6.0 %shard_map.267 = (bf16[3,640,768]{2,1,0:T(8,128)(2,1)S(1)}, bf16[3,640,768]{2,1,0:T(8,128)(2,1)S(1)}, bf16[3,640,768]{2,1,0:T(8,128)(2,1)S(1)}, f32[3,3,8,512]{3,2,1,0:T(8,128)S(1)}) custom-call(s32[17]{0:T(128)S(1)} %copy-done.36, bf16[3,640,768]{2,1,0:T(8,128)(2,1)S(1)} %copy-done.12, ...), custom_call_target="tpu_custom_call", output_to_operand_aliasing={{0}: (6, {}), {1}: (7, {}), {2}: (8, {}), {3}: (9, {})} | custom-call | flops 208333328 | bytes 347222 | tf_op jit(solution)/shard_map/pallas_call | solution.py:222
  351.5 4.2 collective-permute-start.18
  361.2 5.8 %shard_map.268 = (bf16[3,640,768]{2,1,0:T(8,128)(2,1)S(1)}, bf16[3,640,768]{2,1,0:T(8,128)(2,1)S(1)}, bf16[3,640,768]{2,1,0:T(8,128)(2,1)S(1)}, f32[3,3,8,512]{3,2,1,0:T(8,128)S(1)}) custom-call(s32[17]{0:T(128)S(1)} %copy-done.36, bf16[3,640,768]{2,1,0:T(8,128)(2,1)S(1)} %copy-done.12, ...), custom_call_target="tpu_custom_call", output_to_operand_aliasing={{0}: (6, {}), {1}: (7, {}), {2}: (8, {}), {3}: (9, {})} | custom-call | flops 208333328 | bytes 347222 | tf_op jit(solution)/shard_map/pallas_call | solution.py:222
  389.7 8.6 %collective-permute-start.58 = (f32[2,4]{0,1:T(4,128)S(1)}, f32[2,4]{0,1:T(4,128)S(1)}, u32[]{:S(2)}, u32[]{:S(2)}) collective-permute-start(f32[2,4]{0,1:T(4,128)S(1)} %copy-done.58), channel_id=1, source_target_pairs={{0,16},{1,17},{2,18},{3,19},{4,20},{5,21},{6,22},{7,23},{8,24},{9,... | collective-permute-start | bytes 104 | tf_op jit(solution)/shard_map/ppermute | solution.py:739
  404.5 5.6 %collective-permute-done.28 = bf16[768,128]{1,0:T(8,128)(2,1)S(1)} collective-permute-done((bf16[768,128]{1,0:T(8,128)(2,1)}, bf16[768,128]{1,0:T(8,128)(2,1)S(1)}, u32[]{:S(2)}, u32[]{:S(2)}) %collective-permute-start.28) | collective-permute-done | bytes 196640 | tf_op jit(solution)/shard_map/ppermute | solution.py:739
  422.5 8.4 %collective-permute-done.26 = bf16[48,1536]{1,0:T(8,128)(2,1)S(1)} collective-permute-done((bf16[48,1536]{1,0:T(8,128)(2,1)S(1)}, bf16[48,1536]{1,0:T(8,128)(2,1)S(1)}, u32[]{:S(2)}, u32[]{:S(2)}) %collective-permute-start.26) | collective-permute-done | bytes 147488 | tf_op jit(solution)/shard_map/ppermute | solution.py:752
  431.2 3.4 collective-permute-done.27
  437.9 7.5 %collective-permute-done.31 = bf16[48,1536]{1,0:T(8,128)(2,1)S(1)} collective-permute-done((bf16[48,1536]{1,0:T(8,128)(2,1)S(1)}, bf16[48,1536]{1,0:T(8,128)(2,1)S(1)}, u32[]{:S(2)}, u32[]{:S(2)}) %collective-permute-start.31) | collective-permute-done | bytes 147488 | tf_op jit(solution)/shard_map/ppermute | solution.py:752
  447.8 4.0 collective-permute-done.34
  455.2 4.0 collective-permute-done.36
  463.1 5.7 %collective-permute-done.38 = bf16[48,1536]{1,0:T(8,128)(2,1)S(1)} collective-permute-done((bf16[48,1536]{1,0:T(8,128)(2,1)S(1)}, bf16[48,1536]{1,0:T(8,128)(2,1)S(1)}, u32[]{:S(2)}, u32[]{:S(2)}) %collective-permute-start.38) | collective-permute-done | bytes 147488 | tf_op jit(solution)/shard_map/ppermute | solution.py:752
  468.9 9.1 %collective-permute-done.39 = bf16[48,1536]{1,0:T(8,128)(2,1)S(1)} collective-permute-done((bf16[48,1536]{1,0:T(8,128)(2,1)S(1)}, bf16[48,1536]{1,0:T(8,128)(2,1)S(1)}, u32[]{:S(2)}, u32[]{:S(2)}) %collective-permute-start.39) | collective-permute-done | bytes 147488 | tf_op jit(solution)/shard_map/ppermute | solution.py:752
  479.7 5.0 collective-permute-done.41
  488.8 9.8 %collective-permute-done.45 = bf16[96,1536]{1,0:T(8,128)(2,1)S(1)} collective-permute-done((bf16[96,1536]{1,0:T(8,128)(2,1)S(1)}, bf16[96,1536]{1,0:T(8,128)(2,1)S(1)}, u32[]{:S(2)}, u32[]{:S(2)}) %collective-permute-start.45) | collective-permute-done | bytes 294944 | tf_op jit(solution)/shard_map/ppermute | solution.py:752
  504.4 4.1 shard_map.271
  509.7 7.1 %collective-permute-done.51 = bf16[192,1536]{1,0:T(8,128)(2,1)S(1)} collective-permute-done((bf16[192,1536]{1,0:T(8,128)(2,1)S(1)}, bf16[192,1536]{1,0:T(8,128)(2,1)S(1)}, u32[]{:S(2)}, u32[]{:S(2)}) %collective-permute-start.51) | collective-permute-done | bytes 589856 | tf_op jit(solution)/shard_map/ppermute | solution.py:752
  517.1 12.0 %collective-permute-done.52 = bf16[192,1536]{1,0:T(8,128)(2,1)S(1)} collective-permute-done((bf16[192,1536]{1,0:T(8,128)(2,1)S(1)}, bf16[192,1536]{1,0:T(8,128)(2,1)S(1)}, u32[]{:S(2)}, u32[]{:S(2)}) %collective-permute-start.52) | collective-permute-done | bytes 589856 | tf_op jit(solution)/shard_map/ppermute | solution.py:752
  539.0 6.1 %shard_map.272 = f32[768,3072]{1,0:T(8,128)} custom-call(s32[1]{0:T(128)} %bitcast.info.refs_0_, bf16[384,1536]{1,0:T(8,128)(2,1)} %bitcast.149.own_a, bf16[384,1536]{1,0:T(8,128)(2,1)S(1)} %bitcast.348, bf16[384,1536]{1,0:T(8,128)(2,1)} %collective-permute-done.53.other_a, bf16[384,1536]{1,0:T(8,128)(2,1)} %collective-permute-done.54.other_b), custom_call_target="tpu_custom_call" | custom-call | bytes 14000000 | tf_op jit(solution)/shard_map/pallas_call | solution.py:708
  545.1 5.6 %shard_map.273 = (f32[768,2304]{1,0:T(8,128)}, f32[768,768]{1,0:T(8,128)}) custom-call(s32[1]{0:T(128)} %bitcast.info.refs_0_, bf16[384,1536]{1,0:T(8,128)(2,1)S(1)} %bitcast.346, bf16[384,1536]{1,0:T(8,128)(2,1)S(1)} %bitcast.344, bf16[384,1536]{1,0:T(8,128)(2,1)} %collective-permute-done.55.other_a, bf16[384,1536]{1,0:T(8,128)(2,1)} %collective-permute-done.56.other_b), custom_call_target="tpu_custom_call" | custom-call | bytes 14000000 | tf_op jit(solution)/shard_map/pallas_call | solution.py:708
  (377 shorter events, 151.4 us)
Async XLA Ops:
  38.7 38.0 %collective-permute-start.1 = (bf16[640,768]{1,0:T(8,128)(2,1)}, bf16[640,768]{1,0:T(8,128)(2,1)S(1)}, u32[]{:S(2)}, u32[]{:S(2)}) collective-permute-start(bf16[640,768]{1,0:T(8,128)(2,1)} %get-tuple-element.223), channel_id=1, source_target_pairs={{0,16},{1,17},{2,18},{3,19},{4,20},{5,21},{6,22},{7,23},{8,24},{9,... | collective-permute-start | bytes 2949128 | tf_op jit(solution)/shard_map/ppermute | solution.py:739
  74.9 24.4 %collective-permute-start = (bf16[640,768]{1,0:T(8,128)(2,1)}, bf16[640,768]{1,0:T(8,128)(2,1)S(1)}, u32[]{:S(2)}, u32[]{:S(2)}) collective-permute-start(bf16[640,768]{1,0:T(8,128)(2,1)} %get-tuple-element.222), channel_id=1, source_target_pairs={{0,16},{1,17},{2,18},{3,19},{4,20},{5,21},{6,22},{7,23},{8,24},{9,... | collective-permute-start | bytes 2949128 | tf_op jit(solution)/shard_map/ppermute | solution.py:739
  99.3 65.8 %collective-permute-start.3 = (bf16[640,768]{1,0:T(8,128)(2,1)}, bf16[640,768]{1,0:T(8,128)(2,1)S(1)}, u32[]{:S(2)}, u32[]{:S(2)}) collective-permute-start(bf16[640,768]{1,0:T(8,128)(2,1)} %get-tuple-element.277), channel_id=1, source_target_pairs={{16,0},{17,1},{18,2},{19,3},{20,4},{21,5},{22,6},{23,7},{24,8},{25... | collective-permute-start | bytes 2949128 | tf_op jit(solution)/shard_map/ppermute | solution.py:739
  122.7 120.6 %collective-permute-start.2 = (bf16[640,768]{1,0:T(8,128)(2,1)}, bf16[640,768]{1,0:T(8,128)(2,1)}, u32[]{:S(2)}, u32[]{:S(2)}) collective-permute-start(bf16[640,768]{1,0:T(8,128)(2,1)} %get-tuple-element.276), channel_id=1, source_target_pairs={{16,0},{17,1},{18,2},{19,3},{20,4},{21,5},{22,6},{23,7},{24,8},{25... | collective-permute-start | bytes 2949128 | tf_op jit(solution)/shard_map/ppermute | solution.py:739
  266.2 20.0 %collective-permute-start.5 = (bf16[768,768]{1,0:T(8,128)(2,1)}, bf16[768,768]{1,0:T(8,128)(2,1)}, u32[]{:S(2)}, u32[]{:S(2)}) collective-permute-start(bf16[768,768]{1,0:T(8,128)(2,1)} %get-tuple-element.315), channel_id=1, source_target_pairs={{0,1},{1,0},{2,3},{3,2},{4,5},{5,4},{6,7},{7,6},{8,9},{9,8},{10,11... | collective-permute-start | bytes 3538952 | tf_op jit(solution)/shard_map/ppermute | solution.py:752
  281.9 13.3 %collective-permute-start.6 = (bf16[384,1536]{1,0:T(8,128)(2,1)}, bf16[384,1536]{1,0:T(8,128)(2,1)}, u32[]{:S(2)}, u32[]{:S(2)}) collective-permute-start(bf16[384,1536]{1,0:T(8,128)(2,1)} %get-tuple-element.322), channel_id=1, source_target_pairs={{0,1},{1,0},{2,3},{3,2},{4,5},{5,4},{6,7},{7,6},{8,9},{9,8},{10,11... | collective-permute-start | bytes 3538952 | tf_op jit(solution)/shard_map/ppermute | solution.py:752
  284.3 27.4 %collective-permute-start.7 = (bf16[384,768]{1,0:T(8,128)(2,1)}, bf16[384,768]{1,0:T(8,128)(2,1)S(1)}, u32[]{:S(2)}, u32[]{:S(2)}) collective-permute-start(bf16[384,768]{1,0:T(8,128)(2,1)} %dynamic-slice_bitcast_fusion.5), channel_id=1, source_target_pairs={{0,2},{1,3},{2,0},{3,1},{4,6},{5,7},{6,4},{7,5},{8,10},{9,11},{10,... | collective-permute-start | bytes 1769480 | tf_op jit(solution)/shard_map/ppermute | solution.py:752
  286.0 29.9 %collective-permute-start.8 = (bf16[384,1536]{1,0:T(8,128)(2,1)}, bf16[384,1536]{1,0:T(8,128)(2,1)}, u32[]{:S(2)}, u32[]{:S(2)}) collective-permute-start(bf16[384,1536]{1,0:T(8,128)(2,1)} %get-tuple-element.321), channel_id=1, source_target_pairs={{0,1},{1,0},{2,3},{3,2},{4,5},{5,4},{6,7},{7,6},{8,9},{9,8},{10,11... | collective-permute-start | bytes 3538952 | tf_op jit(solution)/shard_map/ppermute | solution.py:752
  289.3 49.6 %collective-permute-start.11 = (bf16[384,768]{1,0:T(8,128)(2,1)}, bf16[384,768]{1,0:T(8,128)(2,1)}, u32[]{:S(2)}, u32[]{:S(2)}) collective-permute-start(bf16[384,768]{1,0:T(8,128)(2,1)} %dynamic-slice_bitcast_fusion.4), channel_id=1, source_target_pairs={{0,2},{1,3},{2,0},{3,1},{4,6},{5,7},{6,4},{7,5},{8,10},{9,11},{10,... | collective-permute-start | bytes 1769480 | tf_op jit(solution)/shard_map/ppermute | solution.py:752
  315.7 23.0 %collective-permute-start.10 = (bf16[192,1536]{1,0:T(8,128)(2,1)S(1)}, bf16[192,1536]{1,0:T(8,128)(2,1)S(1)}, u32[]{:S(2)}, u32[]{:S(2)}) collective-permute-start(bf16[192,1536]{1,0:T(8,128)(2,1)S(1)} %dynamic-slice_bitcast_fusion.3), channel_id=1, source_target_pairs={{0,4},{1,5},{2,6},{3,7},{4,0},{5,1},{6,2},{7,3},{8,12},{9,13},{10,... | collective-permute-start | bytes 1769480 | tf_op jit(solution)/shard_map/ppermute | solution.py:752
  320.2 22.8 %collective-permute-start.12 = (bf16[384,1536]{1,0:T(8,128)(2,1)S(1)}, bf16[384,1536]{1,0:T(8,128)(2,1)S(1)}, u32[]{:S(2)}, u32[]{:S(2)}) collective-permute-start(bf16[384,1536]{1,0:T(8,128)(2,1)S(1)} %shard_map.265), channel_id=1, source_target_pairs={{0,1},{1,0},{2,3},{3,2},{4,5},{5,4},{6,7},{7,6},{8,9},{9,8},{10,11... | collective-permute-start | bytes 3538952 | tf_op jit(solution)/shard_map/ppermute | solution.py:752
  320.3 39.9 %collective-permute-start.16 = (bf16[192,1536]{1,0:T(8,128)(2,1)S(1)}, bf16[192,1536]{1,0:T(8,128)(2,1)S(1)}, u32[]{:S(2)}, u32[]{:S(2)}) collective-permute-start(bf16[192,1536]{1,0:T(8,128)(2,1)S(1)} %dynamic-slice_bitcast_fusion.2), channel_id=1, source_target_pairs={{0,2},{1,3},{2,0},{3,1},{4,6},{5,7},{6,4},{7,5},{8,10},{9,11},{10,... | collective-permute-start | bytes 1769480 | tf_op jit(solution)/shard_map/ppermute | solution.py:752
  323.9 32.7 %collective-permute-start.15 = (bf16[96,768]{1,0:T(8,128)(2,1)S(1)}, bf16[96,768]{1,0:T(8,128)(2,1)S(1)}, u32[]{:S(2)}, u32[]{:S(2)}) collective-permute-start(bf16[96,768]{1,0:T(8,128)(2,1)S(1)} %dynamic-slice_bitcast_fusion.17), channel_id=1, source_target_pairs={{0,8},{1,9},{2,10},{3,11},{4,12},{5,13},{6,14},{7,15},{8,0},{9,1},... | collective-permute-start | bytes 442376 | tf_op jit(solution)/shard_map/ppermute | solution.py:752
  341.3 14.4 %collective-permute-start.14 = (bf16[96,1536]{1,0:T(8,128)(2,1)S(1)}, bf16[96,1536]{1,0:T(8,128)(2,1)S(1)}, u32[]{:S(2)}, u32[]{:S(2)}) collective-permute-start(bf16[96,1536]{1,0:T(8,128)(2,1)S(1)} %dynamic-slice_bitcast_fusion.10), channel_id=1, source_target_pairs={{0,2},{1,3},{2,0},{3,1},{4,6},{5,7},{6,4},{7,5},{8,10},{9,11},{10,... | collective-permute-start | bytes 884744 | tf_op jit(solution)/shard_map/ppermute | solution.py:752
  344.3 26.0 %collective-permute-start.17 = (bf16[192,1536]{1,0:T(8,128)(2,1)}, bf16[192,1536]{1,0:T(8,128)(2,1)}, u32[]{:S(2)}, u32[]{:S(2)}) collective-permute-start(bf16[192,1536]{1,0:T(8,128)(2,1)} %dynamic-slice_bitcast_fusion.1), channel_id=1, source_target_pairs={{0,2},{1,3},{2,0},{3,1},{4,6},{5,7},{6,4},{7,5},{8,10},{9,11},{10,... | collective-permute-start | bytes 1769480 | tf_op jit(solution)/shard_map/ppermute | solution.py:752
  351.5 21.1 %collective-permute-start.18 = (bf16[96,768]{1,0:T(8,128)(2,1)}, bf16[96,768]{1,0:T(8,128)(2,1)}, u32[]{:S(2)}, u32[]{:S(2)}) collective-permute-start(bf16[96,768]{1,0:T(8,128)(2,1)} %dynamic-slice_bitcast_fusion.16), channel_id=1, source_target_pairs={{0,8},{1,9},{2,10},{3,11},{4,12},{5,13},{6,14},{7,15},{8,0},{9,1},... | collective-permute-start | bytes 442376 | tf_op jit(solution)/shard_map/ppermute | solution.py:752
  357.2 25.6 %collective-permute-start.19 = (bf16[96,768]{1,0:T(8,128)(2,1)}, bf16[96,768]{1,0:T(8,128)(2,1)}, u32[]{:S(2)}, u32[]{:S(2)}) collective-permute-start(bf16[96,768]{1,0:T(8,128)(2,1)} %fusion.19), channel_id=1, source_target_pairs={{0,8},{1,9},{2,10},{3,11},{4,12},{5,13},{6,14},{7,15},{8,0},{9,1},... | collective-permute-start | bytes 442376 | tf_op jit(solution)/shard_map/ppermute | solution.py:752
  357.2 26.6 %collective-permute-start.20 = (bf16[48,1536]{1,0:T(8,128)(2,1)}, bf16[48,1536]{1,0:T(8,128)(2,1)}, u32[]{:S(2)}, u32[]{:S(2)}) collective-permute-start(bf16[48,1536]{1,0:T(8,128)(2,1)} %dynamic-slice_bitcast_fusion.15), channel_id=1, source_target_pairs={{0,8},{1,9},{2,10},{3,11},{4,12},{5,13},{6,14},{7,15},{8,0},{9,1},... | collective-permute-start | bytes 442376 | tf_op jit(solution)/shard_map/ppermute | solution.py:752
  361.1 53.4 %collective-permute-start.22 = (bf16[96,1536]{1,0:T(8,128)(2,1)}, bf16[96,1536]{1,0:T(8,128)(2,1)}, u32[]{:S(2)}, u32[]{:S(2)}) collective-permute-start(bf16[96,1536]{1,0:T(8,128)(2,1)} %dynamic-slice_bitcast_fusion.8), channel_id=1, source_target_pairs={{0,4},{1,5},{2,6},{3,7},{4,0},{5,1},{6,2},{7,3},{8,12},{9,13},{10,... | collective-permute-start | bytes 884744 | tf_op jit(solution)/shard_map/ppermute | solution.py:752
  381.8 30.3 %collective-permute-start.21 = (bf16[384,1536]{1,0:T(8,128)(2,1)}, bf16[384,1536]{1,0:T(8,128)(2,1)}, u32[]{:S(2)}, u32[]{:S(2)}) collective-permute-start(bf16[384,1536]{1,0:T(8,128)(2,1)} %shard_map.269), channel_id=1, source_target_pairs={{0,1},{1,0},{2,3},{3,2},{4,5},{5,4},{6,7},{7,6},{8,9},{9,8},{10,11... | collective-permute-start | bytes 3538952 | tf_op jit(solution)/shard_map/ppermute | solution.py:752
  388.3 12.3 %collective-permute-start.57 = (f32[2,4]{0,1:T(4,128)S(1)}, f32[2,4]{0,1:T(4,128)S(1)}, u32[]{:S(2)}, u32[]{:S(2)}) collective-permute-start(f32[2,4]{0,1:T(4,128)S(1)} %copy-done.58), channel_id=1, source_target_pairs={{16,0},{17,1},{18,2},{19,3},{20,4},{21,5},{22,6},{23,7},{24,8},{25... | collective-permute-start | bytes 104 | tf_op jit(solution)/shard_map/ppermute | solution.py:739
  398.3 19.3 %collective-permute-start.23 = (bf16[96,768]{1,0:T(8,128)(2,1)}, bf16[96,768]{1,0:T(8,128)(2,1)S(1)}, u32[]{:S(2)}, u32[]{:S(2)}) collective-permute-start(bf16[96,768]{1,0:T(8,128)(2,1)} %fusion.18), channel_id=1, source_target_pairs={{0,8},{1,9},{2,10},{3,11},{4,12},{5,13},{6,14},{7,15},{8,0},{9,1},... | collective-permute-start | bytes 442376 | tf_op jit(solution)/shard_map/ppermute | solution.py:752
  400.6 19.3 %collective-permute-start.24 = (bf16[96,1536]{1,0:T(8,128)(2,1)}, bf16[96,1536]{1,0:T(8,128)(2,1)S(1)}, u32[]{:S(2)}, u32[]{:S(2)}) collective-permute-start(bf16[96,1536]{1,0:T(8,128)(2,1)} %dynamic-slice_bitcast_fusion.7), channel_id=1, source_target_pairs={{0,4},{1,5},{2,6},{3,7},{4,0},{5,1},{6,2},{7,3},{8,12},{9,13},{10,... | collective-permute-start | bytes 884744 | tf_op jit(solution)/shard_map/ppermute | solution.py:752
  410.1 12.1 %collective-permute-start.25 = (bf16[192,768]{1,0:T(8,128)(2,1)}, bf16[192,768]{1,0:T(8,128)(2,1)S(1)}, u32[]{:S(2)}, u32[]{:S(2)}) collective-permute-start(bf16[192,768]{1,0:T(8,128)(2,1)} %bitcast.441), channel_id=1, source_target_pairs={{0,4},{1,5},{2,6},{3,7},{4,0},{5,1},{6,2},{7,3},{8,12},{9,13},{10,... | collective-permute-start | bytes 884744 | tf_op jit(solution)/shard_map/ppermute | solution.py:752
  412.2 35.1 %collective-permute-start.33 = (bf16[48,1536]{1,0:T(8,128)(2,1)S(1)}, bf16[48,1536]{1,0:T(8,128)(2,1)S(1)}, u32[]{:S(2)}, u32[]{:S(2)}) collective-permute-start(bf16[48,1536]{1,0:T(8,128)(2,1)S(1)} %copy-done.56), channel_id=1, source_target_pairs={{0,8},{1,9},{2,10},{3,11},{4,12},{5,13},{6,14},{7,15},{8,0},{9,1},... | collective-permute-start | bytes 442376 | tf_op jit(solution)/shard_map/ppermute | solution.py:752
  414.5 21.7 %collective-permute-start.29 = (bf16[140,768]{1,0:T(8,128)(2,1)S(1)}, bf16[140,768]{1,0:T(8,128)(2,1)S(1)}, u32[]{:S(2)}, u32[]{:S(2)}) collective-permute-start(bf16[140,768]{1,0:T(8,128)(2,1)S(1)} %pad_maximum_fusion), channel_id=1, source_target_pairs={{0,1},{1,0},{2,3},{3,2},{4,5},{5,4},{6,7},{7,6},{8,9},{9,8},{10,11... | collective-permute-start | bytes 645128 | tf_op jit(solution)/shard_map/ppermute | solution.py:752
  417.6 13.2 %collective-permute-start.26 = (bf16[48,1536]{1,0:T(8,128)(2,1)S(1)}, bf16[48,1536]{1,0:T(8,128)(2,1)S(1)}, u32[]{:S(2)}, u32[]{:S(2)}) collective-permute-start(bf16[48,1536]{1,0:T(8,128)(2,1)S(1)} %dynamic-slice_bitcast_fusion.14), channel_id=1, source_target_pairs={{0,8},{1,9},{2,10},{3,11},{4,12},{5,13},{6,14},{7,15},{8,0},{9,1},... | collective-permute-start | bytes 442376 | tf_op jit(solution)/shard_map/ppermute | solution.py:752
  420.0 14.6 %collective-permute-start.27 = (bf16[192,1536]{1,0:T(8,128)(2,1)S(1)}, bf16[192,1536]{1,0:T(8,128)(2,1)S(1)}, u32[]{:S(2)}, u32[]{:S(2)}) collective-permute-start(bf16[192,1536]{1,0:T(8,128)(2,1)S(1)} %dynamic-slice_bitcast_fusion), channel_id=1, source_target_pairs={{0,2},{1,3},{2,0},{3,1},{4,6},{5,7},{6,4},{7,5},{8,10},{9,11},{10,... | collective-permute-start | bytes 1769480 | tf_op jit(solution)/shard_map/ppermute | solution.py:752
  422.3 14.8 %collective-permute-start.30 = (bf16[48,1536]{1,0:T(8,128)(2,1)S(1)}, bf16[48,1536]{1,0:T(8,128)(2,1)S(1)}, u32[]{:S(2)}, u32[]{:S(2)}) collective-permute-start(bf16[48,1536]{1,0:T(8,128)(2,1)S(1)} %dynamic-slice_bitcast_fusion.13), channel_id=1, source_target_pairs={{0,8},{1,9},{2,10},{3,11},{4,12},{5,13},{6,14},{7,15},{8,0},{9,1},... | collective-permute-start | bytes 442376 | tf_op jit(solution)/shard_map/ppermute | solution.py:752
  430.8 14.9 %collective-permute-start.32 = (bf16[192,768]{1,0:T(8,128)(2,1)S(1)}, bf16[192,768]{1,0:T(8,128)(2,1)S(1)}, u32[]{:S(2)}, u32[]{:S(2)}) collective-permute-start(bf16[192,768]{1,0:T(8,128)(2,1)S(1)} %bitcast.443), channel_id=1, source_target_pairs={{0,4},{1,5},{2,6},{3,7},{4,0},{5,1},{6,2},{7,3},{8,12},{9,13},{10,... | collective-permute-start | bytes 884744 | tf_op jit(solution)/shard_map/ppermute | solution.py:752
  434.6 50.6 %collective-permute-start.42 = (bf16[384,768]{1,0:T(8,128)(2,1)S(1)}, bf16[384,768]{1,0:T(8,128)(2,1)S(1)}, u32[]{:S(2)}, u32[]{:S(2)}) collective-permute-start(bf16[384,768]{1,0:T(8,128)(2,1)S(1)} %bitcast.403), channel_id=1, source_target_pairs={{0,2},{1,3},{2,0},{3,1},{4,6},{5,7},{6,4},{7,5},{8,10},{9,11},{10,... | collective-permute-start | bytes 1769480 | tf_op jit(solution)/shard_map/ppermute | solution.py:752
  437.1 14.7 %collective-permute-start.34 = (bf16[96,1536]{1,0:T(8,128)(2,1)S(1)}, bf16[96,1536]{1,0:T(8,128)(2,1)S(1)}, u32[]{:S(2)}, u32[]{:S(2)}) collective-permute-start(bf16[96,1536]{1,0:T(8,128)(2,1)S(1)} %dynamic-slice_bitcast_fusion.6), channel_id=1, source_target_pairs={{0,4},{1,5},{2,6},{3,7},{4,0},{5,1},{6,2},{7,3},{8,12},{9,13},{10,... | collective-permute-start | bytes 884744 | tf_op jit(solution)/shard_map/ppermute | solution.py:752
  445.7 13.4 %collective-permute-start.36 = (bf16[96,1536]{1,0:T(8,128)(2,1)S(1)}, bf16[96,1536]{1,0:T(8,128)(2,1)S(1)}, u32[]{:S(2)}, u32[]{:S(2)}) collective-permute-start(bf16[96,1536]{1,0:T(8,128)(2,1)S(1)} %bitcast.445), channel_id=1, source_target_pairs={{0,4},{1,5},{2,6},{3,7},{4,0},{5,1},{6,2},{7,3},{8,12},{9,13},{10,... | collective-permute-start | bytes 884744 | tf_op jit(solution)/shard_map/ppermute | solution.py:752
  447.3 13.2 %collective-permute-start.37 = (bf16[48,1536]{1,0:T(8,128)(2,1)S(1)}, bf16[48,1536]{1,0:T(8,128)(2,1)S(1)}, u32[]{:S(2)}, u32[]{:S(2)}) collective-permute-start(bf16[48,1536]{1,0:T(8,128)(2,1)S(1)} %fusion.15), channel_id=1, source_target_pairs={{0,8},{1,9},{2,10},{3,11},{4,12},{5,13},{6,14},{7,15},{8,0},{9,1},... | collective-permute-start | bytes 442376 | tf_op jit(solution)/shard_map/ppermute | solution.py:752
  451.8 36.3 %collective-permute-start.43 = (bf16[96,1536]{1,0:T(8,128)(2,1)S(1)}, bf16[96,1536]{1,0:T(8,128)(2,1)S(1)}, u32[]{:S(2)}, u32[]{:S(2)}) collective-permute-start(bf16[96,1536]{1,0:T(8,128)(2,1)S(1)} %bitcast.447), channel_id=1, source_target_pairs={{0,2},{1,3},{2,0},{3,1},{4,6},{5,7},{6,4},{7,5},{8,10},{9,11},{10,... | collective-permute-start | bytes 884744 | tf_op jit(solution)/shard_map/ppermute | solution.py:752
  455.0 33.4 %collective-permute-start.44 = (bf16[384,768]{1,0:T(8,128)(2,1)S(1)}, bf16[384,768]{1,0:T(8,128)(2,1)S(1)}, u32[]{:S(2)}, u32[]{:S(2)}) collective-permute-start(bf16[384,768]{1,0:T(8,128)(2,1)S(1)} %bitcast.405), channel_id=1, source_target_pairs={{0,2},{1,3},{2,0},{3,1},{4,6},{5,7},{6,4},{7,5},{8,10},{9,11},{10,... | collective-permute-start | bytes 1769480 | tf_op jit(solution)/shard_map/ppermute | solution.py:752
  460.5 17.6 %collective-permute-start.40 = (bf16[96,1536]{1,0:T(8,128)(2,1)S(1)}, bf16[96,1536]{1,0:T(8,128)(2,1)S(1)}, u32[]{:S(2)}, u32[]{:S(2)}) collective-permute-start(bf16[96,1536]{1,0:T(8,128)(2,1)S(1)} %bitcast.449), channel_id=1, source_target_pairs={{0,4},{1,5},{2,6},{3,7},{4,0},{5,1},{6,2},{7,3},{8,12},{9,13},{10,... | collective-permute-start | bytes 884744 | tf_op jit(solution)/shard_map/ppermute | solution.py:752
  478.1 22.5 %collective-permute-start.46 = (bf16[192,1536]{1,0:T(8,128)(2,1)S(1)}, bf16[192,1536]{1,0:T(8,128)(2,1)S(1)}, u32[]{:S(2)}, u32[]{:S(2)}) collective-permute-start(bf16[192,1536]{1,0:T(8,128)(2,1)S(1)} %bitcast.407), channel_id=1, source_target_pairs={{0,2},{1,3},{2,0},{3,1},{4,6},{5,7},{6,4},{7,5},{8,10},{9,11},{10,... | collective-permute-start | bytes 1769480 | tf_op jit(solution)/shard_map/ppermute | solution.py:752
  484.7 14.0 %collective-permute-start.45 = (bf16[96,1536]{1,0:T(8,128)(2,1)S(1)}, bf16[96,1536]{1,0:T(8,128)(2,1)S(1)}, u32[]{:S(2)}, u32[]{:S(2)}) collective-permute-start(bf16[96,1536]{1,0:T(8,128)(2,1)S(1)} %bitcast.439), channel_id=1, source_target_pairs={{0,4},{1,5},{2,6},{3,7},{4,0},{5,1},{6,2},{7,3},{8,12},{9,13},{10,... | collective-permute-start | bytes 884744 | tf_op jit(solution)/shard_map/ppermute | solution.py:752
  485.2 17.8 %collective-permute-start.47 = (bf16[140,768]{1,0:T(8,128)(2,1)S(1)}, bf16[140,768]{1,0:T(8,128)(2,1)S(1)}, u32[]{:S(2)}, u32[]{:S(2)}) collective-permute-start(bf16[140,768]{1,0:T(8,128)(2,1)S(1)} %add_convert_fusion.7), channel_id=1, source_target_pairs={{0,8},{1,9},{2,10},{3,11},{4,12},{5,13},{6,14},{7,15},{8,0},{9,1},... | collective-permute-start | bytes 645128 | tf_op jit(solution)/shard_map/ppermute | solution.py:752
  488.1 16.3 %collective-permute-start.48 = (bf16[768,768]{1,0:T(8,128)(2,1)S(1)}, bf16[768,768]{1,0:T(8,128)(2,1)S(1)}, u32[]{:S(2)}, u32[]{:S(2)}) collective-permute-start(bf16[768,768]{1,0:T(8,128)(2,1)S(1)} %bitcast.349), channel_id=1, source_target_pairs={{0,1},{1,0},{2,3},{3,2},{4,5},{5,4},{6,7},{7,6},{8,9},{9,8},{10,11... | collective-permute-start | bytes 3538952 | tf_op jit(solution)/shard_map/ppermute | solution.py:752
  488.4 21.0 %collective-permute-start.50 = (bf16[192,1536]{1,0:T(8,128)(2,1)S(1)}, bf16[192,1536]{1,0:T(8,128)(2,1)S(1)}, u32[]{:S(2)}, u32[]{:S(2)}) collective-permute-start(bf16[192,1536]{1,0:T(8,128)(2,1)S(1)} %bitcast.411), channel_id=1, source_target_pairs={{0,4},{1,5},{2,6},{3,7},{4,0},{5,1},{6,2},{7,3},{8,12},{9,13},{10,... | collective-permute-start | bytes 1769480 | tf_op jit(solution)/shard_map/ppermute | solution.py:752
  500.7 16.1 %collective-permute-start.51 = (bf16[192,1536]{1,0:T(8,128)(2,1)S(1)}, bf16[192,1536]{1,0:T(8,128)(2,1)S(1)}, u32[]{:S(2)}, u32[]{:S(2)}) collective-permute-start(bf16[192,1536]{1,0:T(8,128)(2,1)S(1)} %bitcast.409), channel_id=1, source_target_pairs={{0,2},{1,3},{2,0},{3,1},{4,6},{5,7},{6,4},{7,5},{8,10},{9,11},{10,... | collective-permute-start | bytes 1769480 | tf_op jit(solution)/shard_map/ppermute | solution.py:752
  503.0 26.0 %collective-permute-start.52 = (bf16[192,1536]{1,0:T(8,128)(2,1)S(1)}, bf16[192,1536]{1,0:T(8,128)(2,1)S(1)}, u32[]{:S(2)}, u32[]{:S(2)}) collective-permute-start(bf16[192,1536]{1,0:T(8,128)(2,1)S(1)} %bitcast.413), channel_id=1, source_target_pairs={{0,2},{1,3},{2,0},{3,1},{4,6},{5,7},{6,4},{7,5},{8,10},{9,11},{10,... | collective-permute-start | bytes 1769480 | tf_op jit(solution)/shard_map/ppermute | solution.py:752
  504.4 34.7 %collective-permute-start.53 = (bf16[384,1536]{1,0:T(8,128)(2,1)}, bf16[384,1536]{1,0:T(8,128)(2,1)}, u32[]{:S(2)}, u32[]{:S(2)}) collective-permute-start(bf16[384,1536]{1,0:T(8,128)(2,1)} %bitcast.149.own_a), channel_id=1, source_target_pairs={{0,1},{1,0},{2,3},{3,2},{4,5},{5,4},{6,7},{7,6},{8,9},{9,8},{10,11... | collective-permute-start | bytes 3538952 | tf_op jit(solution)/shard_map/ppermute | solution.py:752
  509.4 29.6 %collective-permute-start.54 = (bf16[384,1536]{1,0:T(8,128)(2,1)S(1)}, bf16[384,1536]{1,0:T(8,128)(2,1)}, u32[]{:S(2)}, u32[]{:S(2)}) collective-permute-start(bf16[384,1536]{1,0:T(8,128)(2,1)S(1)} %bitcast.347), channel_id=1, source_target_pairs={{0,1},{1,0},{2,3},{3,2},{4,5},{5,4},{6,7},{7,6},{8,9},{9,8},{10,11... | collective-permute-start | bytes 3538952 | tf_op jit(solution)/shard_map/ppermute | solution.py:752
  516.8 28.3 %collective-permute-start.55 = (bf16[384,1536]{1,0:T(8,128)(2,1)S(1)}, bf16[384,1536]{1,0:T(8,128)(2,1)}, u32[]{:S(2)}, u32[]{:S(2)}) collective-permute-start(bf16[384,1536]{1,0:T(8,128)(2,1)S(1)} %bitcast.345), channel_id=1, source_target_pairs={{0,1},{1,0},{2,3},{3,2},{4,5},{5,4},{6,7},{7,6},{8,9},{9,8},{10,11... | collective-permute-start | bytes 3538952 | tf_op jit(solution)/shard_map/ppermute | solution.py:752
  529.1 16.0 %collective-permute-start.56 = (bf16[384,1536]{1,0:T(8,128)(2,1)S(1)}, bf16[384,1536]{1,0:T(8,128)(2,1)}, u32[]{:S(2)}, u32[]{:S(2)}) collective-permute-start(bf16[384,1536]{1,0:T(8,128)(2,1)S(1)} %bitcast.343), channel_id=1, source_target_pairs={{0,1},{1,0},{2,3},{3,2},{4,5},{5,4},{6,7},{7,6},{8,9},{9,8},{10,11... | collective-permute-start | bytes 3538952 | tf_op jit(solution)/shard_map/ppermute | solution.py:752
  (77 other events, 505.3 us)

commit v6 on v5

--- a/solution.py
+++ b/solution.py
@@ -21,11 +21,12 @@
 F32 = jnp.float32
 QROWS = NQ * QLEN
 SLAB = 256
-FFBLOCK = 768
+FFBLOCK = 1536
 VMEM_LIMIT = 56 * 1024 * 1024
 NEG = -1e30
 GRAD_STEPS = 2
 SMALL_VMEM = 26 * 1024 * 1024
+SLAB_VMEM = VMEM_LIMIT
 FLOPS_FFN = 12_000_000_000
 FLOPS_ATTN = 20_000_000_000
 
@@ -110,9 +111,8 @@
     return kernel
 
 
-def attn_fwd_live(micro, info, hid, wq, wk, wv, bq, bv, wm, bm, gain, shift, *rest):
-    x_out, joined_out, lse_out, ctx_out, hid_out, n_out, inv_out, sq_out, acc, qcode, kcode, otr, vtr = rest[-13:]
-    g = pl.program_id(0)
+def attn_fwd_live(g, count, micro, info, hid, wq, wk, wv, bq, bv, wm, bm, gain, shift, *rest):
+    x_out, joined_out, lse_out, ctx_out, hid_out, n_out, inv_out, sq_out, acc, qcode, kcode, otr, vtr = rest
     rows = hid.shape[0]
 
     @pl.when(g == 0)
@@ -151,7 +151,7 @@
     ctx_out[...] = ctx
     acc[...] += dot_nn(ctx, wm[...])
 
-    @pl.when(g == pl.num_programs(0) - 1)
+    @pl.when(g == count - 1)
     def _():
         b1 = acc[...] + bm[...]
         x32 = hid[...].astype(F32)
@@ -162,55 +162,6 @@
         mask = usable_rows(info, micro, rows)
         sq_out[0:1, :] = jnp.sum(mask * x32 * x32, axis=0, keepdims=True)
         sq_out[1:2, :] = jnp.sum(mask * b1 * b1, axis=0, keepdims=True)
-
-
-def attn_forward(phase, micros, info, source, weights, old):
-    (wa, ba, wm, bm, gains, shifts) = weights
-    section, micro = phase // micros, phase % micros
-    width = source.shape[1]
-    rows = source.shape[0] // micros if section == 0 else source.shape[0]
-    place = micro if section == 0 else 0
-    steps = width // SLAB
-    slot = lambda i: slot_of(i, section, micro, micros)
-    at = lambda g, i: step_of(i, section, g)
-    one = lambda *shape: pl.BlockSpec(shape, lambda g, i: (0,) * len(shape))
-    in_specs = [
-        pl.BlockSpec((rows, width), lambda g, i: (place, 0)),
-        pl.BlockSpec((width, SLAB), lambda g, i: (0, at(g, i))),
-        pl.BlockSpec((width, SLAB), lambda g, i: (0, steps + at(g, i))),
-        pl.BlockSpec((width, SLAB), lambda g, i: (0, 2 * steps + at(g, i))),
-        pl.BlockSpec((1, SLAB), lambda g, i: (0, at(g, i))),
-        pl.BlockSpec((1, SLAB), lambda g, i: (0, steps + at(g, i))),
-        pl.BlockSpec((SLAB, width), lambda g, i: (at(g, i), 0)),
-        one(1, width),
-        one(1, width),
-        one(1, width),
-    ]
-    args = [source, wa, wa, wa, ba, ba, wm, bm, gains[0:1], shifts[0:1]]
-    slots = micros + 1
-    rows_at = lambda shape, kind: ((slots,) + shape, kind, (None,) + shape, lambda g, i: (slot(i), 0, 0))
-    shapes = [
-        rows_at((rows, width), BF),
-        ((slots, steps, rows, 3 * SLAB), BF, (None, None, rows, 3 * SLAB), lambda g, i: (slot(i), at(g, i), 0, 0)),
-        ((slots, steps, 8, rows), F32, (None, None, 8, rows), lambda g, i: (slot(i), at(g, i), 0, 0)),
-        ((slots, rows, width), BF, (None, rows, SLAB), lambda g, i: (slot(i), 0, at(g, i))),
-        rows_at((rows, width), BF),
-        rows_at((rows, width), BF),
-        rows_at((rows, 1), F32),
-        rows_at((8, width), F32),
-    ]
-    return call(
-        live_only(attn_fwd_live, section, micro),
-        steps, info, args, in_specs, shapes, old,
-        [
-            pltpu.VMEM((rows, width), F32),
-            pltpu.VMEM((rows, 128), BF),
-            pltpu.VMEM((rows, 128), BF),
-            pltpu.VMEM((SLAB, rows), F32),
-            pltpu.VMEM((SLAB, rows), BF),
-        ],
-        flops=FLOPS_ATTN,
-    )
 
 
 def call(body, steps, info, args, in_specs, shapes, old, scratch, flops, limit=VMEM_LIMIT):
@@ -237,9 +188,8 @@
     )(info, *args)
 
 
-def ffn_fwd_live(micro, info, hid, we, be, wr, br, gain, shift, *rest):
-    act_out, slope_out, out_all, n_out, inv_out, sq_out, send_out, acc = rest[-8:]
-    j = pl.program_id(0)
+def ffn_fwd_live(j, count, micro, info, hid, we, be, wr, br, gain, shift, *rest):
+    act_out, slope_out, out_all, n_out, inv_out, sq_out, send_out, acc = rest
     rows = hid.shape[0]
 
     @pl.when(j == 0)
@@ -253,7 +203,7 @@
     slope_out[...] = slope.astype(BF)
     acc[...] += dot_nn(active, wr[...])
 
-    @pl.when(j == pl.num_programs(0) - 1)
+    @pl.when(j == count - 1)
     def _():
         b2 = acc[...] + br[...]
         n, inv = norm_rows(hid[...].astype(F32) + b2)
@@ -266,28 +216,64 @@
         sq_out[0:1, :] = jnp.sum(mask * b2 * b2, axis=0, keepdims=True)
 
 
-def ffn_forward(phase, micros, info, hidden, weights, old):
-    (we, be, wr, br, gains, shifts) = weights
+def layer_fwd_live(first, second, micro, info, *refs):
+    attn_in, ffn_in = refs[:10], refs[10:16]
+    attn_out, ffn_out = refs[-20:-12], refs[-12:-5]
+    acc, qcode, kcode, otr, vtr = refs[-5:]
+    g = pl.program_id(0)
+
+    @pl.when(g < first)
+    def _():
+        attn_fwd_live(g, first, micro, info, *attn_in, *attn_out, acc, qcode, kcode, otr, vtr)
+
+    @pl.when(g >= first)
+    def _():
+        ffn_fwd_live(g - first, second, micro, info, attn_out[4], *ffn_in, *ffn_out, acc)
+
+
+def layer_forward(phase, micros, info, source, weights, old):
+    (wa, ba, wm, bm, we, be, wr, br, gains, shifts) = weights
     section, micro = phase // micros, phase % micros
-    slots, rows, width = hidden.shape
-    ff = we.shape[1]
-    steps = ff // FFBLOCK
+    width, ff = we.shape
+    rows = source.shape[0] // micros if section == 0 else source.shape[0]
+    place = micro if section == 0 else 0
+    first, second = width // SLAB, ff // FFBLOCK
     slot = lambda i: slot_of(i, section, micro, micros)
-    at = lambda g, i: step_of(i, section, g)
+    at = lambda g, i: step_of(i, section, jnp.minimum(g, first - 1))
+    on = lambda g, i: step_of(i, section, jnp.maximum(g - first, 0))
     one = lambda *shape: pl.BlockSpec(shape, lambda g, i: (0,) * len(shape))
     in_specs = [
-        pl.BlockSpec((None, rows, width), lambda g, i: (slot(i), 0, 0)),
-        pl.BlockSpec((width, FFBLOCK), lambda g, i: (0, at(g, i))),
-        pl.BlockSpec((1, FFBLOCK), lambda g, i: (0, at(g, i))),
-        pl.BlockSpec((FFBLOCK, width), lambda g, i: (at(g, i), 0)),
+        pl.BlockSpec((rows, width), lambda g, i: (place, 0)),
+        pl.BlockSpec((width, SLAB), lambda g, i: (0, at(g, i))),
+        pl.BlockSpec((width, SLAB), lambda g, i: (0, first + at(g, i))),
+        pl.BlockSpec((width, SLAB), lambda g, i: (0, 2 * first + at(g, i))),
+        pl.BlockSpec((1, SLAB), lambda g, i: (0, at(g, i))),
+        pl.BlockSpec((1, SLAB), lambda g, i: (0, first + at(g, i))),
+        pl.BlockSpec((SLAB, width), lambda g, i: (at(g, i), 0)),
+        one(1, width),
+        one(1, width),
+        one(1, width),
+        pl.BlockSpec((width, FFBLOCK), lambda g, i: (0, on(g, i))),
+        pl.BlockSpec((1, FFBLOCK), lambda g, i: (0, on(g, i))),
+        pl.BlockSpec((FFBLOCK, width), lambda g, i: (on(g, i), 0)),
         one(1, width),
         one(1, width),
         one(1, width),
     ]
-    args = [hidden, we, be, wr, br, gains[1:2], shifts[1:2]]
+    args = [source, wa, wa, wa, ba, ba, wm, bm, gains[0:1], shifts[0:1]]
+    args += [we, be, wr, br, gains[1:2], shifts[1:2]]
+    slots = micros + 1
     rows_at = lambda shape, kind: ((slots,) + shape, kind, (None,) + shape, lambda g, i: (slot(i), 0, 0))
-    wide = ((slots, rows, ff), BF, (None, rows, FFBLOCK), lambda g, i: (slot(i), 0, at(g, i)))
+    wide = ((slots, rows, ff), BF, (None, rows, FFBLOCK), lambda g, i: (slot(i), 0, on(g, i)))
     shapes = [
+        rows_at((rows, width), BF),
+        ((slots, first, rows, 3 * SLAB), BF, (None, None, rows, 3 * SLAB), lambda g, i: (slot(i), at(g, i), 0, 0)),
+        ((slots, first, 8, rows), F32, (None, None, 8, rows), lambda g, i: (slot(i), at(g, i), 0, 0)),
+        ((slots, rows, width), BF, (None, rows, SLAB), lambda g, i: (slot(i), 0, at(g, i))),
+        rows_at((rows, width), BF),
+        rows_at((rows, width), BF),
+        rows_at((rows, 1), F32),
+        rows_at((8, width), F32),
         wide,
         wide,
         rows_at((rows, width), BF),
@@ -297,10 +283,16 @@
         ((rows, width), BF, (rows, width), lambda g, i: (0, 0)),
     ]
     return call(
-        live_only(ffn_fwd_live, section, micro),
-        steps, info, args, in_specs, shapes, old,
-        [pltpu.VMEM((rows, width), F32)],
-        flops=FLOPS_FFN,
+        live_only(functools.partial(layer_fwd_live, first, second), section, micro),
+        first + second, info, args, in_specs, shapes, old,
+        [
+            pltpu.VMEM((rows, width), F32),
+            pltpu.VMEM((rows, 128), BF),
+            pltpu.VMEM((rows, 128), BF),
+            pltpu.VMEM((SLAB, rows), F32),
+            pltpu.VMEM((SLAB, rows), BF),
+        ],
+        flops=FLOPS_FFN + FLOPS_ATTN,
     )
 
 
@@ -360,14 +352,13 @@
     return loss, grad_embed.astype(BF)
 
 
-def ffn_bwd_live(with_loss, micros, grad_scale, micro, info, *refs):
+def ffn_bwd_live(j, count, with_loss, micros, grad_scale, micro, info, *refs):
     if with_loss:
         out_all, wc = refs[:2]
     else:
         rec = refs[0]
     n2, inv2, gain2, slope, wr, we, n1, inv1, gain1 = refs[2 if with_loss else 1 :][:9]
-    two_out, inner_out, one_out, emb_out, small_out, ff_out, resid_out, acc, resid = refs[-9:]
-    j = pl.program_id(0)
+    two_out, inner_out, one_out, emb_out, small_out, ff_out, acc, resid = refs[-8:]
 
     @pl.when(j == 0)
     def _():
@@ -395,28 +386,26 @@
     ff_out[0:1, :] = column_sum(d_inner.astype(F32))
     acc[...] += dot_nt(d_inner, we[...])
 
-    @pl.when(j == pl.num_programs(0) - 1)
+    @pl.when(j == count - 1)
     def _():
         upstream = resid[...] + acc[...]
         n = n1[...].astype(F32)
         small_out[3:4, :] = column_sum(upstream * n)
         small_out[4:5, :] = column_sum(upstream)
         d_one = norm_rows_back(upstream, n, inv1[...], gain1[...])
-        resid_out[...] = d_one
+        resid[...] = d_one
         d_one_b = d_one.astype(BF)
         one_out[...] = d_one_b
         small_out[5:6, :] = column_sum(d_one_b.astype(F32))
 
 
-def ffn_backward(phase, micros, grad_scale, info, received, kept, weights, old):
+def ffn_bwd_parts(section, micro, micros, received, kept, weights, step):
     (out_all, n2, inv2, slope, n1, inv1) = kept
     (wc, gains, wr, we) = weights
-    section, micro = 1 - phase // micros, phase % micros
     slots, rows, width = out_all.shape
     ff = we.shape[1]
-    steps = ff // FFBLOCK
     slot = lambda i: slot_of(i, section, micro, micros)
-    at = lambda g, i: step_of(i, section, g)
+    at = lambda g, i: step_of(i, section, step(g))
     one = lambda *shape: pl.BlockSpec(shape, lambda g, i: (0,) * len(shape))
     at_slot = lambda *shape: pl.BlockSpec((None,) + shape, lambda g, i: (slot(i), 0, 0))
     if section == 1:
@@ -445,24 +434,30 @@
         rows_at((rows, wc.shape[1]), BF),
         rows_at((8, width), F32),
         ((slots, 8, ff), F32, (None, 8, FFBLOCK), lambda g, i: (slot(i), 0, at(g, i))),
-        ((rows, width), F32, (rows, width), lambda g, i: (0, 0)),
     ]
+    return in_specs, args, shapes, [pltpu.VMEM((rows, width), F32), pltpu.VMEM((rows, width), F32)]
+
+
+def ffn_backward(phase, micros, grad_scale, info, received, kept, weights, old):
+    section, micro = 1 - phase // micros, phase % micros
+    in_specs, args, shapes, scratch = ffn_bwd_parts(section, micro, micros, received, kept, weights, lambda g: g)
+    steps = weights[3].shape[1] // FFBLOCK
+
+    def body(micro, info, *refs):
+        ffn_bwd_live(pl.program_id(0), steps, section == 1, micros, grad_scale, micro, info, *refs)
+
     return call(
-        live_only(functools.partial(ffn_bwd_live, section == 1, micros, grad_scale), section, micro),
-        steps, info, args, in_specs, shapes, old,
-        [pltpu.VMEM((rows, width), F32), pltpu.VMEM((rows, width), F32)],
-        flops=FLOPS_FFN,
-    )
-
-
-def attn_bwd_live(with_send, micro, info, one_b, joined, lse, ctx, wm, *rest):
+        live_only(body, section, micro), steps, info, args, in_specs, shapes, old, scratch, flops=FLOPS_FFN
+    )
+
+
+def attn_bwd_live(g, count, with_send, micro, info, one_b, joined, lse, ctx, wm, *rest):
     qcode, kcode, dctx, delta, ktr, dqtr = rest[-6:]
     if with_send:
-        resid, wq, wk, wv = rest[:4]
-        dq_out, dk_out, dv_out, sum_out, send_out, acc = rest[-12:-6]
+        wq, wk, wv, resid, acc = rest[:5]
+        dq_out, dk_out, dv_out, sum_out, send_out = rest[-11:-6]
     else:
         dq_out, dk_out, dv_out, sum_out = rest[-10:-6]
-    g = pl.program_id(0)
 
     @pl.when(g == 0)
     def _():
@@ -519,29 +514,25 @@
         jnp.concatenate([dq, dk, dv], axis=1), jnp.concatenate([wq[...], wk[...], wv[...]], axis=1)
     )
 
-    @pl.when(g == pl.num_programs(0) - 1)
+    @pl.when(g == count - 1)
     def _():
         send_out[...] = (resid[...] + acc[...]).astype(BF)
 
 
-def attn_backward(phase, micros, info, resid, one_all, kept, weights, old, slabs=None):
+def attn_bwd_parts(section, micro, micros, shape, kept, weights, step):
     (joined, lse, ctx) = kept
     (wa, wm) = weights
-    section, micro = 1 - phase // micros, phase % micros
-    slots, rows, width = one_all.shape
+    slots, rows, width = shape
     count = width // SLAB
-    slabs = slabs or range(count)
-    with_send = section == 1
     slot = lambda i: slot_of(i, section, micro, micros)
-    at = lambda g, i: step_of(i, section, slabs[0] + g)
+    at = lambda g, i: step_of(i, section, step(g))
     in_specs = [
-        pl.BlockSpec((None, rows, width), lambda g, i: (slot(i), 0, 0)),
         pl.BlockSpec((None, None, rows, 3 * SLAB), lambda g, i: (slot(i), at(g, i), 0, 0)),
         pl.BlockSpec((None, None, 8, rows), lambda g, i: (slot(i), at(g, i), 0, 0)),
         pl.BlockSpec((None, rows, SLAB), lambda g, i: (slot(i), 0, at(g, i))),
         pl.BlockSpec((SLAB, width), lambda g, i: (at(g, i), 0)),
     ]
-    args = [one_all, joined, lse, ctx, wm]
+    args = [joined, lse, ctx, wm]
     slab = ((slots, rows, width), BF, (None, rows, SLAB), lambda g, i: (slot(i), 0, at(g, i)))
     shapes = [
         slab,
@@ -557,21 +548,69 @@
         pltpu.VMEM((SLAB, rows), BF),
         pltpu.VMEM((SLAB, rows), F32),
     ]
-    if with_send:
+    return in_specs, args, shapes, scratch
+
+
+def attn_backward(phase, micros, info, one_all, kept, weights, old, slabs):
+    section, micro = 1 - phase // micros, phase % micros
+    slots, rows, width = one_all.shape
+    in_specs, args, shapes, scratch = attn_bwd_parts(
+        section, micro, micros, one_all.shape, kept, weights, lambda g: slabs[0] + g
+    )
+    in_specs = [pl.BlockSpec((None, rows, width), lambda g, i: (slot_of(i, section, micro, micros), 0, 0))] + in_specs
+
+    def body(micro, info, *refs):
+        attn_bwd_live(pl.program_id(0), len(slabs), False, micro, info, *refs)
+
+    return call(
+        live_only(body, section, micro), len(slabs), info, [one_all] + args, in_specs, shapes, old, scratch,
+        flops=FLOPS_ATTN * len(slabs) * SLAB // width // 32, limit=SLAB_VMEM,
+    )
+
+
+def layer_backward(phase, micros, grad_scale, info, received, ffn_kept, attn_kept, weights, old):
+    (wc, gains, wr, we, wa, wm) = weights
+    section, micro = 1 - phase // micros, phase % micros
+    shape = ffn_kept[0].shape
+    _, rows, width = shape
+    first, second = we.shape[1] // FFBLOCK, width // SLAB
+    in_specs, args, shapes, scratch = ffn_bwd_parts(
+        section, micro, micros, received, ffn_kept, (wc, gains, wr, we), lambda g: jnp.minimum(g, first - 1)
+    )
+    step = lambda g: jnp.maximum(g - first, 0)
+    more = attn_bwd_parts(section, micro, micros, shape, attn_kept, (wa, wm), step)
+    count = len(args)
+    in_specs, args, shapes, scratch = in_specs + more[0], args + more[1], shapes + more[2], scratch + more[3]
+    sends = section == 1
+    if sends:
+        at = lambda g, i: step_of(i, section, step(g))
         in_specs += [
-            pl.BlockSpec((rows, width), lambda g, i: (0, 0)),
-            pl.BlockSpec((width, SLAB), lambda g, i: (0, at(g, i))),
-            pl.BlockSpec((width, SLAB), lambda g, i: (0, count + at(g, i))),
-            pl.BlockSpec((width, SLAB), lambda g, i: (0, 2 * count + at(g, i))),
+            pl.BlockSpec((width, SLAB), lambda g, i, k=k: (0, k * second + at(g, i))) for k in range(3)
         ]
-        args += [resid, wa, wa, wa]
+        args += [wa, wa, wa]
         shapes += [((rows, width), BF, (rows, width), lambda g, i: (0, 0))]
-        scratch = [pltpu.VMEM((rows, width), F32)] + scratch
+
+    def body(micro, info, *refs):
+        ffn_in, attn_in = refs[:count], refs[count : count + 4]
+        ins_q = refs[count + 4 : count + 7]
+        inner = refs[-6:]
+        acc, resid = refs[-8:-6]
+        ends = 11 if sends else 10
+        outs = refs[-8 - ends : -8]
+        g = pl.program_id(0)
+
+        @pl.when(g < first)
+        def _():
+            ffn_bwd_live(g, first, sends, micros, grad_scale, micro, info, *ffn_in, *outs[:6], acc, resid)
+
+        @pl.when(g >= first)
+        def _():
+            extra = ins_q + (resid, acc) if sends else ()
+            attn_bwd_live(g - first, second, sends, micro, info, outs[2], *attn_in, *extra, *outs[6:], *inner)
+
     return call(
-        live_only(functools.partial(attn_bwd_live, with_send), section, micro),
-        len(slabs), info, args, in_specs, shapes, old, scratch,
-        flops=FLOPS_ATTN * len(slabs) // count // (1 if with_send else 32),
-        limit=VMEM_LIMIT if with_send else SMALL_VMEM,
+        live_only(body, section, micro), first + second, info, args, in_specs, shapes, old, scratch,
+        flops=FLOPS_FFN + FLOPS_ATTN,
     )
 
 
@@ -585,7 +624,7 @@
     return bits
 
 
-def grad_call(body, steps, core, in_specs, args, out_shape, out_specs, flops, limit=SMALL_VMEM):
+def grad_call(body, steps, core, in_specs, args, out_shape, out_specs, flops, limit=VMEM_LIMIT):
     return pl.pallas_call(
         body,
         out_shape=out_shape,
@@ -600,38 +639,28 @@
     )(core, *args)
 
 
-def grad_half_body(by_rows, info, left, *refs):
-    rights = refs[: 1 if by_rows else 2]
-    bases, outs = refs[len(rights) : -2], refs[-2:]
-    turned = jnp.transpose(left[...])
-    tall = outs[0].shape[0]
-    for i, out in enumerate(outs):
-        total = dot_nn(turned[i * tall : i * tall + tall], rights[0][...]) if by_rows else dot_nn(turned, rights[i][...])
-        if bases:
-            total = total + bases[i][...].astype(F32)
-        out[...] = total.astype(BF)
-
-
-def grad_half(rows, micro, core, mine, left, right, by_rows, bases):
+def grad_half_body(info, left, right, *refs):
+    total = dot_nn(jnp.transpose(left[...]), right[...])
+    if len(refs) > 1:
+        total = total + refs[0][...].astype(F32)
+    refs[-1][...] = total.astype(BF)
+
+
+def grad_half(rows, micro, core, mine, left, right, base):
     tall, wide = left.shape[1] // 2, right.shape[1]
-    steps = GRAD_STEPS
-    half_of = lambda h: h[0] if mine else 1 - h[0]
-    left_spec = pl.BlockSpec((rows, tall), lambda s, h: (micro, half_of(h)))
-    if by_rows:
-        shape = (tall // 2, wide)
-        rights = [pl.BlockSpec((rows, wide // steps), lambda s, h: (micro, s))]
-    else:
-        shape = (tall, wide // 2)
-        rights = [
-            pl.BlockSpec((rows, wide // 2 // steps), lambda s, h, i=i: (micro, i * steps + s)) for i in range(2)
-        ]
-    spec = pl.BlockSpec((shape[0], shape[1] // steps), lambda s, h: (0, s))
-    args = [left] + [right] * len(rights) + list(bases or ())
-    in_specs = [left_spec] + rights + ([spec, spec] if bases else [])
-    out = jax.ShapeDtypeStruct(shape, BF)
+    block = wide // GRAD_STEPS
+    spec = pl.BlockSpec((tall, block), lambda s, h: (0, s))
+    in_specs = [
+        pl.BlockSpec((rows, tall), lambda s, h: (micro, h[0] if mine else 1 - h[0])),
+        pl.BlockSpec((rows, block), lambda s, h: (micro, s)),
+    ]
+    args = [left, right]
+    if base is not None:
+        in_specs += [spec]
+        args += [base]
     return grad_call(
-        functools.partial(grad_half_body, by_rows), steps, core, in_specs, args,
-        [out, out], [spec, spec], 2 * rows * tall * wide, VMEM_LIMIT,
+        grad_half_body, GRAD_STEPS, core, in_specs, args,
+        jax.ShapeDtypeStruct((tall, wide), BF), spec, 2 * rows * tall * wide, VMEM_LIMIT,
     )
 
 
@@ -677,41 +706,37 @@
     )
 
 
-def widen_body(info, own_a, own_b, other_a, other_b, *outs):
+def widen_body(info, *refs):
     step = pl.program_id(0)
-    for s, (a, b) in enumerate(((own_a, own_b), (other_a, other_b))):
+    count = 2 if len(refs) == 6 else 1
+    outs = refs[2 * count :]
+    for s in range(2):
 
         @pl.when(step == s)
-        def _(a=a, b=b):
-            parts = (a[...].astype(F32), b[...].astype(F32))
-            if len(outs) == 2:
-                width = outs[1].shape[1]
-                outs[1][...] = parts[0][:, :width]
-                slabs = [parts[0][:, width:]] + [
-                    parts[1][:, at : at + 3 * SLAB] for at in range(0, parts[1].shape[1], 3 * SLAB)
-                ]
-                for g, slab in enumerate(slabs):
-                    for kind in range(3):
-                        at = kind * width + g * SLAB
-                        outs[0][:, at : at + SLAB] = slab[:, kind * SLAB : kind * SLAB + SLAB]
-            elif outs[0].shape[1] == parts[0].shape[1]:
-                outs[0][: parts[0].shape[0]] = parts[0]
-                outs[0][parts[0].shape[0] :] = parts[1]
-            else:
-                outs[0][:, : parts[0].shape[1]] = parts[0]
-                outs[0][:, parts[0].shape[1] :] = parts[1]
+        def _(s=s):
+            parts = [ref[...].astype(F32) for ref in refs[s * count : s * count + count]]
+            if count == 1:
+                outs[0][...] = parts[0]
+                return
+            width = outs[1].shape[1]
+            outs[1][...] = parts[0][:, :width]
+            slabs = [parts[0][:, width:]] + [
+                parts[1][:, at : at + 3 * SLAB] for at in range(0, parts[1].shape[1], 3 * SLAB)
+            ]
+            for g, slab in enumerate(slabs):
+                for kind in range(3):
+                    at = kind * width + g * SLAB
+                    outs[0][:, at : at + SLAB] = slab[:, kind * SLAB : kind * SLAB + SLAB]
 
 
 def widened(core, own, other, out_shapes):
-    small = own[0].shape
-    piece_spec = pl.BlockSpec(small, lambda s, h: (0, 0))
     return pl.pallas_call(
         widen_body,
         out_shape=[jax.ShapeDtypeStruct(shape, F32) for shape in out_shapes],
         grid_spec=pltpu.PrefetchScalarGridSpec(
             num_scalar_prefetch=1,
             grid=(2,),
-            in_specs=[piece_spec] * 4,
+            in_specs=[pl.BlockSpec(one.shape, lambda s, h: (0, 0)) for one in own + other],
             out_specs=[
                 pl.BlockSpec((shape[0] // 2, shape[1]), lambda s, h: (jnp.where(s == 0, h[0], 1 - h[0]), 0))
                 for shape in out_shapes
@@ -723,13 +748,13 @@
 
 
 EXCHANGE = (
-    "SR", "KR", "R0", "SE", "R1", "KE", "E1", "S0", "R0", "E0", "PS", "PK", "R0", "E1", "R1", "P0", "S1",
-    "R1", "E1", "R0", "E0", "S2", "P0", "R1", "QS", "R0", "E1", "QK", "Q0", "E0", "R1", "P0", "R0", "E0",
-    "Q0", "V", "P0", "E0", "R1", "E1", "Q0", "V", "E0", "P0", "Q0", "Q0", "P0", "V", "R0", "E1", "R1", "Q0",
-    "E0", "V", "WR", "E1", "P0", "Q0", "WE", "WP",
+    "SR", "KR", "SE", "R", "KE", "E", "S0", "PS", "PK", "R", "S1", "E", "P", "R", "S2", "E", "QS", "R", "QK",
+    "P", "E", "Q", "R", "P", "E", "V", "Q", "P", "R", "V", "E", "Q", "P", "Q", "Q", "R", "P", "V", "Q", "E",
+    "WR", "V", "P", "Q", "WE", "WP",
 )
-ORDERS = {"R0": 0, "R1": 0, "E0": 0, "E1": 1, "P0": 0, "Q0": 0}
-WIDENED = {"WR": ("R0", "R1"), "WE": ("E0", "E1"), "WP": ("P0", "Q0")}
+ORDERS = {"R": 0, "E": 1, "P": 1, "Q": 0}
+WIDENED = {"WR": ("R",), "WE": ("E",), "WP": ("P", "Q")}
+KEEPERS = {"KR": ("R", "SR"), "KE": ("E", "SE"), "PK": ("P", "PS"), "QK": ("Q", "QS")}
 KERNELS = ("SR", "KR", "SE", "KE", "S0", "PS", "PK", "S1", "S2", "QS", "QK")
 
 
@@ -829,7 +854,7 @@
 def exchange_order(digits):
     if digits == 4:
         return EXCHANGE
-    rounds = ("R0", "R1", "E0", "E1", "P0", "Q0") * (2 * digits - 1)
+    rounds = ("R", "E", "P", "Q") * (2 * digits - 1)
     return KERNELS + rounds + ("V",) * digits + tuple(WIDENED)
 
 
@@ -874,55 +899,60 @@
     along_x_first = list(range(1, len(bits)))
     along_z_first = [2, 1] + list(range(3, len(bits)))
     orders = (along_x_first, along_z_first)
-    attn_weights = (wa, attend_bias, wm, mixing_bias, gains, shifts)
-    ffn_weights = (we, expand_bias, wr, reduce_bias, gains, shifts)
-    state = {"attn": None, "ffn": None, "attn_back": None, "ffn_back": None}
+    weights = (wa, attend_bias, wm, mixing_bias, we, expand_bias, wr, reduce_bias, gains, shifts)
+    state = {"fwd": None, "bwd": None}
     arriving, returning = {}, {}
 
     def forward(phase, after=()):
         source = hidden_in if phase < micros else arriving[phase - micros]
-        source = tied(source, *after)
-        attn = attn_forward(phase, micros, info, source, attn_weights, state["attn"])
-        old = state["ffn"]
-        ffn = ffn_forward(phase, micros, info, attn[4], ffn_weights, old and old[:6])
-        state["attn"], state["ffn"] = attn, ffn
+        old = state["fwd"]
+        state["fwd"] = layer_forward(
+            phase, micros, info, tied(source, *after), weights, old and old[:14]
+        )
         if phase < micros:
-            arriving[phase] = passed_along(ffn[6], "pipe", 1)
+            arriving[phase] = passed_along(state["fwd"][14], "pipe", 1)
+
+    def kept():
+        fwd = state["fwd"]
+        return (fwd[10], fwd[11], fwd[12], fwd[9], fwd[5], fwd[6]), (fwd[1], fwd[2], fwd[3])
+
+    def arrived(phase, after):
+        return None if phase < micros else tied(returning[phase - micros], *after)
+
+    def backward(phase, after=()):
+        old = state["bwd"]
+        state["bwd"] = layer_backward(
+            phase, micros, grad_scale, info, arrived(phase, after), *kept(),
+            (colbert_weight, gains, wr, we, wa, wm), old and old[:10],
+        )
+        if phase < micros:
+            returning[phase] = passed_along(state["bwd"][10], "pipe", -1)
 
     def backward_ffn(phase, after=()):
-        attn, ffn, old = state["attn"], state["ffn"], state["ffn_back"]
-        received = None if phase < micros else tied(returning[phase - micros], *after)
-        state["ffn_back"] = ffn_backward(
-            phase, micros, grad_scale, info, received,
-            (ffn[2], ffn[3], ffn[4], ffn[1], attn[5], attn[6]),
-            (colbert_weight, gains, wr, we), old and old[:6],
+        made = ffn_backward(
+            phase, micros, grad_scale, info, arrived(phase, after), kept()[0],
+            (colbert_weight, gains, wr, we), state["bwd"][:6],
         )
-
-    def backward_attn(phase, after=(), slabs=None):
-        attn, old, ffn_back = state["attn"], state["attn_back"], state["ffn_back"]
-        attn_back = attn_backward(
-            phase, micros, tied(info, *after), ffn_back[6], ffn_back[2], (attn[1], attn[2], attn[3]), (wa, wm),
-            old and old[:4], slabs,
+        state["bwd"] = list(made) + list(state["bwd"][6:10])
+
+    def backward_attn(phase, after, slabs):
+        old = state["bwd"]
+        made = attn_backward(
+            phase, micros, tied(info, *after), old[2], kept()[1], (wa, wm), old[6:10], slabs
         )
-        state["attn_back"] = attn_back
-        if phase < micros:
-            returning[phase] = passed_along(attn_back[4], "pipe", -1)
+        state["bwd"] = list(old[:6]) + list(made)
 
     for phase in range(micros):
         forward(phase)
     done = ()
     for phase in range(micros):
         forward(micros + phase, done)
-        backward_ffn(phase)
-        backward_attn(phase)
-        done = (state["attn_back"][3],)
-    for phase in range(micros, 2 * micros - 1):
-        backward_ffn(phase, done)
-        backward_attn(phase)
-        done = (state["attn_back"][3],)
-    inputs, joined, lse, context, hidden, unit_one, inv_one, squares_one = state["attn"]
-    active, slope, outputs, unit_two, inv_two, squares_two, _ = state["ffn"]
-    embeds, losses = state["ffn_back"][3], state["ffn_back"][4]
+        backward(phase)
+        done = (state["bwd"][9],)
+    fwd = state["fwd"]
+    inputs, context, hidden, squares_one = fwd[0], fwd[3], fwd[4], fwd[7]
+    active, outputs, squares_two = fwd[8], fwd[10], fwd[13]
+    embeds, losses = state["bwd"][3:5]
     squares = jnp.stack(
         [
             jnp.sum(squares_one[:micros, 0], axis=1),
@@ -931,14 +961,17 @@
         ],
         axis=1,
     )
-    after_back = state["attn_back"][3]
-    colbert = dot_tn(
-        flatten_rows(outputs[:micros]), flatten_rows(tied(embeds, after_back)[:micros])
-    ).astype(BF)
-    facts = tied(jnp.concatenate([squares, losses[:micros, 6, 0:1]], axis=1), after_back)
+    colbert = dot_tn(flatten_rows(outputs[:micros]), flatten_rows(embeds[:micros])).astype(BF)
+    facts = jnp.concatenate([squares, losses[:micros, 6, 0:1]], axis=1)
+    facts_down, colbert_down = passed_along(facts, "pipe", -1), passed_along(colbert, "pipe", -1)
+    done += (facts, colbert)
+    for phase in range(micros, 2 * micros - 1):
+        backward(phase, done)
+        done = (state["bwd"][9],)
     last = 2 * micros - 1
+    after_back = state["bwd"][9]
     slabs = tuple(range(width // SLAB))
-    ffn_back, attn_back = state["ffn_back"], state["attn_back"]
+    ffn_back, attn_back = state["bwd"][:6], state["bwd"][6:10]
     lefts = [flatten_rows(a) for a in (active, hidden, inputs, context)]
 
     bases = {}
@@ -949,25 +982,24 @@
         for mine in (0, 1):
             old = bases.get(mine, (None,) * 4)
             bases[mine] = (
-                grad_half(rows, micro, first_core, mine, lefts[0], d_two, True, old[0]),
-                grad_half(rows, micro, first_core, mine, lefts[1], d_inner, False, old[1]),
+                grad_half(rows, micro, first_core, mine, lefts[0], d_two, old[0]),
+                grad_half(rows, micro, first_core, mine, lefts[1], d_inner, old[1]),
                 grad_rest(rows, micro, first_core, mine, lefts[2], joined_grads, slabs[:1], lefts[3], d_one, old[2]),
                 grad_rest(rows, micro, first_core, mine, lefts[2], joined_grads, slabs[1:], None, None, old[3]),
             )
-    backward_ffn(last, (colbert, facts) + tuple(jax.tree.leaves(bases)))
+    backward_ffn(last, (facts_down, colbert_down) + tuple(jax.tree.leaves(bases)))
     bases = bases or {0: (None,) * 4, 1: (None,) * 4}
     micro = micros - 1
-    ffn_back = state["ffn_back"]
+    ffn_back = state["bwd"]
     d_two, d_inner, d_one = (flatten_rows(ffn_back[i]) for i in range(3))
     line = Sequence()
 
-    def half_of(mine, left, right, by_rows, which):
-        both = grad_half(rows, micro, line.after(core), mine, left, right, by_rows, bases[mine][which])
-        line.did(*both)
-        return both
+    def half_of(mine, left, right, which):
+        [one] = line.did(grad_half(rows, micro, line.after(core), mine, left, right, bases[mine][which]))
+        return one
 
     def rest_half(mine, some, which):
-        joined_grads = [flatten_rows(a) for a in state["attn_back"][:3]]
+        joined_grads = [flatten_rows(a) for a in state["bwd"][6:9]]
         extra = (lefts[3], d_one) if which == 2 else (None, None)
         [one] = line.did(
             grad_rest(rows, micro, line.after(core), mine, lefts[2], joined_grads, some, *extra, bases[mine][which])
@@ -976,34 +1008,33 @@
 
     def slab_back(slab):
         backward_attn(last, line.last, (slab,))
-        line.did(*state["attn_back"])
+        line.did(*state["bwd"][6:10])
 
     made, pieces, widths = {}, {}, {}
 
     def run_kernel(name):
         made[name] = {
-            "SR": lambda: half_of(0, lefts[0], d_two, True, 0),
-            "KR": lambda: half_of(1, lefts[0], d_two, True, 0),
-            "SE": lambda: half_of(0, lefts[1], d_inner, False, 1),
-            "KE": lambda: half_of(1, lefts[1], d_inner, False, 1),
-            "PS": lambda: [rest_half(0, slabs[:1], 2)],
-            "PK": lambda: [rest_half(1, slabs[:1], 2)],
-            "QS": lambda: [rest_half(0, slabs[1:], 3)],
-            "QK": lambda: [rest_half(1, slabs[1:], 3)],
+            "SR": lambda: half_of(0, lefts[0], d_two, 0),
+            "KR": lambda: half_of(1, lefts[0], d_two, 0),
+            "SE": lambda: half_of(0, lefts[1], d_inner, 1),
+            "KE": lambda: half_of(1, lefts[1], d_inner, 1),
+            "PS": lambda: rest_half(0, slabs[:1], 2),
+            "PK": lambda: rest_half(1, slabs[:1], 2),
+            "QS": lambda: rest_half(0, slabs[1:], 3),
+            "QK": lambda: rest_half(1, slabs[1:], 3),
             "S0": lambda: slab_back(slabs[0]),
             "S1": lambda: slab_back(slabs[1]),
             "S2": lambda: [slab_back(slab) for slab in slabs[2:]],
         }[name]()
 
     def small_sums():
-        small, small_ff, joined_sums = ffn_back[4], ffn_back[5], state["attn_back"][3]
+        small, small_ff, joined_sums = ffn_back[4], ffn_back[5], state["bwd"][9]
         small_sum = jnp.sum(small[:micros], axis=0)
         joined_sum = jnp.sum(joined_sums[:micros, :, 0], axis=0)
         attend_sum = jnp.concatenate(
             [joined_sum[:, :SLAB].reshape(-1), joined_sum[:, SLAB:].reshape(-1)]
         )
-        of_colbert = tied(colbert, *line.last)
-        of_colbert = jnp.where(section_id == 1, of_colbert, passed_along(of_colbert, "pipe", -1))
+        of_colbert = jnp.where(section_id == 1, colbert, colbert_down)
         parts = [
             small_sum[:6],
             attend_sum.reshape(2, width),
@@ -1012,11 +1043,14 @@
         ]
         return jnp.concatenate(parts).astype(BF)
 
-    senders = {"SR": ("R", "KR", 2), "SE": ("E", "KE", 2), "PS": ("P", "PK", 1), "QS": ("Q", "QK", 1)}
     for step in exchange_order(len(bits)):
+        if step == "V" and step not in pieces:
+            pieces[step] = Adder(line, small_sums(), bits)
         if step in pieces:
             pieces[step].take()
         elif step[0] == "W":
+            if step == "WE":
+                made["up"] = passed_along(line.after(facts), "pipe", 1)
             widths[step] = widened(
                 line.after(core), *ends_of_pieces([pieces[one] for one in WIDENED[step]]),
                 {"WR": [wr.shape], "WE": [we.shape], "WP": [wa.shape, wm.shape]}[step],
@@ -1024,17 +1058,11 @@
             line.did(*widths[step])
         else:
             run_kernel(step)
-            for send, (name, keep, count) in senders.items():
-                if keep == step:
-                    for i, (s, k) in enumerate(zip(made[send], made[keep])):
-                        one = name + str(i)
-                        pieces[one] = Piece(line, s, k, bits, orders[ORDERS[one]])
-            if step == "QK":
-                mine = line.after(facts)
-                made["up"], made["down"] = passed_along(mine, "pipe", 1), passed_along(mine, "pipe", -1)
-                pieces["V"] = Adder(line, small_sums(), bits)
+            if step in KEEPERS:
+                name, send = KEEPERS[step]
+                pieces[name] = Piece(line, made[send], made[step], bits, orders[ORDERS[name]])
     first = jnp.where(section_id == 0, facts, made["up"])
-    second = jnp.where(section_id == 0, made["down"], facts)
+    second = jnp.where(section_id == 0, facts_down, facts)
     [big_reduce], [big_expand], (big_attend, big_mixing) = (widths[one] for one in ("WR", "WE", "WP"))
     vector = pieces["V"].value
     vector = vector.astype(F32)

time: 560 us -> 523 us (0.934)
  local copies, waits for them, and re-layouts: 63.8 us -> 26.7 us
  Pallas kernels: 251 us -> 275 us
  starting transfers between devices: 65.3 us -> 54.4 us
  waiting for transfers between devices: 138 us -> 129 us
    unnamed x137 -> x45, local copies, waits for them, and re-layouts: 40.4 us -> 7.35 us
    pallas_call x16, Pallas kernels: 53.4 us -> 75.7 us  [grad_call(): pl.pallas_call(body, out_shape=out_shape, grid_spec=pltpu.PrefetchScalarG...]
    ppermute x52 -> x36, starting transfers between devices: 47.9 us -> 29.2 us  [swapped(): return lax.ppermute(array, axis, [(i, i ^ bit) for i in range(count)])]
    ppermute x7, waiting for transfers between devices: 48.5 us -> 40.1 us  [passed_along(): return lax.ppermute(array, axis, pairs)]
    ppermute x7, starting transfers between devices: 17.4 us -> 25.2 us  [passed_along(): return lax.ppermute(array, axis, pairs)]
    convert_element_type x27 -> x19, other arithmetic: 19.4 us -> 14.7 us  [sum_low(): return (kept.astype(F32) + got.astype(F32)).astype(BF)]
    pallas_call x18 -> x11, Pallas kernels: 182 us -> 186 us  [call(): pl.pallas_call(body, out_shape=[jax.ShapeDtypeStruct(s[0], s[1]) for s in...]
    ppermute x52 -> x36, waiting for transfers between devices: 89.9 us -> 89 us  [swapped(): return lax.ppermute(array, axis, [(i, i ^ bit) for i in range(count)])]
  transfers between devices with their start and end apart: 59 -> 43, of which waited for: 18 -> 15; matrix products, arithmetic and copies ran while one was open for 10% -> 9% of each run, Pallas kernels for 34% -> 42%
where the time goes in v6:
time: 523 us; the launch traced here: 514 us
  Pallas kernels  275 us (53%)
  waiting for transfers between devices  129 us (25%)
  starting transfers between devices  54.4 us (10%)
  local copies, waits for them, and re-layouts  26.7 us (5%)
  other arithmetic  25.2 us (5%)
    pallas_call x11, Pallas kernels, call(): pl.pallas_call(body, out_shape=[jax.ShapeDtypeStruct(s[0], s[1]) for s in...  186 us
    ppermute x36, waiting for transfers between devices, swapped(): return lax.ppermute(array, axis, [(i, i ^ bit) for i in range(count)])  89 us
    pallas_call x16, Pallas kernels, grad_call(): pl.pallas_call(body, out_shape=out_shape, grid_spec=pltpu.PrefetchScalarG...  75.7 us
    ppermute x7, waiting for transfers between devices, passed_along(): return lax.ppermute(array, axis, pairs)  40.1 us
    ppermute x36, starting transfers between devices, swapped(): return lax.ppermute(array, axis, [(i, i ^ bit) for i in range(count)])  29.2 us
    ppermute x7, starting transfers between devices, passed_along(): return lax.ppermute(array, axis, pairs)  25.2 us
    convert_element_type x19, other arithmetic, sum_low(): return (kept.astype(F32) + got.astype(F32)).astype(BF)  14.7 us
    pallas_call x3, Pallas kernels, widened(): pl.pallas_call(widen_body, out_shape=[jax.ShapeDtypeStruct(shape, F32) fo...  13.4 us
  transfers between devices with their start and end apart: 43, of which 15 were waited for; matrix products, arithmetic and copies ran while one was open for 9% of the time, Pallas kernels for 42%

profile of v6, /device:TPU:0, one launch (start us, length us, event | category | flops | bytes accessed | tf_op | source)
XLA Modules:
  0.0 514.3 jit_solution(12141238544876488546)
XLA Ops:
  4.1 32.6 %shard_map.237 = (bf16[3,640,768]{2,1,0:T(8,128)(2,1)}, bf16[3,3,640,768]{3,2,1,0:T(8,128)(2,1)}, f32[3,3,8,640]{3,2,1,0:T(8,128)}, bf16[3,640,768]{2,1,0:T(8,12...) custom-call(s32[17]{0:T(128)} %pad_add_fusion.info, ...), custom_call_target="tpu_custom_call" | custom-call | flops 32000000000 | bytes 20000000 | tf_op jit(solution)/shard_map/pallas_call | solution.py:173
  38.2 32.7 %shard_map.238 = (bf16[3,640,768]{2,1,0:T(8,128)(2,1)}, bf16[3,3,640,768]{3,2,1,0:T(8,128)(2,1)}, f32[3,3,8,640]{3,2,1,0:T(8,128)}, bf16[3,640,768]{2,1,0:T(8,12...) custom-call(s32[17]{0:T(128)} %pad_add_fusion.info, ...), custom_call_target="tpu_custom_call", output_to_operand_aliasing={{0}: (17, {}), {1}: (18, {}), {2}: (19, {}), {3}: (20, {}),... | custom-call | flops 32000000000 | bytes 20000000 | tf_op jit(solution)/shard_map/pallas_call | solution.py:173
  73.5 9.7 %shard_map.239 = (bf16[3,640,768]{2,1,0:T(8,128)(2,1)}, bf16[3,3,640,768]{3,2,1,0:T(8,128)(2,1)}, f32[3,3,8,640]{3,2,1,0:T(8,128)}, bf16[3,640,768]{2,1,0:T(8,12...) custom-call(s32[17]{0:T(128)} %pad_add_fusion.info, ...), custom_call_target="tpu_custom_call", output_to_operand_aliasing={{0}: (17, {}), {1}: (18, {}), {2}: (19, {}), {3}: (20, {}),... | custom-call | flops 32000000000 | bytes 20000000 | tf_op jit(solution)/shard_map/pallas_call | solution.py:173
  83.2 10.3 %shard_map.240 = (bf16[3,640,768]{2,1,0:T(8,128)(2,1)}, bf16[3,640,3072]{2,1,0:T(8,128)(2,1)}, bf16[3,640,768]{2,1,0:T(8,128)(2,1)}, bf16[3,640,128]{2,1,0:T(8,1...) custom-call(s32[17]{0:T(128)} %pad_add_fusion.info, ...), custom_call_target="tpu_custom_call" | custom-call | flops 32000000000 | bytes 20000000 | tf_op jit(solution)/shard_map/pallas_call | solution.py:173
  96.0 9.8 %shard_map.241 = (bf16[3,640,768]{2,1,0:T(8,128)(2,1)}, bf16[3,3,640,768]{3,2,1,0:T(8,128)(2,1)}, f32[3,3,8,640]{3,2,1,0:T(8,128)}, bf16[3,640,768]{2,1,0:T(8,12...) custom-call(s32[17]{0:T(128)} %pad_add_fusion.info, ...), custom_call_target="tpu_custom_call", output_to_operand_aliasing={{0}: (17, {}), {1}: (18, {}), {2}: (19, {}), {3}: (20, {}),... | custom-call | flops 32000000000 | bytes 20000000 | tf_op jit(solution)/shard_map/pallas_call | solution.py:173
  105.8 13.7 %shard_map.242 = (bf16[3,640,768]{2,1,0:T(8,128)(2,1)}, bf16[3,640,3072]{2,1,0:T(8,128)(2,1)}, bf16[3,640,768]{2,1,0:T(8,128)(2,1)}, bf16[3,640,128]{2,1,0:T(8,1...) custom-call(s32[17]{0:T(128)} %pad_add_fusion.info, ...), custom_call_target="tpu_custom_call", output_to_operand_aliasing={{0}: (19, {}), {1}: (20, {}), {2}: (21, {}), {3}: (22, {}),... | custom-call | flops 32000000000 | bytes 20000000 | tf_op jit(solution)/shard_map/pallas_call | solution.py:173
  128.5 29.7 %collective-permute-done.5.refs_0_ = bf16[640,768]{1,0:T(8,128)(2,1)S(1)} collective-permute-done((bf16[640,768]{1,0:T(8,128)(2,1)}, bf16[640,768]{1,0:T(8,128)(2,1)S(1)}, u32[]{:S(2)}, u32[]{:S(2)}) %collective-permute-start.5) | collective-permute-done | bytes 983072 | tf_op jit(solution)/shard_map/ppermute | solution.py:764
  159.2 34.2 %shard_map.243 = (bf16[3,640,768]{2,1,0:T(8,128)(2,1)}, bf16[3,640,3072]{2,1,0:T(8,128)(2,1)}, bf16[3,640,768]{2,1,0:T(8,128)(2,1)}, bf16[3,640,128]{2,1,0:T(8,1...) custom-call(s32[17]{0:T(128)} %pad_add_fusion.info, ...), custom_call_target="tpu_custom_call", output_to_operand_aliasing={{0}: (15, {}), {1}: (16, {}), {2}: (17, {}), {3}: (18, {}),... | custom-call | flops 32000000000 | bytes 20000000 | tf_op jit(solution)/shard_map/pallas_call | solution.py:173
  193.4 3.8 shard_map.251.refs_6_
  197.2 3.8 shard_map.247.refs_6_
  201.0 3.9 shard_map.250.refs_5_
  204.9 3.9 shard_map.246.refs_5_
  208.8 4.9 shard_map.249.refs_0_
  213.7 4.9 shard_map.245.refs_0_
  218.6 5.5 %shard_map.248.refs_0_ = bf16[1536,768]{1,0:T(8,128)(2,1)} custom-call(s32[1]{0:T(128)} %bitcast.info.refs_0_, bf16[1920,3072]{1,0:T(8,128)(2,1)} %bitcast.269, bf16[1920,768]{1,0:T(8,128)(2,1)} %bitcast.277), custom_call_target="tpu_custom_call" | custom-call | flops 94371840 | bytes 100000 | tf_op jit(solution)/shard_map/pallas_call | solution.py:628
  224.1 5.5 %shard_map.244.refs_0_ = bf16[1536,768]{1,0:T(8,128)(2,1)} custom-call(s32[1]{0:T(128)} %bitcast.info.refs_0_, bf16[1920,3072]{1,0:T(8,128)(2,1)} %bitcast.270, bf16[1920,768]{1,0:T(8,128)(2,1)} %bitcast.278), custom_call_target="tpu_custom_call" | custom-call | flops 94371840 | bytes 100000 | tf_op jit(solution)/shard_map/pallas_call | solution.py:628
  229.5 9.4 %collective-permute-done.2.refs_0_ = bf16[640,768]{1,0:T(8,128)(2,1)S(1)} collective-permute-done((bf16[640,768]{1,0:T(8,128)(2,1)S(1)}, bf16[640,768]{1,0:T(8,128)(2,1)S(1)}, u32[]{:S(2)}, u32[]{:S(2)}) %collective-permute-start.2) | collective-permute-done | bytes 983072 | tf_op jit(solution)/shard_map/ppermute | solution.py:764
  239.9 17.3 %shard_map.252 = (bf16[3,640,768]{2,1,0:T(8,128)(2,1)}, bf16[3,640,3072]{2,1,0:T(8,128)(2,1)}, bf16[3,640,768]{2,1,0:T(8,128)(2,1)}, bf16[3,640,128]{2,1,0:T(8,1...) custom-call(s32[17]{0:T(128)} %pad_add_fusion.info, ...), custom_call_target="tpu_custom_call", output_to_operand_aliasing={{0}: (11, {}), {1}: (12, {}), {2}: (13, {}), {3}: (14, {}),... | custom-call | flops 12000000000 | bytes 20000000 | tf_op jit(solution)/shard_map/pallas_call | solution.py:173
  257.2 5.9 %shard_map.253 = bf16[1536,768]{1,0:T(8,128)(2,1)} custom-call(s32[1]{0:T(128)} %bitcast.info.refs_0_, bf16[1920,3072]{1,0:T(8,128)(2,1)} %bitcast.271, bf16[1920,768]{1,0:T(8,128)(2,1)} %bitcast.279, bf16[1536,768]{1,0:T(8,128)(2,1)} %shard_map.244.refs_0_), custom_call_target="tpu_custom_call" | custom-call | flops 94371840 | bytes 100000 | tf_op jit(solution)/shard_map/pallas_call | solution.py:628
  263.1 5.9 %shard_map.254 = bf16[1536,768]{1,0:T(8,128)(2,1)} custom-call(s32[1]{0:T(128)} %bitcast.info.refs_0_, bf16[1920,3072]{1,0:T(8,128)(2,1)} %bitcast.272, bf16[1920,768]{1,0:T(8,128)(2,1)} %bitcast.280, bf16[1536,768]{1,0:T(8,128)(2,1)} %shard_map.248.refs_0_), custom_call_target="tpu_custom_call" | custom-call | flops 94371840 | bytes 100000 | tf_op jit(solution)/shard_map/pallas_call | solution.py:628
  269.0 5.4 %shard_map.255 = bf16[384,3072]{1,0:T(8,128)(2,1)} custom-call(s32[1]{0:T(128)} %bitcast.info.refs_0_, bf16[1920,768]{1,0:T(8,128)(2,1)} %bitcast.283, bf16[1920,3072]{1,0:T(8,128)(2,1)} %bitcast.255, bf16[384,3072]{1,0:T(8,128)(2,1)} %shard_map.245.refs_0_), custom_call_target="tpu_custom_call" | custom-call | flops 94371840 | bytes 100000 | tf_op jit(solution)/shard_map/pallas_call | solution.py:628
  281.3 5.2 %shard_map.256 = bf16[384,3072]{1,0:T(8,128)(2,1)} custom-call(s32[1]{0:T(128)} %bitcast.info.refs_0_, bf16[1920,768]{1,0:T(8,128)(2,1)} %bitcast.284, bf16[1920,3072]{1,0:T(8,128)(2,1)} %bitcast.256, bf16[384,3072]{1,0:T(8,128)(2,1)} %shard_map.249.refs_0_), custom_call_target="tpu_custom_call" | custom-call | flops 94371840 | bytes 100000 | tf_op jit(solution)/shard_map/pallas_call | solution.py:628
  286.6 3.3 add_convert_fusion
  295.7 8.7 %shard_map.257 = (bf16[3,640,768]{2,1,0:T(8,128)(2,1)}, bf16[3,640,768]{2,1,0:T(8,128)(2,1)}, bf16[3,640,768]{2,1,0:T(8,128)(2,1)}, f32[3,3,8,512]{3,2,1,0:T(8,128)}) custom-call(s32[17]{0:T(128)} %pad_add_fusion.info, bf16[3,640,768]{2,1,0:T(8,128)(2,1)} %get-tuple-element.272.refs_0_, ...), custom_call_target="tpu_custom_call", output_to_operand_aliasing={{0}: (6, {}), {1}: (7, {}), {2}: (8, {}), {3}: (9, {})} | custom-call | flops 208333328 | bytes 347222 | tf_op jit(solution)/shard_map/pallas_call | solution.py:173
  304.4 4.3 shard_map.258
  308.7 4.5 shard_map.259
  315.3 8.5 %shard_map.260 = (bf16[3,640,768]{2,1,0:T(8,128)(2,1)}, bf16[3,640,768]{2,1,0:T(8,128)(2,1)}, bf16[3,640,768]{2,1,0:T(8,128)(2,1)}, f32[3,3,8,512]{3,2,1,0:T(8,128)}) custom-call(s32[17]{0:T(128)} %pad_add_fusion.info, bf16[3,640,768]{2,1,0:T(8,128)(2,1)} %get-tuple-element.272.refs_0_, ...), custom_call_target="tpu_custom_call", output_to_operand_aliasing={{0}: (6, {}), {1}: (7, {}), {2}: (8, {}), {3}: (9, {})} | custom-call | flops 208333328 | bytes 347222 | tf_op jit(solution)/shard_map/pallas_call | solution.py:173
  329.0 3.4 collective-permute-done.11
  334.4 2.6 collective-permute-start.13
  337.0 8.7 %shard_map.261 = (bf16[3,640,768]{2,1,0:T(8,128)(2,1)}, bf16[3,640,768]{2,1,0:T(8,128)(2,1)}, bf16[3,640,768]{2,1,0:T(8,128)(2,1)}, f32[3,3,8,512]{3,2,1,0:T(8,128)}) custom-call(s32[17]{0:T(128)} %pad_add_fusion.info, bf16[3,640,768]{2,1,0:T(8,128)(2,1)} %get-tuple-element.272.refs_0_, ...), custom_call_target="tpu_custom_call", output_to_operand_aliasing={{0}: (6, {}), {1}: (7, {}), {2}: (8, {}), {3}: (9, {})} | custom-call | flops 208333328 | bytes 347222 | tf_op jit(solution)/shard_map/pallas_call | solution.py:173
  347.9 4.2 shard_map.262
  358.4 2.7 collective-permute-start.17
  361.1 4.2 shard_map.263
  366.7 4.9 collective-permute-done.15
  373.8 10.4 %collective-permute-done.17 = bf16[192,768]{1,0:T(8,128)(2,1)S(1)} collective-permute-done((bf16[192,768]{1,0:T(8,128)(2,1)S(1)}, bf16[192,768]{1,0:T(8,128)(2,1)S(1)}, u32[]{:S(2)}, u32[]{:S(2)}) %collective-permute-start.17) | collective-permute-done | bytes 294944 | tf_op jit(solution)/shard_map/ppermute | solution.py:777
  386.3 7.4 %collective-permute-done.19 = bf16[48,3072]{1,0:T(8,128)(2,1)S(1)} collective-permute-done((bf16[48,3072]{1,0:T(8,128)(2,1)S(1)}, bf16[48,3072]{1,0:T(8,128)(2,1)S(1)}, u32[]{:S(2)}, u32[]{:S(2)}) %collective-permute-start.19) | collective-permute-done | bytes 294944 | tf_op jit(solution)/shard_map/ppermute | solution.py:777
  398.3 12.4 %collective-permute-done.23 = bf16[384,768]{1,0:T(8,128)(2,1)S(1)} collective-permute-done((bf16[384,768]{1,0:T(8,128)(2,1)S(1)}, bf16[384,768]{1,0:T(8,128)(2,1)S(1)}, u32[]{:S(2)}, u32[]{:S(2)}) %collective-permute-start.23) | collective-permute-done | bytes 589856 | tf_op jit(solution)/shard_map/ppermute | solution.py:777
  411.7 3.1 collective-permute-done.25
  417.9 25.5 %collective-permute-done.28 = bf16[48,1536]{1,0:T(8,128)(2,1)S(1)} collective-permute-done((bf16[48,1536]{1,0:T(8,128)(2,1)S(1)}, bf16[48,1536]{1,0:T(8,128)(2,1)S(1)}, u32[]{:S(2)}, u32[]{:S(2)}) %collective-permute-start.28) | collective-permute-done | bytes 147488 | tf_op jit(solution)/shard_map/ppermute | solution.py:777
  443.5 3.5 collective-permute-start.29
  447.0 5.3 %collective-permute-done.29 = bf16[48,1536]{1,0:T(8,128)(2,1)S(1)} collective-permute-done((bf16[48,1536]{1,0:T(8,128)(2,1)S(1)}, bf16[48,1536]{1,0:T(8,128)(2,1)S(1)}, u32[]{:S(2)}, u32[]{:S(2)}) %collective-permute-start.29) | collective-permute-done | bytes 147488 | tf_op jit(solution)/shard_map/ppermute | solution.py:777
  453.1 2.5 collective-permute-start.36
  456.1 7.1 %collective-permute-done.33 = bf16[96,1536]{1,0:T(8,128)(2,1)S(1)} collective-permute-done((bf16[96,1536]{1,0:T(8,128)(2,1)S(1)}, bf16[96,1536]{1,0:T(8,128)(2,1)S(1)}, u32[]{:S(2)}, u32[]{:S(2)}) %collective-permute-start.33) | collective-permute-done | bytes 294944 | tf_op jit(solution)/shard_map/ppermute | solution.py:777
  465.4 4.1 shard_map.264
  469.7 6.8 %collective-permute-done.37 = bf16[192,1536]{1,0:T(8,128)(2,1)S(1)} collective-permute-done((bf16[192,1536]{1,0:T(8,128)(2,1)S(1)}, bf16[192,1536]{1,0:T(8,128)(2,1)S(1)}, u32[]{:S(2)}, u32[]{:S(2)}) %collective-permute-start.37) | collective-permute-done | bytes 589856 | tf_op jit(solution)/shard_map/ppermute | solution.py:777
  478.8 16.8 %collective-permute-start.42 = (f32[2,4]{0,1:T(4,128)}, f32[2,4]{0,1:T(4,128)}, u32[]{:S(2)}, u32[]{:S(2)}) collective-permute-start(f32[2,4]{0,1:T(4,128)} %pad_maximum_fusion.2), channel_id=1, source_target_pairs={{0,16},{1,17},{2,18},{3,19},{4,20},{5,21},{6,22},{7,23},{8,24},{9,... | collective-permute-start | bytes 104 | tf_op jit(solution)/shard_map/ppermute | solution.py:764
  495.6 4.1 shard_map.265
  508.8 5.3 %shard_map.266 = (f32[768,2304]{1,0:T(8,128)}, f32[768,768]{1,0:T(8,128)}) custom-call(s32[1]{0:T(128)} %bitcast.info.refs_0_, bf16[384,1536]{1,0:T(8,128)(2,1)S(1)} %bitcast.216, bf16[384,1536]{1,0:T(8,128)(2,1)S(1)} %bitcast.214, bf16[384,1536]{1,0:T(8,128)(2,1)S(1)} %collective-permute-done.40.refs_2_, bf16[384,1536]{1,0:T(8,128)(2,1)} %collective-permute-done.41.refs_3_), custom_call_target="tpu_custom_call" | custom-call | bytes 14000000 | tf_op jit(solution)/shard_map/pallas_call | solution.py:733
  (214 shorter events, 80.5 us)
Async XLA Ops:
  36.7 35.8 %collective-permute-start.1 = (bf16[640,768]{1,0:T(8,128)(2,1)}, bf16[640,768]{1,0:T(8,128)(2,1)S(1)}, u32[]{:S(2)}, u32[]{:S(2)}) collective-permute-start(bf16[640,768]{1,0:T(8,128)(2,1)} %get-tuple-element.186), channel_id=1, source_target_pairs={{0,16},{1,17},{2,18},{3,19},{4,20},{5,21},{6,22},{7,23},{8,24},{9,... | collective-permute-start | bytes 2949128 | tf_op jit(solution)/shard_map/ppermute | solution.py:764
  71.0 23.5 %collective-permute-start = (bf16[640,768]{1,0:T(8,128)(2,1)}, bf16[640,768]{1,0:T(8,128)(2,1)S(1)}, u32[]{:S(2)}, u32[]{:S(2)}) collective-permute-start(bf16[640,768]{1,0:T(8,128)(2,1)} %get-tuple-element.185), channel_id=1, source_target_pairs={{0,16},{1,17},{2,18},{3,19},{4,20},{5,21},{6,22},{7,23},{8,24},{9,... | collective-permute-start | bytes 2949128 | tf_op jit(solution)/shard_map/ppermute | solution.py:764
  94.5 63.7 %collective-permute-start.5 = (bf16[640,768]{1,0:T(8,128)(2,1)}, bf16[640,768]{1,0:T(8,128)(2,1)S(1)}, u32[]{:S(2)}, u32[]{:S(2)}) collective-permute-start(bf16[640,768]{1,0:T(8,128)(2,1)} %get-tuple-element.241), channel_id=1, source_target_pairs={{16,0},{17,1},{18,2},{19,3},{20,4},{21,5},{22,6},{23,7},{24,8},{25... | collective-permute-start | bytes 2949128 | tf_op jit(solution)/shard_map/ppermute | solution.py:764
  105.8 13.7 %copy-start.19 = (bf16[3,640,768]{2,1,0:T(8,128)(2,1)S(1)}, bf16[3,640,768]{2,1,0:T(8,128)(2,1)}, u32[]{:S(2)}) copy-start(bf16[3,640,768]{2,1,0:T(8,128)(2,1)} %get-tuple-element.218.refs_0_) | copy-start | bytes 8847364
  121.2 108.3 %collective-permute-start.4 = (bf16[768,128]{1,0:T(8,128)(2,1)S(1)}, bf16[768,128]{1,0:T(8,128)(2,1)S(1)}, u32[]{:S(2)}, u32[]{:S(2)}) collective-permute-start(bf16[768,128]{1,0:T(8,128)(2,1)S(1)} %fusion.6), channel_id=1, source_target_pairs={{16,0},{17,1},{18,2},{19,3},{20,4},{21,5},{22,6},{23,7},{24,8},{25... | collective-permute-start | bytes 589832 | tf_op jit(solution)/shard_map/ppermute | solution.py:764
  123.3 34.9 %copy-start.13 = (f32[2]{0:T(128)}, f32[2]{0:T(128)S(1)}, u32[]{:S(2)}) copy-start(f32[2]{0:T(128)S(1)} %slice_reduce_fusion.6) | copy-start | bytes 28
  125.8 103.7 %collective-permute-start.3 = (f32[2,4]{0,1:T(4,128)}, f32[2,4]{0,1:T(4,128)S(1)}, u32[]{:S(2)}, u32[]{:S(2)}) collective-permute-start(f32[2,4]{0,1:T(4,128)} %pad_maximum_fusion.2), channel_id=1, source_target_pairs={{16,0},{17,1},{18,2},{19,3},{20,4},{21,5},{22,6},{23,7},{24,8},{25... | collective-permute-start | bytes 104 | tf_op jit(solution)/shard_map/ppermute | solution.py:764
  127.2 111.8 %collective-permute-start.2 = (bf16[640,768]{1,0:T(8,128)(2,1)S(1)}, bf16[640,768]{1,0:T(8,128)(2,1)S(1)}, u32[]{:S(2)}, u32[]{:S(2)}) collective-permute-start(bf16[640,768]{1,0:T(8,128)(2,1)S(1)} %copy-done.18), channel_id=1, source_target_pairs={{16,0},{17,1},{18,2},{19,3},{20,4},{21,5},{22,6},{23,7},{24,8},{25... | collective-permute-start | bytes 2949128 | tf_op jit(solution)/shard_map/ppermute | solution.py:764
  229.5 27.7 %copy-start.12 = (f32[2,4]{0,1:T(4,128)}, f32[2,4]{0,1:T(4,128)S(1)}, u32[]{:S(2)}) copy-start(f32[2,4]{0,1:T(4,128)S(1)} %collective-permute-done.3) | copy-start | bytes 100
  263.1 11.8 %collective-permute-start.6 = (bf16[1536,768]{1,0:T(8,128)(2,1)}, bf16[1536,768]{1,0:T(8,128)(2,1)}, u32[]{:S(2)}, u32[]{:S(2)}) collective-permute-start(bf16[1536,768]{1,0:T(8,128)(2,1)} %shard_map.253), channel_id=1, source_target_pairs={{0,1},{1,0},{2,3},{3,2},{4,5},{5,4},{6,7},{7,6},{8,9},{9,8},{10,11... | collective-permute-start | bytes 7077896 | tf_op jit(solution)/shard_map/ppermute | solution.py:777
  274.4 12.2 %collective-permute-start.7 = (bf16[384,3072]{1,0:T(8,128)(2,1)}, bf16[384,3072]{1,0:T(8,128)(2,1)}, u32[]{:S(2)}, u32[]{:S(2)}) collective-permute-start(bf16[384,3072]{1,0:T(8,128)(2,1)} %shard_map.255), channel_id=1, source_target_pairs={{0,1},{1,0},{2,3},{3,2},{4,5},{5,4},{6,7},{7,6},{8,9},{9,8},{10,11... | collective-permute-start | bytes 7077896 | tf_op jit(solution)/shard_map/ppermute | solution.py:777
  279.6 33.6 %collective-permute-start.8 = (bf16[768,768]{1,0:T(8,128)(2,1)}, bf16[768,768]{1,0:T(8,128)(2,1)}, u32[]{:S(2)}, u32[]{:S(2)}) collective-permute-start(bf16[768,768]{1,0:T(8,128)(2,1)} %dynamic-slice_bitcast_fusion.1), channel_id=1, source_target_pairs={{0,2},{1,3},{2,0},{3,1},{4,6},{5,7},{6,4},{7,5},{8,10},{9,11},{10,... | collective-permute-start | bytes 3538952 | tf_op jit(solution)/shard_map/ppermute | solution.py:777
  291.0 32.9 %collective-permute-start.9 = (bf16[192,3072]{1,0:T(8,128)(2,1)}, bf16[192,3072]{1,0:T(8,128)(2,1)}, u32[]{:S(2)}, u32[]{:S(2)}) collective-permute-start(bf16[192,3072]{1,0:T(8,128)(2,1)} %dynamic-slice_bitcast_fusion), channel_id=1, source_target_pairs={{0,4},{1,5},{2,6},{3,7},{4,0},{5,1},{6,2},{7,3},{8,12},{9,13},{10,... | collective-permute-start | bytes 3538952 | tf_op jit(solution)/shard_map/ppermute | solution.py:777
  308.7 17.4 %collective-permute-start.10 = (bf16[384,1536]{1,0:T(8,128)(2,1)}, bf16[384,1536]{1,0:T(8,128)(2,1)S(1)}, u32[]{:S(2)}, u32[]{:S(2)}) collective-permute-start(bf16[384,1536]{1,0:T(8,128)(2,1)} %shard_map.258), channel_id=1, source_target_pairs={{0,1},{1,0},{2,3},{3,2},{4,5},{5,4},{6,7},{7,6},{8,9},{9,8},{10,11... | collective-permute-start | bytes 3538952 | tf_op jit(solution)/shard_map/ppermute | solution.py:777
  314.8 17.7 %collective-permute-start.11 = (bf16[384,768]{1,0:T(8,128)(2,1)S(1)}, bf16[384,768]{1,0:T(8,128)(2,1)}, u32[]{:S(2)}, u32[]{:S(2)}) collective-permute-start(bf16[384,768]{1,0:T(8,128)(2,1)S(1)} %dynamic-slice_bitcast_fusion.5), channel_id=1, source_target_pairs={{0,4},{1,5},{2,6},{3,7},{4,0},{5,1},{6,2},{7,3},{8,12},{9,13},{10,... | collective-permute-start | bytes 1769480 | tf_op jit(solution)/shard_map/ppermute | solution.py:777
  325.7 20.1 %collective-permute-start.12 = (bf16[96,3072]{1,0:T(8,128)(2,1)S(1)}, bf16[96,3072]{1,0:T(8,128)(2,1)S(1)}, u32[]{:S(2)}, u32[]{:S(2)}) collective-permute-start(bf16[96,3072]{1,0:T(8,128)(2,1)S(1)} %dynamic-slice_bitcast_fusion.4), channel_id=1, source_target_pairs={{0,2},{1,3},{2,0},{3,1},{4,6},{5,7},{6,4},{7,5},{8,10},{9,11},{10,... | collective-permute-start | bytes 1769480 | tf_op jit(solution)/shard_map/ppermute | solution.py:777
  327.2 38.1 %collective-permute-start.14 = (bf16[192,1536]{1,0:T(8,128)(2,1)}, bf16[192,1536]{1,0:T(8,128)(2,1)}, u32[]{:S(2)}, u32[]{:S(2)}) collective-permute-start(bf16[192,1536]{1,0:T(8,128)(2,1)} %dynamic-slice_bitcast_fusion.3), channel_id=1, source_target_pairs={{0,4},{1,5},{2,6},{3,7},{4,0},{5,1},{6,2},{7,3},{8,12},{9,13},{10,... | collective-permute-start | bytes 1769480 | tf_op jit(solution)/shard_map/ppermute | solution.py:777
  334.4 23.0 %collective-permute-start.13 = (bf16[192,768]{1,0:T(8,128)(2,1)}, bf16[192,768]{1,0:T(8,128)(2,1)}, u32[]{:S(2)}, u32[]{:S(2)}) collective-permute-start(bf16[192,768]{1,0:T(8,128)(2,1)} %dynamic-slice_bitcast_fusion.9), channel_id=1, source_target_pairs={{0,8},{1,9},{2,10},{3,11},{4,12},{5,13},{6,14},{7,15},{8,0},{9,1},... | collective-permute-start | bytes 884744 | tf_op jit(solution)/shard_map/ppermute | solution.py:777
  346.6 25.0 %collective-permute-start.15 = (bf16[48,3072]{1,0:T(8,128)(2,1)}, bf16[48,3072]{1,0:T(8,128)(2,1)}, u32[]{:S(2)}, u32[]{:S(2)}) collective-permute-start(bf16[48,3072]{1,0:T(8,128)(2,1)} %dynamic-slice_bitcast_fusion.8), channel_id=1, source_target_pairs={{0,8},{1,9},{2,10},{3,11},{4,12},{5,13},{6,14},{7,15},{8,0},{9,1},... | collective-permute-start | bytes 884744 | tf_op jit(solution)/shard_map/ppermute | solution.py:777
  352.1 20.7 %collective-permute-start.16 = (bf16[384,1536]{1,0:T(8,128)(2,1)}, bf16[384,1536]{1,0:T(8,128)(2,1)S(1)}, u32[]{:S(2)}, u32[]{:S(2)}) collective-permute-start(bf16[384,1536]{1,0:T(8,128)(2,1)} %shard_map.262), channel_id=1, source_target_pairs={{0,1},{1,0},{2,3},{3,2},{4,5},{5,4},{6,7},{7,6},{8,9},{9,8},{10,11... | collective-permute-start | bytes 3538952 | tf_op jit(solution)/shard_map/ppermute | solution.py:777
  356.8 36.9 %collective-permute-start.20 = (bf16[140,768]{1,0:T(8,128)(2,1)S(1)}, bf16[140,768]{1,0:T(8,128)(2,1)S(1)}, u32[]{:S(2)}, u32[]{:S(2)}) collective-permute-start(bf16[140,768]{1,0:T(8,128)(2,1)S(1)} %pad_maximum_fusion), channel_id=1, source_target_pairs={{0,1},{1,0},{2,3},{3,2},{4,5},{5,4},{6,7},{7,6},{8,9},{9,8},{10,11... | collective-permute-start | bytes 645128 | tf_op jit(solution)/shard_map/ppermute | solution.py:777
  358.4 25.7 %collective-permute-start.17 = (bf16[192,768]{1,0:T(8,128)(2,1)S(1)}, bf16[192,768]{1,0:T(8,128)(2,1)S(1)}, u32[]{:S(2)}, u32[]{:S(2)}) collective-permute-start(bf16[192,768]{1,0:T(8,128)(2,1)S(1)} %fusion.10), channel_id=1, source_target_pairs={{0,8},{1,9},{2,10},{3,11},{4,12},{5,13},{6,14},{7,15},{8,0},{9,1},... | collective-permute-start | bytes 884744 | tf_op jit(solution)/shard_map/ppermute | solution.py:777
  366.6 17.5 %collective-permute-start.18 = (bf16[96,1536]{1,0:T(8,128)(2,1)S(1)}, bf16[96,1536]{1,0:T(8,128)(2,1)S(1)}, u32[]{:S(2)}, u32[]{:S(2)}) collective-permute-start(bf16[96,1536]{1,0:T(8,128)(2,1)S(1)} %dynamic-slice_bitcast_fusion.7), channel_id=1, source_target_pairs={{0,2},{1,3},{2,0},{3,1},{4,6},{5,7},{6,4},{7,5},{8,10},{9,11},{10,... | collective-permute-start | bytes 884744 | tf_op jit(solution)/shard_map/ppermute | solution.py:777
  372.6 21.1 %collective-permute-start.19 = (bf16[48,3072]{1,0:T(8,128)(2,1)S(1)}, bf16[48,3072]{1,0:T(8,128)(2,1)S(1)}, u32[]{:S(2)}, u32[]{:S(2)}) collective-permute-start(bf16[48,3072]{1,0:T(8,128)(2,1)S(1)} %fusion.9), channel_id=1, source_target_pairs={{0,8},{1,9},{2,10},{3,11},{4,12},{5,13},{6,14},{7,15},{8,0},{9,1},... | collective-permute-start | bytes 884744 | tf_op jit(solution)/shard_map/ppermute | solution.py:777
  373.1 22.8 %collective-permute-start.21 = (bf16[192,1536]{1,0:T(8,128)(2,1)S(1)}, bf16[192,1536]{1,0:T(8,128)(2,1)S(1)}, u32[]{:S(2)}, u32[]{:S(2)}) collective-permute-start(bf16[192,1536]{1,0:T(8,128)(2,1)S(1)} %dynamic-slice_bitcast_fusion.2), channel_id=1, source_target_pairs={{0,2},{1,3},{2,0},{3,1},{4,6},{5,7},{6,4},{7,5},{8,10},{9,11},{10,... | collective-permute-start | bytes 1769480 | tf_op jit(solution)/shard_map/ppermute | solution.py:777
  384.3 12.5 %collective-permute-start.22 = (bf16[48,1536]{1,0:T(8,128)(2,1)S(1)}, bf16[48,1536]{1,0:T(8,128)(2,1)S(1)}, u32[]{:S(2)}, u32[]{:S(2)}) collective-permute-start(bf16[48,1536]{1,0:T(8,128)(2,1)S(1)} %dynamic-slice_bitcast_fusion.11), channel_id=1, source_target_pairs={{0,8},{1,9},{2,10},{3,11},{4,12},{5,13},{6,14},{7,15},{8,0},{9,1},... | collective-permute-start | bytes 442376 | tf_op jit(solution)/shard_map/ppermute | solution.py:777
  384.4 26.4 %collective-permute-start.23 = (bf16[384,768]{1,0:T(8,128)(2,1)S(1)}, bf16[384,768]{1,0:T(8,128)(2,1)S(1)}, u32[]{:S(2)}, u32[]{:S(2)}) collective-permute-start(bf16[384,768]{1,0:T(8,128)(2,1)S(1)} %bitcast.329), channel_id=1, source_target_pairs={{0,4},{1,5},{2,6},{3,7},{4,0},{5,1},{6,2},{7,3},{8,12},{9,13},{10,... | collective-permute-start | bytes 1769480 | tf_op jit(solution)/shard_map/ppermute | solution.py:777
  393.8 17.6 %collective-permute-start.24 = (bf16[140,768]{1,0:T(8,128)(2,1)S(1)}, bf16[140,768]{1,0:T(8,128)(2,1)S(1)}, u32[]{:S(2)}, u32[]{:S(2)}) collective-permute-start(bf16[140,768]{1,0:T(8,128)(2,1)S(1)} %add_convert_fusion.7), channel_id=1, source_target_pairs={{0,2},{1,3},{2,0},{3,1},{4,6},{5,7},{6,4},{7,5},{8,10},{9,11},{10,... | collective-permute-start | bytes 645128 | tf_op jit(solution)/shard_map/ppermute | solution.py:777
  394.4 20.4 %collective-permute-start.25 = (bf16[96,3072]{1,0:T(8,128)(2,1)S(1)}, bf16[96,3072]{1,0:T(8,128)(2,1)S(1)}, u32[]{:S(2)}, u32[]{:S(2)}) collective-permute-start(bf16[96,3072]{1,0:T(8,128)(2,1)S(1)} %bitcast.331), channel_id=1, source_target_pairs={{0,2},{1,3},{2,0},{3,1},{4,6},{5,7},{6,4},{7,5},{8,10},{9,11},{10,... | collective-permute-start | bytes 1769480 | tf_op jit(solution)/shard_map/ppermute | solution.py:777
  396.1 21.0 %collective-permute-start.26 = (bf16[96,1536]{1,0:T(8,128)(2,1)S(1)}, bf16[96,1536]{1,0:T(8,128)(2,1)S(1)}, u32[]{:S(2)}, u32[]{:S(2)}) collective-permute-start(bf16[96,1536]{1,0:T(8,128)(2,1)S(1)} %dynamic-slice_bitcast_fusion.6), channel_id=1, source_target_pairs={{0,4},{1,5},{2,6},{3,7},{4,0},{5,1},{6,2},{7,3},{8,12},{9,13},{10,... | collective-permute-start | bytes 884744 | tf_op jit(solution)/shard_map/ppermute | solution.py:777
  396.8 20.5 %collective-permute-start.27 = (bf16[48,1536]{1,0:T(8,128)(2,1)S(1)}, bf16[48,1536]{1,0:T(8,128)(2,1)S(1)}, u32[]{:S(2)}, u32[]{:S(2)}) collective-permute-start(bf16[48,1536]{1,0:T(8,128)(2,1)S(1)} %fusion.13), channel_id=1, source_target_pairs={{0,8},{1,9},{2,10},{3,11},{4,12},{5,13},{6,14},{7,15},{8,0},{9,1},... | collective-permute-start | bytes 442376 | tf_op jit(solution)/shard_map/ppermute | solution.py:777
  410.8 41.9 %collective-permute-start.30 = (bf16[768,768]{1,0:T(8,128)(2,1)S(1)}, bf16[768,768]{1,0:T(8,128)(2,1)S(1)}, u32[]{:S(2)}, u32[]{:S(2)}) collective-permute-start(bf16[768,768]{1,0:T(8,128)(2,1)S(1)} %bitcast.321), channel_id=1, source_target_pairs={{0,2},{1,3},{2,0},{3,1},{4,6},{5,7},{6,4},{7,5},{8,10},{9,11},{10,... | collective-permute-start | bytes 3538952 | tf_op jit(solution)/shard_map/ppermute | solution.py:777
  411.5 41.6 %collective-permute-start.32 = (bf16[140,768]{1,0:T(8,128)(2,1)S(1)}, bf16[140,768]{1,0:T(8,128)(2,1)S(1)}, u32[]{:S(2)}, u32[]{:S(2)}) collective-permute-start(bf16[140,768]{1,0:T(8,128)(2,1)S(1)} %add_convert_fusion.6), channel_id=1, source_target_pairs={{0,4},{1,5},{2,6},{3,7},{4,0},{5,1},{6,2},{7,3},{8,12},{9,13},{10,... | collective-permute-start | bytes 645128 | tf_op jit(solution)/shard_map/ppermute | solution.py:777
  414.9 50.3 %collective-permute-start.34 = (bf16[192,3072]{1,0:T(8,128)(2,1)S(1)}, bf16[192,3072]{1,0:T(8,128)(2,1)S(1)}, u32[]{:S(2)}, u32[]{:S(2)}) collective-permute-start(bf16[192,3072]{1,0:T(8,128)(2,1)S(1)} %bitcast.323), channel_id=1, source_target_pairs={{0,4},{1,5},{2,6},{3,7},{4,0},{5,1},{6,2},{7,3},{8,12},{9,13},{10,... | collective-permute-start | bytes 3538952 | tf_op jit(solution)/shard_map/ppermute | solution.py:777
  417.2 26.3 %collective-permute-start.28 = (bf16[48,1536]{1,0:T(8,128)(2,1)S(1)}, bf16[48,1536]{1,0:T(8,128)(2,1)S(1)}, u32[]{:S(2)}, u32[]{:S(2)}) collective-permute-start(bf16[48,1536]{1,0:T(8,128)(2,1)S(1)} %dynamic-slice_bitcast_fusion.10), channel_id=1, source_target_pairs={{0,8},{1,9},{2,10},{3,11},{4,12},{5,13},{6,14},{7,15},{8,0},{9,1},... | collective-permute-start | bytes 442376 | tf_op jit(solution)/shard_map/ppermute | solution.py:777
  417.3 35.6 %collective-permute-start.31 = (bf16[96,1536]{1,0:T(8,128)(2,1)S(1)}, bf16[96,1536]{1,0:T(8,128)(2,1)S(1)}, u32[]{:S(2)}, u32[]{:S(2)}) collective-permute-start(bf16[96,1536]{1,0:T(8,128)(2,1)S(1)} %bitcast.351), channel_id=1, source_target_pairs={{0,2},{1,3},{2,0},{3,1},{4,6},{5,7},{6,4},{7,5},{8,10},{9,11},{10,... | collective-permute-start | bytes 884744 | tf_op jit(solution)/shard_map/ppermute | solution.py:777
  443.5 8.8 %collective-permute-start.29 = (bf16[48,1536]{1,0:T(8,128)(2,1)S(1)}, bf16[48,1536]{1,0:T(8,128)(2,1)S(1)}, u32[]{:S(2)}, u32[]{:S(2)}) collective-permute-start(bf16[48,1536]{1,0:T(8,128)(2,1)S(1)} %fusion.12), channel_id=1, source_target_pairs={{0,8},{1,9},{2,10},{3,11},{4,12},{5,13},{6,14},{7,15},{8,0},{9,1},... | collective-permute-start | bytes 442376 | tf_op jit(solution)/shard_map/ppermute | solution.py:777
  452.3 10.8 %collective-permute-start.33 = (bf16[96,1536]{1,0:T(8,128)(2,1)S(1)}, bf16[96,1536]{1,0:T(8,128)(2,1)S(1)}, u32[]{:S(2)}, u32[]{:S(2)}) collective-permute-start(bf16[96,1536]{1,0:T(8,128)(2,1)S(1)} %bitcast.349), channel_id=1, source_target_pairs={{0,4},{1,5},{2,6},{3,7},{4,0},{5,1},{6,2},{7,3},{8,12},{9,13},{10,... | collective-permute-start | bytes 884744 | tf_op jit(solution)/shard_map/ppermute | solution.py:777
  452.8 12.6 %collective-permute-start.35 = (bf16[1536,768]{1,0:T(8,128)(2,1)S(1)}, bf16[1536,768]{1,0:T(8,128)(2,1)S(1)}, u32[]{:S(2)}, u32[]{:S(2)}) collective-permute-start(bf16[1536,768]{1,0:T(8,128)(2,1)S(1)} %bitcast.209), channel_id=1, source_target_pairs={{0,1},{1,0},{2,3},{3,2},{4,5},{5,4},{6,7},{7,6},{8,9},{9,8},{10,11... | collective-permute-start | bytes 7077896 | tf_op jit(solution)/shard_map/ppermute | solution.py:777
  453.1 16.4 %collective-permute-start.36 = (bf16[140,768]{1,0:T(8,128)(2,1)S(1)}, bf16[140,768]{1,0:T(8,128)(2,1)S(1)}, u32[]{:S(2)}, u32[]{:S(2)}) collective-permute-start(bf16[140,768]{1,0:T(8,128)(2,1)S(1)} %add_convert_fusion.5), channel_id=1, source_target_pairs={{0,8},{1,9},{2,10},{3,11},{4,12},{5,13},{6,14},{7,15},{8,0},{9,1},... | collective-permute-start | bytes 645128 | tf_op jit(solution)/shard_map/ppermute | solution.py:777
  455.6 20.9 %collective-permute-start.37 = (bf16[192,1536]{1,0:T(8,128)(2,1)S(1)}, bf16[192,1536]{1,0:T(8,128)(2,1)S(1)}, u32[]{:S(2)}, u32[]{:S(2)}) collective-permute-start(bf16[192,1536]{1,0:T(8,128)(2,1)S(1)} %bitcast.333), channel_id=1, source_target_pairs={{0,4},{1,5},{2,6},{3,7},{4,0},{5,1},{6,2},{7,3},{8,12},{9,13},{10,... | collective-permute-start | bytes 1769480 | tf_op jit(solution)/shard_map/ppermute | solution.py:777
  463.2 13.6 %collective-permute-start.38 = (bf16[192,1536]{1,0:T(8,128)(2,1)S(1)}, bf16[192,1536]{1,0:T(8,128)(2,1)S(1)}, u32[]{:S(2)}, u32[]{:S(2)}) collective-permute-start(bf16[192,1536]{1,0:T(8,128)(2,1)S(1)} %bitcast.335), channel_id=1, source_target_pairs={{0,2},{1,3},{2,0},{3,1},{4,6},{5,7},{6,4},{7,5},{8,10},{9,11},{10,... | collective-permute-start | bytes 1769480 | tf_op jit(solution)/shard_map/ppermute | solution.py:777
  465.3 30.3 %collective-permute-start.39 = (bf16[384,3072]{1,0:T(8,128)(2,1)S(1)}, bf16[384,3072]{1,0:T(8,128)(2,1)S(1)}, u32[]{:S(2)}, u32[]{:S(2)}) collective-permute-start(bf16[384,3072]{1,0:T(8,128)(2,1)S(1)} %bitcast.211), channel_id=1, source_target_pairs={{0,1},{1,0},{2,3},{3,2},{4,5},{5,4},{6,7},{7,6},{8,9},{9,8},{10,11... | collective-permute-start | bytes 7077896 | tf_op jit(solution)/shard_map/ppermute | solution.py:777
  469.6 8.4 %copy-start.5 = (bf16[140,768]{1,0:T(8,128)(2,1)}, bf16[140,768]{1,0:T(8,128)(2,1)S(1)}, u32[]{:S(2)}) copy-start(bf16[140,768]{1,0:T(8,128)(2,1)S(1)} %get-tuple-element.358) | copy-start | bytes 645124
  476.5 32.2 %collective-permute-start.40 = (bf16[384,1536]{1,0:T(8,128)(2,1)S(1)}, bf16[384,1536]{1,0:T(8,128)(2,1)S(1)}, u32[]{:S(2)}, u32[]{:S(2)}) collective-permute-start(bf16[384,1536]{1,0:T(8,128)(2,1)S(1)} %bitcast.215), channel_id=1, source_target_pairs={{0,1},{1,0},{2,3},{3,2},{4,5},{5,4},{6,7},{7,6},{8,9},{9,8},{10,11... | collective-permute-start | bytes 3538952 | tf_op jit(solution)/shard_map/ppermute | solution.py:777
  476.8 32.0 %collective-permute-start.41 = (bf16[384,1536]{1,0:T(8,128)(2,1)S(1)}, bf16[384,1536]{1,0:T(8,128)(2,1)}, u32[]{:S(2)}, u32[]{:S(2)}) collective-permute-start(bf16[384,1536]{1,0:T(8,128)(2,1)S(1)} %bitcast.213), channel_id=1, source_target_pairs={{0,1},{1,0},{2,3},{3,2},{4,5},{5,4},{6,7},{7,6},{8,9},{9,8},{10,11... | collective-permute-start | bytes 3538952 | tf_op jit(solution)/shard_map/ppermute | solution.py:777
  478.8 27.3 %copy-start.9 = (f32[2]{0:T(128)S(1)}, f32[2]{0:T(128)}, u32[]{:S(2)}) copy-start(f32[2]{0:T(128)} %copy-done.8) | copy-start | bytes 28
  478.8 27.3 %collective-permute-start.42 = (f32[2,4]{0,1:T(4,128)}, f32[2,4]{0,1:T(4,128)}, u32[]{:S(2)}, u32[]{:S(2)}) collective-permute-start(f32[2,4]{0,1:T(4,128)} %pad_maximum_fusion.2), channel_id=1, source_target_pairs={{0,16},{1,17},{2,18},{3,19},{4,20},{5,21},{6,22},{7,23},{8,24},{9,... | collective-permute-start | bytes 104 | tf_op jit(solution)/shard_map/ppermute | solution.py:764
  (15 other events, 50.1 us)

commit v7 on v6

--- a/solution.py
+++ b/solution.py
@@ -952,7 +952,6 @@
     fwd = state["fwd"]
     inputs, context, hidden, squares_one = fwd[0], fwd[3], fwd[4], fwd[7]
     active, outputs, squares_two = fwd[8], fwd[10], fwd[13]
-    embeds, losses = state["bwd"][3:5]
     squares = jnp.stack(
         [
             jnp.sum(squares_one[:micros, 0], axis=1),
@@ -961,34 +960,30 @@
         ],
         axis=1,
     )
-    colbert = dot_tn(flatten_rows(outputs[:micros]), flatten_rows(embeds[:micros])).astype(BF)
-    facts = jnp.concatenate([squares, losses[:micros, 6, 0:1]], axis=1)
-    facts_down, colbert_down = passed_along(facts, "pipe", -1), passed_along(colbert, "pipe", -1)
-    done += (facts, colbert)
     for phase in range(micros, 2 * micros - 1):
         backward(phase, done)
         done = (state["bwd"][9],)
     last = 2 * micros - 1
     after_back = state["bwd"][9]
+    colbert = dot_tn(flatten_rows(outputs[:micros]), flatten_rows(tied(state["bwd"][3], after_back)[:micros])).astype(BF)
+    facts = jnp.concatenate([squares, tied(state["bwd"][4], after_back)[:micros, 6, 0:1]], axis=1)
+    facts_down, colbert_down = passed_along(facts, "pipe", -1), passed_along(colbert, "pipe", -1)
     slabs = tuple(range(width // SLAB))
-    ffn_back, attn_back = state["bwd"][:6], state["bwd"][6:10]
+    ffn_back = state["bwd"][:6]
     lefts = [flatten_rows(a) for a in (active, hidden, inputs, context)]
 
     bases = {}
     for micro in range(micros - 1):
         first_core = tied(core, after_back)
-        d_two, d_inner, d_one = (flatten_rows(ffn_back[i]) for i in range(3))
-        joined_grads = [flatten_rows(a) for a in attn_back[:3]]
+        d_two, d_inner = (flatten_rows(ffn_back[i]) for i in range(2))
         for mine in (0, 1):
-            old = bases.get(mine, (None,) * 4)
+            old = bases.get(mine, (None,) * 2)
             bases[mine] = (
                 grad_half(rows, micro, first_core, mine, lefts[0], d_two, old[0]),
                 grad_half(rows, micro, first_core, mine, lefts[1], d_inner, old[1]),
-                grad_rest(rows, micro, first_core, mine, lefts[2], joined_grads, slabs[:1], lefts[3], d_one, old[2]),
-                grad_rest(rows, micro, first_core, mine, lefts[2], joined_grads, slabs[1:], None, None, old[3]),
             )
-    backward_ffn(last, (facts_down, colbert_down) + tuple(jax.tree.leaves(bases)))
-    bases = bases or {0: (None,) * 4, 1: (None,) * 4}
+    backward_ffn(last, (facts, colbert, facts_down, colbert_down) + tuple(jax.tree.leaves(bases)))
+    bases = bases or {0: (None,) * 2, 1: (None,) * 2}
     micro = micros - 1
     ffn_back = state["bwd"]
     d_two, d_inner, d_one = (flatten_rows(ffn_back[i]) for i in range(3))
@@ -1002,7 +997,7 @@
         joined_grads = [flatten_rows(a) for a in state["bwd"][6:9]]
         extra = (lefts[3], d_one) if which == 2 else (None, None)
         [one] = line.did(
-            grad_rest(rows, micro, line.after(core), mine, lefts[2], joined_grads, some, *extra, bases[mine][which])
+            grad_rest(micros * rows, 0, line.after(core), mine, lefts[2], joined_grads, some, *extra, None)
         )
         return one
 

time: 523 us -> 506 us (0.967)
  Pallas kernels: 275 us -> 261 us
  starting transfers between devices: 54.4 us -> 43.1 us
  waiting for transfers between devices: 129 us -> 139 us
    ppermute x7, waiting for transfers between devices: 40.1 us -> 54.2 us  [passed_along(): return lax.ppermute(array, axis, pairs)]
    ppermute x7, starting transfers between devices: 25.2 us -> 13.3 us  [passed_along(): return lax.ppermute(array, axis, pairs)]
    pallas_call x16 -> x12, Pallas kernels: 75.7 us -> 64.8 us  [grad_call(): pl.pallas_call(body, out_shape=out_shape, grid_spec=pltpu.PrefetchScalarG...]
  transfers between devices with their start and end apart: 43 -> 43, of which waited for: 15 -> 16; matrix products, arithmetic and copies ran while one was open for 9% -> 9% of each run, Pallas kernels for 42% -> 40%
where the time goes in v7:
time: 506 us; the launch traced here: 498 us
  Pallas kernels  261 us (52%)
  waiting for transfers between devices  139 us (27%)
  starting transfers between devices  43.1 us (9%)
  local copies, waits for them, and re-layouts  25.8 us (5%)
  other arithmetic  25.2 us (5%)
    pallas_call x11, Pallas kernels, call(): pl.pallas_call(body, out_shape=[jax.ShapeDtypeStruct(s[0], s[1]) for s in...  182 us
    ppermute x36, waiting for transfers between devices, swapped(): return lax.ppermute(array, axis, [(i, i ^ bit) for i in range(count)])  85.3 us
    pallas_call x12, Pallas kernels, grad_call(): pl.pallas_call(body, out_shape=out_shape, grid_spec=pltpu.PrefetchScalarG...  64.8 us
    ppermute x7, waiting for transfers between devices, passed_along(): return lax.ppermute(array, axis, pairs)  54.2 us
    ppermute x36, starting transfers between devices, swapped(): return lax.ppermute(array, axis, [(i, i ^ bit) for i in range(count)])  29.9 us
    convert_element_type x19, other arithmetic, sum_low(): return (kept.astype(F32) + got.astype(F32)).astype(BF)  14.7 us
    pallas_call x3, Pallas kernels, widened(): pl.pallas_call(widen_body, out_shape=[jax.ShapeDtypeStruct(shape, F32) fo...  13.4 us
    ppermute x7, starting transfers between devices, passed_along(): return lax.ppermute(array, axis, pairs)  13.3 us
  transfers between devices with their start and end apart: 43, of which 16 were waited for; matrix products, arithmetic and copies ran while one was open for 9% of the time, Pallas kernels for 40%

profile of v7, /device:TPU:0, one launch (start us, length us, event | category | flops | bytes accessed | tf_op | source)
XLA Modules:
  0.0 497.8 jit_solution(4916747242301762697)
XLA Ops:
  4.1 32.6 %shard_map.237 = (bf16[3,640,768]{2,1,0:T(8,128)(2,1)}, bf16[3,3,640,768]{3,2,1,0:T(8,128)(2,1)}, f32[3,3,8,640]{3,2,1,0:T(8,128)}, bf16[3,640,768]{2,1,0:T(8,12...) custom-call(s32[17]{0:T(128)} %pad_add_fusion.info, ...), custom_call_target="tpu_custom_call" | custom-call | flops 32000000000 | bytes 20000000 | tf_op jit(solution)/shard_map/pallas_call | solution.py:173
  38.5 32.7 %shard_map.238 = (bf16[3,640,768]{2,1,0:T(8,128)(2,1)}, bf16[3,3,640,768]{3,2,1,0:T(8,128)(2,1)}, f32[3,3,8,640]{3,2,1,0:T(8,128)}, bf16[3,640,768]{2,1,0:T(8,12...) custom-call(s32[17]{0:T(128)} %pad_add_fusion.info, ...), custom_call_target="tpu_custom_call", output_to_operand_aliasing={{0}: (17, {}), {1}: (18, {}), {2}: (19, {}), {3}: (20, {}),... | custom-call | flops 32000000000 | bytes 20000000 | tf_op jit(solution)/shard_map/pallas_call | solution.py:173
  73.8 9.7 %shard_map.239 = (bf16[3,640,768]{2,1,0:T(8,128)(2,1)}, bf16[3,3,640,768]{3,2,1,0:T(8,128)(2,1)}, f32[3,3,8,640]{3,2,1,0:T(8,128)}, bf16[3,640,768]{2,1,0:T(8,12...) custom-call(s32[17]{0:T(128)} %pad_add_fusion.info, ...), custom_call_target="tpu_custom_call", output_to_operand_aliasing={{0}: (17, {}), {1}: (18, {}), {2}: (19, {}), {3}: (20, {}),... | custom-call | flops 32000000000 | bytes 20000000 | tf_op jit(solution)/shard_map/pallas_call | solution.py:173
  83.5 10.1 %shard_map.240 = (bf16[3,640,768]{2,1,0:T(8,128)(2,1)}, bf16[3,640,3072]{2,1,0:T(8,128)(2,1)}, bf16[3,640,768]{2,1,0:T(8,128)(2,1)}, bf16[3,640,128]{2,1,0:T(8,1...) custom-call(s32[17]{0:T(128)} %pad_add_fusion.info, ...), custom_call_target="tpu_custom_call" | custom-call | flops 32000000000 | bytes 20000000 | tf_op jit(solution)/shard_map/pallas_call | solution.py:173
  96.5 9.8 %shard_map.241 = (bf16[3,640,768]{2,1,0:T(8,128)(2,1)}, bf16[3,3,640,768]{3,2,1,0:T(8,128)(2,1)}, f32[3,3,8,640]{3,2,1,0:T(8,128)}, bf16[3,640,768]{2,1,0:T(8,12...) custom-call(s32[17]{0:T(128)} %pad_add_fusion.info, ...), custom_call_target="tpu_custom_call", output_to_operand_aliasing={{0}: (17, {}), {1}: (18, {}), {2}: (19, {}), {3}: (20, {}),... | custom-call | flops 32000000000 | bytes 20000000 | tf_op jit(solution)/shard_map/pallas_call | solution.py:173
  106.3 10.1 %shard_map.242 = (bf16[3,640,768]{2,1,0:T(8,128)(2,1)}, bf16[3,640,3072]{2,1,0:T(8,128)(2,1)}, bf16[3,640,768]{2,1,0:T(8,128)(2,1)}, bf16[3,640,128]{2,1,0:T(8,1...) custom-call(s32[17]{0:T(128)} %pad_add_fusion.info, ...), custom_call_target="tpu_custom_call", output_to_operand_aliasing={{0}: (19, {}), {1}: (20, {}), {2}: (21, {}), {3}: (22, {}),... | custom-call | flops 32000000000 | bytes 20000000 | tf_op jit(solution)/shard_map/pallas_call | solution.py:173
  119.8 38.2 %collective-permute-done.3.refs_0_ = bf16[640,768]{1,0:T(8,128)(2,1)S(1)} collective-permute-done((bf16[640,768]{1,0:T(8,128)(2,1)}, bf16[640,768]{1,0:T(8,128)(2,1)S(1)}, u32[]{:S(2)}, u32[]{:S(2)}) %collective-permute-start.3) | collective-permute-done | bytes 983072 | tf_op jit(solution)/shard_map/ppermute | solution.py:764
  158.9 34.4 %shard_map.243 = (bf16[3,640,768]{2,1,0:T(8,128)(2,1)}, bf16[3,640,3072]{2,1,0:T(8,128)(2,1)}, bf16[3,640,768]{2,1,0:T(8,128)(2,1)}, bf16[3,640,128]{2,1,0:T(8,1...) custom-call(s32[17]{0:T(128)} %pad_add_fusion.info, ...), custom_call_target="tpu_custom_call", output_to_operand_aliasing={{0}: (15, {}), {1}: (16, {}), {2}: (17, {}), {3}: (18, {}),... | custom-call | flops 32000000000 | bytes 20000000 | tf_op jit(solution)/shard_map/pallas_call | solution.py:173
  199.4 5.0 %shard_map.247.refs_0_ = bf16[384,3072]{1,0:T(8,128)(2,1)} custom-call(s32[1]{0:T(128)} %bitcast.info.refs_0_, bf16[1920,768]{1,0:T(8,128)(2,1)} %bitcast.251, bf16[1920,3072]{1,0:T(8,128)(2,1)} %bitcast.213), custom_call_target="tpu_custom_call" | custom-call | flops 94371840 | bytes 100000 | tf_op jit(solution)/shard_map/pallas_call | solution.py:628
  204.4 4.9 shard_map.245.refs_0_
  209.3 5.5 %shard_map.246.refs_0_ = bf16[1536,768]{1,0:T(8,128)(2,1)} custom-call(s32[1]{0:T(128)} %bitcast.info.refs_0_, bf16[1920,3072]{1,0:T(8,128)(2,1)} %bitcast.235, bf16[1920,768]{1,0:T(8,128)(2,1)} %bitcast.243), custom_call_target="tpu_custom_call" | custom-call | flops 94371840 | bytes 100000 | tf_op jit(solution)/shard_map/pallas_call | solution.py:628
  214.8 5.5 %shard_map.244.refs_0_ = bf16[1536,768]{1,0:T(8,128)(2,1)} custom-call(s32[1]{0:T(128)} %bitcast.info.refs_0_, bf16[1920,3072]{1,0:T(8,128)(2,1)} %bitcast.236, bf16[1920,768]{1,0:T(8,128)(2,1)} %bitcast.244), custom_call_target="tpu_custom_call" | custom-call | flops 94371840 | bytes 100000 | tf_op jit(solution)/shard_map/pallas_call | solution.py:628
  220.3 11.3 %collective-permute-done.2.refs_0_ = bf16[640,768]{1,0:T(8,128)(2,1)S(1)} collective-permute-done((bf16[640,768]{1,0:T(8,128)(2,1)}, bf16[640,768]{1,0:T(8,128)(2,1)S(1)}, u32[]{:S(2)}, u32[]{:S(2)}) %collective-permute-start.2) | collective-permute-done | bytes 983072 | tf_op jit(solution)/shard_map/ppermute | solution.py:764
  231.7 3.5 collective-permute-done.4
  235.1 17.0 %shard_map.248 = (bf16[3,640,768]{2,1,0:T(8,128)(2,1)}, bf16[3,640,3072]{2,1,0:T(8,128)(2,1)}, bf16[3,640,768]{2,1,0:T(8,128)(2,1)}, bf16[3,640,128]{2,1,0:T(8,1...) custom-call(s32[17]{0:T(128)} %pad_add_fusion.info, ...), custom_call_target="tpu_custom_call", output_to_operand_aliasing={{0}: (11, {}), {1}: (12, {}), {2}: (13, {}), {3}: (14, {}),... | custom-call | flops 12000000000 | bytes 20000000 | tf_op jit(solution)/shard_map/pallas_call | solution.py:173
  252.1 5.9 %shard_map.249 = bf16[1536,768]{1,0:T(8,128)(2,1)} custom-call(s32[1]{0:T(128)} %bitcast.info.refs_0_, bf16[1920,3072]{1,0:T(8,128)(2,1)} %bitcast.237, bf16[1920,768]{1,0:T(8,128)(2,1)} %bitcast.245, bf16[1536,768]{1,0:T(8,128)(2,1)} %shard_map.244.refs_0_), custom_call_target="tpu_custom_call" | custom-call | flops 94371840 | bytes 100000 | tf_op jit(solution)/shard_map/pallas_call | solution.py:628
  258.0 6.1 %shard_map.250 = bf16[1536,768]{1,0:T(8,128)(2,1)} custom-call(s32[1]{0:T(128)} %bitcast.info.refs_0_, bf16[1920,3072]{1,0:T(8,128)(2,1)} %bitcast.238, bf16[1920,768]{1,0:T(8,128)(2,1)} %bitcast.246, bf16[1536,768]{1,0:T(8,128)(2,1)} %shard_map.246.refs_0_), custom_call_target="tpu_custom_call" | custom-call | flops 94371840 | bytes 100000 | tf_op jit(solution)/shard_map/pallas_call | solution.py:628
  264.1 5.5 %shard_map.251 = bf16[384,3072]{1,0:T(8,128)(2,1)} custom-call(s32[1]{0:T(128)} %bitcast.info.refs_0_, bf16[1920,768]{1,0:T(8,128)(2,1)} %bitcast.253, bf16[1920,3072]{1,0:T(8,128)(2,1)} %bitcast.215, bf16[384,3072]{1,0:T(8,128)(2,1)} %shard_map.245.refs_0_), custom_call_target="tpu_custom_call" | custom-call | flops 94371840 | bytes 100000 | tf_op jit(solution)/shard_map/pallas_call | solution.py:628
  270.1 2.3 add_convert_fusion.1
  276.5 5.2 %shard_map.252 = bf16[384,3072]{1,0:T(8,128)(2,1)} custom-call(s32[1]{0:T(128)} %bitcast.info.refs_0_, bf16[1920,768]{1,0:T(8,128)(2,1)} %bitcast.254, bf16[1920,3072]{1,0:T(8,128)(2,1)} %bitcast.216, bf16[384,3072]{1,0:T(8,128)(2,1)} %shard_map.247.refs_0_), custom_call_target="tpu_custom_call" | custom-call | flops 94371840 | bytes 100000 | tf_op jit(solution)/shard_map/pallas_call | solution.py:628
  281.7 3.3 add_convert_fusion
  290.8 8.7 %shard_map.253 = (bf16[3,640,768]{2,1,0:T(8,128)(2,1)}, bf16[3,640,768]{2,1,0:T(8,128)(2,1)}, bf16[3,640,768]{2,1,0:T(8,128)(2,1)}, f32[3,3,8,512]{3,2,1,0:T(8,128)}) custom-call(s32[17]{0:T(128)} %pad_add_fusion.info, bf16[3,640,768]{2,1,0:T(8,128)(2,1)} %get-tuple-element.272.refs_0_, ...), custom_call_target="tpu_custom_call", output_to_operand_aliasing={{0}: (6, {}), {1}: (7, {}), {2}: (8, {}), {3}: (9, {})} | custom-call | flops 208333328 | bytes 347222 | tf_op jit(solution)/shard_map/pallas_call | solution.py:173
  299.5 5.4 %shard_map.254 = bf16[384,1536]{1,0:T(8,128)(2,1)} custom-call(s32[1]{0:T(128)} %bitcast.info.refs_0_, bf16[1920,768]{1,0:T(8,128)(2,1)} %bitcast.247, bf16[1920,768]{1,0:T(8,128)(2,1)} %bitcast.241, bf16[1920,768]{1,0:T(8,128)(2,1)} %bitcast.239, bf16[1920,768]{1,0:T(8,128)(2,1)} %bitcast.217, bf16[1920,768]{1,0:T(8,128)(2,1)} %bitcast.223, ...), custom_call_target="tpu_custom_call" | custom-call | flops 94371840 | bytes 100000 | tf_op jit(solution)/shard_map/pallas_call | solution.py:628
  304.9 5.6 %shard_map.255 = bf16[384,1536]{1,0:T(8,128)(2,1)} custom-call(s32[1]{0:T(128)} %bitcast.info.refs_0_, bf16[1920,768]{1,0:T(8,128)(2,1)} %bitcast.248, bf16[1920,768]{1,0:T(8,128)(2,1)} %bitcast.242, bf16[1920,768]{1,0:T(8,128)(2,1)} %bitcast.240, bf16[1920,768]{1,0:T(8,128)(2,1)} %bitcast.218, bf16[1920,768]{1,0:T(8,128)(2,1)} %bitcast.224, ...), custom_call_target="tpu_custom_call" | custom-call | flops 94371840 | bytes 100000 | tf_op jit(solution)/shard_map/pallas_call | solution.py:628
  312.7 8.5 %shard_map.256 = (bf16[3,640,768]{2,1,0:T(8,128)(2,1)}, bf16[3,640,768]{2,1,0:T(8,128)(2,1)}, bf16[3,640,768]{2,1,0:T(8,128)(2,1)}, f32[3,3,8,512]{3,2,1,0:T(8,128)}) custom-call(s32[17]{0:T(128)} %pad_add_fusion.info, bf16[3,640,768]{2,1,0:T(8,128)(2,1)} %get-tuple-element.272.refs_0_, ...), custom_call_target="tpu_custom_call", output_to_operand_aliasing={{0}: (6, {}), {1}: (7, {}), {2}: (8, {}), {3}: (9, {})} | custom-call | flops 208333328 | bytes 347222 | tf_op jit(solution)/shard_map/pallas_call | solution.py:173
  326.4 2.0 collective-permute-done.11
  330.4 2.5 collective-permute-start.13
  332.8 8.8 %shard_map.257 = (bf16[3,640,768]{2,1,0:T(8,128)(2,1)}, bf16[3,640,768]{2,1,0:T(8,128)(2,1)}, bf16[3,640,768]{2,1,0:T(8,128)(2,1)}, f32[3,3,8,512]{3,2,1,0:T(8,128)}) custom-call(s32[17]{0:T(128)} %pad_add_fusion.info, bf16[3,640,768]{2,1,0:T(8,128)(2,1)} %get-tuple-element.272.refs_0_, ...), custom_call_target="tpu_custom_call", output_to_operand_aliasing={{0}: (6, {}), {1}: (7, {}), {2}: (8, {}), {3}: (9, {})} | custom-call | flops 208333328 | bytes 347222 | tf_op jit(solution)/shard_map/pallas_call | solution.py:173
  343.9 5.1 %shard_map.258 = bf16[384,1536]{1,0:T(8,128)(2,1)} custom-call(s32[1]{0:T(128)} %bitcast.info.refs_0_, bf16[1920,768]{1,0:T(8,128)(2,1)} %bitcast.249, bf16[1920,768]{1,0:T(8,128)(2,1)} %bitcast.219, bf16[1920,768]{1,0:T(8,128)(2,1)} %bitcast.225, bf16[1920,768]{1,0:T(8,128)(2,1)} %bitcast.231, bf16[1920,768]{1,0:T(8,128)(2,1)} %bitcast.220, ...), custom_call_target="tpu_custom_call" | custom-call | flops 94371840 | bytes 100000 | tf_op jit(solution)/shard_map/pallas_call | solution.py:628
  355.4 2.5 collective-permute-start.17
  358.0 5.1 %shard_map.259 = bf16[384,1536]{1,0:T(8,128)(2,1)} custom-call(s32[1]{0:T(128)} %bitcast.info.refs_0_, bf16[1920,768]{1,0:T(8,128)(2,1)} %bitcast.250, bf16[1920,768]{1,0:T(8,128)(2,1)} %bitcast.221, bf16[1920,768]{1,0:T(8,128)(2,1)} %bitcast.227, bf16[1920,768]{1,0:T(8,128)(2,1)} %bitcast.233, bf16[1920,768]{1,0:T(8,128)(2,1)} %bitcast.222, ...), custom_call_target="tpu_custom_call" | custom-call | flops 94371840 | bytes 100000 | tf_op jit(solution)/shard_map/pallas_call | solution.py:628
  364.7 3.3 collective-permute-done.15
  370.7 9.8 %collective-permute-done.17 = bf16[192,768]{1,0:T(8,128)(2,1)S(1)} collective-permute-done((bf16[192,768]{1,0:T(8,128)(2,1)S(1)}, bf16[192,768]{1,0:T(8,128)(2,1)S(1)}, u32[]{:S(2)}, u32[]{:S(2)}) %collective-permute-start.17) | collective-permute-done | bytes 294944 | tf_op jit(solution)/shard_map/ppermute | solution.py:777
  382.3 7.8 %collective-permute-done.19 = bf16[48,3072]{1,0:T(8,128)(2,1)S(1)} collective-permute-done((bf16[48,3072]{1,0:T(8,128)(2,1)S(1)}, bf16[48,3072]{1,0:T(8,128)(2,1)S(1)}, u32[]{:S(2)}, u32[]{:S(2)}) %collective-permute-start.19) | collective-permute-done | bytes 294944 | tf_op jit(solution)/shard_map/ppermute | solution.py:777
  394.3 13.2 %collective-permute-done.23 = bf16[384,768]{1,0:T(8,128)(2,1)S(1)} collective-permute-done((bf16[384,768]{1,0:T(8,128)(2,1)S(1)}, bf16[384,768]{1,0:T(8,128)(2,1)S(1)}, u32[]{:S(2)}, u32[]{:S(2)}) %collective-permute-start.23) | collective-permute-done | bytes 589856 | tf_op jit(solution)/shard_map/ppermute | solution.py:777
  408.6 2.6 collective-permute-done.25
  411.3 2.5 collective-permute-done.26
  414.8 25.5 %collective-permute-done.28 = bf16[48,1536]{1,0:T(8,128)(2,1)S(1)} collective-permute-done((bf16[48,1536]{1,0:T(8,128)(2,1)S(1)}, bf16[48,1536]{1,0:T(8,128)(2,1)S(1)}, u32[]{:S(2)}, u32[]{:S(2)}) %collective-permute-start.28) | collective-permute-done | bytes 147488 | tf_op jit(solution)/shard_map/ppermute | solution.py:777
  440.4 3.5 collective-permute-start.29
  443.9 4.8 collective-permute-done.29
  449.5 2.2 collective-permute-start.36
  451.7 1.9 collective-permute-start.37
  453.7 7.9 %collective-permute-done.33 = bf16[96,1536]{1,0:T(8,128)(2,1)S(1)} collective-permute-done((bf16[96,1536]{1,0:T(8,128)(2,1)S(1)}, bf16[96,1536]{1,0:T(8,128)(2,1)S(1)}, u32[]{:S(2)}, u32[]{:S(2)}) %collective-permute-start.33) | collective-permute-done | bytes 294944 | tf_op jit(solution)/shard_map/ppermute | solution.py:777
  463.4 4.1 shard_map.260
  467.7 5.2 %collective-permute-done.37 = bf16[192,1536]{1,0:T(8,128)(2,1)S(1)} collective-permute-done((bf16[192,1536]{1,0:T(8,128)(2,1)S(1)}, bf16[192,1536]{1,0:T(8,128)(2,1)S(1)}, u32[]{:S(2)}, u32[]{:S(2)}) %collective-permute-start.37) | collective-permute-done | bytes 589856 | tf_op jit(solution)/shard_map/ppermute | solution.py:777
  475.2 3.7 collective-permute-start.42
  478.9 4.1 shard_map.261
  492.1 5.3 %shard_map.262 = (f32[768,2304]{1,0:T(8,128)}, f32[768,768]{1,0:T(8,128)}) custom-call(s32[1]{0:T(128)} %bitcast.info.refs_0_, bf16[384,1536]{1,0:T(8,128)(2,1)S(1)} %bitcast.212, bf16[384,1536]{1,0:T(8,128)(2,1)S(1)} %bitcast.210, bf16[384,1536]{1,0:T(8,128)(2,1)S(1)} %collective-permute-done.40.refs_2_, bf16[384,1536]{1,0:T(8,128)(2,1)} %collective-permute-done.41.refs_3_), custom_call_target="tpu_custom_call" | custom-call | bytes 14000000 | tf_op jit(solution)/shard_map/pallas_call | solution.py:733
  (208 shorter events, 75.8 us)
Async XLA Ops:
  36.7 36.1 %collective-permute-start.1 = (bf16[640,768]{1,0:T(8,128)(2,1)}, bf16[640,768]{1,0:T(8,128)(2,1)S(1)}, u32[]{:S(2)}, u32[]{:S(2)}) collective-permute-start(bf16[640,768]{1,0:T(8,128)(2,1)} %get-tuple-element.188), channel_id=1, source_target_pairs={{0,16},{1,17},{2,18},{3,19},{4,20},{5,21},{6,22},{7,23},{8,24},{9,... | collective-permute-start | bytes 2949128 | tf_op jit(solution)/shard_map/ppermute | solution.py:764
  71.3 23.5 %collective-permute-start = (bf16[640,768]{1,0:T(8,128)(2,1)}, bf16[640,768]{1,0:T(8,128)(2,1)S(1)}, u32[]{:S(2)}, u32[]{:S(2)}) collective-permute-start(bf16[640,768]{1,0:T(8,128)(2,1)} %get-tuple-element.187), channel_id=1, source_target_pairs={{0,16},{1,17},{2,18},{3,19},{4,20},{5,21},{6,22},{7,23},{8,24},{9,... | collective-permute-start | bytes 2949128 | tf_op jit(solution)/shard_map/ppermute | solution.py:764
  94.8 63.2 %collective-permute-start.3 = (bf16[640,768]{1,0:T(8,128)(2,1)}, bf16[640,768]{1,0:T(8,128)(2,1)S(1)}, u32[]{:S(2)}, u32[]{:S(2)}) collective-permute-start(bf16[640,768]{1,0:T(8,128)(2,1)} %get-tuple-element.241), channel_id=1, source_target_pairs={{16,0},{17,1},{18,2},{19,3},{20,4},{21,5},{22,6},{23,7},{24,8},{25... | collective-permute-start | bytes 2949128 | tf_op jit(solution)/shard_map/ppermute | solution.py:764
  116.3 115.3 %collective-permute-start.2 = (bf16[640,768]{1,0:T(8,128)(2,1)}, bf16[640,768]{1,0:T(8,128)(2,1)S(1)}, u32[]{:S(2)}, u32[]{:S(2)}) collective-permute-start(bf16[640,768]{1,0:T(8,128)(2,1)} %get-tuple-element.238), channel_id=1, source_target_pairs={{16,0},{17,1},{18,2},{19,3},{20,4},{21,5},{22,6},{23,7},{24,8},{25... | collective-permute-start | bytes 2949128 | tf_op jit(solution)/shard_map/ppermute | solution.py:764
  118.8 78.4 %copy-start.8 = (f32[2]{0:T(128)}, f32[2]{0:T(128)S(1)}, u32[]{:S(2)}) copy-start(f32[2]{0:T(128)S(1)} %slice_reduce_fusion.3) | copy-start | bytes 28
  119.7 77.4 %copy-start.10 = (f32[2]{0:T(128)}, f32[2]{0:T(128)S(1)}, u32[]{:S(2)}) copy-start(f32[2]{0:T(128)S(1)} %get-tuple-element.359) | copy-start | bytes 28
  119.8 77.4 %copy-start.11 = (f32[2]{0:T(128)}, f32[2]{0:T(128)S(1)}, u32[]{:S(2)}) copy-start(f32[2]{0:T(128)S(1)} %get-tuple-element.360) | copy-start | bytes 28
  158.9 34.4 %copy-start.18 = (bf16[3,640,768]{2,1,0:T(8,128)(2,1)S(1)}, bf16[3,640,768]{2,1,0:T(8,128)(2,1)}, u32[]{:S(2)}) copy-start(bf16[3,640,768]{2,1,0:T(8,128)(2,1)} %get-tuple-element.220.refs_0_) | copy-start | bytes 8847364
  195.0 40.1 %collective-permute-start.5 = (bf16[768,128]{1,0:T(8,128)(2,1)S(1)}, bf16[768,128]{1,0:T(8,128)(2,1)S(1)}, u32[]{:S(2)}, u32[]{:S(2)}) collective-permute-start(bf16[768,128]{1,0:T(8,128)(2,1)S(1)} %fusion.6), channel_id=1, source_target_pairs={{16,0},{17,1},{18,2},{19,3},{20,4},{21,5},{22,6},{23,7},{24,8},{25... | collective-permute-start | bytes 589832 | tf_op jit(solution)/shard_map/ppermute | solution.py:764
  197.7 37.4 %collective-permute-start.4 = (f32[2,4]{0,1:T(4,128)}, f32[2,4]{0,1:T(4,128)S(1)}, u32[]{:S(2)}, u32[]{:S(2)}) collective-permute-start(f32[2,4]{0,1:T(4,128)} %pad_maximum_fusion.2), channel_id=1, source_target_pairs={{16,0},{17,1},{18,2},{19,3},{20,4},{21,5},{22,6},{23,7},{24,8},{25... | collective-permute-start | bytes 104 | tf_op jit(solution)/shard_map/ppermute | solution.py:764
  235.1 17.0 %copy-start.12 = (f32[2,4]{0,1:T(4,128)}, f32[2,4]{0,1:T(4,128)S(1)}, u32[]{:S(2)}) copy-start(f32[2,4]{0,1:T(4,128)S(1)} %collective-permute-done.4) | copy-start | bytes 100
  258.0 12.0 %collective-permute-start.6 = (bf16[1536,768]{1,0:T(8,128)(2,1)}, bf16[1536,768]{1,0:T(8,128)(2,1)}, u32[]{:S(2)}, u32[]{:S(2)}) collective-permute-start(bf16[1536,768]{1,0:T(8,128)(2,1)} %shard_map.249), channel_id=1, source_target_pairs={{0,1},{1,0},{2,3},{3,2},{4,5},{5,4},{6,7},{7,6},{8,9},{9,8},{10,11... | collective-permute-start | bytes 7077896 | tf_op jit(solution)/shard_map/ppermute | solution.py:777
  269.6 12.2 %collective-permute-start.7 = (bf16[384,3072]{1,0:T(8,128)(2,1)}, bf16[384,3072]{1,0:T(8,128)(2,1)}, u32[]{:S(2)}, u32[]{:S(2)}) collective-permute-start(bf16[384,3072]{1,0:T(8,128)(2,1)} %shard_map.251), channel_id=1, source_target_pairs={{0,1},{1,0},{2,3},{3,2},{4,5},{5,4},{6,7},{7,6},{8,9},{9,8},{10,11... | collective-permute-start | bytes 7077896 | tf_op jit(solution)/shard_map/ppermute | solution.py:777
  274.8 35.8 %collective-permute-start.8 = (bf16[768,768]{1,0:T(8,128)(2,1)}, bf16[768,768]{1,0:T(8,128)(2,1)}, u32[]{:S(2)}, u32[]{:S(2)}) collective-permute-start(bf16[768,768]{1,0:T(8,128)(2,1)} %dynamic-slice_bitcast_fusion.1), channel_id=1, source_target_pairs={{0,2},{1,3},{2,0},{3,1},{4,6},{5,7},{6,4},{7,5},{8,10},{9,11},{10,... | collective-permute-start | bytes 3538952 | tf_op jit(solution)/shard_map/ppermute | solution.py:777
  286.1 35.1 %collective-permute-start.9 = (bf16[192,3072]{1,0:T(8,128)(2,1)}, bf16[192,3072]{1,0:T(8,128)(2,1)}, u32[]{:S(2)}, u32[]{:S(2)}) collective-permute-start(bf16[192,3072]{1,0:T(8,128)(2,1)} %dynamic-slice_bitcast_fusion), channel_id=1, source_target_pairs={{0,4},{1,5},{2,6},{3,7},{4,0},{5,1},{6,2},{7,3},{8,12},{9,13},{10,... | collective-permute-start | bytes 3538952 | tf_op jit(solution)/shard_map/ppermute | solution.py:777
  304.9 18.5 %collective-permute-start.10 = (bf16[384,1536]{1,0:T(8,128)(2,1)}, bf16[384,1536]{1,0:T(8,128)(2,1)S(1)}, u32[]{:S(2)}, u32[]{:S(2)}) collective-permute-start(bf16[384,1536]{1,0:T(8,128)(2,1)} %shard_map.254), channel_id=1, source_target_pairs={{0,1},{1,0},{2,3},{3,2},{4,5},{5,4},{6,7},{7,6},{8,9},{9,8},{10,11... | collective-permute-start | bytes 3538952 | tf_op jit(solution)/shard_map/ppermute | solution.py:777
  312.2 16.3 %collective-permute-start.11 = (bf16[384,768]{1,0:T(8,128)(2,1)S(1)}, bf16[384,768]{1,0:T(8,128)(2,1)}, u32[]{:S(2)}, u32[]{:S(2)}) collective-permute-start(bf16[384,768]{1,0:T(8,128)(2,1)S(1)} %dynamic-slice_bitcast_fusion.5), channel_id=1, source_target_pairs={{0,4},{1,5},{2,6},{3,7},{4,0},{5,1},{6,2},{7,3},{8,12},{9,13},{10,... | collective-permute-start | bytes 1769480 | tf_op jit(solution)/shard_map/ppermute | solution.py:777
  323.0 18.6 %collective-permute-start.12 = (bf16[96,3072]{1,0:T(8,128)(2,1)S(1)}, bf16[96,3072]{1,0:T(8,128)(2,1)S(1)}, u32[]{:S(2)}, u32[]{:S(2)}) collective-permute-start(bf16[96,3072]{1,0:T(8,128)(2,1)S(1)} %dynamic-slice_bitcast_fusion.4), channel_id=1, source_target_pairs={{0,2},{1,3},{2,0},{3,1},{4,6},{5,7},{6,4},{7,5},{8,10},{9,11},{10,... | collective-permute-start | bytes 1769480 | tf_op jit(solution)/shard_map/ppermute | solution.py:777
  324.6 38.5 %collective-permute-start.14 = (bf16[192,1536]{1,0:T(8,128)(2,1)}, bf16[192,1536]{1,0:T(8,128)(2,1)}, u32[]{:S(2)}, u32[]{:S(2)}) collective-permute-start(bf16[192,1536]{1,0:T(8,128)(2,1)} %dynamic-slice_bitcast_fusion.3), channel_id=1, source_target_pairs={{0,4},{1,5},{2,6},{3,7},{4,0},{5,1},{6,2},{7,3},{8,12},{9,13},{10,... | collective-permute-start | bytes 1769480 | tf_op jit(solution)/shard_map/ppermute | solution.py:777
  330.4 24.0 %collective-permute-start.13 = (bf16[192,768]{1,0:T(8,128)(2,1)}, bf16[192,768]{1,0:T(8,128)(2,1)}, u32[]{:S(2)}, u32[]{:S(2)}) collective-permute-start(bf16[192,768]{1,0:T(8,128)(2,1)} %dynamic-slice_bitcast_fusion.9), channel_id=1, source_target_pairs={{0,8},{1,9},{2,10},{3,11},{4,12},{5,13},{6,14},{7,15},{8,0},{9,1},... | collective-permute-start | bytes 884744 | tf_op jit(solution)/shard_map/ppermute | solution.py:777
  342.5 25.4 %collective-permute-start.15 = (bf16[48,3072]{1,0:T(8,128)(2,1)}, bf16[48,3072]{1,0:T(8,128)(2,1)}, u32[]{:S(2)}, u32[]{:S(2)}) collective-permute-start(bf16[48,3072]{1,0:T(8,128)(2,1)} %dynamic-slice_bitcast_fusion.8), channel_id=1, source_target_pairs={{0,8},{1,9},{2,10},{3,11},{4,12},{5,13},{6,14},{7,15},{8,0},{9,1},... | collective-permute-start | bytes 884744 | tf_op jit(solution)/shard_map/ppermute | solution.py:777
  349.1 20.0 %collective-permute-start.16 = (bf16[384,1536]{1,0:T(8,128)(2,1)}, bf16[384,1536]{1,0:T(8,128)(2,1)S(1)}, u32[]{:S(2)}, u32[]{:S(2)}) collective-permute-start(bf16[384,1536]{1,0:T(8,128)(2,1)} %shard_map.258), channel_id=1, source_target_pairs={{0,1},{1,0},{2,3},{3,2},{4,5},{5,4},{6,7},{7,6},{8,9},{9,8},{10,11... | collective-permute-start | bytes 3538952 | tf_op jit(solution)/shard_map/ppermute | solution.py:777
  353.8 36.3 %collective-permute-start.20 = (bf16[140,768]{1,0:T(8,128)(2,1)S(1)}, bf16[140,768]{1,0:T(8,128)(2,1)S(1)}, u32[]{:S(2)}, u32[]{:S(2)}) collective-permute-start(bf16[140,768]{1,0:T(8,128)(2,1)S(1)} %pad_maximum_fusion), channel_id=1, source_target_pairs={{0,1},{1,0},{2,3},{3,2},{4,5},{5,4},{6,7},{7,6},{8,9},{9,8},{10,11... | collective-permute-start | bytes 645128 | tf_op jit(solution)/shard_map/ppermute | solution.py:777
  355.4 25.1 %collective-permute-start.17 = (bf16[192,768]{1,0:T(8,128)(2,1)S(1)}, bf16[192,768]{1,0:T(8,128)(2,1)S(1)}, u32[]{:S(2)}, u32[]{:S(2)}) collective-permute-start(bf16[192,768]{1,0:T(8,128)(2,1)S(1)} %fusion.10), channel_id=1, source_target_pairs={{0,8},{1,9},{2,10},{3,11},{4,12},{5,13},{6,14},{7,15},{8,0},{9,1},... | collective-permute-start | bytes 884744 | tf_op jit(solution)/shard_map/ppermute | solution.py:777
  364.4 16.1 %collective-permute-start.18 = (bf16[96,1536]{1,0:T(8,128)(2,1)S(1)}, bf16[96,1536]{1,0:T(8,128)(2,1)S(1)}, u32[]{:S(2)}, u32[]{:S(2)}) collective-permute-start(bf16[96,1536]{1,0:T(8,128)(2,1)S(1)} %dynamic-slice_bitcast_fusion.7), channel_id=1, source_target_pairs={{0,2},{1,3},{2,0},{3,1},{4,6},{5,7},{6,4},{7,5},{8,10},{9,11},{10,... | collective-permute-start | bytes 884744 | tf_op jit(solution)/shard_map/ppermute | solution.py:777
  369.0 21.1 %collective-permute-start.19 = (bf16[48,3072]{1,0:T(8,128)(2,1)S(1)}, bf16[48,3072]{1,0:T(8,128)(2,1)S(1)}, u32[]{:S(2)}, u32[]{:S(2)}) collective-permute-start(bf16[48,3072]{1,0:T(8,128)(2,1)S(1)} %fusion.9), channel_id=1, source_target_pairs={{0,8},{1,9},{2,10},{3,11},{4,12},{5,13},{6,14},{7,15},{8,0},{9,1},... | collective-permute-start | bytes 884744 | tf_op jit(solution)/shard_map/ppermute | solution.py:777
  369.4 22.8 %collective-permute-start.21 = (bf16[192,1536]{1,0:T(8,128)(2,1)S(1)}, bf16[192,1536]{1,0:T(8,128)(2,1)S(1)}, u32[]{:S(2)}, u32[]{:S(2)}) collective-permute-start(bf16[192,1536]{1,0:T(8,128)(2,1)S(1)} %dynamic-slice_bitcast_fusion.2), channel_id=1, source_target_pairs={{0,2},{1,3},{2,0},{3,1},{4,6},{5,7},{6,4},{7,5},{8,10},{9,11},{10,... | collective-permute-start | bytes 1769480 | tf_op jit(solution)/shard_map/ppermute | solution.py:777
  380.7 12.5 %collective-permute-start.22 = (bf16[48,1536]{1,0:T(8,128)(2,1)S(1)}, bf16[48,1536]{1,0:T(8,128)(2,1)S(1)}, u32[]{:S(2)}, u32[]{:S(2)}) collective-permute-start(bf16[48,1536]{1,0:T(8,128)(2,1)S(1)} %dynamic-slice_bitcast_fusion.11), channel_id=1, source_target_pairs={{0,8},{1,9},{2,10},{3,11},{4,12},{5,13},{6,14},{7,15},{8,0},{9,1},... | collective-permute-start | bytes 442376 | tf_op jit(solution)/shard_map/ppermute | solution.py:777
  380.7 26.8 %collective-permute-start.23 = (bf16[384,768]{1,0:T(8,128)(2,1)S(1)}, bf16[384,768]{1,0:T(8,128)(2,1)S(1)}, u32[]{:S(2)}, u32[]{:S(2)}) collective-permute-start(bf16[384,768]{1,0:T(8,128)(2,1)S(1)} %bitcast.299), channel_id=1, source_target_pairs={{0,4},{1,5},{2,6},{3,7},{4,0},{5,1},{6,2},{7,3},{8,12},{9,13},{10,... | collective-permute-start | bytes 1769480 | tf_op jit(solution)/shard_map/ppermute | solution.py:777
  390.2 18.1 %collective-permute-start.24 = (bf16[140,768]{1,0:T(8,128)(2,1)S(1)}, bf16[140,768]{1,0:T(8,128)(2,1)S(1)}, u32[]{:S(2)}, u32[]{:S(2)}) collective-permute-start(bf16[140,768]{1,0:T(8,128)(2,1)S(1)} %add_convert_fusion.7), channel_id=1, source_target_pairs={{0,2},{1,3},{2,0},{3,1},{4,6},{5,7},{6,4},{7,5},{8,10},{9,11},{10,... | collective-permute-start | bytes 645128 | tf_op jit(solution)/shard_map/ppermute | solution.py:777
  391.3 19.9 %collective-permute-start.25 = (bf16[96,3072]{1,0:T(8,128)(2,1)S(1)}, bf16[96,3072]{1,0:T(8,128)(2,1)S(1)}, u32[]{:S(2)}, u32[]{:S(2)}) collective-permute-start(bf16[96,3072]{1,0:T(8,128)(2,1)S(1)} %bitcast.301), channel_id=1, source_target_pairs={{0,2},{1,3},{2,0},{3,1},{4,6},{5,7},{6,4},{7,5},{8,10},{9,11},{10,... | collective-permute-start | bytes 1769480 | tf_op jit(solution)/shard_map/ppermute | solution.py:777
  392.5 21.4 %collective-permute-start.26 = (bf16[96,1536]{1,0:T(8,128)(2,1)S(1)}, bf16[96,1536]{1,0:T(8,128)(2,1)S(1)}, u32[]{:S(2)}, u32[]{:S(2)}) collective-permute-start(bf16[96,1536]{1,0:T(8,128)(2,1)S(1)} %dynamic-slice_bitcast_fusion.6), channel_id=1, source_target_pairs={{0,4},{1,5},{2,6},{3,7},{4,0},{5,1},{6,2},{7,3},{8,12},{9,13},{10,... | collective-permute-start | bytes 884744 | tf_op jit(solution)/shard_map/ppermute | solution.py:777
  393.2 20.9 %collective-permute-start.27 = (bf16[48,1536]{1,0:T(8,128)(2,1)S(1)}, bf16[48,1536]{1,0:T(8,128)(2,1)S(1)}, u32[]{:S(2)}, u32[]{:S(2)}) collective-permute-start(bf16[48,1536]{1,0:T(8,128)(2,1)S(1)} %fusion.13), channel_id=1, source_target_pairs={{0,8},{1,9},{2,10},{3,11},{4,12},{5,13},{6,14},{7,15},{8,0},{9,1},... | collective-permute-start | bytes 442376 | tf_op jit(solution)/shard_map/ppermute | solution.py:777
  407.6 41.5 %collective-permute-start.30 = (bf16[768,768]{1,0:T(8,128)(2,1)S(1)}, bf16[768,768]{1,0:T(8,128)(2,1)S(1)}, u32[]{:S(2)}, u32[]{:S(2)}) collective-permute-start(bf16[768,768]{1,0:T(8,128)(2,1)S(1)} %bitcast.291), channel_id=1, source_target_pairs={{0,2},{1,3},{2,0},{3,1},{4,6},{5,7},{6,4},{7,5},{8,10},{9,11},{10,... | collective-permute-start | bytes 3538952 | tf_op jit(solution)/shard_map/ppermute | solution.py:777
  408.3 41.1 %collective-permute-start.32 = (bf16[140,768]{1,0:T(8,128)(2,1)S(1)}, bf16[140,768]{1,0:T(8,128)(2,1)S(1)}, u32[]{:S(2)}, u32[]{:S(2)}) collective-permute-start(bf16[140,768]{1,0:T(8,128)(2,1)S(1)} %add_convert_fusion.6), channel_id=1, source_target_pairs={{0,4},{1,5},{2,6},{3,7},{4,0},{5,1},{6,2},{7,3},{8,12},{9,13},{10,... | collective-permute-start | bytes 645128 | tf_op jit(solution)/shard_map/ppermute | solution.py:777
  411.3 51.9 %collective-permute-start.34 = (bf16[192,3072]{1,0:T(8,128)(2,1)S(1)}, bf16[192,3072]{1,0:T(8,128)(2,1)S(1)}, u32[]{:S(2)}, u32[]{:S(2)}) collective-permute-start(bf16[192,3072]{1,0:T(8,128)(2,1)S(1)} %bitcast.293), channel_id=1, source_target_pairs={{0,4},{1,5},{2,6},{3,7},{4,0},{5,1},{6,2},{7,3},{8,12},{9,13},{10,... | collective-permute-start | bytes 3538952 | tf_op jit(solution)/shard_map/ppermute | solution.py:777
  413.9 26.4 %collective-permute-start.28 = (bf16[48,1536]{1,0:T(8,128)(2,1)S(1)}, bf16[48,1536]{1,0:T(8,128)(2,1)S(1)}, u32[]{:S(2)}, u32[]{:S(2)}) collective-permute-start(bf16[48,1536]{1,0:T(8,128)(2,1)S(1)} %dynamic-slice_bitcast_fusion.10), channel_id=1, source_target_pairs={{0,8},{1,9},{2,10},{3,11},{4,12},{5,13},{6,14},{7,15},{8,0},{9,1},... | collective-permute-start | bytes 442376 | tf_op jit(solution)/shard_map/ppermute | solution.py:777
  414.1 35.3 %collective-permute-start.31 = (bf16[96,1536]{1,0:T(8,128)(2,1)S(1)}, bf16[96,1536]{1,0:T(8,128)(2,1)S(1)}, u32[]{:S(2)}, u32[]{:S(2)}) collective-permute-start(bf16[96,1536]{1,0:T(8,128)(2,1)S(1)} %bitcast.321), channel_id=1, source_target_pairs={{0,2},{1,3},{2,0},{3,1},{4,6},{5,7},{6,4},{7,5},{8,10},{9,11},{10,... | collective-permute-start | bytes 884744 | tf_op jit(solution)/shard_map/ppermute | solution.py:777
  440.4 8.4 %collective-permute-start.29 = (bf16[48,1536]{1,0:T(8,128)(2,1)S(1)}, bf16[48,1536]{1,0:T(8,128)(2,1)S(1)}, u32[]{:S(2)}, u32[]{:S(2)}) collective-permute-start(bf16[48,1536]{1,0:T(8,128)(2,1)S(1)} %fusion.12), channel_id=1, source_target_pairs={{0,8},{1,9},{2,10},{3,11},{4,12},{5,13},{6,14},{7,15},{8,0},{9,1},... | collective-permute-start | bytes 442376 | tf_op jit(solution)/shard_map/ppermute | solution.py:777
  448.7 12.9 %collective-permute-start.33 = (bf16[96,1536]{1,0:T(8,128)(2,1)S(1)}, bf16[96,1536]{1,0:T(8,128)(2,1)S(1)}, u32[]{:S(2)}, u32[]{:S(2)}) collective-permute-start(bf16[96,1536]{1,0:T(8,128)(2,1)S(1)} %bitcast.319), channel_id=1, source_target_pairs={{0,4},{1,5},{2,6},{3,7},{4,0},{5,1},{6,2},{7,3},{8,12},{9,13},{10,... | collective-permute-start | bytes 884744 | tf_op jit(solution)/shard_map/ppermute | solution.py:777
  449.2 14.2 %collective-permute-start.35 = (bf16[1536,768]{1,0:T(8,128)(2,1)S(1)}, bf16[1536,768]{1,0:T(8,128)(2,1)S(1)}, u32[]{:S(2)}, u32[]{:S(2)}) collective-permute-start(bf16[1536,768]{1,0:T(8,128)(2,1)S(1)} %bitcast.205), channel_id=1, source_target_pairs={{0,1},{1,0},{2,3},{3,2},{4,5},{5,4},{6,7},{7,6},{8,9},{9,8},{10,11... | collective-permute-start | bytes 7077896 | tf_op jit(solution)/shard_map/ppermute | solution.py:777
  449.5 18.0 %collective-permute-start.36 = (bf16[140,768]{1,0:T(8,128)(2,1)S(1)}, bf16[140,768]{1,0:T(8,128)(2,1)S(1)}, u32[]{:S(2)}, u32[]{:S(2)}) collective-permute-start(bf16[140,768]{1,0:T(8,128)(2,1)S(1)} %add_convert_fusion.5), channel_id=1, source_target_pairs={{0,8},{1,9},{2,10},{3,11},{4,12},{5,13},{6,14},{7,15},{8,0},{9,1},... | collective-permute-start | bytes 645128 | tf_op jit(solution)/shard_map/ppermute | solution.py:777
  451.7 21.2 %collective-permute-start.37 = (bf16[192,1536]{1,0:T(8,128)(2,1)S(1)}, bf16[192,1536]{1,0:T(8,128)(2,1)S(1)}, u32[]{:S(2)}, u32[]{:S(2)}) collective-permute-start(bf16[192,1536]{1,0:T(8,128)(2,1)S(1)} %bitcast.303), channel_id=1, source_target_pairs={{0,4},{1,5},{2,6},{3,7},{4,0},{5,1},{6,2},{7,3},{8,12},{9,13},{10,... | collective-permute-start | bytes 1769480 | tf_op jit(solution)/shard_map/ppermute | solution.py:777
  461.6 11.5 %collective-permute-start.38 = (bf16[192,1536]{1,0:T(8,128)(2,1)S(1)}, bf16[192,1536]{1,0:T(8,128)(2,1)S(1)}, u32[]{:S(2)}, u32[]{:S(2)}) collective-permute-start(bf16[192,1536]{1,0:T(8,128)(2,1)S(1)} %bitcast.305), channel_id=1, source_target_pairs={{0,2},{1,3},{2,0},{3,1},{4,6},{5,7},{6,4},{7,5},{8,10},{9,11},{10,... | collective-permute-start | bytes 1769480 | tf_op jit(solution)/shard_map/ppermute | solution.py:777
  463.3 15.6 %collective-permute-start.39 = (bf16[384,3072]{1,0:T(8,128)(2,1)S(1)}, bf16[384,3072]{1,0:T(8,128)(2,1)S(1)}, u32[]{:S(2)}, u32[]{:S(2)}) collective-permute-start(bf16[384,3072]{1,0:T(8,128)(2,1)S(1)} %bitcast.207), channel_id=1, source_target_pairs={{0,1},{1,0},{2,3},{3,2},{4,5},{5,4},{6,7},{7,6},{8,9},{9,8},{10,11... | collective-permute-start | bytes 7077896 | tf_op jit(solution)/shard_map/ppermute | solution.py:777
  472.9 19.2 %collective-permute-start.40 = (bf16[384,1536]{1,0:T(8,128)(2,1)S(1)}, bf16[384,1536]{1,0:T(8,128)(2,1)S(1)}, u32[]{:S(2)}, u32[]{:S(2)}) collective-permute-start(bf16[384,1536]{1,0:T(8,128)(2,1)S(1)} %bitcast.211), channel_id=1, source_target_pairs={{0,1},{1,0},{2,3},{3,2},{4,5},{5,4},{6,7},{7,6},{8,9},{9,8},{10,11... | collective-permute-start | bytes 3538952 | tf_op jit(solution)/shard_map/ppermute | solution.py:777
  473.2 18.9 %collective-permute-start.41 = (bf16[384,1536]{1,0:T(8,128)(2,1)S(1)}, bf16[384,1536]{1,0:T(8,128)(2,1)}, u32[]{:S(2)}, u32[]{:S(2)}) collective-permute-start(bf16[384,1536]{1,0:T(8,128)(2,1)S(1)} %bitcast.209), channel_id=1, source_target_pairs={{0,1},{1,0},{2,3},{3,2},{4,5},{5,4},{6,7},{7,6},{8,9},{9,8},{10,11... | collective-permute-start | bytes 3538952 | tf_op jit(solution)/shard_map/ppermute | solution.py:777
  475.2 14.2 %collective-permute-start.42 = (f32[2,4]{0,1:T(4,128)}, f32[2,4]{0,1:T(4,128)}, u32[]{:S(2)}, u32[]{:S(2)}) collective-permute-start(f32[2,4]{0,1:T(4,128)} %pad_maximum_fusion.2), channel_id=1, source_target_pairs={{0,16},{1,17},{2,18},{3,19},{4,20},{5,21},{6,22},{7,23},{8,24},{9,... | collective-permute-start | bytes 104 | tf_op jit(solution)/shard_map/ppermute | solution.py:764
  (14 other events, 65.0 us)

commit v8 on v7

--- a/solution.py
+++ b/solution.py
@@ -22,6 +22,7 @@
 QROWS = NQ * QLEN
 SLAB = 256
 FFBLOCK = 1536
+BACKBLOCK = 768
 VMEM_LIMIT = 56 * 1024 * 1024
 NEG = -1e30
 GRAD_STEPS = 2
@@ -418,9 +419,9 @@
         at_slot(rows, width),
         at_slot(rows, 1),
         one(1, width),
-        pl.BlockSpec((None, rows, FFBLOCK), lambda g, i: (slot(i), 0, at(g, i))),
-        pl.BlockSpec((FFBLOCK, width), lambda g, i: (at(g, i), 0)),
-        pl.BlockSpec((width, FFBLOCK), lambda g, i: (0, at(g, i))),
+        pl.BlockSpec((None, rows, BACKBLOCK), lambda g, i: (slot(i), 0, at(g, i))),
+        pl.BlockSpec((BACKBLOCK, width), lambda g, i: (at(g, i), 0)),
+        pl.BlockSpec((width, BACKBLOCK), lambda g, i: (0, at(g, i))),
         at_slot(rows, width),
         at_slot(rows, 1),
         one(1, width),
@@ -429,11 +430,11 @@
     rows_at = lambda shape, kind: ((slots,) + shape, kind, (None,) + shape, lambda g, i: (slot(i), 0, 0))
     shapes = [
         rows_at((rows, width), BF),
-        ((slots, rows, ff), BF, (None, rows, FFBLOCK), lambda g, i: (slot(i), 0, at(g, i))),
+        ((slots, rows, ff), BF, (None, rows, BACKBLOCK), lambda g, i: (slot(i), 0, at(g, i))),
         rows_at((rows, width), BF),
         rows_at((rows, wc.shape[1]), BF),
         rows_at((8, width), F32),
-        ((slots, 8, ff), F32, (None, 8, FFBLOCK), lambda g, i: (slot(i), 0, at(g, i))),
+        ((slots, 8, ff), F32, (None, 8, BACKBLOCK), lambda g, i: (slot(i), 0, at(g, i))),
     ]
     return in_specs, args, shapes, [pltpu.VMEM((rows, width), F32), pltpu.VMEM((rows, width), F32)]
 
@@ -441,7 +442,7 @@
 def ffn_backward(phase, micros, grad_scale, info, received, kept, weights, old):
     section, micro = 1 - phase // micros, phase % micros
     in_specs, args, shapes, scratch = ffn_bwd_parts(section, micro, micros, received, kept, weights, lambda g: g)
-    steps = weights[3].shape[1] // FFBLOCK
+    steps = weights[3].shape[1] // BACKBLOCK
 
     def body(micro, info, *refs):
         ffn_bwd_live(pl.program_id(0), steps, section == 1, micros, grad_scale, micro, info, *refs)
@@ -573,7 +574,7 @@
     section, micro = 1 - phase // micros, phase % micros
     shape = ffn_kept[0].shape
     _, rows, width = shape
-    first, second = we.shape[1] // FFBLOCK, width // SLAB
+    first, second = we.shape[1] // BACKBLOCK, width // SLAB
     in_specs, args, shapes, scratch = ffn_bwd_parts(
         section, micro, micros, received, ffn_kept, (wc, gains, wr, we), lambda g: jnp.minimum(g, first - 1)
     )

time: 506 us -> 505 us (level)
  no operation moved by 1% of the time
where the time goes in v8:
time: 505 us; the launch traced here: 496 us
  Pallas kernels  260 us (51%)
  waiting for transfers between devices  141 us (28%)
  starting transfers between devices  41 us (8%)
  local copies, waits for them, and re-layouts  25.8 us (5%)
  other arithmetic  25.2 us (5%)
    pallas_call x11, Pallas kernels, call(): pl.pallas_call(body, out_shape=[jax.ShapeDtypeStruct(s[0], s[1]) for s in...  181 us
    ppermute x36, waiting for transfers between devices, swapped(): return lax.ppermute(array, axis, [(i, i ^ bit) for i in range(count)])  85.3 us
    pallas_call x12, Pallas kernels, grad_call(): pl.pallas_call(body, out_shape=out_shape, grid_spec=pltpu.PrefetchScalarG...  65.2 us
    ppermute x7, waiting for transfers between devices, passed_along(): return lax.ppermute(array, axis, pairs)  55.8 us
    ppermute x36, starting transfers between devices, swapped(): return lax.ppermute(array, axis, [(i, i ^ bit) for i in range(count)])  30 us
    convert_element_type x19, other arithmetic, sum_low(): return (kept.astype(F32) + got.astype(F32)).astype(BF)  14.7 us
    pallas_call x3, Pallas kernels, widened(): pl.pallas_call(widen_body, out_shape=[jax.ShapeDtypeStruct(shape, F32) fo...  13.4 us
    ppermute x7, starting transfers between devices, passed_along(): return lax.ppermute(array, axis, pairs)  11.1 us
  transfers between devices with their start and end apart: 43, of which 16 were waited for; matrix products, arithmetic and copies ran while one was open for 9% of the time, Pallas kernels for 40%

profile of v8, /device:TPU:0, one launch (start us, length us, event | category | flops | bytes accessed | tf_op | source)
XLA Modules:
  0.0 496.4 jit_solution(9755415550994301179)
XLA Ops:
  4.1 32.6 %shard_map.237 = (bf16[3,640,768]{2,1,0:T(8,128)(2,1)}, bf16[3,3,640,768]{3,2,1,0:T(8,128)(2,1)}, f32[3,3,8,640]{3,2,1,0:T(8,128)}, bf16[3,640,768]{2,1,0:T(8,12...) custom-call(s32[17]{0:T(128)} %pad_add_fusion.info, ...), custom_call_target="tpu_custom_call" | custom-call | flops 32000000000 | bytes 20000000 | tf_op jit(solution)/shard_map/pallas_call | solution.py:174
  38.3 32.7 %shard_map.238 = (bf16[3,640,768]{2,1,0:T(8,128)(2,1)}, bf16[3,3,640,768]{3,2,1,0:T(8,128)(2,1)}, f32[3,3,8,640]{3,2,1,0:T(8,128)}, bf16[3,640,768]{2,1,0:T(8,12...) custom-call(s32[17]{0:T(128)} %pad_add_fusion.info, ...), custom_call_target="tpu_custom_call", output_to_operand_aliasing={{0}: (17, {}), {1}: (18, {}), {2}: (19, {}), {3}: (20, {}),... | custom-call | flops 32000000000 | bytes 20000000 | tf_op jit(solution)/shard_map/pallas_call | solution.py:174
  73.7 9.7 %shard_map.239 = (bf16[3,640,768]{2,1,0:T(8,128)(2,1)}, bf16[3,3,640,768]{3,2,1,0:T(8,128)(2,1)}, f32[3,3,8,640]{3,2,1,0:T(8,128)}, bf16[3,640,768]{2,1,0:T(8,12...) custom-call(s32[17]{0:T(128)} %pad_add_fusion.info, ...), custom_call_target="tpu_custom_call", output_to_operand_aliasing={{0}: (17, {}), {1}: (18, {}), {2}: (19, {}), {3}: (20, {}),... | custom-call | flops 32000000000 | bytes 20000000 | tf_op jit(solution)/shard_map/pallas_call | solution.py:174
  83.5 9.6 %shard_map.240 = (bf16[3,640,768]{2,1,0:T(8,128)(2,1)}, bf16[3,640,3072]{2,1,0:T(8,128)(2,1)}, bf16[3,640,768]{2,1,0:T(8,128)(2,1)}, bf16[3,640,128]{2,1,0:T(8,1...) custom-call(s32[17]{0:T(128)} %pad_add_fusion.info, ...), custom_call_target="tpu_custom_call" | custom-call | flops 32000000000 | bytes 20000000 | tf_op jit(solution)/shard_map/pallas_call | solution.py:174
  95.8 10.0 %shard_map.241 = (bf16[3,640,768]{2,1,0:T(8,128)(2,1)}, bf16[3,3,640,768]{3,2,1,0:T(8,128)(2,1)}, f32[3,3,8,640]{3,2,1,0:T(8,128)}, bf16[3,640,768]{2,1,0:T(8,12...) custom-call(s32[17]{0:T(128)} %pad_add_fusion.info, ...), custom_call_target="tpu_custom_call", output_to_operand_aliasing={{0}: (17, {}), {1}: (18, {}), {2}: (19, {}), {3}: (20, {}),... | custom-call | flops 32000000000 | bytes 20000000 | tf_op jit(solution)/shard_map/pallas_call | solution.py:174
  105.8 9.8 %shard_map.242 = (bf16[3,640,768]{2,1,0:T(8,128)(2,1)}, bf16[3,640,3072]{2,1,0:T(8,128)(2,1)}, bf16[3,640,768]{2,1,0:T(8,128)(2,1)}, bf16[3,640,128]{2,1,0:T(8,1...) custom-call(s32[17]{0:T(128)} %pad_add_fusion.info, ...), custom_call_target="tpu_custom_call", output_to_operand_aliasing={{0}: (19, {}), {1}: (20, {}), {2}: (21, {}), {3}: (22, {}),... | custom-call | flops 32000000000 | bytes 20000000 | tf_op jit(solution)/shard_map/pallas_call | solution.py:174
  118.9 39.2 %collective-permute-done.3.refs_0_ = bf16[640,768]{1,0:T(8,128)(2,1)S(1)} collective-permute-done((bf16[640,768]{1,0:T(8,128)(2,1)}, bf16[640,768]{1,0:T(8,128)(2,1)S(1)}, u32[]{:S(2)}, u32[]{:S(2)}) %collective-permute-start.3) | collective-permute-done | bytes 983072 | tf_op jit(solution)/shard_map/ppermute | solution.py:765
  159.0 34.3 %shard_map.243 = (bf16[3,640,768]{2,1,0:T(8,128)(2,1)}, bf16[3,640,3072]{2,1,0:T(8,128)(2,1)}, bf16[3,640,768]{2,1,0:T(8,128)(2,1)}, bf16[3,640,128]{2,1,0:T(8,1...) custom-call(s32[17]{0:T(128)} %pad_add_fusion.info, ...), custom_call_target="tpu_custom_call", output_to_operand_aliasing={{0}: (15, {}), {1}: (16, {}), {2}: (17, {}), {3}: (18, {}),... | custom-call | flops 32000000000 | bytes 20000000 | tf_op jit(solution)/shard_map/pallas_call | solution.py:174
  199.0 5.4 %shard_map.247.refs_0_ = bf16[384,3072]{1,0:T(8,128)(2,1)} custom-call(s32[1]{0:T(128)} %bitcast.info.refs_0_, bf16[1920,768]{1,0:T(8,128)(2,1)} %bitcast.251, bf16[1920,3072]{1,0:T(8,128)(2,1)} %bitcast.213), custom_call_target="tpu_custom_call" | custom-call | flops 94371840 | bytes 100000 | tf_op jit(solution)/shard_map/pallas_call | solution.py:629
  204.4 4.9 shard_map.245.refs_0_
  209.3 5.5 %shard_map.246.refs_0_ = bf16[1536,768]{1,0:T(8,128)(2,1)} custom-call(s32[1]{0:T(128)} %bitcast.info.refs_0_, bf16[1920,3072]{1,0:T(8,128)(2,1)} %bitcast.235, bf16[1920,768]{1,0:T(8,128)(2,1)} %bitcast.243), custom_call_target="tpu_custom_call" | custom-call | flops 94371840 | bytes 100000 | tf_op jit(solution)/shard_map/pallas_call | solution.py:629
  214.8 5.5 %shard_map.244.refs_0_ = bf16[1536,768]{1,0:T(8,128)(2,1)} custom-call(s32[1]{0:T(128)} %bitcast.info.refs_0_, bf16[1920,3072]{1,0:T(8,128)(2,1)} %bitcast.236, bf16[1920,768]{1,0:T(8,128)(2,1)} %bitcast.244), custom_call_target="tpu_custom_call" | custom-call | flops 94371840 | bytes 100000 | tf_op jit(solution)/shard_map/pallas_call | solution.py:629
  220.3 11.7 %collective-permute-done.2.refs_0_ = bf16[640,768]{1,0:T(8,128)(2,1)S(1)} collective-permute-done((bf16[640,768]{1,0:T(8,128)(2,1)}, bf16[640,768]{1,0:T(8,128)(2,1)S(1)}, u32[]{:S(2)}, u32[]{:S(2)}) %collective-permute-start.2) | collective-permute-done | bytes 983072 | tf_op jit(solution)/shard_map/ppermute | solution.py:765
  232.0 3.5 collective-permute-done.4
  235.4 16.6 %shard_map.248 = (bf16[3,640,768]{2,1,0:T(8,128)(2,1)}, bf16[3,640,3072]{2,1,0:T(8,128)(2,1)}, bf16[3,640,768]{2,1,0:T(8,128)(2,1)}, bf16[3,640,128]{2,1,0:T(8,1...) custom-call(s32[17]{0:T(128)} %pad_add_fusion.info, ...), custom_call_target="tpu_custom_call", output_to_operand_aliasing={{0}: (11, {}), {1}: (12, {}), {2}: (13, {}), {3}: (14, {}),... | custom-call | flops 12000000000 | bytes 20000000 | tf_op jit(solution)/shard_map/pallas_call | solution.py:174
  252.1 5.9 %shard_map.249 = bf16[1536,768]{1,0:T(8,128)(2,1)} custom-call(s32[1]{0:T(128)} %bitcast.info.refs_0_, bf16[1920,3072]{1,0:T(8,128)(2,1)} %bitcast.237, bf16[1920,768]{1,0:T(8,128)(2,1)} %bitcast.245, bf16[1536,768]{1,0:T(8,128)(2,1)} %shard_map.244.refs_0_), custom_call_target="tpu_custom_call" | custom-call | flops 94371840 | bytes 100000 | tf_op jit(solution)/shard_map/pallas_call | solution.py:629
  258.0 5.9 %shard_map.250 = bf16[1536,768]{1,0:T(8,128)(2,1)} custom-call(s32[1]{0:T(128)} %bitcast.info.refs_0_, bf16[1920,3072]{1,0:T(8,128)(2,1)} %bitcast.238, bf16[1920,768]{1,0:T(8,128)(2,1)} %bitcast.246, bf16[1536,768]{1,0:T(8,128)(2,1)} %shard_map.246.refs_0_), custom_call_target="tpu_custom_call" | custom-call | flops 94371840 | bytes 100000 | tf_op jit(solution)/shard_map/pallas_call | solution.py:629
  263.9 5.6 %shard_map.251 = bf16[384,3072]{1,0:T(8,128)(2,1)} custom-call(s32[1]{0:T(128)} %bitcast.info.refs_0_, bf16[1920,768]{1,0:T(8,128)(2,1)} %bitcast.253, bf16[1920,3072]{1,0:T(8,128)(2,1)} %bitcast.215, bf16[384,3072]{1,0:T(8,128)(2,1)} %shard_map.245.refs_0_), custom_call_target="tpu_custom_call" | custom-call | flops 94371840 | bytes 100000 | tf_op jit(solution)/shard_map/pallas_call | solution.py:629
  270.0 2.3 add_convert_fusion.1
  276.5 5.2 %shard_map.252 = bf16[384,3072]{1,0:T(8,128)(2,1)} custom-call(s32[1]{0:T(128)} %bitcast.info.refs_0_, bf16[1920,768]{1,0:T(8,128)(2,1)} %bitcast.254, bf16[1920,3072]{1,0:T(8,128)(2,1)} %bitcast.216, bf16[384,3072]{1,0:T(8,128)(2,1)} %shard_map.247.refs_0_), custom_call_target="tpu_custom_call" | custom-call | flops 94371840 | bytes 100000 | tf_op jit(solution)/shard_map/pallas_call | solution.py:629
  281.7 3.3 add_convert_fusion
  290.8 8.5 %shard_map.253 = (bf16[3,640,768]{2,1,0:T(8,128)(2,1)}, bf16[3,640,768]{2,1,0:T(8,128)(2,1)}, bf16[3,640,768]{2,1,0:T(8,128)(2,1)}, f32[3,3,8,512]{3,2,1,0:T(8,128)}) custom-call(s32[17]{0:T(128)} %pad_add_fusion.info, bf16[3,640,768]{2,1,0:T(8,128)(2,1)} %get-tuple-element.272.refs_0_, ...), custom_call_target="tpu_custom_call", output_to_operand_aliasing={{0}: (6, {}), {1}: (7, {}), {2}: (8, {}), {3}: (9, {})} | custom-call | flops 208333328 | bytes 347222 | tf_op jit(solution)/shard_map/pallas_call | solution.py:174
  299.3 5.4 %shard_map.254 = bf16[384,1536]{1,0:T(8,128)(2,1)} custom-call(s32[1]{0:T(128)} %bitcast.info.refs_0_, bf16[1920,768]{1,0:T(8,128)(2,1)} %bitcast.247, bf16[1920,768]{1,0:T(8,128)(2,1)} %bitcast.241, bf16[1920,768]{1,0:T(8,128)(2,1)} %bitcast.239, bf16[1920,768]{1,0:T(8,128)(2,1)} %bitcast.217, bf16[1920,768]{1,0:T(8,128)(2,1)} %bitcast.223, ...), custom_call_target="tpu_custom_call" | custom-call | flops 94371840 | bytes 100000 | tf_op jit(solution)/shard_map/pallas_call | solution.py:629
  304.7 5.6 %shard_map.255 = bf16[384,1536]{1,0:T(8,128)(2,1)} custom-call(s32[1]{0:T(128)} %bitcast.info.refs_0_, bf16[1920,768]{1,0:T(8,128)(2,1)} %bitcast.248, bf16[1920,768]{1,0:T(8,128)(2,1)} %bitcast.242, bf16[1920,768]{1,0:T(8,128)(2,1)} %bitcast.240, bf16[1920,768]{1,0:T(8,128)(2,1)} %bitcast.218, bf16[1920,768]{1,0:T(8,128)(2,1)} %bitcast.224, ...), custom_call_target="tpu_custom_call" | custom-call | flops 94371840 | bytes 100000 | tf_op jit(solution)/shard_map/pallas_call | solution.py:629
  312.5 8.5 %shard_map.256 = (bf16[3,640,768]{2,1,0:T(8,128)(2,1)}, bf16[3,640,768]{2,1,0:T(8,128)(2,1)}, bf16[3,640,768]{2,1,0:T(8,128)(2,1)}, f32[3,3,8,512]{3,2,1,0:T(8,128)}) custom-call(s32[17]{0:T(128)} %pad_add_fusion.info, bf16[3,640,768]{2,1,0:T(8,128)(2,1)} %get-tuple-element.272.refs_0_, ...), custom_call_target="tpu_custom_call", output_to_operand_aliasing={{0}: (6, {}), {1}: (7, {}), {2}: (8, {}), {3}: (9, {})} | custom-call | flops 208333328 | bytes 347222 | tf_op jit(solution)/shard_map/pallas_call | solution.py:174
  326.2 2.1 collective-permute-done.11
  330.3 2.4 collective-permute-start.13
  332.6 8.7 %shard_map.257 = (bf16[3,640,768]{2,1,0:T(8,128)(2,1)}, bf16[3,640,768]{2,1,0:T(8,128)(2,1)}, bf16[3,640,768]{2,1,0:T(8,128)(2,1)}, f32[3,3,8,512]{3,2,1,0:T(8,128)}) custom-call(s32[17]{0:T(128)} %pad_add_fusion.info, bf16[3,640,768]{2,1,0:T(8,128)(2,1)} %get-tuple-element.272.refs_0_, ...), custom_call_target="tpu_custom_call", output_to_operand_aliasing={{0}: (6, {}), {1}: (7, {}), {2}: (8, {}), {3}: (9, {})} | custom-call | flops 208333328 | bytes 347222 | tf_op jit(solution)/shard_map/pallas_call | solution.py:174
  343.7 5.1 %shard_map.258 = bf16[384,1536]{1,0:T(8,128)(2,1)} custom-call(s32[1]{0:T(128)} %bitcast.info.refs_0_, bf16[1920,768]{1,0:T(8,128)(2,1)} %bitcast.249, bf16[1920,768]{1,0:T(8,128)(2,1)} %bitcast.219, bf16[1920,768]{1,0:T(8,128)(2,1)} %bitcast.225, bf16[1920,768]{1,0:T(8,128)(2,1)} %bitcast.231, bf16[1920,768]{1,0:T(8,128)(2,1)} %bitcast.220, ...), custom_call_target="tpu_custom_call" | custom-call | flops 94371840 | bytes 100000 | tf_op jit(solution)/shard_map/pallas_call | solution.py:629
  355.3 2.4 collective-permute-start.17
  357.7 5.1 %shard_map.259 = bf16[384,1536]{1,0:T(8,128)(2,1)} custom-call(s32[1]{0:T(128)} %bitcast.info.refs_0_, bf16[1920,768]{1,0:T(8,128)(2,1)} %bitcast.250, bf16[1920,768]{1,0:T(8,128)(2,1)} %bitcast.221, bf16[1920,768]{1,0:T(8,128)(2,1)} %bitcast.227, bf16[1920,768]{1,0:T(8,128)(2,1)} %bitcast.233, bf16[1920,768]{1,0:T(8,128)(2,1)} %bitcast.222, ...), custom_call_target="tpu_custom_call" | custom-call | flops 94371840 | bytes 100000 | tf_op jit(solution)/shard_map/pallas_call | solution.py:629
  364.4 3.3 collective-permute-done.15
  370.4 9.8 %collective-permute-done.17 = bf16[192,768]{1,0:T(8,128)(2,1)S(1)} collective-permute-done((bf16[192,768]{1,0:T(8,128)(2,1)S(1)}, bf16[192,768]{1,0:T(8,128)(2,1)S(1)}, u32[]{:S(2)}, u32[]{:S(2)}) %collective-permute-start.17) | collective-permute-done | bytes 294944 | tf_op jit(solution)/shard_map/ppermute | solution.py:778
  382.1 7.8 %collective-permute-done.19 = bf16[48,3072]{1,0:T(8,128)(2,1)S(1)} collective-permute-done((bf16[48,3072]{1,0:T(8,128)(2,1)S(1)}, bf16[48,3072]{1,0:T(8,128)(2,1)S(1)}, u32[]{:S(2)}, u32[]{:S(2)}) %collective-permute-start.19) | collective-permute-done | bytes 294944 | tf_op jit(solution)/shard_map/ppermute | solution.py:778
  394.1 13.2 %collective-permute-done.23 = bf16[384,768]{1,0:T(8,128)(2,1)S(1)} collective-permute-done((bf16[384,768]{1,0:T(8,128)(2,1)S(1)}, bf16[384,768]{1,0:T(8,128)(2,1)S(1)}, u32[]{:S(2)}, u32[]{:S(2)}) %collective-permute-start.23) | collective-permute-done | bytes 589856 | tf_op jit(solution)/shard_map/ppermute | solution.py:778
  408.4 2.6 collective-permute-done.25
  411.1 2.5 collective-permute-done.26
  414.6 25.5 %collective-permute-done.28 = bf16[48,1536]{1,0:T(8,128)(2,1)S(1)} collective-permute-done((bf16[48,1536]{1,0:T(8,128)(2,1)S(1)}, bf16[48,1536]{1,0:T(8,128)(2,1)S(1)}, u32[]{:S(2)}, u32[]{:S(2)}) %collective-permute-start.28) | collective-permute-done | bytes 147488 | tf_op jit(solution)/shard_map/ppermute | solution.py:778
  440.1 3.5 collective-permute-start.29
  443.7 4.8 collective-permute-done.29
  449.3 2.2 collective-permute-start.36
  451.5 1.9 collective-permute-start.37
  453.5 7.9 %collective-permute-done.33 = bf16[96,1536]{1,0:T(8,128)(2,1)S(1)} collective-permute-done((bf16[96,1536]{1,0:T(8,128)(2,1)S(1)}, bf16[96,1536]{1,0:T(8,128)(2,1)S(1)}, u32[]{:S(2)}, u32[]{:S(2)}) %collective-permute-start.33) | collective-permute-done | bytes 294944 | tf_op jit(solution)/shard_map/ppermute | solution.py:778
  463.3 4.1 shard_map.260
  467.6 5.1 %collective-permute-done.37 = bf16[192,1536]{1,0:T(8,128)(2,1)S(1)} collective-permute-done((bf16[192,1536]{1,0:T(8,128)(2,1)S(1)}, bf16[192,1536]{1,0:T(8,128)(2,1)S(1)}, u32[]{:S(2)}, u32[]{:S(2)}) %collective-permute-start.37) | collective-permute-done | bytes 589856 | tf_op jit(solution)/shard_map/ppermute | solution.py:778
  475.0 2.6 collective-permute-start.42
  477.6 4.1 shard_map.261
  490.7 5.3 %shard_map.262 = (f32[768,2304]{1,0:T(8,128)}, f32[768,768]{1,0:T(8,128)}) custom-call(s32[1]{0:T(128)} %bitcast.info.refs_0_, bf16[384,1536]{1,0:T(8,128)(2,1)S(1)} %bitcast.212, bf16[384,1536]{1,0:T(8,128)(2,1)S(1)} %bitcast.210, bf16[384,1536]{1,0:T(8,128)(2,1)S(1)} %collective-permute-done.40.refs_2_, bf16[384,1536]{1,0:T(8,128)(2,1)} %collective-permute-done.41.refs_3_), custom_call_target="tpu_custom_call" | custom-call | bytes 14000000 | tf_op jit(solution)/shard_map/pallas_call | solution.py:734
  (208 shorter events, 75.3 us)
Async XLA Ops:
  36.7 36.1 %collective-permute-start.1 = (bf16[640,768]{1,0:T(8,128)(2,1)}, bf16[640,768]{1,0:T(8,128)(2,1)S(1)}, u32[]{:S(2)}, u32[]{:S(2)}) collective-permute-start(bf16[640,768]{1,0:T(8,128)(2,1)} %get-tuple-element.188), channel_id=1, source_target_pairs={{0,16},{1,17},{2,18},{3,19},{4,20},{5,21},{6,22},{7,23},{8,24},{9,... | collective-permute-start | bytes 2949128 | tf_op jit(solution)/shard_map/ppermute | solution.py:765
  71.0 23.5 %collective-permute-start = (bf16[640,768]{1,0:T(8,128)(2,1)}, bf16[640,768]{1,0:T(8,128)(2,1)S(1)}, u32[]{:S(2)}, u32[]{:S(2)}) collective-permute-start(bf16[640,768]{1,0:T(8,128)(2,1)} %get-tuple-element.187), channel_id=1, source_target_pairs={{0,16},{1,17},{2,18},{3,19},{4,20},{5,21},{6,22},{7,23},{8,24},{9,... | collective-permute-start | bytes 2949128 | tf_op jit(solution)/shard_map/ppermute | solution.py:765
  94.5 63.6 %collective-permute-start.3 = (bf16[640,768]{1,0:T(8,128)(2,1)}, bf16[640,768]{1,0:T(8,128)(2,1)S(1)}, u32[]{:S(2)}, u32[]{:S(2)}) collective-permute-start(bf16[640,768]{1,0:T(8,128)(2,1)} %get-tuple-element.241), channel_id=1, source_target_pairs={{16,0},{17,1},{18,2},{19,3},{20,4},{21,5},{22,6},{23,7},{24,8},{25... | collective-permute-start | bytes 2949128 | tf_op jit(solution)/shard_map/ppermute | solution.py:765
  115.7 116.3 %collective-permute-start.2 = (bf16[640,768]{1,0:T(8,128)(2,1)}, bf16[640,768]{1,0:T(8,128)(2,1)S(1)}, u32[]{:S(2)}, u32[]{:S(2)}) collective-permute-start(bf16[640,768]{1,0:T(8,128)(2,1)} %get-tuple-element.238), channel_id=1, source_target_pairs={{16,0},{17,1},{18,2},{19,3},{20,4},{21,5},{22,6},{23,7},{24,8},{25... | collective-permute-start | bytes 2949128 | tf_op jit(solution)/shard_map/ppermute | solution.py:765
  117.9 79.3 %copy-start.8 = (f32[2]{0:T(128)}, f32[2]{0:T(128)S(1)}, u32[]{:S(2)}) copy-start(f32[2]{0:T(128)S(1)} %slice_reduce_fusion.3) | copy-start | bytes 28
  118.8 78.3 %copy-start.10 = (f32[2]{0:T(128)}, f32[2]{0:T(128)S(1)}, u32[]{:S(2)}) copy-start(f32[2]{0:T(128)S(1)} %get-tuple-element.359) | copy-start | bytes 28
  118.8 78.3 %copy-start.11 = (f32[2]{0:T(128)}, f32[2]{0:T(128)S(1)}, u32[]{:S(2)}) copy-start(f32[2]{0:T(128)S(1)} %get-tuple-element.360) | copy-start | bytes 28
  159.0 34.3 %copy-start.18 = (bf16[3,640,768]{2,1,0:T(8,128)(2,1)S(1)}, bf16[3,640,768]{2,1,0:T(8,128)(2,1)}, u32[]{:S(2)}) copy-start(bf16[3,640,768]{2,1,0:T(8,128)(2,1)} %get-tuple-element.220.refs_0_) | copy-start | bytes 8847364
  195.0 40.4 %collective-permute-start.5 = (bf16[768,128]{1,0:T(8,128)(2,1)S(1)}, bf16[768,128]{1,0:T(8,128)(2,1)S(1)}, u32[]{:S(2)}, u32[]{:S(2)}) collective-permute-start(bf16[768,128]{1,0:T(8,128)(2,1)S(1)} %fusion.6), channel_id=1, source_target_pairs={{16,0},{17,1},{18,2},{19,3},{20,4},{21,5},{22,6},{23,7},{24,8},{25... | collective-permute-start | bytes 589832 | tf_op jit(solution)/shard_map/ppermute | solution.py:765
  197.7 37.7 %collective-permute-start.4 = (f32[2,4]{0,1:T(4,128)}, f32[2,4]{0,1:T(4,128)S(1)}, u32[]{:S(2)}, u32[]{:S(2)}) collective-permute-start(f32[2,4]{0,1:T(4,128)} %pad_maximum_fusion.2), channel_id=1, source_target_pairs={{16,0},{17,1},{18,2},{19,3},{20,4},{21,5},{22,6},{23,7},{24,8},{25... | collective-permute-start | bytes 104 | tf_op jit(solution)/shard_map/ppermute | solution.py:765
  235.4 16.6 %copy-start.12 = (f32[2,4]{0,1:T(4,128)}, f32[2,4]{0,1:T(4,128)S(1)}, u32[]{:S(2)}) copy-start(f32[2,4]{0,1:T(4,128)S(1)} %collective-permute-done.4) | copy-start | bytes 100
  258.0 12.1 %collective-permute-start.6 = (bf16[1536,768]{1,0:T(8,128)(2,1)}, bf16[1536,768]{1,0:T(8,128)(2,1)}, u32[]{:S(2)}, u32[]{:S(2)}) collective-permute-start(bf16[1536,768]{1,0:T(8,128)(2,1)} %shard_map.249), channel_id=1, source_target_pairs={{0,1},{1,0},{2,3},{3,2},{4,5},{5,4},{6,7},{7,6},{8,9},{9,8},{10,11... | collective-permute-start | bytes 7077896 | tf_op jit(solution)/shard_map/ppermute | solution.py:778
  269.5 12.3 %collective-permute-start.7 = (bf16[384,3072]{1,0:T(8,128)(2,1)}, bf16[384,3072]{1,0:T(8,128)(2,1)}, u32[]{:S(2)}, u32[]{:S(2)}) collective-permute-start(bf16[384,3072]{1,0:T(8,128)(2,1)} %shard_map.251), channel_id=1, source_target_pairs={{0,1},{1,0},{2,3},{3,2},{4,5},{5,4},{6,7},{7,6},{8,9},{9,8},{10,11... | collective-permute-start | bytes 7077896 | tf_op jit(solution)/shard_map/ppermute | solution.py:778
  274.8 35.6 %collective-permute-start.8 = (bf16[768,768]{1,0:T(8,128)(2,1)}, bf16[768,768]{1,0:T(8,128)(2,1)}, u32[]{:S(2)}, u32[]{:S(2)}) collective-permute-start(bf16[768,768]{1,0:T(8,128)(2,1)} %dynamic-slice_bitcast_fusion.1), channel_id=1, source_target_pairs={{0,2},{1,3},{2,0},{3,1},{4,6},{5,7},{6,4},{7,5},{8,10},{9,11},{10,... | collective-permute-start | bytes 3538952 | tf_op jit(solution)/shard_map/ppermute | solution.py:778
  286.1 34.9 %collective-permute-start.9 = (bf16[192,3072]{1,0:T(8,128)(2,1)}, bf16[192,3072]{1,0:T(8,128)(2,1)}, u32[]{:S(2)}, u32[]{:S(2)}) collective-permute-start(bf16[192,3072]{1,0:T(8,128)(2,1)} %dynamic-slice_bitcast_fusion), channel_id=1, source_target_pairs={{0,4},{1,5},{2,6},{3,7},{4,0},{5,1},{6,2},{7,3},{8,12},{9,13},{10,... | collective-permute-start | bytes 3538952 | tf_op jit(solution)/shard_map/ppermute | solution.py:778
  304.7 18.5 %collective-permute-start.10 = (bf16[384,1536]{1,0:T(8,128)(2,1)}, bf16[384,1536]{1,0:T(8,128)(2,1)S(1)}, u32[]{:S(2)}, u32[]{:S(2)}) collective-permute-start(bf16[384,1536]{1,0:T(8,128)(2,1)} %shard_map.254), channel_id=1, source_target_pairs={{0,1},{1,0},{2,3},{3,2},{4,5},{5,4},{6,7},{7,6},{8,9},{9,8},{10,11... | collective-permute-start | bytes 3538952 | tf_op jit(solution)/shard_map/ppermute | solution.py:778
  312.0 16.3 %collective-permute-start.11 = (bf16[384,768]{1,0:T(8,128)(2,1)S(1)}, bf16[384,768]{1,0:T(8,128)(2,1)}, u32[]{:S(2)}, u32[]{:S(2)}) collective-permute-start(bf16[384,768]{1,0:T(8,128)(2,1)S(1)} %dynamic-slice_bitcast_fusion.5), channel_id=1, source_target_pairs={{0,4},{1,5},{2,6},{3,7},{4,0},{5,1},{6,2},{7,3},{8,12},{9,13},{10,... | collective-permute-start | bytes 1769480 | tf_op jit(solution)/shard_map/ppermute | solution.py:778
  322.8 18.5 %collective-permute-start.12 = (bf16[96,3072]{1,0:T(8,128)(2,1)S(1)}, bf16[96,3072]{1,0:T(8,128)(2,1)S(1)}, u32[]{:S(2)}, u32[]{:S(2)}) collective-permute-start(bf16[96,3072]{1,0:T(8,128)(2,1)S(1)} %dynamic-slice_bitcast_fusion.4), channel_id=1, source_target_pairs={{0,2},{1,3},{2,0},{3,1},{4,6},{5,7},{6,4},{7,5},{8,10},{9,11},{10,... | collective-permute-start | bytes 1769480 | tf_op jit(solution)/shard_map/ppermute | solution.py:778
  324.4 38.5 %collective-permute-start.14 = (bf16[192,1536]{1,0:T(8,128)(2,1)}, bf16[192,1536]{1,0:T(8,128)(2,1)}, u32[]{:S(2)}, u32[]{:S(2)}) collective-permute-start(bf16[192,1536]{1,0:T(8,128)(2,1)} %dynamic-slice_bitcast_fusion.3), channel_id=1, source_target_pairs={{0,4},{1,5},{2,6},{3,7},{4,0},{5,1},{6,2},{7,3},{8,12},{9,13},{10,... | collective-permute-start | bytes 1769480 | tf_op jit(solution)/shard_map/ppermute | solution.py:778
  330.3 24.0 %collective-permute-start.13 = (bf16[192,768]{1,0:T(8,128)(2,1)}, bf16[192,768]{1,0:T(8,128)(2,1)}, u32[]{:S(2)}, u32[]{:S(2)}) collective-permute-start(bf16[192,768]{1,0:T(8,128)(2,1)} %dynamic-slice_bitcast_fusion.9), channel_id=1, source_target_pairs={{0,8},{1,9},{2,10},{3,11},{4,12},{5,13},{6,14},{7,15},{8,0},{9,1},... | collective-permute-start | bytes 884744 | tf_op jit(solution)/shard_map/ppermute | solution.py:778
  342.3 25.5 %collective-permute-start.15 = (bf16[48,3072]{1,0:T(8,128)(2,1)}, bf16[48,3072]{1,0:T(8,128)(2,1)}, u32[]{:S(2)}, u32[]{:S(2)}) collective-permute-start(bf16[48,3072]{1,0:T(8,128)(2,1)} %dynamic-slice_bitcast_fusion.8), channel_id=1, source_target_pairs={{0,8},{1,9},{2,10},{3,11},{4,12},{5,13},{6,14},{7,15},{8,0},{9,1},... | collective-permute-start | bytes 884744 | tf_op jit(solution)/shard_map/ppermute | solution.py:778
  348.9 20.0 %collective-permute-start.16 = (bf16[384,1536]{1,0:T(8,128)(2,1)}, bf16[384,1536]{1,0:T(8,128)(2,1)S(1)}, u32[]{:S(2)}, u32[]{:S(2)}) collective-permute-start(bf16[384,1536]{1,0:T(8,128)(2,1)} %shard_map.258), channel_id=1, source_target_pairs={{0,1},{1,0},{2,3},{3,2},{4,5},{5,4},{6,7},{7,6},{8,9},{9,8},{10,11... | collective-permute-start | bytes 3538952 | tf_op jit(solution)/shard_map/ppermute | solution.py:778
  353.7 36.2 %collective-permute-start.20 = (bf16[140,768]{1,0:T(8,128)(2,1)S(1)}, bf16[140,768]{1,0:T(8,128)(2,1)S(1)}, u32[]{:S(2)}, u32[]{:S(2)}) collective-permute-start(bf16[140,768]{1,0:T(8,128)(2,1)S(1)} %pad_maximum_fusion), channel_id=1, source_target_pairs={{0,1},{1,0},{2,3},{3,2},{4,5},{5,4},{6,7},{7,6},{8,9},{9,8},{10,11... | collective-permute-start | bytes 645128 | tf_op jit(solution)/shard_map/ppermute | solution.py:778
  355.3 25.0 %collective-permute-start.17 = (bf16[192,768]{1,0:T(8,128)(2,1)S(1)}, bf16[192,768]{1,0:T(8,128)(2,1)S(1)}, u32[]{:S(2)}, u32[]{:S(2)}) collective-permute-start(bf16[192,768]{1,0:T(8,128)(2,1)S(1)} %fusion.10), channel_id=1, source_target_pairs={{0,8},{1,9},{2,10},{3,11},{4,12},{5,13},{6,14},{7,15},{8,0},{9,1},... | collective-permute-start | bytes 884744 | tf_op jit(solution)/shard_map/ppermute | solution.py:778
  364.2 16.1 %collective-permute-start.18 = (bf16[96,1536]{1,0:T(8,128)(2,1)S(1)}, bf16[96,1536]{1,0:T(8,128)(2,1)S(1)}, u32[]{:S(2)}, u32[]{:S(2)}) collective-permute-start(bf16[96,1536]{1,0:T(8,128)(2,1)S(1)} %dynamic-slice_bitcast_fusion.7), channel_id=1, source_target_pairs={{0,2},{1,3},{2,0},{3,1},{4,6},{5,7},{6,4},{7,5},{8,10},{9,11},{10,... | collective-permute-start | bytes 884744 | tf_op jit(solution)/shard_map/ppermute | solution.py:778
  368.8 21.1 %collective-permute-start.19 = (bf16[48,3072]{1,0:T(8,128)(2,1)S(1)}, bf16[48,3072]{1,0:T(8,128)(2,1)S(1)}, u32[]{:S(2)}, u32[]{:S(2)}) collective-permute-start(bf16[48,3072]{1,0:T(8,128)(2,1)S(1)} %fusion.9), channel_id=1, source_target_pairs={{0,8},{1,9},{2,10},{3,11},{4,12},{5,13},{6,14},{7,15},{8,0},{9,1},... | collective-permute-start | bytes 884744 | tf_op jit(solution)/shard_map/ppermute | solution.py:778
  369.2 22.8 %collective-permute-start.21 = (bf16[192,1536]{1,0:T(8,128)(2,1)S(1)}, bf16[192,1536]{1,0:T(8,128)(2,1)S(1)}, u32[]{:S(2)}, u32[]{:S(2)}) collective-permute-start(bf16[192,1536]{1,0:T(8,128)(2,1)S(1)} %dynamic-slice_bitcast_fusion.2), channel_id=1, source_target_pairs={{0,2},{1,3},{2,0},{3,1},{4,6},{5,7},{6,4},{7,5},{8,10},{9,11},{10,... | collective-permute-start | bytes 1769480 | tf_op jit(solution)/shard_map/ppermute | solution.py:778
  380.4 12.5 %collective-permute-start.22 = (bf16[48,1536]{1,0:T(8,128)(2,1)S(1)}, bf16[48,1536]{1,0:T(8,128)(2,1)S(1)}, u32[]{:S(2)}, u32[]{:S(2)}) collective-permute-start(bf16[48,1536]{1,0:T(8,128)(2,1)S(1)} %dynamic-slice_bitcast_fusion.11), channel_id=1, source_target_pairs={{0,8},{1,9},{2,10},{3,11},{4,12},{5,13},{6,14},{7,15},{8,0},{9,1},... | collective-permute-start | bytes 442376 | tf_op jit(solution)/shard_map/ppermute | solution.py:778
  380.5 26.8 %collective-permute-start.23 = (bf16[384,768]{1,0:T(8,128)(2,1)S(1)}, bf16[384,768]{1,0:T(8,128)(2,1)S(1)}, u32[]{:S(2)}, u32[]{:S(2)}) collective-permute-start(bf16[384,768]{1,0:T(8,128)(2,1)S(1)} %bitcast.299), channel_id=1, source_target_pairs={{0,4},{1,5},{2,6},{3,7},{4,0},{5,1},{6,2},{7,3},{8,12},{9,13},{10,... | collective-permute-start | bytes 1769480 | tf_op jit(solution)/shard_map/ppermute | solution.py:778
  390.0 18.1 %collective-permute-start.24 = (bf16[140,768]{1,0:T(8,128)(2,1)S(1)}, bf16[140,768]{1,0:T(8,128)(2,1)S(1)}, u32[]{:S(2)}, u32[]{:S(2)}) collective-permute-start(bf16[140,768]{1,0:T(8,128)(2,1)S(1)} %add_convert_fusion.7), channel_id=1, source_target_pairs={{0,2},{1,3},{2,0},{3,1},{4,6},{5,7},{6,4},{7,5},{8,10},{9,11},{10,... | collective-permute-start | bytes 645128 | tf_op jit(solution)/shard_map/ppermute | solution.py:778
  391.1 19.9 %collective-permute-start.25 = (bf16[96,3072]{1,0:T(8,128)(2,1)S(1)}, bf16[96,3072]{1,0:T(8,128)(2,1)S(1)}, u32[]{:S(2)}, u32[]{:S(2)}) collective-permute-start(bf16[96,3072]{1,0:T(8,128)(2,1)S(1)} %bitcast.301), channel_id=1, source_target_pairs={{0,2},{1,3},{2,0},{3,1},{4,6},{5,7},{6,4},{7,5},{8,10},{9,11},{10,... | collective-permute-start | bytes 1769480 | tf_op jit(solution)/shard_map/ppermute | solution.py:778
  392.3 21.4 %collective-permute-start.26 = (bf16[96,1536]{1,0:T(8,128)(2,1)S(1)}, bf16[96,1536]{1,0:T(8,128)(2,1)S(1)}, u32[]{:S(2)}, u32[]{:S(2)}) collective-permute-start(bf16[96,1536]{1,0:T(8,128)(2,1)S(1)} %dynamic-slice_bitcast_fusion.6), channel_id=1, source_target_pairs={{0,4},{1,5},{2,6},{3,7},{4,0},{5,1},{6,2},{7,3},{8,12},{9,13},{10,... | collective-permute-start | bytes 884744 | tf_op jit(solution)/shard_map/ppermute | solution.py:778
  393.0 20.9 %collective-permute-start.27 = (bf16[48,1536]{1,0:T(8,128)(2,1)S(1)}, bf16[48,1536]{1,0:T(8,128)(2,1)S(1)}, u32[]{:S(2)}, u32[]{:S(2)}) collective-permute-start(bf16[48,1536]{1,0:T(8,128)(2,1)S(1)} %fusion.13), channel_id=1, source_target_pairs={{0,8},{1,9},{2,10},{3,11},{4,12},{5,13},{6,14},{7,15},{8,0},{9,1},... | collective-permute-start | bytes 442376 | tf_op jit(solution)/shard_map/ppermute | solution.py:778
  407.3 41.5 %collective-permute-start.30 = (bf16[768,768]{1,0:T(8,128)(2,1)S(1)}, bf16[768,768]{1,0:T(8,128)(2,1)S(1)}, u32[]{:S(2)}, u32[]{:S(2)}) collective-permute-start(bf16[768,768]{1,0:T(8,128)(2,1)S(1)} %bitcast.291), channel_id=1, source_target_pairs={{0,2},{1,3},{2,0},{3,1},{4,6},{5,7},{6,4},{7,5},{8,10},{9,11},{10,... | collective-permute-start | bytes 3538952 | tf_op jit(solution)/shard_map/ppermute | solution.py:778
  408.1 41.1 %collective-permute-start.32 = (bf16[140,768]{1,0:T(8,128)(2,1)S(1)}, bf16[140,768]{1,0:T(8,128)(2,1)S(1)}, u32[]{:S(2)}, u32[]{:S(2)}) collective-permute-start(bf16[140,768]{1,0:T(8,128)(2,1)S(1)} %add_convert_fusion.6), channel_id=1, source_target_pairs={{0,4},{1,5},{2,6},{3,7},{4,0},{5,1},{6,2},{7,3},{8,12},{9,13},{10,... | collective-permute-start | bytes 645128 | tf_op jit(solution)/shard_map/ppermute | solution.py:778
  411.0 52.0 %collective-permute-start.34 = (bf16[192,3072]{1,0:T(8,128)(2,1)S(1)}, bf16[192,3072]{1,0:T(8,128)(2,1)S(1)}, u32[]{:S(2)}, u32[]{:S(2)}) collective-permute-start(bf16[192,3072]{1,0:T(8,128)(2,1)S(1)} %bitcast.293), channel_id=1, source_target_pairs={{0,4},{1,5},{2,6},{3,7},{4,0},{5,1},{6,2},{7,3},{8,12},{9,13},{10,... | collective-permute-start | bytes 3538952 | tf_op jit(solution)/shard_map/ppermute | solution.py:778
  413.7 26.4 %collective-permute-start.28 = (bf16[48,1536]{1,0:T(8,128)(2,1)S(1)}, bf16[48,1536]{1,0:T(8,128)(2,1)S(1)}, u32[]{:S(2)}, u32[]{:S(2)}) collective-permute-start(bf16[48,1536]{1,0:T(8,128)(2,1)S(1)} %dynamic-slice_bitcast_fusion.10), channel_id=1, source_target_pairs={{0,8},{1,9},{2,10},{3,11},{4,12},{5,13},{6,14},{7,15},{8,0},{9,1},... | collective-permute-start | bytes 442376 | tf_op jit(solution)/shard_map/ppermute | solution.py:778
  413.9 35.3 %collective-permute-start.31 = (bf16[96,1536]{1,0:T(8,128)(2,1)S(1)}, bf16[96,1536]{1,0:T(8,128)(2,1)S(1)}, u32[]{:S(2)}, u32[]{:S(2)}) collective-permute-start(bf16[96,1536]{1,0:T(8,128)(2,1)S(1)} %bitcast.321), channel_id=1, source_target_pairs={{0,2},{1,3},{2,0},{3,1},{4,6},{5,7},{6,4},{7,5},{8,10},{9,11},{10,... | collective-permute-start | bytes 884744 | tf_op jit(solution)/shard_map/ppermute | solution.py:778
  440.1 8.4 %collective-permute-start.29 = (bf16[48,1536]{1,0:T(8,128)(2,1)S(1)}, bf16[48,1536]{1,0:T(8,128)(2,1)S(1)}, u32[]{:S(2)}, u32[]{:S(2)}) collective-permute-start(bf16[48,1536]{1,0:T(8,128)(2,1)S(1)} %fusion.12), channel_id=1, source_target_pairs={{0,8},{1,9},{2,10},{3,11},{4,12},{5,13},{6,14},{7,15},{8,0},{9,1},... | collective-permute-start | bytes 442376 | tf_op jit(solution)/shard_map/ppermute | solution.py:778
  448.5 12.9 %collective-permute-start.33 = (bf16[96,1536]{1,0:T(8,128)(2,1)S(1)}, bf16[96,1536]{1,0:T(8,128)(2,1)S(1)}, u32[]{:S(2)}, u32[]{:S(2)}) collective-permute-start(bf16[96,1536]{1,0:T(8,128)(2,1)S(1)} %bitcast.319), channel_id=1, source_target_pairs={{0,4},{1,5},{2,6},{3,7},{4,0},{5,1},{6,2},{7,3},{8,12},{9,13},{10,... | collective-permute-start | bytes 884744 | tf_op jit(solution)/shard_map/ppermute | solution.py:778
  449.0 14.3 %collective-permute-start.35 = (bf16[1536,768]{1,0:T(8,128)(2,1)S(1)}, bf16[1536,768]{1,0:T(8,128)(2,1)S(1)}, u32[]{:S(2)}, u32[]{:S(2)}) collective-permute-start(bf16[1536,768]{1,0:T(8,128)(2,1)S(1)} %bitcast.205), channel_id=1, source_target_pairs={{0,1},{1,0},{2,3},{3,2},{4,5},{5,4},{6,7},{7,6},{8,9},{9,8},{10,11... | collective-permute-start | bytes 7077896 | tf_op jit(solution)/shard_map/ppermute | solution.py:778
  449.3 18.1 %collective-permute-start.36 = (bf16[140,768]{1,0:T(8,128)(2,1)S(1)}, bf16[140,768]{1,0:T(8,128)(2,1)S(1)}, u32[]{:S(2)}, u32[]{:S(2)}) collective-permute-start(bf16[140,768]{1,0:T(8,128)(2,1)S(1)} %add_convert_fusion.5), channel_id=1, source_target_pairs={{0,8},{1,9},{2,10},{3,11},{4,12},{5,13},{6,14},{7,15},{8,0},{9,1},... | collective-permute-start | bytes 645128 | tf_op jit(solution)/shard_map/ppermute | solution.py:778
  451.5 21.2 %collective-permute-start.37 = (bf16[192,1536]{1,0:T(8,128)(2,1)S(1)}, bf16[192,1536]{1,0:T(8,128)(2,1)S(1)}, u32[]{:S(2)}, u32[]{:S(2)}) collective-permute-start(bf16[192,1536]{1,0:T(8,128)(2,1)S(1)} %bitcast.303), channel_id=1, source_target_pairs={{0,4},{1,5},{2,6},{3,7},{4,0},{5,1},{6,2},{7,3},{8,12},{9,13},{10,... | collective-permute-start | bytes 1769480 | tf_op jit(solution)/shard_map/ppermute | solution.py:778
  461.4 11.5 %collective-permute-start.38 = (bf16[192,1536]{1,0:T(8,128)(2,1)S(1)}, bf16[192,1536]{1,0:T(8,128)(2,1)S(1)}, u32[]{:S(2)}, u32[]{:S(2)}) collective-permute-start(bf16[192,1536]{1,0:T(8,128)(2,1)S(1)} %bitcast.305), channel_id=1, source_target_pairs={{0,2},{1,3},{2,0},{3,1},{4,6},{5,7},{6,4},{7,5},{8,10},{9,11},{10,... | collective-permute-start | bytes 1769480 | tf_op jit(solution)/shard_map/ppermute | solution.py:778
  463.2 14.4 %collective-permute-start.39 = (bf16[384,3072]{1,0:T(8,128)(2,1)S(1)}, bf16[384,3072]{1,0:T(8,128)(2,1)S(1)}, u32[]{:S(2)}, u32[]{:S(2)}) collective-permute-start(bf16[384,3072]{1,0:T(8,128)(2,1)S(1)} %bitcast.207), channel_id=1, source_target_pairs={{0,1},{1,0},{2,3},{3,2},{4,5},{5,4},{6,7},{7,6},{8,9},{9,8},{10,11... | collective-permute-start | bytes 7077896 | tf_op jit(solution)/shard_map/ppermute | solution.py:778
  472.7 18.0 %collective-permute-start.40 = (bf16[384,1536]{1,0:T(8,128)(2,1)S(1)}, bf16[384,1536]{1,0:T(8,128)(2,1)S(1)}, u32[]{:S(2)}, u32[]{:S(2)}) collective-permute-start(bf16[384,1536]{1,0:T(8,128)(2,1)S(1)} %bitcast.211), channel_id=1, source_target_pairs={{0,1},{1,0},{2,3},{3,2},{4,5},{5,4},{6,7},{7,6},{8,9},{9,8},{10,11... | collective-permute-start | bytes 3538952 | tf_op jit(solution)/shard_map/ppermute | solution.py:778
  473.0 17.7 %collective-permute-start.41 = (bf16[384,1536]{1,0:T(8,128)(2,1)S(1)}, bf16[384,1536]{1,0:T(8,128)(2,1)}, u32[]{:S(2)}, u32[]{:S(2)}) collective-permute-start(bf16[384,1536]{1,0:T(8,128)(2,1)S(1)} %bitcast.209), channel_id=1, source_target_pairs={{0,1},{1,0},{2,3},{3,2},{4,5},{5,4},{6,7},{7,6},{8,9},{9,8},{10,11... | collective-permute-start | bytes 3538952 | tf_op jit(solution)/shard_map/ppermute | solution.py:778
  475.0 13.0 %collective-permute-start.42 = (f32[2,4]{0,1:T(4,128)}, f32[2,4]{0,1:T(4,128)}, u32[]{:S(2)}, u32[]{:S(2)}) collective-permute-start(f32[2,4]{0,1:T(4,128)} %pad_maximum_fusion.2), channel_id=1, source_target_pairs={{0,16},{1,17},{2,18},{3,19},{4,20},{5,21},{6,22},{7,23},{8,24},{9,... | collective-permute-start | bytes 104 | tf_op jit(solution)/shard_map/ppermute | solution.py:765
  (14 other events, 63.7 us)
